TPU v7x, 32 devices: a whole 2x2x4 slice. The times are simulated.
32 devices in a mesh: rep: 8 (over z, x), shard: 4 (over y, core).
Axes of the slice: x: 2, y: 2, z: 4, core: 2. Of those that a mesh axis runs over, the one named last changes fastest.
Arguments:
- latents: float32 [64, 4096], P(('rep', 'shard')), may hold values from -6 to 6
- noises: float32 [64, 4096], P(('rep', 'shard')), may hold values from -6 to 6
- velocity: float32 [64, 4096], P(('rep', 'shard')), may hold values from -6 to 6
- times: int32 [64], P(('rep', 'shard')), may hold values from 0 to 988, as said below
- labels: int32 [64], P(('rep', 'shard')), may hold values from 0 to 999
- dropped: int32 [64], P(('rep', 'shard')), may hold values 0 or 1
- blocks_in: float32 [1, 768, 9984], P(None, None, 'shard'), may hold values from -0.21875 to 0.21875
- blocks_out: float32 [1, 3840, 768], P(None, None, 'shard'), may hold values from -0.21875 to 0.21875
- head_side: float32 [768, 2320], P(None, 'shard'), may hold values from -0.21875 to 0.21875
- embed_side: float32 [1273, 768], P(None, 'shard'), may hold values from -1.5 to 1.5
- state_in_row: float32 [1, 768], replicated, may hold values from 327.68 to 4915.2
- state_in_col: float32 [1, 9984], P(None, 'shard'), may hold values from 327.68 to 4915.2
- state_out_row: float32 [1, 3840], replicated, may hold values from 327.68 to 4915.2
- state_out_col: float32 [1, 768], P(None, 'shard'), may hold values from 327.68 to 4915.2
- state_head_row: float32 [768], replicated, may hold values from 327.68 to 4915.2
- state_head_col: float32 [2320], P('shard'), may hold values from 327.68 to 4915.2
- state_embed_row: float32 [1273], replicated, may hold values from 327.68 to 4915.2
- state_embed_col: float32 [768], P('shard'), may hold values from 327.68 to 4915.2
Outputs:
- loss_sum: float32 [], replicated
- update_rms: float32 [], replicated
- grad_in: float32 [1, 768, 9984], P(None, None, 'shard')
- grad_out: float32 [1, 3840, 768], P(None, None, 'shard')
- grad_head: float32 [768, 2320], P(None, 'shard')
- grad_embed: float32 [1273, 768], P(None, 'shard')
- new_in_row: float32 [1, 768], replicated
- new_in_col: float32 [1, 9984], P(None, 'shard')
- new_out_row: float32 [1, 3840], replicated
- new_out_col: float32 [1, 768], P(None, 'shard')
- new_head_row: float32 [768], replicated
- new_head_col: float32 [2320], P('shard')
- new_embed_row: float32 [1273], replicated
- new_embed_col: float32 [768], P('shard')
- new_in: float32 [1, 768, 9984], P(None, None, 'shard')
- new_out: float32 [1, 3840, 768], P(None, None, 'shard')
- new_head: float32 [768, 2320], P(None, 'shard')
- new_embed: float32 [1273, 768], P(None, 'shard')
Inputs may be any that keep to these rules, and one draw needn't show every extreme that they name: `times`: the time index of latent i is below 1000 (64 + 2 i) / 192; the first latent's is 0 and the last latent's is the largest value.
All inputs are finite; a program needn't handle non-finite values. No bound on the sum of `dropped` on one device may be relied on, other than what follows from the above.
Results may differ from a plain program's by a relative error of at most 0.012.
The roundings to bfloat16 on the way count: a program that leaves them out, or rounds other values in their place, can miss the bound.
Values may be sent and summed in bfloat16 or wider, within the bound.
A program may use at most 704 MiB of HBM per device.

v0:
```python
import math

import jax
import jax.numpy as jnp
from jax import lax
from jax.sharding import PartitionSpec as P

HEADS = 12
CLASSES = 1001
FREQ = 256
GRID = 16
PATCH = 16
LAYERS = 1
TOK = 256


decay = 0.5
eps_norm = 1e-06
eps_one = 1e-30
eps_two = 0.001
clip_level = 0.1
rate = 8.0
step_count = 1000.0


def silu(value):
    return value * jax.nn.sigmoid(value)


def gelu(value):
    return 0.5 * value * (1.0 + jnp.tanh(0.7978845608 * (value + 0.044715 * value * value * value)))


def norm_mod(hidden, shift, scale):
    center = hidden - jnp.mean(hidden, -1, keepdims=True)
    spread = jnp.mean(center * center, -1, keepdims=True)
    return center * lax.rsqrt(spread + eps_norm) * (1.0 + scale[:, None, :]) + shift[:, None, :]


def positions(grid, width):
    quarter = width // 4
    omega = 1.0 / 10000.0 ** (jnp.arange(quarter, dtype=jnp.float32) / quarter)
    index = jnp.arange(grid * grid, dtype=jnp.int32)
    row_pos = (index // grid).astype(jnp.float32)[:, None] * omega[None, :]
    col_pos = (index % grid).astype(jnp.float32)[:, None] * omega[None, :]
    return jnp.concatenate(
        [jnp.sin(row_pos), jnp.cos(row_pos), jnp.sin(col_pos), jnp.cos(col_pos)], 1
    )


def time_freq(t_value, width):
    half = width // 2
    freqs = jnp.exp(-math.log(10000.0) * jnp.arange(half, dtype=jnp.float32) / half)
    angles = (t_value * step_count)[:, None] * freqs[None, :]
    return jnp.concatenate([jnp.cos(angles), jnp.sin(angles)], -1)


def forward_product(left, weight):
    return jnp.matmul(left, weight, preferred_element_type=jnp.float32)


def weight_grad(left, back):
    flat_left = left.reshape(-1, left.shape[-1])
    flat_back = back.reshape(-1, back.shape[-1])
    return lax.dot_general(
        flat_left, flat_back, (((0,), (0,)), ((), ())), preferred_element_type=jnp.float32
    )


def input_grad(back, weight):
    return lax.dot_general(
        back, weight, (((back.ndim - 1,), (1,)), ((), ())), preferred_element_type=jnp.float32
    )


def split_heads(qkv_low):
    batch, count, triple = qkv_low.shape
    width = triple // 3
    parts = qkv_low.reshape(batch, count, 3, HEADS, width // HEADS)
    return (parts[:, :, 0], parts[:, :, 1], parts[:, :, 2])


def probabilities(query, key):
    score = jnp.einsum(
        "bnhe,bmhe->bhnm", query, key, preferred_element_type=jnp.float32
    ) / math.sqrt(query.shape[-1])
    expo = jnp.exp(score - jnp.max(score, -1, keepdims=True))
    return expo / jnp.sum(expo, -1, keepdims=True)


def layer_forward(hidden, cond, w_in, w_out):
    width = hidden.shape[-1]
    modul = forward_product(cond, w_in[:, : 6 * width])
    pieces = jnp.split(modul, 6, axis=-1)
    normed = norm_mod(hidden, pieces[0], pieces[1]).astype(jnp.bfloat16)
    qkv_low = forward_product(normed, w_in[:, 6 * width : 9 * width]).astype(jnp.bfloat16)
    query, key, value = split_heads(qkv_low)
    probs = probabilities(query, key)
    mixed = jnp.einsum(
        "bhnm,bmhe->bnhe", probs.astype(jnp.bfloat16), value, preferred_element_type=jnp.float32
    )
    attn = mixed.reshape(hidden.shape).astype(jnp.bfloat16)
    proj = forward_product(attn, w_out[:width])
    middle = hidden + pieces[2][:, None, :] * proj
    normed_two = norm_mod(middle, pieces[3], pieces[4]).astype(jnp.bfloat16)
    upper = forward_product(normed_two, w_in[:, 9 * width :])
    active = gelu(upper).astype(jnp.bfloat16)
    mlp = forward_product(active, w_out[width:])
    result = middle + pieces[5][:, None, :] * mlp
    return (
        result,
        (pieces, normed, qkv_low, probs, attn, proj, middle, normed_two, upper, active, mlp),
    )


def attention_back(qkv_low, probs, d_attn):
    query, key, value = split_heads(qkv_low)
    scale = 1.0 / math.sqrt(query.shape[-1])
    d_mixed = d_attn.reshape(query.shape)
    d_value = jnp.einsum(
        "bhnm,bnhe->bmhe", probs.astype(jnp.bfloat16), d_mixed, preferred_element_type=jnp.float32
    )
    d_prob = jnp.einsum("bnhe,bmhe->bhnm", d_mixed, value, preferred_element_type=jnp.float32)
    d_score = (probs * (d_prob - jnp.sum(probs * d_prob, -1, keepdims=True))).astype(jnp.bfloat16)
    d_query = (
        jnp.einsum("bhnm,bmhe->bnhe", d_score, key, preferred_element_type=jnp.float32) * scale
    )
    d_key = (
        jnp.einsum("bhnm,bnhe->bmhe", d_score, query, preferred_element_type=jnp.float32) * scale
    )
    return jnp.stack([d_query, d_key, d_value], 2).reshape(qkv_low.shape).astype(jnp.bfloat16)


def layer_backward(hidden, cond, w_in, w_out, back):
    width = hidden.shape[-1]
    _, kept = layer_forward(hidden, cond, w_in, w_out)
    pieces, normed, qkv_low, probs, attn, proj, middle, normed_two, upper, active, mlp = kept
    d_gate_two = jnp.sum(back * mlp, 1)
    d_mlp = (pieces[5][:, None, :] * back).astype(jnp.bfloat16)
    g_fc_two = weight_grad(active, d_mlp)
    d_active = input_grad(d_mlp, w_out[width:])
    _, gelu_pull = jax.vjp(gelu, upper)
    d_upper = gelu_pull(d_active)[0].astype(jnp.bfloat16)
    g_fc_one = weight_grad(normed_two, d_upper)
    d_normed_two = input_grad(d_upper, w_in[:, 9 * width :])
    _, norm_pull = jax.vjp(norm_mod, middle, pieces[3], pieces[4])
    d_from_norm, d_shift_two, d_scale_two = norm_pull(d_normed_two)
    d_middle = back + d_from_norm
    d_gate_one = jnp.sum(d_middle * proj, 1)
    d_proj = (pieces[2][:, None, :] * d_middle).astype(jnp.bfloat16)
    g_attn_out = weight_grad(attn, d_proj)
    d_attn = input_grad(d_proj, w_out[:width]).astype(jnp.bfloat16)
    d_qkv = attention_back(qkv_low, probs, d_attn)
    g_qkv = weight_grad(normed, d_qkv)
    d_normed = input_grad(d_qkv, w_in[:, 6 * width : 9 * width])
    _, first_pull = jax.vjp(norm_mod, hidden, pieces[0], pieces[1])
    d_from_first, d_shift_one, d_scale_one = first_pull(d_normed)
    d_hidden = d_middle + d_from_first
    d_modul = jnp.concatenate(
        [d_shift_one, d_scale_one, d_gate_one, d_shift_two, d_scale_two, d_gate_two], -1
    )
    d_modul = d_modul.astype(jnp.bfloat16)
    g_modul = weight_grad(cond, d_modul)
    d_cond = input_grad(d_modul, w_in[:, : 6 * width])
    grad_in_layer = jnp.concatenate([g_modul, g_qkv, g_fc_one], 1)
    grad_out_layer = jnp.concatenate([g_attn_out, g_fc_two], 0)
    return (d_hidden, d_cond, grad_in_layer, grad_out_layer)


def on_device(
    latents,
    noises,
    velocity,
    times,
    labels,
    dropped,
    blocks_in,
    blocks_out,
    head_side,
    embed_side,
    state_in_row,
    state_in_col,
    state_out_row,
    state_out_col,
    state_head_row,
    state_head_col,
    state_embed_row,
    state_embed_col,
):
    full = (
        lax.all_gather(blocks_in.astype(jnp.bfloat16), "shard", axis=2, tiled=True),
        lax.all_gather(blocks_out.astype(jnp.bfloat16), "shard", axis=2, tiled=True),
        lax.all_gather(head_side.astype(jnp.bfloat16), "shard", axis=1, tiled=True),
        lax.all_gather(embed_side.astype(jnp.bfloat16), "shard", axis=1, tiled=True),
    )
    w_in, w_out, w_head, w_embed = full
    images = latents.shape[0]
    width = w_head.shape[0]
    t_value = (times.astype(jnp.float32) + 1.0) / step_count
    tcol = t_value[:, None, None]
    state = (
        (1.0 - tcol) * latents.reshape(images, TOK, PATCH)
        + tcol * noises.reshape(images, TOK, PATCH)
    ).astype(jnp.bfloat16)
    target = velocity.reshape(images, TOK, PATCH)
    hidden = forward_product(state, w_embed[:PATCH]) + positions(GRID, width)[None]
    freq_low = time_freq(t_value, FREQ).astype(jnp.bfloat16)
    time_one = forward_product(freq_low, w_embed[PATCH : PATCH + FREQ])
    time_act = silu(time_one).astype(jnp.bfloat16)
    time_two = forward_product(time_act, w_head[:, :width])
    classes = jnp.where(dropped == 1, CLASSES - 1, labels)
    onehot = (classes[:, None] == jnp.arange(CLASSES, dtype=jnp.int32)[None, :]).astype(
        jnp.bfloat16
    )
    cond_full = time_two + forward_product(onehot, w_embed[PATCH + FREQ :])
    cond = silu(cond_full).astype(jnp.bfloat16)
    layer_index = 0
    inputs = [hidden]
    hidden, _ = layer_forward(hidden, cond, w_in[layer_index], w_out[layer_index])
    final_mod = forward_product(cond, w_head[:, width : 3 * width])
    final_low = norm_mod(hidden, final_mod[:, :width], final_mod[:, width:]).astype(jnp.bfloat16)
    output = forward_product(final_low, w_head[:, 3 * width :])
    diff = output - target
    loss_local = 0.5 * jnp.sum(tcol * diff * diff)
    d_output = (tcol * diff).astype(jnp.bfloat16)
    g_head = weight_grad(final_low, d_output)
    d_final = input_grad(d_output, w_head[:, 3 * width :])
    _, final_pull = jax.vjp(norm_mod, hidden, final_mod[:, :width], final_mod[:, width:])
    d_hidden, d_shift, d_scale = final_pull(d_final)
    d_fmod = jnp.concatenate([d_shift, d_scale], -1).astype(jnp.bfloat16)
    g_fmod = weight_grad(cond, d_fmod)
    d_cond = input_grad(d_fmod, w_head[:, width : 3 * width])
    w_in, w_out, w_head, w_embed = (
        lax.all_gather(blocks_in.astype(jnp.bfloat16), "shard", axis=2, tiled=True),
        lax.all_gather(blocks_out.astype(jnp.bfloat16), "shard", axis=2, tiled=True),
        lax.all_gather(head_side.astype(jnp.bfloat16), "shard", axis=1, tiled=True),
        lax.all_gather(embed_side.astype(jnp.bfloat16), "shard", axis=1, tiled=True),
    )
    grads_in = [None] * LAYERS
    grads_out = [None] * LAYERS
    for layer_index in reversed(range(LAYERS)):
        d_hidden, d_layer_cond, grads_in[layer_index], grads_out[layer_index] = layer_backward(
            inputs[layer_index], cond, w_in[layer_index], w_out[layer_index], d_hidden
        )
        d_cond = d_cond + d_layer_cond
    _, silu_pull = jax.vjp(silu, cond_full)
    d_full = silu_pull(d_cond)[0]
    d_two = d_full.astype(jnp.bfloat16)
    g_time_two = weight_grad(time_act, d_two)
    d_act = input_grad(d_two, w_head[:, :width])
    _, time_pull = jax.vjp(silu, time_one)
    d_one = time_pull(d_act)[0].astype(jnp.bfloat16)
    g_time_one = weight_grad(freq_low, d_one)
    g_table = lax.dot_general(
        onehot.astype(jnp.float32),
        d_full,
        (((0,), (0,)), ((), ())),
        precision=lax.Precision.HIGHEST,
    )
    g_patch = weight_grad(state, d_hidden.astype(jnp.bfloat16))
    local_in = jnp.stack(grads_in, 0)
    local_out = jnp.stack(grads_out, 0)
    local_head = jnp.concatenate([g_time_two, g_fmod, g_head], 1)
    local_embed = jnp.concatenate([g_patch, g_time_one, g_table], 0)
    parts = (
        lax.psum_scatter(local_in, "shard", scatter_dimension=2, tiled=True),
        lax.psum_scatter(local_out, "shard", scatter_dimension=2, tiled=True),
        lax.psum_scatter(local_head, "shard", scatter_dimension=1, tiled=True),
        lax.psum_scatter(local_embed, "shard", scatter_dimension=1, tiled=True),
    )
    reduced = (
        lax.psum_scatter(parts[0], "rep", scatter_dimension=1, tiled=True),
        lax.psum_scatter(parts[1], "rep", scatter_dimension=1, tiled=True),
        lax.psum_scatter(parts[2], "rep", scatter_dimension=0, tiled=True),
    )
    spread = (
        lax.all_gather(reduced[0], "rep", axis=1, tiled=True),
        lax.all_gather(reduced[1], "rep", axis=1, tiled=True),
        lax.all_gather(reduced[2], "rep", axis=0, tiled=True),
    )
    embed_sum = lax.psum(parts[3], "rep")
    totals = (spread[0], spread[1], spread[2], embed_sum)
    loss_sum = lax.psum(loss_local, ("rep", "shard"))
    weights = (blocks_in, blocks_out, head_side, embed_side)
    rows_old = (state_in_row, state_out_row, state_head_row, state_embed_row)
    cols_old = (state_in_col, state_out_col, state_head_col, state_embed_col)
    shard_count = lax.axis_size("shard")
    cols_new = [
        decay * col_state + (1.0 - decay) * (jnp.mean(gradient * gradient, -2) + eps_one)
        for gradient, col_state in zip(totals, cols_old)
    ]
    row_parts = [jnp.sum(gradient * gradient, -1) for gradient in totals]
    weight_sq = [jnp.sum(weight * weight, axis=(-2, -1)) for weight in weights]
    stats = lax.psum(
        (
            row_parts[0],
            row_parts[1],
            row_parts[2],
            row_parts[3],
            weight_sq[0],
            weight_sq[1],
            weight_sq[2],
            weight_sq[3],
        ),
        "shard",
    )
    rows_new = [
        decay * row_state
        + (1.0 - decay) * (stats[index] / (totals[index].shape[-1] * shard_count) + eps_one)
        for index, row_state in enumerate(rows_old)
    ]
    row_means = [jnp.mean(row_next, -1) for row_next in rows_new]
    updates = [
        gradient
        * lax.rsqrt(row_next[..., :, None] * col_next[..., None, :] / row_mean[..., None, None])
        for gradient, row_next, col_next, row_mean in zip(totals, rows_new, cols_new, row_means)
    ]
    total_sq = lax.psum(sum((jnp.sum(update * update) for update in updates)), "shard")
    count = sum((weight.size for weight in weights)) * shard_count
    update_rms = jnp.sqrt(total_sq / count)
    factor = jnp.maximum(1.0, update_rms / clip_level)
    news = []
    for index in range(4):
        numel = weights[index].shape[-2] * weights[index].shape[-1] * shard_count
        weight_rms = jnp.sqrt(stats[4 + index] / numel)
        step_size = rate * jnp.maximum(eps_two, weight_rms)
        news.append(
            weights[index] - jnp.asarray(step_size)[..., None, None] * updates[index] / factor
        )
    return (
        loss_sum,
        update_rms,
        totals[0],
        totals[1],
        totals[2],
        totals[3],
        rows_new[0],
        cols_new[0],
        rows_new[1],
        cols_new[1],
        rows_new[2],
        cols_new[2],
        rows_new[3],
        cols_new[3],
        news[0],
        news[1],
        news[2],
        news[3],
    )


def solution(mesh):
    placed = (
        P(("rep", "shard"), None),
        P(("rep", "shard"), None),
        P(("rep", "shard"), None),
        P(("rep", "shard")),
        P(("rep", "shard")),
        P(("rep", "shard")),
        P(None, None, "shard"),
        P(None, None, "shard"),
        P(None, "shard"),
        P(None, "shard"),
        P(),
        P(None, "shard"),
        P(),
        P(None, "shard"),
        P(),
        P("shard"),
        P(),
        P("shard"),
    )
    return jax.shard_map(
        on_device,
        mesh=mesh,
        in_specs=placed,
        out_specs=(
            P(),
            P(),
            P(None, None, "shard"),
            P(None, None, "shard"),
            P(None, "shard"),
            P(None, "shard"),
            P(),
            P(None, "shard"),
            P(),
            P(None, "shard"),
            P(),
            P("shard"),
            P(),
            P("shard"),
            P(None, None, "shard"),
            P(None, None, "shard"),
            P(None, "shard"),
            P(None, "shard"),
        ),
        check_vma=False,
    )
```

profile of v0, /device:TPU:0, one launch (start us, length us, event | category | flops | bytes accessed | tf_op | source)
XLA Modules:
  0.0 2042.2 jit_solution(13240122209804210891)
XLA Ops:
  39.6 28.9 %all-gather.21.cloned.1.call-done = bf16[4,580,768]{2,1,0:T(8,128)(2,1)} async-done(((bf16[1,580,768]{2,1,0:T(8,128)(2,1)}), bf16[4,580,768]{2,1,0:T(8,128)(2,1)}) %all-gather.21.cloned.1.call-update) | async-done | bytes 3563536 | tf_op jit(solution)/shard_map/all_gather | solution.py:193
  78.5 89.9 %all-gather.11.cloned.1.call-done = bf16[1,768,9984]{1,2,0:T(8,128)(2,1)} async-done(((bf16[1,768,2496]{1,2,0:T(8,128)(2,1)}), bf16[1,768,9984]{1,2,0:T(8,128)(2,1)}) %all-gather.11.cloned.1.call-update) | async-done | bytes 15335440 | tf_op jit(solution)/shard_map/all_gather | solution.py:191
  168.4 20.3 copy.185
  272.3 10.2 convolution_bitcast_fusion.1
  307.1 24.7 %copy.208 = f32[1,3840,768]{1,0,2:T(1,128)} copy(f32[1,3840,768]{2,1,0:T(8,128)} %maximum_bitcast_fusion.1) | data formatting | bytes 23592960 | tf_op jit(solution)/shard_map/stack | solution.py:262
  373.7 21.8 %maximum_bitcast_fusion = f32[1,768,9984]{2,1,0:T(8,128)} fusion(f32[768,3072]{1,0:T(8,128)} %convolution_bitcast_fusion.2, f32[768,2304]{1,0:T(8,128)} %convolution_bitcast_fusion, f32[768,4608]{1,0:T(8,128)} %fusion.95), kind=kLoop, calls=%fused_computation.3 | loop fusion | flops 15335424 | bytes 61341696 | tf_op jit(solution)/shard_map/stack | solution.py:261
  395.5 63.9 %copy.204 = f32[1,768,9984]{1,0,2:T(1,128)} copy(f32[1,768,9984]{2,1,0:T(8,128)} %maximum_bitcast_fusion) | data formatting | bytes 61341696 | tf_op jit(solution)/shard_map/stack | solution.py:261
  462.0 205.2 %all-reduce.16.cloned.1.call-done = (f32[1,3840,768]{1,0,2:T(1,128)}, f32[768,2320]{1,0:T(8,128)}) async-done(((f32[1,3840,768]{1,0,2:T(1,128)}, f32[768,2320]{1,0:T(8,128)}), (f32[1,3840,768]{1,0,2:T(1,128)}, f32[768,2320]{1,0:T(8,128)})) %all-reduce.16.cloned.1.call-update) | async-done | bytes 18923536
  671.0 175.5 %copy.234 = f32[1,3840,192]{0,2,1:T(8,128)} copy(f32[1,3840,192]{1,0,2:T(1,128)S(1)} %constant_dynamic-slice_fusion.1) | data formatting | bytes 5898240
  850.5 142.9 %bitcast_reduce_fusion = f32[3840,192]{1,0:T(8,128)} fusion(f32[1,3840,192]{0,2,1:T(8,128)} %copy.234), kind=kLoop, calls=%fused_computation.1 | loop fusion | bytes 5898240
  996.8 230.2 %all-reduce.12.cloned.1.call-done = f32[1,768,9984]{1,0,2:T(1,128)} async-done(((f32[1,768,9984]{1,0,2:T(1,128)}), f32[1,768,9984]{1,0,2:T(1,128)}) %all-reduce.12.cloned.1.call-update) | async-done | bytes 30670864
  1234.7 25.1 %copy.205 = f32[1,768,2496]{2,0,1:T(1,128)} copy(f32[1,768,2496]{1,0,2:T(1,128)} %constant_dynamic-slice_fusion.3) | data formatting | bytes 15335424 | tf_op jit(solution)/shard_map/reduce_scatter | solution.py:266
  1259.8 38.4 %reduce-scatter.9.cloned.1.call-done = f32[96,580]{1,0:T(8,128)} async-done(((f32[768,580]{1,0:T(8,128)}), f32[96,580]{1,0:T(8,128)}) %reduce-scatter.9.cloned.1.call-update) | async-done | bytes 222736 | tf_op jit(solution)/shard_map/reduce_scatter | solution.py:274
  1298.5 87.7 %reduce-scatter.11.cloned.1.call-done = f32[480,192]{1,0:T(8,128)} async-done(((f32[3840,192]{1,0:T(8,128)}), f32[480,192]{1,0:T(8,128)}) %reduce-scatter.11.cloned.1.call-update) | async-done | bytes 368656
  1386.2 17.0 reshape_bitcast_fusion
  1403.2 27.2 %copy.209 = f32[1,480,192]{2,0,1:T(1,128)} copy(f32[1,480,192]{0,2,1:T(8,128)} %reshape_bitcast_fusion) | data formatting | bytes 737280 | tf_op jit(solution)/shard_map/reduce_scatter | solution.py:273
  1431.7 251.4 %all-reduce.14.cloned.1.call-done = (f32[1,768,2496]{2,0,1:T(1,128)}, f32[1273,192]{1,0:T(8,128)}) async-done(((f32[1,768,2496]{2,0,1:T(1,128)}, f32[1273,192]{1,0:T(8,128)}), (f32[1,768,2496]{2,0,1:T(1,128)}, f32[1273,192]{1,0:T(8,128)})) %all-reduce.14.cloned.1.call-update) | async-done | bytes 8645392
  1689.3 40.2 %psum.77 = f32[]{:T(128)} all-reduce(f32[]{:T(128)S(6)} %mul.672), channel_id=1, replica_groups=mesh['rep'=8,'shard'=4] {'rep','shard'}, use_global_device_ids=true, to_apply=%region_9.10 | all-reduce | flops 1 | bytes 8 | tf_op jit(solution)/shard_map/psum | solution.py:283
  1735.4 68.6 %all-gather.17.cloned.1.call-done = f32[1,3840,192]{2,0,1:T(1,128)} async-done(((f32[1,480,192]{2,0,1:T(1,128)}), f32[1,3840,192]{2,0,1:T(1,128)}) %all-gather.17.cloned.1.call-update) | async-done | bytes 2949136 | tf_op jit(solution)/shard_map/all_gather | solution.py:278
  1804.0 29.9 %multiply_reduce_fusion.8 = (f32[192]{0:T(256)S(1)}, f32[3840]{0:T(1024)S(1)}) fusion(f32[1,3840,192]{2,0,1:T(1,128)} %all-gather.17.cloned.1.call-done), kind=kLoop, calls=%fused_computation.59 | loop fusion | flops 2207808 | bytes 2965248 | tf_op jit(solution)/shard_map/reduce_sum | solution.py:289
  1844.6 78.9 %all-gather.15.cloned.1.call-done = f32[1,768,2496]{2,0,1:T(1,128)} async-done(((f32[1,96,2496]{2,0,1:T(1,128)}), f32[1,768,2496]{2,0,1:T(1,128)}) %all-gather.15.cloned.1.call-update) | async-done | bytes 7667728 | tf_op jit(solution)/shard_map/all_gather | solution.py:277
  1923.6 30.6 %multiply_reduce_fusion.4 = (f32[2496]{0:T(1024)S(1)}, f32[768]{0:T(1024)S(1)}) fusion(f32[1,768,2496]{2,0,1:T(1,128)} %all-gather.15.cloned.1.call-done), kind=kLoop, calls=%fused_computation.38 | loop fusion | flops 5747520 | bytes 7680768 | tf_op jit(solution)/shard_map/reduce_sum | solution.py:289
  1954.1 11.0 all-reduce.6
  1970.8 16.7 copy.206
  (395 shorter events, 277.4 us)
Async XLA Ops:
  7.2 28.0 %all-gather.9.cloned.1.call-start = ((), (), s32[]{:S(2)}) async-start(), calls=%async_computation.3 | async-start | bytes 2457600 | tf_op jit(solution)/shard_map/all_gather | solution.py:194
  10.5 58.0 %all-gather.21.cloned.1.call-start = ((), (), s32[]{:S(2)}) async-start(), calls=%async_computation.10 | async-start | bytes 4485120 | tf_op jit(solution)/shard_map/all_gather | solution.py:193
  12.5 155.9 %all-gather.11.cloned.1.call-start = ((), (), s32[]{:S(2)}) async-start(), calls=%async_computation.4 | async-start | bytes 19169280 | tf_op jit(solution)/shard_map/all_gather | solution.py:191
  22.3 193.0 %all-gather.13.cloned.1.call-start = ((), (), s32[]{:S(2)}) async-start(), calls=%async_computation.5 | async-start | bytes 7372800 | tf_op jit(solution)/shard_map/all_gather | solution.py:192
  26.7 640.5 %all-reduce.16.cloned.1.call-start = ((), (), s32[]{:S(2)}) async-start(), calls=%async_computation.15 | async-start | bytes 38535168
  78.5 148.9 %copy-start.86 = (f32[2,768]{1,0:T(2,128)}, f32[2,768]{1,0:T(2,128)S(1)}, u32[]{:S(2)}) copy-start(f32[2,768]{1,0:T(2,128)S(1)} %get-tuple-element.174) | copy-start | bytes 18436
  78.5 153.0 %copy-start.39 = (f32[2,768]{1,0:T(2,128)}, f32[2,768]{1,0:T(2,128)S(1)}, u32[]{:S(2)}) copy-start(f32[2,768]{1,0:T(2,128)S(1)} %get-tuple-element.173) | copy-start | bytes 18436
  78.5 110.1 %copy-start.28 = (f32[2,768]{1,0:T(2,128)S(1)}, f32[2,768]{1,0:T(2,128)}, u32[]{:S(2)}) copy-start(f32[2,768]{1,0:T(2,128)} %copy-done.27) | copy-start | bytes 18436
  338.1 656.0 %reduce-scatter.13.cloned.1.call-start = ((), (), s32[]{:S(2)}) async-start(), calls=%async_computation.12 | async-start | bytes 4915200
  353.5 873.5 %all-reduce.12.cloned.1.call-start = ((), (), s32[]{:S(2)}) async-start(), calls=%async_computation.13 | async-start | bytes 61341696
  459.4 838.8 %reduce-scatter.9.cloned.1.call-start = ((), (), s32[]{:S(2)}) async-start(), calls=%async_computation.8 | async-start | bytes 2211840 | tf_op jit(solution)/shard_map/reduce_scatter | solution.py:274
  850.5 535.8 %reduce-scatter.11.cloned.1.call-start = ((), (), s32[]{:S(2)}) async-start(), calls=%async_computation.11 | async-start | bytes 4423680
  993.4 689.7 %all-reduce.14.cloned.1.call-start = ((), (), s32[]{:S(2)}) async-start(), calls=%async_computation.14 | async-start | bytes 18350080
  1259.8 472.4 %all-gather.19.cloned.1.call-start = ((), (), s32[]{:S(2)}) async-start(), calls=%async_computation.9 | async-start | bytes 2211840 | tf_op jit(solution)/shard_map/all_gather | solution.py:279
  1298.2 505.8 %all-gather.17.cloned.1.call-start = ((), (), s32[]{:S(2)}) async-start(), calls=%async_computation.7 | async-start | bytes 4423680 | tf_op jit(solution)/shard_map/all_gather | solution.py:278
  1430.4 255.0 %copy-start.14 = (f32[768,580]{0,1:T(8,128)S(1)}, f32[768,580]{0,1:T(8,128)}, u32[]{:S(2)}) copy-start(f32[768,580]{0,1:T(8,128)} %param.26) | copy-start | bytes 5345284
  1430.4 493.2 %all-gather.15.cloned.1.call-start = ((), (), s32[]{:S(2)}) async-start(), calls=%async_computation.6 | async-start | bytes 8847360 | tf_op jit(solution)/shard_map/all_gather | solution.py:277
  1735.4 287.8 %copy-start.43 = (f32[580]{0:T(1024)}, f32[580]{0:T(1024)S(1)}, u32[]{:S(2)}) copy-start(f32[580]{0:T(1024)S(1)} %add_multiply_fusion.3) | copy-start | bytes 6964
  1842.9 176.3 %copy-start.78 = (f32[1,192]{1,0:T(1,128)}, f32[1,192]{1,0:T(1,128)S(1)}, u32[]{:S(2)}) copy-start(f32[1,192]{1,0:T(1,128)S(1)} %add_multiply_fusion.7) | copy-start | bytes 2308
  1844.6 185.6 %copy-start.79 = (f32[192]{0:T(256)}, f32[192]{0:T(256)S(1)}, u32[]{:S(2)}) copy-start(f32[192]{0:T(256)S(1)} %add_multiply_fusion.6) | copy-start | bytes 2308
  1844.6 120.6 %copy-start.97 = (f32[1,768]{1,0:T(1,128)S(1)}, f32[1,768]{1,0:T(1,128)}, u32[]{:S(2)}) copy-start(f32[1,768]{1,0:T(1,128)} %param.28) | copy-start | bytes 9220
  1844.6 122.4 %copy-start.96 = (f32[768]{0:T(1024)S(1)}, f32[768]{0:T(1024)}, u32[]{:S(2)}) copy-start(f32[768]{0:T(1024)} %param.32) | copy-start | bytes 9220
  1844.6 123.7 %copy-start.77 = (f32[1,2496]{1,0:T(1,128)S(1)}, f32[1,2496]{1,0:T(1,128)}, u32[]{:S(2)}) copy-start(f32[1,2496]{1,0:T(1,128)} %param.29) | copy-start | bytes 29956
  1844.6 124.3 %copy-start.70 = (f32[1,3840]{1,0:T(1,128)S(1)}, f32[1,3840]{1,0:T(1,128)}, u32[]{:S(2)}) copy-start(f32[1,3840]{1,0:T(1,128)} %param.30) | copy-start | bytes 46084
  (106 other events, 717.6 us)
Sparse Core Ops, SparseCore 0:
  10.6 24.5 all-gather.8
  37.4 31.0 all-gather.20
  70.6 97.7 all-gather.10
  170.4 44.1 all-gather.12
  338.3 328.8 all-reduce.15
  669.6 43.0 reduce-scatter.12
  715.3 511.6 all-reduce.11
  1231.1 67.1 reduce-scatter.8
  1302.9 83.2 reduce-scatter.10
  1390.7 292.2 all-reduce.13
  1685.3 46.8 all-gather.18
  1734.8 69.1 all-gather.16
  1806.8 116.7 all-gather.14
where the time goes:
time: 2050 us; the launch traced here: 2040 us
  waiting for transfers between devices  1090 us (53%)
  local copies, waits for them, and re-layouts  586 us (29%)
  other arithmetic  166 us (8%)
  matrix products  117 us (6%)
  blocking collectives  58 us (3%)
  between operations  28.6 us (1%)
    unnamed x18, waiting for transfers between devices  775 us
    unnamed x257, local copies, waits for them, and re-layouts  391 us
    all_gather x1, waiting for transfers between devices, on_device(): lax.all_gather(blocks_in.astype(jnp.bfloat16), 'shard', axis=2, tiled=True)  89.9 us
    all_gather x1, waiting for transfers between devices, on_device(): lax.all_gather(reduced[0], 'rep', axis=1, tiled=True)  78.9 us
    all_gather x1, waiting for transfers between devices, on_device(): lax.all_gather(reduced[1], 'rep', axis=1, tiled=True)  68.6 us
    another operation x1, local copies, waits for them, and re-layouts, on_device(): local_in = jnp.stack(grads_in, 0)  63.9 us
    reduce_sum x4, other arithmetic, on_device(): jnp.mean(gradient * gradient, -2) + eps_one  61 us
    dot_general x10, matrix products, weight_grad(): lax.dot_general(flat_left, flat_back, (((0,), (0,)), ((), ())), preferred...  42.2 us
  transfers between devices with their start and end apart: 13, of which 11 were waited for; matrix products, arithmetic and copies ran while one was open for 32% of the time, Pallas kernels for 0%

commit v1 on v0

v1 whole, which is shorter than its diff:
```python
import math

import jax
import jax.numpy as jnp
from jax import lax
from jax.sharding import PartitionSpec as P

HEADS = 12
CLASSES = 1001
FREQ = 256
GRID = 16
PATCH = 16
LAYERS = 1
TOK = 256


decay = 0.5
eps_norm = 1e-06
eps_one = 1e-30
eps_two = 0.001
clip_level = 0.1
rate = 8.0
step_count = 1000.0


def silu(value):
    return value * jax.nn.sigmoid(value)


def gelu(value):
    return 0.5 * value * (1.0 + jnp.tanh(0.7978845608 * (value + 0.044715 * value * value * value)))


def norm_mod(hidden, shift, scale):
    center = hidden - jnp.mean(hidden, -1, keepdims=True)
    spread = jnp.mean(center * center, -1, keepdims=True)
    return center * lax.rsqrt(spread + eps_norm) * (1.0 + scale[:, None, :]) + shift[:, None, :]


def positions(grid, width):
    quarter = width // 4
    omega = 1.0 / 10000.0 ** (jnp.arange(quarter, dtype=jnp.float32) / quarter)
    index = jnp.arange(grid * grid, dtype=jnp.int32)
    row_pos = (index // grid).astype(jnp.float32)[:, None] * omega[None, :]
    col_pos = (index % grid).astype(jnp.float32)[:, None] * omega[None, :]
    return jnp.concatenate(
        [jnp.sin(row_pos), jnp.cos(row_pos), jnp.sin(col_pos), jnp.cos(col_pos)], 1
    )


def time_freq(t_value, width):
    half = width // 2
    freqs = jnp.exp(-math.log(10000.0) * jnp.arange(half, dtype=jnp.float32) / half)
    angles = (t_value * step_count)[:, None] * freqs[None, :]
    return jnp.concatenate([jnp.cos(angles), jnp.sin(angles)], -1)


def forward_product(left, weight):
    return jnp.matmul(left, weight, preferred_element_type=jnp.float32)


def weight_grad(left, back):
    flat_left = left.reshape(-1, left.shape[-1])
    flat_back = back.reshape(-1, back.shape[-1])
    return lax.dot_general(
        flat_left, flat_back, (((0,), (0,)), ((), ())), preferred_element_type=jnp.float32
    )


def input_grad(back, weight):
    return lax.dot_general(
        back, weight, (((back.ndim - 1,), (1,)), ((), ())), preferred_element_type=jnp.float32
    )


def split_heads(qkv_low):
    batch, count, triple = qkv_low.shape
    width = triple // 3
    parts = qkv_low.reshape(batch, count, 3, HEADS, width // HEADS)
    return (parts[:, :, 0], parts[:, :, 1], parts[:, :, 2])


def probabilities(query, key):
    score = jnp.einsum(
        "bnhe,bmhe->bhnm", query, key, preferred_element_type=jnp.float32
    ) / math.sqrt(query.shape[-1])
    expo = jnp.exp(score - jnp.max(score, -1, keepdims=True))
    return expo / jnp.sum(expo, -1, keepdims=True)


def input_grad_t(back, weight_t):
    return jnp.matmul(back, weight_t, preferred_element_type=jnp.float32)


def forward_t(left, weight_t):
    return lax.dot_general(
        left, weight_t, (((left.ndim - 1,), (1,)), ((), ())), preferred_element_type=jnp.float32
    )


def attention_back(qkv_low, probs, d_attn):
    query, key, value = split_heads(qkv_low)
    scale = 1.0 / math.sqrt(query.shape[-1])
    d_mixed = d_attn.reshape(query.shape)
    d_value = jnp.einsum(
        "bhnm,bnhe->bmhe", probs.astype(jnp.bfloat16), d_mixed, preferred_element_type=jnp.float32
    )
    d_prob = jnp.einsum("bnhe,bmhe->bhnm", d_mixed, value, preferred_element_type=jnp.float32)
    d_score = (probs * (d_prob - jnp.sum(probs * d_prob, -1, keepdims=True))).astype(jnp.bfloat16)
    d_query = (
        jnp.einsum("bhnm,bmhe->bnhe", d_score, key, preferred_element_type=jnp.float32) * scale
    )
    d_key = (
        jnp.einsum("bhnm,bnhe->bmhe", d_score, query, preferred_element_type=jnp.float32) * scale
    )
    return jnp.concatenate(
        [item.reshape(item.shape[:2] + (-1,)) for item in (d_query, d_key, d_value)], -1
    ).astype(jnp.bfloat16)


def gather_heavy(in_low, out_low, shard_count):
    width = in_low.shape[0]
    all_in = lax.all_gather(in_low, "shard", axis=1, tiled=True)
    all_out = lax.all_gather(out_low, "shard", axis=1, tiled=True)
    return all_in[:, 6 * width : 9 * width].T, all_in[:, 9 * width :].T, all_out.T


def reduce_heavy(g_in_t, g_out_t, in_cols, out_cols):
    width = g_in_t.shape[1]
    total_in = lax.psum(g_in_t.astype(jnp.bfloat16), ("rep", "shard"))
    total_out = lax.psum(g_out_t.astype(jnp.bfloat16), ("rep", "shard"))
    place = lax.axis_index("shard")
    padded = jnp.pad(total_in, ((6 * width, 0), (0, 0)))
    own_in = lax.dynamic_slice_in_dim(padded, place * in_cols, in_cols, 0)
    own_out = lax.dynamic_slice_in_dim(total_out, place * out_cols, out_cols, 0)
    return own_in.T.astype(jnp.float32), own_out.T.astype(jnp.float32)


def on_device(
    latents,
    noises,
    velocity,
    times,
    labels,
    dropped,
    blocks_in,
    blocks_out,
    head_side,
    embed_side,
    state_in_row,
    state_in_col,
    state_out_row,
    state_out_col,
    state_head_row,
    state_head_col,
    state_embed_row,
    state_embed_col,
):
    both = ("rep", "shard")
    images = latents.shape[0]
    width = head_side.shape[0]
    shard_count = lax.axis_size("shard")
    place = lax.axis_index("shard")
    rep_place = lax.axis_index("rep")
    in_cols = blocks_in.shape[2]
    out_cols = blocks_out.shape[2]
    head_cols = head_side.shape[1]
    embed_cols = embed_side.shape[1]
    group = images * shard_count
    in_low = blocks_in[0].astype(jnp.bfloat16)
    out_low = blocks_out[0].astype(jnp.bfloat16)
    head_low = head_side.astype(jnp.bfloat16)
    embed_low = embed_side.astype(jnp.bfloat16)
    qkv_t, fc1_t, out_t = gather_heavy(in_low, out_low, shard_count)
    o_t, fc2_t = out_t[:, :width], out_t[:, width:]
    marks = lax.all_gather(jnp.stack([times, labels, dropped]), both, axis=1, tiled=True)
    t_all = (marks[0].astype(jnp.float32) + 1.0) / step_count
    classes = jnp.where(marks[2] == 1, CLASSES - 1, marks[1])
    onehot = (classes[:, None] == jnp.arange(CLASSES, dtype=jnp.int32)[None, :]).astype(
        jnp.bfloat16
    )
    freq_low = time_freq(t_all, FREQ).astype(jnp.bfloat16)
    time_one = forward_product(freq_low, embed_low[PATCH : PATCH + FREQ])
    table_part = forward_product(onehot, embed_low[PATCH + FREQ :])
    time_act = lax.all_gather(silu(time_one).astype(jnp.bfloat16), "shard", axis=1, tiled=True)
    two_part = forward_product(time_act, head_low)
    sides = lax.all_gather(
        jnp.concatenate([two_part, table_part], 1), "shard", axis=0, tiled=False
    )
    time_two = jnp.concatenate([sides[j, :, :head_cols] for j in range(shard_count)], 1)[:, :width]
    table_rows = jnp.concatenate([sides[j, :, head_cols:] for j in range(shard_count)], 1)
    cond_full = time_two + table_rows
    cond = silu(cond_full).astype(jnp.bfloat16)
    cond_group = lax.dynamic_slice_in_dim(cond, rep_place * group, group, 0)
    mod_part = jnp.concatenate(
        [forward_product(cond_group, in_low), forward_product(cond_group, head_low)], 1
    )
    mods = lax.all_gather(mod_part, "shard", axis=0, tiled=False)
    mods = lax.dynamic_slice_in_dim(mods, place * images, images, 1)
    modul = jnp.concatenate([mods[j, :, :in_cols] for j in range(shard_count)], 1)[:, : 6 * width]
    final_mod = jnp.concatenate([mods[j, :, in_cols:] for j in range(shard_count)], 1)
    final_mod = final_mod[:, width : 3 * width]
    small = jnp.concatenate(
        [
            lax.all_gather(embed_low[:PATCH], "shard", axis=1, tiled=True),
            lax.all_gather(head_low, "shard", axis=1, tiled=True)[:, 3 * width :].T,
        ],
        0,
    )
    patch_w, head_t = small[:PATCH], small[PATCH:]
    t_value = (times.astype(jnp.float32) + 1.0) / step_count
    tcol = t_value[:, None, None]
    state = (
        (1.0 - tcol) * latents.reshape(images, TOK, PATCH)
        + tcol * noises.reshape(images, TOK, PATCH)
    ).astype(jnp.bfloat16)
    target = velocity.reshape(images, TOK, PATCH)
    hidden = forward_product(state, patch_w) + positions(GRID, width)[None]
    pieces = jnp.split(modul, 6, axis=-1)
    normed, first_pull = jax.vjp(norm_mod, hidden, pieces[0], pieces[1])
    normed = normed.astype(jnp.bfloat16)
    qkv_low = forward_t(normed, qkv_t).astype(jnp.bfloat16)
    query, key, value = split_heads(qkv_low)
    probs = probabilities(query, key)
    mixed = jnp.einsum(
        "bhnm,bmhe->bnhe", probs.astype(jnp.bfloat16), value, preferred_element_type=jnp.float32
    )
    attn = mixed.reshape(hidden.shape).astype(jnp.bfloat16)
    proj = forward_t(attn, o_t)
    middle = hidden + pieces[2][:, None, :] * proj
    normed_two, norm_pull = jax.vjp(norm_mod, middle, pieces[3], pieces[4])
    normed_two = normed_two.astype(jnp.bfloat16)
    upper = forward_t(normed_two, fc1_t)
    active, gelu_pull = jax.vjp(gelu, upper)
    active = active.astype(jnp.bfloat16)
    mlp = forward_t(active, fc2_t)
    result = middle + pieces[5][:, None, :] * mlp
    final, final_pull = jax.vjp(norm_mod, result, final_mod[:, :width], final_mod[:, width:])
    final_low = final.astype(jnp.bfloat16)
    output = forward_t(final_low, head_t)
    diff = output - target
    loss_local = 0.5 * jnp.sum(tcol * diff * diff)
    d_output = (tcol * diff).astype(jnp.bfloat16)
    g_head_t = weight_grad(d_output, final_low)
    d_final = input_grad_t(d_output, head_t)
    back, d_shift, d_scale = final_pull(d_final)
    d_gate_two = jnp.sum(back * mlp, 1)
    d_mlp = (pieces[5][:, None, :] * back).astype(jnp.bfloat16)
    g_fc2_t = weight_grad(d_mlp, active)
    d_active = input_grad_t(d_mlp, fc2_t)
    d_upper = gelu_pull(d_active)[0].astype(jnp.bfloat16)
    g_fc1_t = weight_grad(d_upper, normed_two)
    d_normed_two = input_grad_t(d_upper, fc1_t)
    d_from_norm, d_shift_two, d_scale_two = norm_pull(d_normed_two)
    d_middle = back + d_from_norm
    d_gate_one = jnp.sum(d_middle * proj, 1)
    d_proj = (pieces[2][:, None, :] * d_middle).astype(jnp.bfloat16)
    g_o_t = weight_grad(d_proj, attn)
    d_attn = input_grad_t(d_proj, o_t).astype(jnp.bfloat16)
    d_qkv = attention_back(qkv_low, probs, d_attn)
    g_qkv_t = weight_grad(d_qkv, normed)
    d_normed = input_grad_t(d_qkv, qkv_t)
    d_from_first, d_shift_one, d_scale_one = first_pull(d_normed)
    d_hidden = d_middle + d_from_first
    g_patch = weight_grad(state, d_hidden.astype(jnp.bfloat16))
    heavy_in, heavy_out = reduce_heavy(
        jnp.concatenate([g_qkv_t, g_fc1_t], 0),
        jnp.concatenate([g_o_t, g_fc2_t], 1),
        in_cols,
        out_cols,
    )
    d_low = jnp.concatenate(
        [d_shift_one, d_scale_one, d_gate_one, d_shift_two, d_scale_two, d_gate_two, d_shift, d_scale],
        -1,
    ).astype(jnp.bfloat16)
    d_low = lax.all_gather(d_low, both, axis=0, tiled=True)
    full_in = in_cols * shard_count
    full_head = head_cols * shard_count
    d_in = jnp.pad(d_low[:, : 6 * width], ((0, 0), (0, full_in - 6 * width)))
    d_in = lax.dynamic_slice_in_dim(d_in, place * in_cols, in_cols, 1)
    d_fin = jnp.pad(d_low[:, 6 * width :], ((0, 0), (width, full_head - 3 * width)))
    d_fin = lax.dynamic_slice_in_dim(d_fin, place * head_cols, head_cols, 1)
    d_cond = lax.psum(input_grad(d_in, in_low) + input_grad(d_fin, head_low), "shard")
    _, silu_pull = jax.vjp(silu, cond_full)
    d_full = silu_pull(d_cond)[0]
    d_two = jnp.pad(d_full.astype(jnp.bfloat16), ((0, 0), (0, full_head - width)))
    d_two = lax.dynamic_slice_in_dim(d_two, place * head_cols, head_cols, 1)
    d_act = lax.psum_scatter(input_grad(d_two, head_low), "shard", scatter_dimension=1, tiled=True)
    _, time_pull = jax.vjp(silu, time_one)
    d_one = time_pull(d_act)[0].astype(jnp.bfloat16)
    d_full_own = lax.dynamic_slice_in_dim(d_full, place * embed_cols, embed_cols, 1)
    g_table = lax.dot_general(
        onehot.astype(jnp.float32),
        d_full_own,
        (((0,), (0,)), ((), ())),
        precision=lax.Precision.HIGHEST,
    )
    loss_sum, g_small = lax.psum((loss_local, jnp.concatenate([g_patch, g_head_t], 0)), both)
    own_patch = lax.dynamic_slice_in_dim(g_small[:PATCH], place * embed_cols, embed_cols, 1)
    own_head = jnp.pad(g_small[PATCH:].T, ((0, 0), (3 * width, 0)))
    own_head = lax.dynamic_slice_in_dim(own_head, place * head_cols, head_cols, 1)
    totals = (
        (weight_grad(cond, d_in) + heavy_in)[None],
        heavy_out[None],
        weight_grad(time_act, d_two) + weight_grad(cond, d_fin) + own_head,
        jnp.concatenate([own_patch, weight_grad(freq_low, d_one), g_table], 0),
    )
    weights = (blocks_in, blocks_out, head_side, embed_side)
    rows_old = (state_in_row, state_out_row, state_head_row, state_embed_row)
    cols_old = (state_in_col, state_out_col, state_head_col, state_embed_col)
    cols_new = [
        decay * col_state + (1.0 - decay) * (jnp.mean(gradient * gradient, -2) + eps_one)
        for gradient, col_state in zip(totals, cols_old)
    ]
    row_parts = [jnp.sum(gradient * gradient, -1) for gradient in totals]
    row_scaled = [
        jnp.sum(gradient * gradient / col_next[..., None, :], -1)
        for gradient, col_next in zip(totals, cols_new)
    ]
    weight_sq = [jnp.sum(weight * weight, axis=(-2, -1)) for weight in weights]
    row_sums, row_scaled, weight_sq = lax.psum((row_parts, row_scaled, weight_sq), "shard")
    rows_new = [
        decay * row_state
        + (1.0 - decay) * (row_sum / (gradient.shape[-1] * shard_count) + eps_one)
        for row_sum, gradient, row_state in zip(row_sums, totals, rows_old)
    ]
    row_means = [jnp.mean(row_next, -1) for row_next in rows_new]
    total_sq = sum(
        jnp.sum(row_mean * jnp.sum(scaled / row_next, -1))
        for scaled, row_next, row_mean in zip(row_scaled, rows_new, row_means)
    )
    count = sum((weight.size for weight in weights)) * shard_count
    update_rms = jnp.sqrt(total_sq / count)
    factor = jnp.maximum(1.0, update_rms / clip_level)
    news = []
    for index in range(4):
        numel = weights[index].shape[-2] * weights[index].shape[-1] * shard_count
        weight_rms = jnp.sqrt(weight_sq[index] / numel)
        step_size = rate * jnp.maximum(eps_two, weight_rms) / factor
        row_scale = jnp.asarray(step_size)[..., None] * lax.rsqrt(
            rows_new[index] / row_means[index][..., None]
        )
        news.append(
            weights[index]
            - totals[index] * row_scale[..., :, None] * lax.rsqrt(cols_new[index])[..., None, :]
        )
    return (
        loss_sum,
        update_rms,
        totals[0],
        totals[1],
        totals[2],
        totals[3],
        rows_new[0],
        cols_new[0],
        rows_new[1],
        cols_new[1],
        rows_new[2],
        cols_new[2],
        rows_new[3],
        cols_new[3],
        news[0],
        news[1],
        news[2],
        news[3],
    )


def solution(mesh):
    placed = (
        P(("rep", "shard"), None),
        P(("rep", "shard"), None),
        P(("rep", "shard"), None),
        P(("rep", "shard")),
        P(("rep", "shard")),
        P(("rep", "shard")),
        P(None, None, "shard"),
        P(None, None, "shard"),
        P(None, "shard"),
        P(None, "shard"),
        P(),
        P(None, "shard"),
        P(),
        P(None, "shard"),
        P(),
        P("shard"),
        P(),
        P("shard"),
    )
    return jax.shard_map(
        on_device,
        mesh=mesh,
        in_specs=placed,
        out_specs=(
            P(),
            P(),
            P(None, None, "shard"),
            P(None, None, "shard"),
            P(None, "shard"),
            P(None, "shard"),
            P(),
            P(None, "shard"),
            P(),
            P(None, "shard"),
            P(),
            P("shard"),
            P(),
            P("shard"),
            P(None, None, "shard"),
            P(None, None, "shard"),
            P(None, "shard"),
            P(None, "shard"),
        ),
        check_vma=False,
    )
```

time: 2050 us -> 853 us (0.42)
  waiting for transfers between devices: 1090 us -> 403 us
  local copies, waits for them, and re-layouts: 586 us -> 61.5 us
  blocking collectives: 58 us -> 179 us
  other arithmetic: 166 us -> 86.3 us
  matrix products: 117 us -> 91.1 us
    unnamed x18 -> x8, waiting for transfers between devices: 775 us -> 19.4 us
    unnamed x257 -> x212, local copies, waits for them, and re-layouts: 391 us -> 17.7 us
    psum x0 -> x3, waiting for transfers between devices: none -> 348 us  [the longest x1 252 us: reduce_heavy(): total_in = lax.psum(g_in_t.astype(jnp.bfloat16), ('rep', 'shard'))]
    all_gather x7 -> x3, waiting for transfers between devices: 273 us -> 34.8 us  [the longest x1 31.1 us: gather_heavy(): all_in = lax.all_gather(in_low, 'shard', axis=1, tiled=True)]
    all_gather x0 -> x6, blocking collectives: none -> 125 us  [the longest x1 45.6 us: on_device(): d_low = lax.all_gather(d_low, both, axis=0, tiled=True)]
    another operation x3 -> x1, local copies, waits for them, and re-layouts: 88.9 us -> 2.37 us  [the longest x1 63.9 us: on_device(): local_in = jnp.stack(grads_in, 0)]
    reduce_sum x4 -> x2, other arithmetic: 61 us -> 1.9 us  [on_device(): jnp.mean(gradient * gradient, -2) + eps_one]
    reduce_scatter x2 -> x0, local copies, waits for them, and re-layouts: 52.3 us -> none  [the longest x1 27.2 us: on_device(): lax.psum_scatter(parts[1], 'rep', scatter_dimension=1, tiled=True)]
  transfers between devices with their start and end apart: 13 -> 7, of which waited for: 11 -> 6; matrix products, arithmetic and copies ran while one was open for 32% -> 11% of each run, Pallas kernels for 0% -> 0%
where the time goes in v1:
time: 853 us; the launch traced here: 846 us
  waiting for transfers between devices  403 us (47%)
  blocking collectives  179 us (21%)
  matrix products  91.1 us (11%)
  other arithmetic  86.3 us (10%)
  local copies, waits for them, and re-layouts  61.5 us (7%)
  between operations  25.6 us (3%)
    psum x1, waiting for transfers between devices, reduce_heavy(): total_in = lax.psum(g_in_t.astype(jnp.bfloat16), ('rep', 'shard'))  252 us
    psum x1, waiting for transfers between devices, on_device(): lax.psum((loss_local, jnp.concatenate([g_patch, g_head_t], 0)), both)  77.3 us
    all_gather x1, blocking collectives, on_device(): d_low = lax.all_gather(d_low, both, axis=0, tiled=True)  45.6 us
    all_gather x1, blocking collectives, on_device(): lax.all_gather(jnp.stack([times, labels, dropped]), both, axis=1, tiled=T...  43.3 us
    psum x1, blocking collectives, on_device(): lax.psum((loss_local, jnp.concatenate([g_patch, g_head_t], 0)), both)  39.4 us
    all_gather x1, waiting for transfers between devices, gather_heavy(): all_in = lax.all_gather(in_low, 'shard', axis=1, tiled=True)  31.1 us
    dot_general x10, matrix products, weight_grad(): lax.dot_general(flat_left, flat_back, (((0,), (0,)), ((), ())), preferred...  23.7 us
    dot_general x5, matrix products, input_grad_t(): return jnp.matmul(back, weight_t, preferred_element_type=jnp.float32)  20.8 us
  transfers between devices with their start and end apart: 7, of which 6 were waited for; matrix products, arithmetic and copies ran while one was open for 11% of the time, Pallas kernels for 0%

profile of v1, /device:TPU:0, one launch (start us, length us, event | category | flops | bytes accessed | tf_op | source)
XLA Modules:
  0.0 846.1 jit_solution(821177138511907284)
XLA Ops:
  11.2 9.8 %multiply_reduce_fusion = (f32[]{:T(128)}, bf16[1,768,2496]{1,2,0:T(8,128)(2,1)}) fusion(f32[1,768,2496]{1,2,0:T(8,128)} %param.24), kind=kLoop, calls=%fused_computation.11 | loop fusion | flops 5750783 | bytes 11501572 | tf_op jit(solution)/shard_map/reduce_sum | solution.py:320
  25.7 43.3 %all-gather.5 = s32[32,2,3]{2,1,0:T(2,128)S(1)} all-gather(s32[1,2,3]{2,1,0:T(2,128)S(1)} %bitcast.247), channel_id=1, replica_groups=mesh['rep'=8,'shard'=4] {'rep','shard'}, dimensions={0}, use_global_device_ids=true | all-gather | bytes 792 | tf_op jit(solution)/shard_map/all_gather | solution.py:176
  70.7 5.3 all-gather.4
  78.3 6.2 all-gather.6
  85.6 14.9 %all-gather = f32[256,772]{1,0:T(8,128)S(1)} all-gather(f32[64,772]{1,0:T(8,128)S(1)} %pad_maximum_fusion.6), channel_id=2, replica_groups=mesh['rep'=8,'shard'=4] {'shard'}, dimensions={0}, use_global_device_ids=true | all-gather | bytes 988160 | tf_op jit(solution)/shard_map/all_gather | solution.py:187
  102.4 9.7 %all-gather.1 = f32[32,3076]{1,0:T(8,128)S(1)} all-gather(f32[8,3076]{1,0:T(8,128)S(1)} %pad_maximum_fusion.8), channel_id=3, replica_groups=mesh['rep'=8,'shard'=4] {'shard'}, dimensions={0}, use_global_device_ids=true | all-gather | bytes 492160 | tf_op jit(solution)/shard_map/all_gather | solution.py:198
  121.5 31.1 %all-gather.13.cloned.1.call-done = bf16[1,768,9984]{1,2,0:T(8,128)(2,1)} async-done(((bf16[1,768,2496]{1,2,0:T(8,128)(2,1)}), bf16[1,768,9984]{1,2,0:T(8,128)(2,1)}) %all-gather.13.cloned.1.call-update) | async-done | bytes 15335440 | tf_op jit(solution)/shard_map/all_gather | solution.py:123
  152.6 20.1 %copy.91 = bf16[1,768,9984]{2,1,0:T(8,128)(2,1)} copy(bf16[1,768,9984]{1,2,0:T(8,128)(2,1)} %all-gather.13.cloned.1.call-done) | data formatting | bytes 30670848 | tf_op jit(solution)/shard_map/all_gather | solution.py:123
  172.7 5.6 convolution_convert_fusion
  201.7 5.1 fusion.20
  216.8 6.9 fusion.4
  228.6 5.1 multiply_reduce_fusion.15
  247.2 5.1 fusion.37
  252.3 6.8 multiply_reduce_fusion.3
  273.7 5.0 multiply_reduce_fusion.9
  284.6 45.6 %all-gather.8 = bf16[32,2,6144]{2,1,0:T(2,128)(2,1)} all-gather(bf16[1,2,6144]{2,1,0:T(2,128)(2,1)S(1)} %bitcast.244), channel_id=1, replica_groups=mesh['rep'=8,'shard'=4] {'rep','shard'}, dimensions={0}, use_global_device_ids=true | all-gather | bytes 811008 | tf_op jit(solution)/shard_map/all_gather | solution.py:276
  345.2 7.2 pad_maximum_fusion
  354.0 19.0 %all-reduce.11.cloned.1.call-done = f32[64,768]{1,0:T(8,128)} async-done(((f32[64,768]{1,0:T(8,128)}), f32[64,768]{1,0:T(8,128)}) %all-reduce.11.cloned.1.call-update) | async-done | bytes 196624 | tf_op jit(solution)/shard_map/psum | solution.py:283
  377.0 5.3 pad_maximum_fusion.1
  383.9 39.4 %psum.119 = f32[]{:T(128)} all-reduce(f32[]{:T(128)S(6)} %mul.651), channel_id=1, replica_groups=mesh['rep'=8,'shard'=4] {'rep','shard'}, use_global_device_ids=true, to_apply=%region_9.10 | all-reduce | flops 1 | bytes 8 | tf_op jit(solution)/shard_map/psum | solution.py:298
  423.3 77.3 %all-reduce.13.cloned.1.call-done = f32[32,768]{1,0:T(8,128)} async-done(((f32[32,768]{1,0:T(8,128)}), f32[32,768]{1,0:T(8,128)}) %all-reduce.13.cloned.1.call-update) | async-done | bytes 98320 | tf_op jit(solution)/shard_map/psum | solution.py:298
  506.1 19.3 %reduce-scatter.4.cloned.1.call-done = f32[192,64]{1,0:T(8,128)} async-done(((f32[768,64]{1,0:T(8,128)}), f32[192,64]{1,0:T(8,128)}) %reduce-scatter.4.cloned.1.call-update) | async-done | bytes 49168
  528.8 252.0 %all-reduce.15.cloned.1.call-done = (bf16[5376,768]{1,0:T(8,128)(2,1)}, bf16[768,3840]{1,0:T(8,128)(2,1)}) async-done(((bf16[5376,768]{1,0:T(8,128)(2,1)}, bf16[768,3840]{1,0:T(8,128)(2,1)}), (bf16[5376,768]{1,0:T(8,128)(2,1)}, bf16[768,3840]{1,0:T(8,128)(2,1)})) %all-reduce.15.cloned.1.call-update) | async-done | bytes 14155792 | tf_op jit(solution)/shard_map/psum | solution.py:130
  795.2 14.4 %all-reduce.5 = (f32[1,768]{1,0:T(1,128)}, f32[1,768]{1,0:T(1,128)}, f32[1,3840]{1,0:T(1,128)}, f32[1,3840]{1,0:T(1,128)}, f32[768]{0:T(1024)}, /*index=5*/f32[7...) all-reduce(f32[1,768]{1,0:T(1,128)S(1)} %reduce_sum.517, ...), channel_id=1, replica_groups=mesh['rep'=8,'shard'=4] {'shard'}, use_global_device_ids=true, to_apply=%region_29.30 | all-reduce | flops 13302 | bytes 106416 | tf_op jit(solution)/shard_map/psum | solution.py:321
  (358 shorter events, 161.2 us)
Async XLA Ops:
  7.2 110.7 %all-gather.17.cloned.1.call-start = ((), (), s32[]{:S(2)}) async-start(), calls=%async_computation.5 | async-start | bytes 4485120 | tf_op jit(solution)/shard_map/all_gather | solution.py:206
  11.2 141.4 %all-gather.13.cloned.1.call-start = ((), (), s32[]{:S(2)}) async-start(), calls=%async_computation.3 | async-start | bytes 19169280 | tf_op jit(solution)/shard_map/all_gather | solution.py:123
  21.1 48.1 %copy-start.52 = (f32[2,4096]{1,0:T(2,128)S(1)}, f32[2,4096]{1,0:T(2,128)}, u32[]{:S(2)}) copy-start(f32[2,4096]{1,0:T(2,128)} %param.18) | copy-start | bytes 98308
  21.1 48.3 %copy-start.53 = (f32[2,4096]{1,0:T(2,128)S(1)}, f32[2,4096]{1,0:T(2,128)}, u32[]{:S(2)}) copy-start(f32[2,4096]{1,0:T(2,128)} %param.19) | copy-start | bytes 98308
  21.1 177.8 %all-gather.15.cloned.1.call-start = ((), (), s32[]{:S(2)}) async-start(), calls=%async_computation.4 | async-start | bytes 7372800 | tf_op jit(solution)/shard_map/all_gather | solution.py:124
  25.5 44.1 %copy-start.54 = (f32[2,4096]{1,0:T(2,128)S(1)}, f32[2,4096]{1,0:T(2,128)}, u32[]{:S(2)}) copy-start(f32[2,4096]{1,0:T(2,128)} %param.20) | copy-start | bytes 98308
  25.5 45.0 %copy-start.11 = (f32[1273,192]{0,1:T(8,128)S(1)}, f32[1273,192]{0,1:T(8,128)}, u32[]{:S(2)}) copy-start(f32[1273,192]{0,1:T(8,128)} %param.27) | copy-start | bytes 2932996
  25.5 347.5 %all-reduce.11.cloned.1.call-start = ((), (), s32[]{:S(2)}) async-start(), calls=%async_computation.1 | async-start | bytes 393216 | tf_op jit(solution)/shard_map/psum | solution.py:283
  345.1 28.0 %copy-start.19 = (f32[64,580]{1,0:T(8,128)S(1)}, f32[64,580]{1,0:T(8,128)}, u32[]{:S(2)}) copy-start(f32[64,580]{1,0:T(8,128)} %copy-done.18) | copy-start | bytes 445444
  345.1 155.5 %all-reduce.13.cloned.1.call-start = ((), (), s32[]{:S(2)}) async-start(), calls=%async_computation.2 | async-start | bytes 196608 | tf_op jit(solution)/shard_map/psum | solution.py:298
  352.4 24.6 %copy-start.15 = (bf16[768,768]{1,0:T(8,128)(2,1)S(1)}, bf16[768,768]{1,0:T(8,128)(2,1)}, u32[]{:S(2)}) copy-start(bf16[768,768]{1,0:T(8,128)(2,1)} %copy.109) | copy-start | bytes 3538948
  354.0 171.4 %reduce-scatter.4.cloned.1.call-start = ((), (), s32[]{:S(2)}) async-start(), calls=%async_computation.6 | async-start | bytes 491520
  376.9 403.9 %all-reduce.15.cloned.1.call-start = ((), (), s32[]{:S(2)}) async-start(), calls=%async_computation.7 | async-start | bytes 28311552 | tf_op jit(solution)/shard_map/psum | solution.py:130
  382.3 119.3 %copy-start.22 = (bf16[768,64]{0,1:T(8,128)(2,1)S(1)}, bf16[768,64]{0,1:T(8,128)(2,1)}, u32[]{:S(2)}) copy-start(bf16[768,64]{0,1:T(8,128)(2,1)} %copy-done.21) | copy-start | bytes 294916
  382.3 119.3 %copy-start.24 = (bf16[64,768]{1,0:T(8,128)(2,1)S(1)}, bf16[64,768]{1,0:T(8,128)(2,1)}, u32[]{:S(2)}) copy-start(bf16[64,768]{1,0:T(8,128)(2,1)} %copy-done.23) | copy-start | bytes 294916
  503.0 23.3 %copy-start.34 = (f32[64,192]{1,0:T(8,128)S(1)}, f32[64,192]{1,0:T(8,128)}, u32[]{:S(2)}) copy-start(f32[64,192]{1,0:T(8,128)} %copy-done.33) | copy-start | bytes 147460
  503.0 23.3 %copy-start.41 = (bf16[64,128]{1,0:T(8,128)(2,1)S(1)}, bf16[64,128]{1,0:T(8,128)(2,1)}, u32[]{:S(2)}) copy-start(bf16[64,128]{1,0:T(8,128)(2,1)} %copy-done.40) | copy-start | bytes 49156
  503.1 23.3 %copy-start.43 = (bf16[64,128]{1,0:T(8,128)(2,1)S(1)}, bf16[64,128]{1,0:T(8,128)(2,1)}, u32[]{:S(2)}) copy-start(bf16[64,128]{1,0:T(8,128)(2,1)} %copy-done.42) | copy-start | bytes 49156
  503.7 21.7 %copy-start.63 = (f32[580]{0:T(1024)}, f32[580]{0:T(1024)S(1)}, u32[]{:S(2)}) copy-start(f32[580]{0:T(1024)S(1)} %get-tuple-element.62) | copy-start | bytes 6964
  505.2 22.1 %copy-start.83 = (f32[192]{0:T(256)S(1)}, f32[192]{0:T(256)}, u32[]{:S(2)}) copy-start(f32[192]{0:T(256)} %param.35) | copy-start | bytes 2308
  527.1 258.7 %copy-start.7 = (f32[1273,192]{0,1:T(8,128)}, f32[1273,192]{0,1:T(8,128)S(1)}, u32[]{:S(2)}) copy-start(f32[1273,192]{0,1:T(8,128)S(1)} %concatenate.65) | copy-start | bytes 2932996
  528.0 252.8 %copy-start.79 = (f32[192]{0:T(256)}, f32[192]{0:T(256)S(1)}, u32[]{:S(2)}) copy-start(f32[192]{0:T(256)S(1)} %get-tuple-element.60) | copy-start | bytes 2308
  792.4 41.5 %slice-start.2 = ((s8[7667712]{0:T(1024)(128)(4,1)}), s8[3473408]{0:T(1024)(128)(4,1)S(1)}, s32[]{:S(2)}) async-start(s8[7667712]{0:T(1024)(128)(4,1)} %bitcast.210), calls=%async_computation.10 | async-start | bytes 6946816
  795.2 31.1 %copy-start.65 = (f32[580]{0:T(1024)S(1)}, f32[580]{0:T(1024)}, u32[]{:S(2)}) copy-start(f32[580]{0:T(1024)} %get-tuple-element.61) | copy-start | bytes 6964
  (81 other events, 352.2 us)
Sparse Core Ops, SparseCore 0:
  11.3 33.8 all-gather.16
  46.8 105.7 all-gather.12
  154.7 44.1 all-gather.14
  345.2 27.7 all-reduce.10
  380.0 120.5 all-reduce.12
  503.7 21.6 reduce-scatter.3
  533.5 247.2 all-reduce.14

commit v2 on v1

--- a/solution.py
+++ b/solution.py
@@ -1,8 +1,11 @@
+import functools
 import math
 
 import jax
 import jax.numpy as jnp
 from jax import lax
+from jax.experimental import pallas as pl
+from jax.experimental.pallas import tpu as pltpu
 from jax.sharding import PartitionSpec as P
 
 HEADS = 12
@@ -125,14 +128,326 @@
     return all_in[:, 6 * width : 9 * width].T, all_in[:, 9 * width :].T, all_out.T
 
 
-def reduce_heavy(g_in_t, g_out_t, in_cols, out_cols):
-    width = g_in_t.shape[1]
-    total_in = lax.psum(g_in_t.astype(jnp.bfloat16), ("rep", "shard"))
-    total_out = lax.psum(g_out_t.astype(jnp.bfloat16), ("rep", "shard"))
+MESH = pl.DeviceIdType.MESH
+PIECES = 4
+
+
+def heavy_chunks(width):
+    half = width // 2
+    return (
+        (0, 0, width, 0, width, False),
+        (0, 0, width, 2 * width, width, False),
+        (1, 0, 2 * width, 0, half, True),
+        (1, 2 * width, 2 * width, 0, half, True),
+        (2, 0, width, 0, half, False),
+        (3, 0, width, 0, half, False),
+        (3, width, width, 0, half, True),
+        (3, 2 * width, width, 0, half, True),
+    )
+
+
+def add_rows(target, left, right, rows):
+    block = 48
+
+    def body(index, carry):
+        span = pl.ds(pl.multiple_of(index * block, block), block)
+        target[span] = left[span] + right[span]
+        return carry
+
+    lax.fori_loop(0, rows // block, body, 0)
+
+
+def reduce_kernel(lines, chunks, g0, g1, g2, g3, f0, f1, f2, f3, *scratch):
+    count = len(chunks)
+    grads, finals = (g0, g1, g2, g3), (f0, f1, f2, f3)
+    by_core, by_y, by_x, by_z = (scratch[k * count : (k + 1) * count] for k in range(4))
+    send, recv, zsend, zrecv, wsend, wrecv = scratch[4 * count :]
+    rep, shard = lax.axis_index("rep"), lax.axis_index("shard")
+    x, z = lax.rem(rep, 2), lax.div(rep, 2)
+    core, y = lax.rem(shard, 2), lax.div(shard, 2)
+    to_core = (rep, shard + 1 - 2 * core)
+    to_y = (rep, shard + 2 - 4 * y)
+    to_x = (rep + 1 - 2 * x, shard)
+
+    def line_peer(step):
+        return lax.rem(z + step, lines)
+
+    barrier = pltpu.get_barrier_semaphore()
+    for peer in (to_core, to_y, to_x):
+        pl.semaphore_signal(barrier, inc=1, device_id=peer, device_id_type=MESH)
+    for step in range(1, lines):
+        pl.semaphore_signal(
+            barrier, inc=1, device_id=(line_peer(step) * 2 + x, shard), device_id_type=MESH
+        )
+    pl.semaphore_wait(barrier, 3 + lines - 1)
+
+    stride = lines // PIECES
+    owns = lax.rem(z, stride) == 0
+    mine = lax.div(z, stride)
+    sends = []
+
+    def remote(source, target, send_sem, recv_sem, peer):
+        return pltpu.make_async_remote_copy(
+            src_ref=source,
+            dst_ref=target,
+            send_sem=send_sem,
+            recv_sem=recv_sem,
+            device_id=peer,
+            device_id_type=MESH,
+        )
+
+    def rows_of(ref, start, size):
+        return ref.at[pl.ds(pl.multiple_of(start, 16), size)]
+
+    def lanes_at(index, ref, row, rows, which):
+        _, _, _, lane, lanes, _ = chunks[index]
+        return ref.at[
+            pl.ds(pl.multiple_of(row, 16), rows), pl.ds(pl.multiple_of(lane + which * lanes, 128), lanes)
+        ]
+
+    def core_copy(i):
+        array, row, rows = chunks[i][:3]
+        return remote(
+            lanes_at(i, grads[array], row, rows, 1 - core), by_core[i], send.at[i, 0], recv.at[i, 0], to_core
+        )
+
+    def y_copy(i):
+        half = chunks[i][2] // 2
+        return remote(
+            rows_of(by_core[i], (1 - y) * half, half), by_y[i], send.at[i, 1], recv.at[i, 1], to_y
+        )
+
+    def x_copy(i):
+        quarter = chunks[i][2] // 4
+        return remote(
+            rows_of(by_y[i], (1 - x) * quarter, quarter), by_x[i], send.at[i, 2], recv.at[i, 2], to_x
+        )
+
+    def z_copy(i, piece):
+        size = chunks[i][2] // 4 // PIECES
+        owner = piece * stride
+        slot = lax.rem(z - owner - 1 + lines, lines)
+        return remote(
+            by_x[i].at[pl.ds(piece * size, size)],
+            by_z[i].at[slot],
+            zsend.at[i, piece],
+            zrecv.at[i, slot],
+            (owner * 2 + x, shard),
+        )
+
+    def final_rows(i, side, start, size, which):
+        array, row, rows = chunks[i][:3]
+        return lanes_at(i, finals[array], row + side * (rows // 2) + start, size, which)
+
+    def cross_copy(i):
+        size = chunks[i][2] // 4 // PIECES
+        part = final_rows(i, 0, (x * PIECES + mine) * size, size, core)
+        return remote(part, part, send.at[i, 3], recv.at[i, 3], to_y)
+
+    def line_copy(i, which, side, step):
+        size = chunks[i][2] // 4 // PIECES
+        part = final_rows(i, side, (x * PIECES + mine) * size, size, core)
+        return remote(
+            part, part, wsend.at[i, which, step - 1], wrecv.at[i, which, mine], (line_peer(step) * 2 + x, shard)
+        )
+
+    def line_arrival(i, which, side, piece):
+        size = chunks[i][2] // 4 // PIECES
+        part = final_rows(i, side, (x * PIECES + piece) * size, size, core)
+        return remote(part, part, wsend.at[i, which, 0], wrecv.at[i, which, piece], to_core)
+
+    def pair_copy(i, which, side, column):
+        quarter = chunks[i][2] // 4
+        part = final_rows(i, side, column * quarter, quarter, core)
+        return remote(part, part, send.at[i, 4 + which], recv.at[i, 4 + which], to_x)
+
+    def last_copy(i, which, side, half):
+        rows = chunks[i][2] // 2
+        part = final_rows(i, side, 0, rows, half)
+        return remote(part, part, send.at[i, 6 + which], recv.at[i, 6 + which], to_core)
+
+    def sides(i, action):
+        if chunks[i][5]:
+
+            @pl.when(y == 1)
+            def _():
+                action(0, 1)
+                action(1, 0)
+
+        else:
+            action(0, y)
+
+    def stage0(i):
+        core_copy(i).start()
+
+    def stage1(i):
+        array, row, rows = chunks[i][:3]
+        core_copy(i).wait_recv()
+        add_rows(by_core[i], by_core[i], lanes_at(i, grads[array], row, rows, core), rows)
+        y_copy(i).start()
+
+    def stage2(i):
+        half = chunks[i][2] // 2
+        y_copy(i).wait_recv()
+        add_rows(by_y[i], by_y[i], rows_of(by_core[i], y * half, half), half)
+        x_copy(i).start()
+
+    def stage3(i):
+        quarter = chunks[i][2] // 4
+        x_copy(i).wait_recv()
+        add_rows(by_x[i], by_x[i], rows_of(by_y[i], x * quarter, quarter), quarter)
+        for piece in range(PIECES):
+
+            @pl.when(z != piece * stride)
+            def _():
+                z_copy(i, piece).start()
+
+    def stage4(i):
+        size = chunks[i][2] // 4 // PIECES
+
+        @pl.when(owns)
+        def _():
+            for slot in range(lines - 1):
+                remote(
+                    by_z[i].at[slot], by_z[i].at[slot], zsend.at[i, 0], zrecv.at[i, slot], to_core
+                ).wait_recv()
+            target = final_rows(i, y, (x * PIECES + mine) * size, size, core)
+
+            def body(index, carry):
+                total = by_x[i][
+                    pl.ds(pl.multiple_of(mine * size + index * 16, 16), 16)
+                ].astype(jnp.float32)
+                for slot in range(lines - 1):
+                    total += by_z[i][slot, pl.ds(pl.multiple_of(index * 16, 16), 16)].astype(jnp.float32)
+                target[pl.ds(pl.multiple_of(index * 16, 16), 16)] = total.astype(jnp.bfloat16)
+                return carry
+
+            lax.fori_loop(0, size // 16, body, 0)
+            if chunks[i][5]:
+
+                @pl.when(y == 0)
+                def _():
+                    cross_copy(i).start()
+
+                @pl.when(y == 1)
+                def _():
+                    for step in range(1, lines):
+                        line_copy(i, 0, 1, step).start()
+            else:
+                for step in range(1, lines):
+                    line_copy(i, 0, y, step).start()
+
+    def stage5(i):
+        if chunks[i][5]:
+
+            @pl.when(jnp.logical_and(owns, y == 1))
+            def _():
+                cross_copy(i).wait_recv()
+                for step in range(1, lines):
+                    line_copy(i, 1, 0, step).start()
+
+    def stage6(i):
+        def action(which, side):
+            for piece in range(PIECES):
+
+                @pl.when(z != piece * stride)
+                def _():
+                    line_arrival(i, which, side, piece).wait_recv()
+
+            pair_copy(i, which, side, x).start()
+
+        sides(i, action)
+
+    def stage7(i):
+        def action(which, side):
+            pair_copy(i, which, side, 1 - x).wait_recv()
+            last_copy(i, which, side, core).start()
+
+        sides(i, action)
+
+    def stage8(i):
+        sides(i, lambda which, side: last_copy(i, which, side, 1 - core).wait_recv())
+
+    stages = (stage0, stage1, stage2, stage3, stage4, stage5, stage6, stage7, stage8)
+    for tick in range(count + len(stages) - 1):
+        for k, stage in enumerate(stages):
+            if 0 <= tick - k < count:
+                stage(tick - k)
+
+    for i in range(count):
+        core_copy(i).wait_send()
+        y_copy(i).wait_send()
+        x_copy(i).wait_send()
+        for piece in range(PIECES):
+
+            @pl.when(z != piece * stride)
+            def _():
+                z_copy(i, piece).wait_send()
+
+        if chunks[i][5]:
+
+            @pl.when(jnp.logical_and(owns, y == 0))
+            def _():
+                cross_copy(i).wait_send()
+
+        def action(which, side):
+            @pl.when(owns)
+            def _():
+                for step in range(1, lines):
+                    line_copy(i, which, side, step).wait_send()
+
+            pair_copy(i, which, side, x).wait_send()
+            last_copy(i, which, side, core).wait_send()
+
+        sides(i, action)
+
+
+def reduce_call(lines, g_fc2_t, g_fc1_t, g_o_t, g_qkv_t):
+    width = g_o_t.shape[0]
+    chunks = heavy_chunks(width)
+    count = len(chunks)
+    grads = (g_fc2_t, g_fc1_t, g_o_t, g_qkv_t)
+    low = jnp.bfloat16
+    sizes = [(rows, lanes) for _, _, rows, _, lanes, _ in chunks]
+    return pl.pallas_call(
+        functools.partial(reduce_kernel, lines, chunks),
+        out_shape=[jax.ShapeDtypeStruct(item.shape, low) for item in grads],
+        in_specs=[pl.BlockSpec(memory_space=pltpu.VMEM)] * 4,
+        out_specs=[pl.BlockSpec(memory_space=pltpu.VMEM)] * 4,
+        scratch_shapes=[pltpu.VMEM((rows, lanes), low) for rows, lanes in sizes]
+        + [pltpu.VMEM((rows // 2, lanes), low) for rows, lanes in sizes]
+        + [pltpu.VMEM((rows // 4, lanes), low) for rows, lanes in sizes]
+        + [pltpu.VMEM((lines - 1, rows // 4 // PIECES, lanes), low) for rows, lanes in sizes]
+        + [
+            pltpu.SemaphoreType.DMA((count, 8)),
+            pltpu.SemaphoreType.DMA((count, 8)),
+            pltpu.SemaphoreType.DMA((count, PIECES)),
+            pltpu.SemaphoreType.DMA((count, lines - 1)),
+            pltpu.SemaphoreType.DMA((count, 2, lines - 1)),
+            pltpu.SemaphoreType.DMA((count, 2, PIECES)),
+        ],
+        compiler_params=pltpu.CompilerParams(
+            collective_id=1, has_side_effects=True, vmem_limit_bytes=60 * 1024 * 1024
+        ),
+    )(*grads)
+
+
+def reduce_heavy(g_fc2_t, g_fc1_t, g_o_t, g_qkv_t, in_cols, out_cols):
+    width = g_o_t.shape[1]
+    fc2, fc1, attn_out, qkv = reduce_call(
+        lax.axis_size("rep") // 2,
+        *(item.astype(jnp.bfloat16) for item in (g_fc2_t, g_fc1_t, g_o_t, g_qkv_t)),
+    )
     place = lax.axis_index("shard")
-    padded = jnp.pad(total_in, ((6 * width, 0), (0, 0)))
+    padded = jnp.concatenate([jnp.zeros((6 * width, width), jnp.bfloat16), qkv, fc1], 0)
     own_in = lax.dynamic_slice_in_dim(padded, place * in_cols, in_cols, 0)
-    own_out = lax.dynamic_slice_in_dim(total_out, place * out_cols, out_cols, 0)
+    own_out = jnp.concatenate(
+        [
+            lax.dynamic_slice_in_dim(item, place * out_cols, out_cols, 0)
+            for item in (attn_out, fc2)
+        ],
+        1,
+    )
     return own_in.T.astype(jnp.float32), own_out.T.astype(jnp.float32)
 
 
@@ -263,12 +578,7 @@
     d_from_first, d_shift_one, d_scale_one = first_pull(d_normed)
     d_hidden = d_middle + d_from_first
     g_patch = weight_grad(state, d_hidden.astype(jnp.bfloat16))
-    heavy_in, heavy_out = reduce_heavy(
-        jnp.concatenate([g_qkv_t, g_fc1_t], 0),
-        jnp.concatenate([g_o_t, g_fc2_t], 1),
-        in_cols,
-        out_cols,
-    )
+    heavy_in, heavy_out = reduce_heavy(g_fc2_t, g_fc1_t, g_o_t, g_qkv_t, in_cols, out_cols)
     d_low = jnp.concatenate(
         [d_shift_one, d_scale_one, d_gate_one, d_shift_two, d_scale_two, d_gate_two, d_shift, d_scale],
         -1,

time: 853 us -> 743 us (0.87)
  waiting for transfers between devices: 403 us -> 148 us
  Pallas kernels: 0 us -> 119 us
  blocking collectives: 179 us -> 221 us
  other arithmetic: 86.3 us -> 68.9 us
    psum x1 -> x0, waiting for transfers between devices: 252 us -> none  [reduce_heavy(): total_in = lax.psum(g_in_t.astype(jnp.bfloat16), ('rep', 'shard'))]
    pallas_call x0 -> x1, Pallas kernels: none -> 119 us  [reduce_call(): pl.pallas_call(functools.partial(reduce_kernel, lines, chunks), out_shape...]
    psum x1, blocking collectives: 39.4 us -> 84 us  [on_device(): lax.psum((loss_local, jnp.concatenate([g_patch, g_head_t], 0)), both)]
    psum x1, waiting for transfers between devices: 77.3 us -> 59 us  [on_device(): lax.psum((loss_local, jnp.concatenate([g_patch, g_head_t], 0)), both)]
    psum x1, waiting for transfers between devices: 19 us -> 33.7 us  [on_device(): lax.psum(input_grad(d_in, in_low) + input_grad(d_fin, head_low), 'shard')]
    concatenate x2 -> x0, other arithmetic: 12.5 us -> none  [the longest x1 7.22 us: on_device(): jnp.concatenate([g_qkv_t, g_fc1_t], 0)]
    unnamed x8 -> x7, waiting for transfers between devices: 19.4 us -> 17.3 us
    unnamed x212 -> x186, local copies, waits for them, and re-layouts: 17.7 us -> 16.4 us
  transfers between devices with their start and end apart: 7 -> 6, of which waited for: 6 -> 5; matrix products, arithmetic and copies ran while one was open for 11% -> 12% of each run, Pallas kernels for 0% -> 0%
where the time goes in v2:
time: 743 us; the launch traced here: 736 us
  blocking collectives  221 us (30%)
  waiting for transfers between devices  148 us (20%)
  Pallas kernels  119 us (16%)
  matrix products  93.9 us (13%)
  other arithmetic  68.9 us (9%)
  local copies, waits for them, and re-layouts  59.7 us (8%)
  between operations  25.9 us (3%)
    pallas_call x1, Pallas kernels, reduce_call(): pl.pallas_call(functools.partial(reduce_kernel, lines, chunks), out_shape...  119 us
    psum x1, blocking collectives, on_device(): lax.psum((loss_local, jnp.concatenate([g_patch, g_head_t], 0)), both)  84 us
    psum x1, waiting for transfers between devices, on_device(): lax.psum((loss_local, jnp.concatenate([g_patch, g_head_t], 0)), both)  59 us
    all_gather x1, blocking collectives, on_device(): d_low = lax.all_gather(d_low, both, axis=0, tiled=True)  45.6 us
    all_gather x1, blocking collectives, on_device(): lax.all_gather(jnp.stack([times, labels, dropped]), both, axis=1, tiled=T...  43.3 us
    psum x1, waiting for transfers between devices, on_device(): lax.psum(input_grad(d_in, in_low) + input_grad(d_fin, head_low), 'shard')  33.7 us
    all_gather x1, waiting for transfers between devices, gather_heavy(): all_in = lax.all_gather(in_low, 'shard', axis=1, tiled=True)  33 us
    dot_general x10, matrix products, weight_grad(): lax.dot_general(flat_left, flat_back, (((0,), (0,)), ((), ())), preferred...  26.8 us
  transfers between devices with their start and end apart: 6, of which 5 were waited for; matrix products, arithmetic and copies ran while one was open for 12% of the time, Pallas kernels for 0%

profile of v2, /device:TPU:0, one launch (start us, length us, event | category | flops | bytes accessed | tf_op | source)
XLA Modules:
  0.0 735.8 jit_solution(14478534032716312304)
XLA Ops:
  11.2 9.8 %multiply_reduce_fusion = (f32[]{:T(128)}, bf16[1,768,2496]{1,2,0:T(8,128)(2,1)}) fusion(f32[1,768,2496]{1,2,0:T(8,128)} %param.24), kind=kLoop, calls=%fused_computation.11 | loop fusion | flops 5750783 | bytes 11501572 | tf_op jit(solution)/shard_map/reduce_sum | solution.py:630
  25.8 43.3 %all-gather.5 = s32[32,2,3]{2,1,0:T(2,128)S(1)} all-gather(s32[1,2,3]{2,1,0:T(2,128)S(1)} %bitcast.244), channel_id=1, replica_groups=mesh['rep'=8,'shard'=4] {'rep','shard'}, dimensions={0}, use_global_device_ids=true | all-gather | bytes 792 | tf_op jit(solution)/shard_map/all_gather | solution.py:491
  70.4 5.3 all-gather.4
  76.6 6.2 all-gather.6
  84.6 14.9 %all-gather = f32[256,772]{1,0:T(8,128)S(1)} all-gather(f32[64,772]{1,0:T(8,128)S(1)} %pad_maximum_fusion.5), channel_id=2, replica_groups=mesh['rep'=8,'shard'=4] {'shard'}, dimensions={0}, use_global_device_ids=true | all-gather | bytes 988160 | tf_op jit(solution)/shard_map/all_gather | solution.py:502
  102.2 9.4 %all-gather.1 = f32[32,3076]{1,0:T(8,128)S(1)} all-gather(f32[8,3076]{1,0:T(8,128)S(1)} %pad_maximum_fusion.7), channel_id=3, replica_groups=mesh['rep'=8,'shard'=4] {'shard'}, dimensions={0}, use_global_device_ids=true | all-gather | bytes 492160 | tf_op jit(solution)/shard_map/all_gather | solution.py:513
  119.6 33.0 %all-gather.13.cloned.1.call-done = bf16[1,768,9984]{1,2,0:T(8,128)(2,1)} async-done(((bf16[1,768,2496]{1,2,0:T(8,128)(2,1)}), bf16[1,768,9984]{1,2,0:T(8,128)(2,1)}) %all-gather.13.cloned.1.call-update) | async-done | bytes 15335440 | tf_op jit(solution)/shard_map/all_gather | solution.py:126
  152.6 20.1 %copy.93 = bf16[1,768,9984]{2,1,0:T(8,128)(2,1)} copy(bf16[1,768,9984]{1,2,0:T(8,128)(2,1)} %all-gather.13.cloned.1.call-done) | data formatting | bytes 30670848 | tf_op jit(solution)/shard_map/all_gather | solution.py:126
  172.7 5.6 convolution_convert_fusion
  201.4 5.3 fusion.22
  216.1 6.9 fusion.4
  227.8 5.1 multiply_reduce_fusion.15
  244.4 4.9 fusion.39
  249.4 6.8 multiply_reduce_fusion.3
  268.8 5.0 multiply_reduce_fusion.9
  279.1 45.6 %all-gather.8 = bf16[32,2,6144]{2,1,0:T(2,128)(2,1)} all-gather(bf16[1,2,6144]{2,1,0:T(2,128)(2,1)S(1)} %bitcast.242), channel_id=1, replica_groups=mesh['rep'=8,'shard'=4] {'rep','shard'}, dimensions={0}, use_global_device_ids=true | all-gather | bytes 811008 | tf_op jit(solution)/shard_map/all_gather | solution.py:586
  327.8 118.7 %shard_map.313 = (bf16[768,3072]{1,0:T(8,128)(2,1)}, bf16[3072,768]{1,0:T(8,128)(2,1)}, bf16[768,768]{1,0:T(8,128)(2,1)}, bf16[2304,768]{1,0:T(8,128)(2,1)}) custom-call(bf16[768,3072]{1,0:T(8,128)(2,1)} %bitcast_convert_fusion.1.g0, bf16[3072,768]{1,0:T(8,128)(2,1)} %bitcast_convert_fusion.g1, bf16[768,768]{1,0:T(8,128)(2,1)} %bitcast_convert_fusion.3.g2, ...), custom_call_target="tpu_custom_call" | custom-call | tf_op jit(solution)/shard_map/pallas_call | solution.py:412
  457.7 7.2 multiply_reduce_fusion.1
  473.0 84.0 %psum.105 = f32[]{:T(128)} all-reduce(f32[]{:T(128)S(6)} %mul.652), channel_id=1, replica_groups=mesh['rep'=8,'shard'=4] {'rep','shard'}, use_global_device_ids=true, to_apply=%region_9.10 | all-reduce | flops 1 | bytes 8 | tf_op jit(solution)/shard_map/psum | solution.py:608
  559.7 59.0 %all-reduce.10.cloned.1.call-done = f32[32,768]{1,0:T(8,128)} async-done(((f32[32,768]{1,0:T(8,128)}), f32[32,768]{1,0:T(8,128)}) %all-reduce.10.cloned.1.call-update) | async-done | bytes 98320 | tf_op jit(solution)/shard_map/psum | solution.py:608
  620.4 33.7 %all-reduce.8.cloned.1.call-done = f32[64,768]{1,0:T(8,128)} async-done(((f32[64,768]{1,0:T(8,128)}), f32[64,768]{1,0:T(8,128)}) %all-reduce.8.cloned.1.call-update) | async-done | bytes 196624 | tf_op jit(solution)/shard_map/psum | solution.py:593
  660.9 17.2 %reduce-scatter.4.cloned.1.call-done = f32[192,64]{1,0:T(8,128)} async-done(((f32[768,64]{1,0:T(8,128)}), f32[192,64]{1,0:T(8,128)}) %reduce-scatter.4.cloned.1.call-update) | async-done | bytes 49168
  686.0 11.8 %all-reduce.4 = (f32[1,768]{1,0:T(1,128)}, f32[1,768]{1,0:T(1,128)}, f32[1,3840]{1,0:T(1,128)}, f32[1,3840]{1,0:T(1,128)}, f32[768]{0:T(1024)}, /*index=5*/f32[7...) all-reduce(f32[1,768]{1,0:T(1,128)} %reduce_sum.517, ...), channel_id=1, replica_groups=mesh['rep'=8,'shard'=4] {'shard'}, use_global_device_ids=true, to_apply=%region_28.29 | all-reduce | flops 13302 | bytes 106416 | tf_op jit(solution)/shard_map/psum | solution.py:631
  721.6 5.9 bitcast_subtract_fusion
  (330 shorter events, 145.3 us)
Async XLA Ops:
  7.2 108.7 %all-gather.17.cloned.1.call-start = ((), (), s32[]{:S(2)}) async-start(), calls=%async_computation.5 | async-start | bytes 4485120 | tf_op jit(solution)/shard_map/all_gather | solution.py:521
  11.2 141.4 %all-gather.13.cloned.1.call-start = ((), (), s32[]{:S(2)}) async-start(), calls=%async_computation.3 | async-start | bytes 19169280 | tf_op jit(solution)/shard_map/all_gather | solution.py:126
  21.1 177.8 %all-gather.15.cloned.1.call-start = ((), (), s32[]{:S(2)}) async-start(), calls=%async_computation.4 | async-start | bytes 7372800 | tf_op jit(solution)/shard_map/all_gather | solution.py:127
  25.5 43.6 %copy-start.12 = (f32[1273,192]{0,1:T(8,128)S(1)}, f32[1273,192]{0,1:T(8,128)}, u32[]{:S(2)}) copy-start(f32[1273,192]{0,1:T(8,128)} %param.27) | copy-start | bytes 2932996
  25.5 44.1 %copy-start.52 = (f32[2,4096]{1,0:T(2,128)S(1)}, f32[2,4096]{1,0:T(2,128)}, u32[]{:S(2)}) copy-start(f32[2,4096]{1,0:T(2,128)} %param.18) | copy-start | bytes 98308
  25.5 44.4 %copy-start.53 = (f32[2,4096]{1,0:T(2,128)S(1)}, f32[2,4096]{1,0:T(2,128)}, u32[]{:S(2)}) copy-start(f32[2,4096]{1,0:T(2,128)} %param.19) | copy-start | bytes 98308
  25.5 44.6 %copy-start.54 = (f32[2,4096]{1,0:T(2,128)S(1)}, f32[2,4096]{1,0:T(2,128)}, u32[]{:S(2)}) copy-start(f32[2,4096]{1,0:T(2,128)} %param.20) | copy-start | bytes 98308
  25.6 593.2 %all-reduce.10.cloned.1.call-start = ((), (), s32[]{:S(2)}) async-start(), calls=%async_computation.2 | async-start | bytes 196608 | tf_op jit(solution)/shard_map/psum | solution.py:608
  115.8 162.4 %copy-start.58 = (f32[2,256]{1,0:T(2,128)}, f32[2,256]{1,0:T(2,128)S(1)}, u32[]{:S(2)}) copy-start(f32[2,256]{1,0:T(2,128)S(1)} %fusion.86) | copy-start | bytes 6148
  115.9 162.2 %copy-start.49 = (f32[2,768]{1,0:T(2,128)}, f32[2,768]{1,0:T(2,128)S(1)}, u32[]{:S(2)}) copy-start(f32[2,768]{1,0:T(2,128)S(1)} %get-tuple-element.109) | copy-start | bytes 18436
  278.1 46.6 %copy-start.56 = (f32[2,256]{1,0:T(2,128)}, f32[2,256]{1,0:T(2,128)S(1)}, u32[]{:S(2)}) copy-start(f32[2,256]{1,0:T(2,128)S(1)} %multiply_multiply_fusion.3) | copy-start | bytes 6148
  454.5 199.5 %all-reduce.8.cloned.1.call-start = ((), (), s32[]{:S(2)}) async-start(), calls=%async_computation.1 | async-start | bytes 393216 | tf_op jit(solution)/shard_map/psum | solution.py:593
  471.9 182.1 %copy-start.19 = (f32[64,580]{1,0:T(8,128)S(1)}, f32[64,580]{1,0:T(8,128)}, u32[]{:S(2)}) copy-start(f32[64,580]{1,0:T(8,128)} %copy-done.18) | copy-start | bytes 445444
  471.9 182.1 %copy-start.21 = (f32[64,580]{1,0:T(8,128)S(1)}, f32[64,580]{1,0:T(8,128)}, u32[]{:S(2)}) copy-start(f32[64,580]{1,0:T(8,128)} %copy-done.20) | copy-start | bytes 445444
  471.9 182.1 %copy-start.28 = (f32[64,192]{1,0:T(8,128)S(1)}, f32[64,192]{1,0:T(8,128)}, u32[]{:S(2)}) copy-start(f32[64,192]{1,0:T(8,128)} %copy-done.27) | copy-start | bytes 147460
  471.9 182.1 %copy-start.30 = (f32[64,192]{1,0:T(8,128)S(1)}, f32[64,192]{1,0:T(8,128)}, u32[]{:S(2)}) copy-start(f32[64,192]{1,0:T(8,128)} %copy-done.29) | copy-start | bytes 147460
  471.9 182.1 %copy-start.32 = (f32[64,192]{1,0:T(8,128)S(1)}, f32[64,192]{1,0:T(8,128)}, u32[]{:S(2)}) copy-start(f32[64,192]{1,0:T(8,128)} %copy-done.31) | copy-start | bytes 147460
  472.0 182.1 %copy-start.34 = (f32[64,192]{1,0:T(8,128)S(1)}, f32[64,192]{1,0:T(8,128)}, u32[]{:S(2)}) copy-start(f32[64,192]{1,0:T(8,128)} %copy-done.33) | copy-start | bytes 147460
  473.0 183.5 %copy-start.23 = (bf16[768,64]{0,1:T(8,128)(2,1)S(1)}, bf16[768,64]{0,1:T(8,128)(2,1)}, u32[]{:S(2)}) copy-start(bf16[768,64]{0,1:T(8,128)(2,1)} %copy-done.22) | copy-start | bytes 294916
  559.4 118.6 %reduce-scatter.4.cloned.1.call-start = ((), (), s32[]{:S(2)}) async-start(), calls=%async_computation.6 | async-start | bytes 491520
  659.4 23.3 %copy-start.60 = (f32[580]{0:T(1024)}, f32[580]{0:T(1024)S(1)}, u32[]{:S(2)}) copy-start(f32[580]{0:T(1024)S(1)} %get-tuple-element.68) | copy-start | bytes 6964
  680.0 28.6 %copy-start.62 = (f32[1,3840]{1,0:T(1,128)S(1)}, f32[1,3840]{1,0:T(1,128)}, u32[]{:S(2)}) copy-start(f32[1,3840]{1,0:T(1,128)} %param.30) | copy-start | bytes 46084
  680.0 41.6 %slice-start = ((s8[7667712]{0:T(1024)(128)(4,1)}), s8[3473408]{0:T(1024)(128)(4,1)S(1)}, s32[]{:S(2)}) async-start(s8[7667712]{0:T(1024)(128)(4,1)} %bitcast.207), calls=%async_computation.7 | async-start | bytes 6946816
  684.6 29.8 %copy-start.68 = (f32[192]{0:T(256)}, f32[192]{0:T(256)S(1)}, u32[]{:S(2)}) copy-start(f32[192]{0:T(256)S(1)} %get-tuple-element.66) | copy-start | bytes 2308
  (67 other events, 410.1 us)
Sparse Core Ops, SparseCore 0:
  11.3 33.8 all-gather.16
  46.8 105.7 all-gather.12
  154.7 44.1 all-gather.14
  454.6 164.1 all-reduce.9
  621.5 32.5 all-reduce.7
  657.2 20.8 reduce-scatter.3

commit v3 on v2

v3 whole, which is shorter than its diff:
```python
import functools
import math

import jax
import jax.numpy as jnp
from jax import lax
from jax.experimental import pallas as pl
from jax.experimental.pallas import tpu as pltpu
from jax.sharding import PartitionSpec as P

HEADS = 12
CLASSES = 1001
FREQ = 256
GRID = 16
PATCH = 16
LAYERS = 1
TOK = 256


decay = 0.5
eps_norm = 1e-06
eps_one = 1e-30
eps_two = 0.001
clip_level = 0.1
rate = 8.0
step_count = 1000.0


def silu(value):
    return value * jax.nn.sigmoid(value)


def positions(grid, width):
    quarter = width // 4
    omega = 1.0 / 10000.0 ** (jnp.arange(quarter, dtype=jnp.float32) / quarter)
    index = jnp.arange(grid * grid, dtype=jnp.int32)
    row_pos = (index // grid).astype(jnp.float32)[:, None] * omega[None, :]
    col_pos = (index % grid).astype(jnp.float32)[:, None] * omega[None, :]
    return jnp.concatenate(
        [jnp.sin(row_pos), jnp.cos(row_pos), jnp.sin(col_pos), jnp.cos(col_pos)], 1
    )


def time_freq(t_value, width):
    half = width // 2
    freqs = jnp.exp(-math.log(10000.0) * jnp.arange(half, dtype=jnp.float32) / half)
    angles = (t_value * step_count)[:, None] * freqs[None, :]
    return jnp.concatenate([jnp.cos(angles), jnp.sin(angles)], -1)


def weight_grad(left, back):
    flat_left = left.reshape(-1, left.shape[-1])
    flat_back = back.reshape(-1, back.shape[-1])
    return lax.dot_general(
        flat_left, flat_back, (((0,), (0,)), ((), ())), preferred_element_type=jnp.float32
    )


MESH = pl.DeviceIdType.MESH
LINE = 4
PIECES = 4


def heavy_chunks(width):
    half, third = width // 2, width // 3
    parts = [(0, 0, width, 2 * third * k, third, False) for k in range(6)]
    parts += [(1, 2 * third * k, 2 * third, 0, half, True) for k in range(6)]
    parts += [(2, 0, width, 0, half, False), (3, 0, width, 0, half, False)]
    parts += [(3, width + 2 * third * k, 2 * third, 0, half, True) for k in range(3)]
    return tuple(parts)


def add_rows(target, left, right, rows):
    block = 16

    def body(index, carry):
        span = pl.ds(pl.multiple_of(index * block, block), block)
        target[span] = left[span] + right[span]
        return carry

    lax.fori_loop(0, rows // block, body, 0)


def reduce_kernel(lines, chunks, tables, *refs):
    count = len(chunks)
    grads, refs = refs[:4], refs[4:]
    (d_mod, d_fm, few, in_t, head_t, cond_full, time_one), refs = refs[:7], refs[7:]
    finals, refs = refs[:4], refs[4:]
    (d_in, d_head, d_two, d_full, d_one, few_sum), scratch = refs[:6], refs[6:]
    by_core, by_y, by_x, by_z = (scratch[k * count : (k + 1) * count] for k in range(4))
    send, recv, zsend, zrecv, wsend, wrecv = scratch[4 * count : 4 * count + 6]
    (
        few_got, few_held, few_line, group_slot, pair_own, pair_got, line_slot, part_own, part_slot, act_own, act_slot,
        few_send, few_recv, group_send, group_recv, line_send, line_recv,
    ) = scratch[4 * count + 6 :]
    (in_starts, in_tiles), (head_starts, head_tiles), (embed_starts, embed_tiles), shards = tables
    rep, shard = lax.axis_index("rep"), lax.axis_index("shard")
    place = lax.rem(rep, 2 * lines)
    base = rep - place
    x, z = lax.rem(place, 2), lax.div(place, 2)
    core, y = lax.rem(shard, 2), lax.div(shard, 2)
    to_core = (rep, shard + 1 - 2 * core)
    to_y = (rep, shard + 2 - 4 * y)
    to_x = (rep + 1 - 2 * x, shard)

    def line_peer(step):
        return (base + lax.rem(z + step, lines) * 2 + x, shard)

    barrier = pltpu.get_barrier_semaphore()
    to_far = (rep, shards - 1 - shard)
    for peer in (to_core, to_y, to_x, to_far):
        pl.semaphore_signal(barrier, inc=1, device_id=peer, device_id_type=MESH)
    for step in range(1, lines):
        pl.semaphore_signal(
            barrier, inc=1, device_id=line_peer(step), device_id_type=MESH
        )
    pl.semaphore_wait(barrier, 4 + lines - 1)

    stride = lines // PIECES
    owns = lax.rem(z, stride) == 0
    mine = lax.div(z, stride)
    sends = []

    def remote(source, target, send_sem, recv_sem, peer):
        return pltpu.make_async_remote_copy(
            src_ref=source,
            dst_ref=target,
            send_sem=send_sem,
            recv_sem=recv_sem,
            device_id=peer,
            device_id_type=MESH,
        )

    def rows_of(ref, start, size):
        return ref.at[pl.ds(pl.multiple_of(start, 16), size)]

    def lanes_at(index, ref, row, rows, which):
        _, _, _, lane, lanes, _ = chunks[index]
        return ref.at[
            pl.ds(pl.multiple_of(row, 16), rows), pl.ds(pl.multiple_of(lane + which * lanes, 128), lanes)
        ]

    def core_copy(i):
        array, row, rows = chunks[i][:3]
        return remote(
            lanes_at(i, grads[array], row, rows, 1 - core), by_core[i], send.at[i, 0], recv.at[i, 0], to_core
        )

    def y_copy(i):
        half = chunks[i][2] // 2
        return remote(
            rows_of(by_core[i], (1 - y) * half, half), by_y[i], send.at[i, 1], recv.at[i, 1], to_y
        )

    def x_copy(i):
        quarter = chunks[i][2] // 4
        return remote(
            rows_of(by_y[i], (1 - x) * quarter, quarter), by_x[i], send.at[i, 2], recv.at[i, 2], to_x
        )

    def z_copy(i, piece):
        size = chunks[i][2] // 4 // PIECES
        owner = piece * stride
        slot = lax.rem(z - owner - 1 + lines, lines)
        return remote(
            by_x[i].at[pl.ds(piece * size, size)],
            by_z[i].at[slot],
            zsend.at[i, piece],
            zrecv.at[i, slot],
            (base + owner * 2 + x, shard),
        )

    def final_rows(i, side, start, size, which):
        array, row, rows = chunks[i][:3]
        return lanes_at(i, finals[array], row + side * (rows // 2) + start, size, which)

    def cross_copy(i):
        size = chunks[i][2] // 4 // PIECES
        part = final_rows(i, 0, (x * PIECES + mine) * size, size, core)
        return remote(part, part, send.at[i, 3], recv.at[i, 3], to_y)

    def line_copy(i, which, side, step):
        size = chunks[i][2] // 4 // PIECES
        part = final_rows(i, side, (x * PIECES + mine) * size, size, core)
        return remote(
            part, part, wsend.at[i, which, step - 1], wrecv.at[i, which, mine], line_peer(step)
        )

    def line_arrival(i, which, side, piece):
        size = chunks[i][2] // 4 // PIECES
        part = final_rows(i, side, (x * PIECES + piece) * size, size, core)
        return remote(part, part, wsend.at[i, which, 0], wrecv.at[i, which, piece], to_core)

    def pair_copy(i, which, side, column):
        quarter = chunks[i][2] // 4
        part = final_rows(i, side, column * quarter, quarter, core)
        return remote(part, part, send.at[i, 4 + which], recv.at[i, 4 + which], to_x)

    def last_copy(i, which, side, half):
        rows = chunks[i][2] // 2
        part = final_rows(i, side, 0, rows, half)
        return remote(part, part, send.at[i, 6 + which], recv.at[i, 6 + which], to_core)

    def sides(i, action):
        if chunks[i][5]:

            @pl.when(y == 1)
            def _():
                action(0, 1)
                action(1, 0)

        else:
            action(0, y)

    def stage0(i):
        core_copy(i).start()

    def stage1(i):
        array, row, rows = chunks[i][:3]
        core_copy(i).wait_recv()
        add_rows(by_core[i], by_core[i], lanes_at(i, grads[array], row, rows, core), rows)
        y_copy(i).start()

    def stage2(i):
        half = chunks[i][2] // 2
        y_copy(i).wait_recv()
        add_rows(by_y[i], by_y[i], rows_of(by_core[i], y * half, half), half)
        x_copy(i).start()

    def stage3(i):
        quarter = chunks[i][2] // 4
        x_copy(i).wait_recv()
        add_rows(by_x[i], by_x[i], rows_of(by_y[i], x * quarter, quarter), quarter)
        for piece in range(PIECES):

            @pl.when(z != piece * stride)
            def _():
                z_copy(i, piece).start()

    def stage4(i):
        size = chunks[i][2] // 4 // PIECES

        @pl.when(owns)
        def _():
            for slot in range(lines - 1):
                remote(
                    by_z[i].at[slot], by_z[i].at[slot], zsend.at[i, 0], zrecv.at[i, slot], to_core
                ).wait_recv()
            target = final_rows(i, y, (x * PIECES + mine) * size, size, core)

            def body(index, carry):
                total = by_x[i][
                    pl.ds(pl.multiple_of(mine * size + index * 16, 16), 16)
                ].astype(jnp.float32)
                for slot in range(lines - 1):
                    total += by_z[i][slot, pl.ds(pl.multiple_of(index * 16, 16), 16)].astype(jnp.float32)
                target[pl.ds(pl.multiple_of(index * 16, 16), 16)] = total.astype(jnp.bfloat16)
                return carry

            lax.fori_loop(0, size // 16, body, 0)
            if chunks[i][5]:

                @pl.when(y == 0)
                def _():
                    cross_copy(i).start()

                @pl.when(y == 1)
                def _():
                    for step in range(1, lines):
                        line_copy(i, 0, 1, step).start()
            else:
                for step in range(1, lines):
                    line_copy(i, 0, y, step).start()

    def stage5(i):
        if chunks[i][5]:

            @pl.when(jnp.logical_and(owns, y == 1))
            def _():
                cross_copy(i).wait_recv()
                for step in range(1, lines):
                    line_copy(i, 1, 0, step).start()

    def stage6(i):
        def action(which, side):
            for piece in range(PIECES):

                @pl.when(z != piece * stride)
                def _():
                    line_arrival(i, which, side, piece).wait_recv()

            pair_copy(i, which, side, x).start()

        sides(i, action)

    def stage7(i):
        def action(which, side):
            pair_copy(i, which, side, 1 - x).wait_recv()
            last_copy(i, which, side, core).start()

        sides(i, action)

    def stage8(i):
        sides(i, lambda which, side: last_copy(i, which, side, 1 - core).wait_recv())


    width = in_t.shape[1]
    mod_tiles, wide = 6 * width // 128, width // 128
    images = pair_own.shape[0]
    in_lanes = in_tiles * 128
    head_places = [o for o in range(shards) if head_starts[o] < wide]

    def few_copy(k, peer):
        return remote(few if k == 0 else few_held.at[k - 1], few_got.at[k], few_send.at[k], few_recv.at[k], peer)

    def few_line_copy(step):
        return remote(
            few_line.at[z], few_line.at[z], few_send.at[2 + step], few_recv.at[2 + step], line_peer(step)
        )

    def few_line_arrival(step):
        origin = lax.rem(z + lines - step, lines)
        return remote(few_line.at[origin], few_line.at[origin], few_send.at[2 + step], few_recv.at[2 + step], to_core)

    def group_parts(place):
        parts = []
        tiles = min(in_tiles, mod_tiles - in_starts[place])
        if tiles > 0:
            parts.append((0, in_starts[place] * 128, 0, tiles * 128))
        first, final = max(head_starts[place], wide), min(head_starts[place] + head_tiles, 3 * wide)
        if final > first:
            lead = (first - head_starts[place]) * 128
            parts.append((1, (first - wide) * 128, in_lanes + lead, (final - first) * 128))
        return parts

    def group_copy(place, k, origin):
        which, lane, own, lanes = group_parts(place)[k]
        step = lax.rem(place - origin + shards, shards) - 1
        return remote(
            (d_mod, d_fm)[which].at[:, pl.ds(lane, lanes)],
            group_slot.at[origin, :, pl.ds(own, lanes)],
            group_send.at[k, step],
            group_recv.at[k, step],
            (rep, jnp.int32(place)),
        )

    def to_others(kind, source, slots, step):
        return remote(
            source,
            slots.at[shard],
            group_send.at[kind, step - 1],
            group_recv.at[kind, step - 1],
            (rep, lax.rem(shard + step, shards)),
        )

    def from_others(kind, slots, step):
        origin = lax.rem(shard + shards - step, shards)
        return remote(slots.at[origin], slots.at[origin], group_send.at[kind, 0], group_recv.at[kind, step - 1], to_core)

    def pair_x_copy():
        return remote(pair_own, pair_got, few_send.at[lines + 2], few_recv.at[lines + 2], to_x)

    def line_d_copy(step):
        return remote(
            line_slot.at[z], line_slot.at[z], line_send.at[step - 1], line_recv.at[step - 1], line_peer(step)
        )

    def line_d_arrival(step):
        origin = lax.rem(z + lines - step, lines)
        return remote(line_slot.at[origin], line_slot.at[origin], line_send.at[0], line_recv.at[step - 1], to_core)

    def is_in(where, places):
        return functools.reduce(jnp.logical_or, [where == o for o in places])

    def side0():
        few_copy(0, to_core).start()
        for place in range(shards):
            for k, (which, lane, own, lanes) in enumerate(group_parts(place)):

                @pl.when(shard != place)
                def _():
                    group_copy(place, k, shard).start()

    def side1():
        few_copy(0, to_core).wait_recv()
        few_held[0] = few[...] + few_got[0]
        few_copy(1, to_y).start()
        pair_own[...] = jnp.zeros_like(pair_own)
        for place in range(shards):

            @pl.when(shard == place)
            def _():
                for k, (which, lane, own, lanes) in enumerate(group_parts(place)):
                    total = (d_mod, d_fm)[which][:, lane : lane + lanes]
                    for origin in range(shards):
                        if origin != place:
                            group_copy(place, k, jnp.int32(origin)).wait_recv()
                            total += group_slot[origin, :, own : own + lanes]
                    pair_own[:, own : own + lanes] = total

        pair_x_copy().start()

    def side2():
        few_copy(1, to_y).wait_recv()
        few_held[1] = few_held[0] + few_got[1]
        few_copy(2, to_x).start()
        pair_x_copy().wait_recv()
        own, got = pair_own[...], pair_got[...]
        both = jnp.concatenate([jnp.where(x == 0, own, got), jnp.where(x == 0, got, own)], 0)
        line_slot[z] = both.astype(jnp.bfloat16)
        for step in range(1, lines):
            line_d_copy(step).start()

    def side3():
        few_copy(2, to_x).wait_recv()
        few_line[z] = few_held[1] + few_got[2]
        for step in range(1, lines):
            few_line_copy(step).start()
        for step in range(1, lines):
            line_d_arrival(step).wait_recv()
        for at in range(lines):
            span = slice(at * 2 * images, (at + 1) * 2 * images)
            d_in[span, :] = line_slot[at, :, :in_lanes]
            d_head[span, :] = line_slot[at, :, in_lanes:]
        part_own[...] = jnp.dot(d_in[...], in_t[...], preferred_element_type=jnp.float32) + jnp.dot(
            d_head[...], head_t[...], preferred_element_type=jnp.float32
        )
        part_slot[shard] = part_own[...]
        for step in range(1, shards):
            to_others(2, part_own, part_slot, step).start()

    def side4():
        for step in range(1, lines):
            few_line_arrival(step).wait_recv()
        few_sum[...] = functools.reduce(jnp.add, [few_line[at] for at in range(lines)])
        for step in range(1, shards):
            from_others(2, part_slot, step).wait_recv()
        d_cond = functools.reduce(jnp.add, [part_slot[o] for o in range(shards)])
        value = cond_full[...]
        gate = jax.nn.sigmoid(value)
        d_full[...] = d_cond * (gate + value * gate * (1.0 - gate))
        d_two[...] = jnp.zeros_like(d_two)
        for place in head_places:

            @pl.when(shard == place)
            def _():
                lanes = min(head_tiles, wide - head_starts[place]) * 128
                first = head_starts[place] * 128
                d_two[:, :lanes] = d_full[:, first : first + lanes].astype(jnp.bfloat16)

        @pl.when(is_in(shard, head_places))
        def _():
            act_own[...] = jnp.dot(d_two[...], head_t[...], preferred_element_type=jnp.float32)
            act_slot[shard] = act_own[...]
            for step in range(1, shards):
                to_others(3, act_own, act_slot, step).start()

    def side5():
        for step in range(1, shards):

            @pl.when(is_in(lax.rem(shard + shards - step, shards), head_places))
            def _():
                from_others(3, act_slot, step).wait_recv()

        value = time_one[...]
        gate = jax.nn.sigmoid(value)
        slope = gate + value * gate * (1.0 - gate)
        for place in range(shards):

            @pl.when(shard == place)
            def _():
                first = embed_starts[place] * 128
                d_act = functools.reduce(
                    jnp.add, [act_slot[o, :, first : first + embed_tiles * 128] for o in head_places]
                )
                d_one[...] = (slope * d_act).astype(jnp.bfloat16)

    def side_end():
        for k, peer in enumerate((to_core, to_y, to_x)):
            few_copy(k, peer).wait_send()
        pair_x_copy().wait_send()
        for step in range(1, lines):
            few_line_copy(step).wait_send()
            line_d_copy(step).wait_send()
        for place in range(shards):
            for k in range(len(group_parts(place))):

                @pl.when(shard != place)
                def _():
                    group_copy(place, k, shard).wait_send()

        for step in range(1, shards):
            to_others(2, part_own, part_slot, step).wait_send()

        @pl.when(is_in(shard, head_places))
        def _():
            for step in range(1, shards):
                to_others(3, act_own, act_slot, step).wait_send()

    beside = (side0, side1, side2, side3, side4, side5)
    stages = (stage0, stage1, stage2, stage3, stage4, stage5, stage6, stage7, stage8)
    for tick in range(count + len(stages) - 1):
        if tick < len(beside):
            beside[tick]()
        for k, stage in enumerate(stages):
            if 0 <= tick - k < count:
                stage(tick - k)

    side_end()
    for i in range(count):
        core_copy(i).wait_send()
        y_copy(i).wait_send()
        x_copy(i).wait_send()
        for piece in range(PIECES):

            @pl.when(z != piece * stride)
            def _():
                z_copy(i, piece).wait_send()

        if chunks[i][5]:

            @pl.when(jnp.logical_and(owns, y == 0))
            def _():
                cross_copy(i).wait_send()

        def action(which, side):
            @pl.when(owns)
            def _():
                for step in range(1, lines):
                    line_copy(i, which, side, step).wait_send()

            pair_copy(i, which, side, x).wait_send()
            last_copy(i, which, side, core).wait_send()

        sides(i, action)


def reduce_call(lines, tables, heavy, light):
    width = heavy[2].shape[0]
    chunks = heavy_chunks(width)
    count = len(chunks)
    low, full = jnp.bfloat16, jnp.float32
    (_, in_tiles), (_, head_tiles), (_, embed_tiles), shards = tables
    few, cond_full = light[2], light[5]
    group, rows = light[0].shape[0], cond_full.shape[0]
    lanes = (in_tiles + head_tiles) * 128
    sizes = [(part_rows, part_lanes) for _, _, part_rows, _, part_lanes, _ in chunks]
    dma = pltpu.SemaphoreType.DMA
    shapes = [(item.shape, low) for item in heavy] + [
        ((rows, in_tiles * 128), low),
        ((rows, head_tiles * 128), low),
        ((rows, head_tiles * 128), low),
        ((rows, width), full),
        ((rows, embed_tiles * 128), low),
        (few.shape, full),
    ]
    scratch = [
        ((3,) + few.shape, full),
        ((2,) + few.shape, full),
        ((lines,) + few.shape, full),
        ((shards, group, lanes), full),
        ((group, lanes), full),
        ((group, lanes), full),
        ((lines, 2 * group, lanes), low),
        ((rows, width), full),
        ((shards, rows, width), full),
        ((rows, width), full),
        ((shards, rows, width), full),
    ]
    return pl.pallas_call(
        functools.partial(reduce_kernel, lines, chunks, tables),
        out_shape=[jax.ShapeDtypeStruct(*item) for item in shapes],
        in_specs=[pl.BlockSpec(memory_space=pltpu.VMEM)] * (4 + len(light)),
        out_specs=[pl.BlockSpec(memory_space=pltpu.VMEM)] * len(shapes),
        scratch_shapes=[pltpu.VMEM((r, c), low) for r, c in sizes]
        + [pltpu.VMEM((r // 2, c), low) for r, c in sizes]
        + [pltpu.VMEM((r // 4, c), low) for r, c in sizes]
        + [pltpu.VMEM((lines - 1, r // 4 // PIECES, c), low) for r, c in sizes]
        + [
            dma((count, 8)),
            dma((count, 8)),
            dma((count, PIECES)),
            dma((count, lines - 1)),
            dma((count, 2, lines - 1)),
            dma((count, 2, PIECES)),
        ]
        + [pltpu.VMEM(*item) for item in scratch]
        + [
            dma((lines + 3,)),
            dma((lines + 3,)),
            dma((4, shards - 1)),
            dma((4, shards - 1)),
            dma((lines - 1,)),
            dma((lines - 1,)),
        ],
        compiler_params=pltpu.CompilerParams(
            collective_id=1, has_side_effects=True, vmem_limit_bytes=63 * 1024 * 1024
        ),
    )(*heavy, *light)


def own_heavy(sums, in_cols, out_cols):
    fc2, fc1, attn_out, qkv = sums
    width = attn_out.shape[1]
    place = lax.axis_index("shard")
    padded = jnp.concatenate([jnp.zeros((6 * width, width), jnp.bfloat16), qkv, fc1], 0)
    own_in = lax.dynamic_slice_in_dim(padded, place * in_cols, in_cols, 0)
    own_out = jnp.concatenate(
        [
            lax.dynamic_slice_in_dim(item, place * out_cols, out_cols, 0)
            for item in (attn_out, fc2)
        ],
        1,
    )
    return own_in.T.astype(jnp.float32), own_out.T.astype(jnp.float32)


def windows(cols, shards):
    starts = [place * cols // 128 for place in range(shards)]
    tiles = max(-(-(place + 1) * cols // 128) - start for place, start in enumerate(starts))
    return starts, tiles


def heavy_segments(width, in_cols, in_starts, out_rows, shards):
    every = []
    for place in range(shards):
        parts = []
        for array, low, high, most in ((3, 6 * width, 9 * width, 960), (1, 9 * width, 13 * width, 832)):
            first, last = max(low, place * in_cols), min(high, (place + 1) * in_cols)
            while first < last:
                rows = min(most, last - first)
                parts.append((0, first - in_starts[place] * 128, array, first - low, rows, 0, 0, width))
                first += rows
            if array == 3:
                parts.append((1, 0, 2, place * out_rows, out_rows, 0, 0, width))
        parts.append((1, 0, 0, place * out_rows, out_rows, width, 0, 4 * width))
        every.append(parts)
    return every


def gather_kernel(
    plan, in_t, out_t, head_t, embed, traits,
    fc2, fc1, attn_out, qkv, cond_full, time_act, time_one, modul, fmod, patch, last, all_traits,
    s1_slot, tab_slot, patch_slot, two_slot, two_own, mod_slot, mod_own, fm_slot, fm_own, last_own,
    ysend, yrecv, xsend, xrecv, zsend, zrecv, csend, crecv, osend, orecv, small_send, small_recv, local_sem,
    trait_slot, trait_own, trait_got, line_slot, trait_send, trait_recv,
):
    segments, (in_starts, in_tiles), (head_starts, head_tiles), (embed_starts, embed_tiles), lines = plan
    shards = len(segments)
    arrays = (fc2, fc1, attn_out, qkv)
    sources = (in_t, out_t)
    rep, shard = lax.axis_index("rep"), lax.axis_index("shard")
    place_here = lax.rem(rep, 2 * lines)
    x, z = lax.rem(place_here, 2), lax.div(place_here, 2)
    zb = lax.rem(z, 2)
    core, y = lax.rem(shard, 2), lax.div(shard, 2)
    to_core = (rep, shard + 1 - 2 * core)
    to_y = (rep, shard + 2 - 4 * y)
    to_x = (rep + 1 - 2 * x, shard)
    to_z = (rep + 2 - 4 * zb, shard)
    width = head_t.shape[1]

    barrier = pltpu.get_barrier_semaphore()
    others = [(rep, lax.rem(shard + step, shards)) for step in range(1, shards)]

    def line_peer(step):
        return (rep - place_here + lax.rem(z + step, lines) * 2 + x, shard)

    for peer in others + [to_x] + [line_peer(step) for step in range(1, lines)]:
        pl.semaphore_signal(barrier, inc=1, device_id=peer, device_id_type=MESH)
    pl.semaphore_wait(barrier, shards + lines - 1)

    def remote(source, target, send_sem, recv_sem, peer):
        return pltpu.make_async_remote_copy(
            src_ref=source, dst_ref=target, send_sem=send_sem, recv_sem=recv_sem, device_id=peer, device_id_type=MESH
        )

    def small(kind, source, slots, step):
        return remote(
            source, slots.at[shard], small_send.at[kind, step - 1], small_recv.at[kind, step - 1], others[step - 1]
        )

    def small_arrival(kind, slots, step):
        origin = lax.rem(shard + shards - step, shards)
        return remote(
            slots.at[origin], slots.at[origin], small_send.at[kind, step - 1], small_recv.at[kind, step - 1], to_core
        )

    def exchange(kind, source, slots, origins=None):
        for step in range(1, shards):
            if origins is None:
                small(kind, source, slots, step).start()
            else:
                sends = functools.reduce(jnp.logical_or, [shard == o for o in origins])

                @pl.when(sends)
                def _():
                    small(kind, source, slots, step).start()

    def arrive(kind, slots, origins=None):
        for step in range(1, shards):
            if origins is None:
                small_arrival(kind, slots, step).wait_recv()
            else:
                origin = lax.rem(shard + shards - step, shards)

                @pl.when(functools.reduce(jnp.logical_or, [origin == o for o in origins]))
                def _():
                    small_arrival(kind, slots, step).wait_recv()

    def sent(kind, source, slots, origins=None):
        for step in range(1, shards):
            if origins is None:
                small(kind, source, slots, step).wait_send()
            else:

                @pl.when(functools.reduce(jnp.logical_or, [shard == o for o in origins]))
                def _():
                    small(kind, source, slots, step).wait_send()

    def place_tiles(target, slots, starts, tiles, origins, dtype, first=0):
        total = target.shape[1] // 128
        for tile in range(total):
            parts = [
                slots[o, :, (tile + first - starts[o]) * 128 : (tile + first - starts[o] + 1) * 128]
                for o in origins
                if 0 <= tile + first - starts[o] < tiles
            ]
            target[:, tile * 128 : (tile + 1) * 128] = functools.reduce(jnp.add, parts).astype(dtype)

    def source_part(place, k):
        source, row, array, _, rows, lane, _, lanes = segments[place][k]
        return sources[source].at[pl.ds(row, rows), pl.ds(lane, lanes)]

    def target_part(place, k, start=0, rows=None):
        _, _, array, row, total, _, lane, lanes = segments[place][k]
        start = row + start
        if not isinstance(start, int):
            start = pl.multiple_of(start, 16)
        return arrays[array].at[pl.ds(start, total if rows is None else rows), pl.ds(lane, lanes)]

    def quarter(place, k, index):
        size = segments[place][k][4] // 4
        return target_part(place, k, index * size, size)

    def half_of(place, k, index, second):
        size = segments[place][k][4] // 4
        cut = -(-size // 32) * 16
        return target_part(place, k, index * size + (cut if second else 0), size - cut if second else cut)

    me = x * 2 + zb
    across_x, along_z, corner = (1 - x) * 2 + zb, x * 2 + 1 - zb, (1 - x) * 2 + 1 - zb

    def y_copy(place, k):
        size = segments[place][k][4] // 4
        source, row, _, _, _, lane, _, lanes = segments[place][k]
        part = sources[source].at[pl.ds(pl.multiple_of(row + me * size, 16), size), pl.ds(lane, lanes)]
        return remote(part, quarter(place, k, me), ysend.at[k], yrecv.at[k], to_y)

    def owner_copy(place, k):
        return remote(source_part(place, k), target_part(place, k), osend.at[k], orecv.at[k], to_core)

    def own_copy(place, k):
        return pltpu.make_async_copy(source_part(place, k), target_part(place, k), local_sem.at[k])

    def hop(part, sems, k, slot, peer):
        return remote(part, part, sems[0].at[k, slot], sems[1].at[k, slot], peer)

    xs, zs, cs = (xsend, xrecv), (zsend, zrecv), (csend, crecv)

    for place in range(shards):

        @pl.when(shard == place)
        def _():
            for k in range(len(segments[place])):
                y_copy(place, k).start()
                owner_copy(place, k).start()
                own_copy(place, k).start()

    def trait_line(step):
        return remote(
            line_slot.at[z], line_slot.at[z], trait_send.at[step], trait_recv.at[step], line_peer(step)
        )

    def trait_line_arrival(step):
        origin = lax.rem(z + lines - step, lines)
        return remote(line_slot.at[origin], line_slot.at[origin], trait_send.at[step], trait_recv.at[step], to_core)

    trait_pair = remote(trait_own, trait_got, trait_send.at[0], trait_recv.at[0], to_x)
    trait_slot[shard] = traits[...]
    exchange(7, traits, trait_slot)
    arrive(7, trait_slot)
    trait_own[...] = functools.reduce(jnp.add, [trait_slot[o] for o in range(shards)])
    trait_pair.start()
    trait_pair.wait_recv()
    own, got = trait_own[...], trait_got[...]
    line_slot[z] = jnp.concatenate([jnp.where(x == 0, own, got), jnp.where(x == 0, got, own)], 0)
    for step in range(1, lines):
        trait_line(step).start()
    for step in range(1, lines):
        trait_line_arrival(step).wait_recv()
    count_in_line = 2 * traits.shape[0]
    for at in range(lines):
        all_traits[at * count_in_line : (at + 1) * count_in_line, :] = line_slot[at]
    freq = all_traits[:, :FREQ].astype(jnp.bfloat16)
    classes = embed.shape[0] - PATCH - FREQ
    named = lax.broadcasted_iota(jnp.int32, (all_traits.shape[0], classes), 1).astype(jnp.float32)
    onehot = jnp.where(named == all_traits[:, FREQ : FREQ + 1], 1.0, 0.0).astype(jnp.bfloat16)

    own_one = jnp.dot(freq, embed[PATCH : PATCH + FREQ, :], preferred_element_type=jnp.float32)
    time_one[...] = own_one
    s1_slot[shard] = (own_one * jax.nn.sigmoid(own_one)).astype(jnp.bfloat16)
    tab_slot[shard] = jnp.dot(onehot, embed[PATCH + FREQ :, :], preferred_element_type=jnp.float32)
    patch_slot[shard] = embed[0:PATCH, :]
    exchange(0, s1_slot.at[shard], s1_slot)
    exchange(1, tab_slot.at[shard], tab_slot)
    exchange(2, patch_slot.at[shard], patch_slot)
    last_place = [o for o in range(shards) if 0 <= 3 * width // 128 - head_starts[o] < head_tiles][-1]
    last_row = (3 * width // 128 - head_starts[last_place]) * 128
    last_own[...] = head_t[last_row : last_row + 16, :]

    @pl.when(shard == last_place)
    def _():
        last[...] = last_own[...]
        for step in range(1, shards):
            remote(last_own, last, small_send.at[6, step - 1], small_recv.at[6, 0], others[step - 1]).start()

    def relay(place, stage, k):
        if stage == 0:
            y_copy(place, k).wait_recv()
            hop(quarter(place, k, me), xs, k, 0, to_x).start()
            hop(quarter(place, k, me), zs, k, 0, to_z).start()
            hop(quarter(place, k, me), cs, k, 0, to_core).start()
        elif stage == 1:
            hop(quarter(place, k, across_x), xs, k, 0, to_x).wait_recv()
            hop(half_of(place, k, across_x, False), zs, k, 1, to_z).start()
            hop(quarter(place, k, along_z), zs, k, 0, to_z).wait_recv()
            hop(half_of(place, k, along_z, True), xs, k, 1, to_x).start()
            hop(quarter(place, k, across_x), cs, k, 1, to_core).start()
            hop(quarter(place, k, along_z), cs, k, 2, to_core).start()
        else:
            hop(half_of(place, k, corner, False), zs, k, 1, to_z).wait_recv()
            hop(half_of(place, k, corner, True), xs, k, 1, to_x).wait_recv()
            hop(quarter(place, k, corner), cs, k, 3, to_core).start()

    def relay_tick(tick):
        for place in range(shards):

            @pl.when(to_y[1] == place)
            def _():
                for stage in range(3):
                    if 0 <= tick - stage < len(segments[place]):
                        relay(place, stage, tick - stage)

    ticks = max(len(parts) for parts in segments) + 2
    head_places = [o for o in range(shards) if head_starts[o] * 128 < width]
    fm_places = [o for o in range(shards) if (head_starts[o] + head_tiles) * 128 > width]
    mod_places = [o for o in range(shards) if in_starts[o] * 128 < 6 * width]
    nt = (((1,), (1,)), ((), ()))
    group = modul.shape[0]

    arrive(0, s1_slot)
    place_tiles(time_act, s1_slot, embed_starts, embed_tiles, range(shards), jnp.bfloat16)
    two_own[...] = lax.dot_general(time_act[...], head_t[...], nt, preferred_element_type=jnp.float32)
    two_slot[shard] = two_own[...]
    exchange(3, two_own, two_slot, head_places)
    relay_tick(0)
    arrive(1, tab_slot)
    arrive(3, two_slot, head_places)
    place_tiles(cond_full, tab_slot, embed_starts, embed_tiles, range(shards), jnp.float32)
    for tile in range(width // 128):
        span = slice(tile * 128, (tile + 1) * 128)
        for o in head_places:
            if 0 <= tile - head_starts[o] < head_tiles:
                cond_full[:, span] += two_slot[o, :, (tile - head_starts[o]) * 128 : (tile - head_starts[o] + 1) * 128]
    mine = cond_full[pl.ds(pl.multiple_of(place_here * group, 8), group), :]
    cond = (mine * jax.nn.sigmoid(mine)).astype(jnp.bfloat16)
    mod_own[...] = lax.dot_general(cond, in_t[...], nt, preferred_element_type=jnp.float32)
    mod_slot[shard] = mod_own[...]
    exchange(4, mod_own, mod_slot, mod_places)
    fm_own[...] = lax.dot_general(cond, head_t[...], nt, preferred_element_type=jnp.float32)
    fm_slot[shard] = fm_own[...]
    exchange(5, fm_own, fm_slot, fm_places)
    relay_tick(1)
    arrive(2, patch_slot)
    place_tiles(patch, patch_slot, embed_starts, embed_tiles, range(shards), jnp.bfloat16)
    arrive(4, mod_slot, mod_places)
    arrive(5, fm_slot, fm_places)
    place_tiles(modul, mod_slot, in_starts, in_tiles, mod_places, jnp.float32)
    place_tiles(fmod, fm_slot, head_starts, head_tiles, fm_places, jnp.float32, width // 128)
    for tick in range(2, ticks):
        relay_tick(tick)

    for place in range(shards):
        count = len(segments[place])

        @pl.when(shard == place)
        def _():
            for k in range(count):
                y_copy(place, k).wait_send()
                owner_copy(place, k).wait_send()
                own_copy(place, k).wait()

        @pl.when(to_core[1] == place)
        def _():
            for k in range(count):
                remote(target_part(place, k), target_part(place, k), osend.at[k], orecv.at[k], to_core).wait_recv()

        @pl.when(to_y[1] == place)
        def _():
            for k in range(count):
                hop(quarter(place, k, me), xs, k, 0, to_x).wait_send()
                hop(quarter(place, k, me), zs, k, 0, to_z).wait_send()
                hop(half_of(place, k, across_x, False), zs, k, 1, to_z).wait_send()
                hop(half_of(place, k, along_z, True), xs, k, 1, to_x).wait_send()
                for slot, index in enumerate((me, across_x, along_z, corner)):
                    hop(quarter(place, k, index), cs, k, slot, to_core).wait_send()

        @pl.when(shards - 1 - shard == place)
        def _():
            for k in range(count):
                for slot, index in enumerate((me, across_x, along_z, corner)):
                    remote(
                        quarter(place, k, index), quarter(place, k, index), csend.at[k, slot], crecv.at[k, slot], to_core
                    ).wait_recv()

    trait_pair.wait_send()
    for step in range(1, lines):
        trait_line(step).wait_send()
    sent(7, traits, trait_slot)
    sent(0, s1_slot.at[shard], s1_slot)
    sent(1, tab_slot.at[shard], tab_slot)
    sent(2, patch_slot.at[shard], patch_slot)
    sent(3, two_own, two_slot, head_places)
    sent(4, mod_own, mod_slot, mod_places)
    sent(5, fm_own, fm_slot, fm_places)

    @pl.when(shard == last_place)
    def _():
        for step in range(1, shards):
            remote(last_own, last, small_send.at[6, step - 1], small_recv.at[6, 0], others[step - 1]).wait_send()

    @pl.when(shard != last_place)
    def _():
        remote(last_own, last, small_send.at[6, 0], small_recv.at[6, 0], to_core).wait_recv()


def gather_call(in_low, out_low, head_low, embed_low, traits, shards, lines):
    place = lax.axis_index("shard")
    width = head_low.shape[0]
    low, full = jnp.bfloat16, jnp.float32

    def window(item_t, starts, tiles, cols):
        offsets = jnp.asarray([o * cols - start * 128 for o, start in enumerate(starts)], jnp.int32)
        target = jnp.zeros((tiles * 128, item_t.shape[1]), item_t.dtype)
        return lax.dynamic_update_slice_in_dim(target, item_t, offsets[place], 0)

    in_cols, head_cols, embed_cols = in_low.shape[1], head_low.shape[1], embed_low.shape[1]
    in_starts, in_tiles = windows(in_cols, shards)
    head_starts, head_tiles = windows(head_cols, shards)
    embed_starts, embed_tiles = windows(embed_cols, shards)
    in_t = window(in_low.T, in_starts, in_tiles, in_cols)
    head_t = window(head_low.T, head_starts, head_tiles, head_cols)
    embed = window(embed_low.T, embed_starts, embed_tiles, embed_cols).T
    segments = heavy_segments(width, in_cols, in_starts, out_low.shape[1], shards)
    plan = (segments, (in_starts, in_tiles), (head_starts, head_tiles), (embed_starts, embed_tiles), lines)
    group = traits.shape[0]
    rows = 2 * lines * group
    most = max(len(parts) for parts in segments)
    shapes = [
        ((width, 4 * width), low),
        ((4 * width, width), low),
        ((width, width), low),
        ((3 * width, width), low),
        ((rows, width), full),
        ((rows, width), low),
        ((rows, embed_tiles * 128), full),
        ((group, 6 * width), full),
        ((group, 2 * width), full),
        ((PATCH, width), low),
        ((PATCH, width), low),
        ((rows, traits.shape[1]), full),
    ]
    scratch = [
        ((shards, rows, embed_tiles * 128), low),
        ((shards, rows, embed_tiles * 128), full),
        ((shards, PATCH, embed_tiles * 128), low),
        ((shards, rows, head_tiles * 128), full),
        ((rows, head_tiles * 128), full),
        ((shards, group, in_tiles * 128), full),
        ((group, in_tiles * 128), full),
        ((shards, group, head_tiles * 128), full),
        ((group, head_tiles * 128), full),
        ((PATCH, width), low),
    ]
    dma = pltpu.SemaphoreType.DMA
    outs = pl.pallas_call(
        functools.partial(gather_kernel, plan),
        out_shape=[jax.ShapeDtypeStruct(*item) for item in shapes],
        in_specs=[pl.BlockSpec(memory_space=pltpu.VMEM)] * 5,
        out_specs=[pl.BlockSpec(memory_space=pltpu.VMEM)] * len(shapes),
        scratch_shapes=[pltpu.VMEM(*item) for item in scratch]
        + [dma((most,)), dma((most,))]
        + [dma((most, 2))] * 4
        + [dma((most, 4))] * 2
        + [dma((most,)), dma((most,)), dma((8, shards - 1)), dma((8, shards - 1)), dma((most,))]
        + [
            pltpu.VMEM((shards,) + traits.shape, full),
            pltpu.VMEM(traits.shape, full),
            pltpu.VMEM(traits.shape, full),
            pltpu.VMEM((lines, 2 * group, traits.shape[1]), full),
            dma((lines,)),
            dma((lines,)),
        ],
        compiler_params=pltpu.CompilerParams(
            collective_id=2, has_side_effects=True, vmem_limit_bytes=60 * 1024 * 1024
        ),
    )(in_t, out_low.T, head_t, embed, traits)
    return in_t, head_t, outs


NN = (((1,), (0,)), ((), ()))
NT = (((1,), (1,)), ((), ()))
TN = (((0,), (0,)), ((), ()))


def mxu(left, right, kind):
    return lax.dot_general(left, right, kind, preferred_element_type=jnp.float32)


def blocks_of(total, size, body):
    def step(index, carry):
        body(pl.ds(pl.multiple_of(index * size, size), size))
        return carry

    lax.fori_loop(0, total // size, step, 0)


def pass_kernel(
    images, state, target, weight_t, pos, patch, last, modul, fmod, fc2, fc1, attn_out, qkv,
    g_fc2, g_fc1, g_o, g_qkv, few, d_mod, d_fm,
    stream, hat_one, hat_two, root_one, root_two, a_low, qkv_low, mixed, proj, b_low, upper, active, mlp, back, d_qkv,
):
    width = patch.shape[1]
    tokens = images * TOK
    low = jnp.bfloat16
    shard = lax.axis_index("shard")
    row = [shard * images + image for image in range(images)]
    span = [pl.ds(image * TOK, TOK) for image in range(images)]
    cut = 256

    def piece(ref, image, index):
        return ref[pl.ds(row[image], 1), pl.ds(index * width, width)]

    def normed(value):
        center = value - jnp.mean(value, -1, keepdims=True)
        root = lax.rsqrt(jnp.mean(center * center, -1, keepdims=True) + eps_norm)
        return center * root, root

    def norm_back(d_hat, hat, root):
        return root * (d_hat - jnp.mean(d_hat, -1, keepdims=True) - hat * jnp.mean(d_hat * hat, -1, keepdims=True))

    def put_row(ref, image, index, value):
        ref[pl.ds(row[image], 1), pl.ds(index * width, width)] = (
            jnp.sum(value, 0, keepdims=True).astype(low).astype(jnp.float32)
        )

    d_mod[...] = jnp.zeros_like(d_mod)
    d_fm[...] = jnp.zeros_like(d_fm)

    for image in range(images):
        value = mxu(state[span[image], :], patch[...], NN) + pos[...]
        stream[span[image], :] = value
        hat, root = normed(value)
        hat_one[span[image], :] = hat
        root_one[span[image], :] = root
        a_low[span[image], :] = (hat * (1.0 + piece(modul, image, 1)) + piece(modul, image, 0)).astype(low)

    def qkv_block(part):
        qkv_low[:, part] = mxu(a_low[...], qkv[part, :], NT).astype(low)

    blocks_of(3 * width, cut, qkv_block)
    lane = lax.broadcasted_iota(jnp.int32, (TOK, 128), 1)
    first = lane < 64
    scale = 0.125

    def softmax(query, key):
        score = mxu(query, key, NT) * scale
        expo = jnp.exp(score - jnp.max(score, -1, keepdims=True))
        return expo / jnp.sum(expo, -1, keepdims=True)

    def take(ref, image, start):
        return ref[span[image], pl.ds(pl.multiple_of(start, 128), 128)]

    def attend(pair, carry):
        for image in range(images):
            query, key, value = (take(qkv_low, image, index * width + pair * 128) for index in range(3))
            outs = []
            for side in (first, jnp.logical_not(first)):
                probs = softmax(jnp.where(side, query, jnp.zeros_like(query)), key)
                outs.append(mxu(probs.astype(low), value, NN))
            mixed[span[image], pl.ds(pl.multiple_of(pair * 128, 128), 128)] = jnp.where(first, outs[0], outs[1]).astype(low)
        return carry

    lax.fori_loop(0, width // 128, attend, 0)
    for image in range(images):
        got = mxu(mixed[span[image], :], attn_out[...], NT)
        proj[span[image], :] = got
        value = stream[span[image], :] + piece(modul, image, 2) * got
        stream[span[image], :] = value
        hat, root = normed(value)
        hat_two[span[image], :] = hat
        root_two[span[image], :] = root
        b_low[span[image], :] = (hat * (1.0 + piece(modul, image, 4)) + piece(modul, image, 3)).astype(low)

    def upper_block(part):
        value = mxu(b_low[...], fc1[part, :], NT)
        upper[:, part] = value
        active[:, part] = (
            0.5 * value * (1.0 + jnp.tanh(0.7978845608 * (value + 0.044715 * value * value * value)))
        ).astype(low)

    blocks_of(4 * width, cut, upper_block)

    def mlp_block(part):
        mlp[:, part] = mxu(active[...], fc2[part, :], NT)

    blocks_of(width, cut, mlp_block)
    loss = jnp.zeros((), jnp.float32)
    g_last = jnp.zeros((PATCH, width), jnp.float32)
    for image in range(images):
        value = stream[span[image], :] + piece(modul, image, 5) * mlp[span[image], :]
        hat, root = normed(value)
        gain = 1.0 + piece(fmod, image, 1)
        final = (hat * gain + piece(fmod, image, 0)).astype(low)
        diff = mxu(final, last[...], NT) - target[span[image], :]
        share = weight_t[span[image], :] * diff
        loss += 0.5 * jnp.sum(share * diff)
        d_out = share.astype(low)
        g_last += mxu(d_out, final, TN)
        d_final = mxu(d_out, last[...], NN)
        put_row(d_fm, image, 0, d_final)
        put_row(d_fm, image, 1, d_final * hat)
        d_value = norm_back(d_final * gain, hat, root)
        back[span[image], :] = d_value
        put_row(d_mod, image, 5, d_value * mlp[span[image], :])
        d_qkv[span[image], pl.ds(0, width)] = (piece(modul, image, 5) * d_value).astype(low)
    few[pl.ds(PATCH, PATCH), :] = g_last
    few[pl.ds(2 * PATCH, 8), :] = jnp.full((8, width), loss, jnp.float32)

    d_mlp = d_qkv.at[:, pl.ds(0, width)]

    def fc2_block(part):
        g_fc2[:, part] = mxu(d_mlp[...], active[:, part], TN).astype(low)
        value = upper[:, part]
        inner = jnp.tanh(0.7978845608 * (value + 0.044715 * value * value * value))
        slope = 0.5 * (1.0 + inner) + 0.5 * value * (1.0 - inner * inner) * 0.7978845608 * (
            1.0 + 3.0 * 0.044715 * value * value
        )
        active[:, part] = (slope * mxu(d_mlp[...], fc2[:, part], NN)).astype(low)

    blocks_of(4 * width, cut, fc2_block)

    def fc1_block(part):
        g_fc1[part, :] = mxu(active[:, part], b_low[...], TN).astype(low)

    blocks_of(4 * width, cut, fc1_block)
    for image in range(images):
        d_normed = mxu(active[span[image], :], fc1[...], NN)
        hat = hat_two[span[image], :]
        put_row(d_mod, image, 3, d_normed)
        put_row(d_mod, image, 4, d_normed * hat)
        d_value = back[span[image], :] + norm_back(
            d_normed * (1.0 + piece(modul, image, 4)), hat, root_two[span[image], :]
        )
        back[span[image], :] = d_value
        put_row(d_mod, image, 2, d_value * proj[span[image], :])
        b_low[span[image], :] = (piece(modul, image, 2) * d_value).astype(low)

    def o_block(part):
        g_o[part, :] = mxu(b_low[:, part], mixed[...], TN).astype(low)

    blocks_of(width, cut, o_block)
    d_mixed = active.at[:, pl.ds(0, width)]
    d_mixed[...] = mxu(b_low[...], attn_out[...], NN).astype(low)

    def attend_back(pair, carry):
        for image in range(images):
            query, key, value = (take(qkv_low, image, index * width + pair * 128) for index in range(3))
            d_out = take(active, image, pair * 128)
            d_query, d_key, d_value = [], [], []
            for side in (first, jnp.logical_not(first)):
                none = jnp.zeros_like(query)
                probs = softmax(jnp.where(side, query, none), key)
                d_prob = mxu(jnp.where(side, d_out, none), value, NT)
                d_score = (probs * (d_prob - jnp.sum(probs * d_prob, -1, keepdims=True))).astype(low)
                d_value.append(mxu(probs.astype(low), d_out, TN))
                d_query.append(mxu(d_score, key, NN) * scale)
                d_key.append(mxu(d_score, query, TN) * scale)
            for index, both in enumerate((d_query, d_key, d_value)):
                d_qkv[span[image], pl.ds(pl.multiple_of(index * width + pair * 128, 128), 128)] = jnp.where(
                    first, both[0], both[1]
                ).astype(low)
        return carry

    lax.fori_loop(0, width // 128, attend_back, 0)

    def g_qkv_block(part):
        g_qkv[part, :] = mxu(d_qkv[:, part], a_low[...], TN).astype(low)

    blocks_of(3 * width, cut, g_qkv_block)
    g_patch = jnp.zeros((PATCH, width), jnp.float32)
    for image in range(images):
        d_normed = mxu(d_qkv[span[image], :], qkv[...], NN)
        hat = hat_one[span[image], :]
        put_row(d_mod, image, 0, d_normed)
        put_row(d_mod, image, 1, d_normed * hat)
        d_value = back[span[image], :] + norm_back(
            d_normed * (1.0 + piece(modul, image, 1)), hat, root_one[span[image], :]
        )
        g_patch += mxu(state[span[image], :], d_value.astype(low), TN)
    few[pl.ds(0, PATCH), :] = g_patch


def pass_scratch(tokens, width):
    low, full = jnp.bfloat16, jnp.float32
    return [
        ((tokens, width), full),
        ((tokens, width), full),
        ((tokens, width), full),
        ((tokens, 1), full),
        ((tokens, 1), full),
        ((tokens, width), low),
        ((tokens, 3 * width), low),
        ((tokens, width), low),
        ((tokens, width), full),
        ((tokens, width), low),
        ((tokens, 4 * width), full),
        ((tokens, 4 * width), low),
        ((tokens, width), full),
        ((tokens, width), full),
        ((tokens, 3 * width), low),
    ]


def pass_call(images, state, target, weight_t, pos, patch, last, modul, fmod, heavy):
    width = patch.shape[1]
    low, full = jnp.bfloat16, jnp.float32
    shapes = [(item.shape, low) for item in heavy] + [
        ((2 * PATCH + 8, width), full),
        (modul.shape, full),
        (fmod.shape, full),
    ]
    return pl.pallas_call(
        functools.partial(pass_kernel, images),
        out_shape=[jax.ShapeDtypeStruct(*item) for item in shapes],
        in_specs=[pl.BlockSpec(memory_space=pltpu.VMEM)] * 12,
        out_specs=[pl.BlockSpec(memory_space=pltpu.VMEM)] * len(shapes),
        scratch_shapes=[pltpu.VMEM(*item) for item in pass_scratch(state.shape[0], width)],
        compiler_params=pltpu.CompilerParams(vmem_limit_bytes=63 * 1024 * 1024),
    )(state, target, weight_t, pos, patch, last, modul, fmod, *heavy)


def exchange_kernel(shards, own, total, slots, send, recv):
    rep, shard = lax.axis_index("rep"), lax.axis_index("shard")
    barrier = pltpu.get_barrier_semaphore()
    for step in range(1, shards):
        peer = (rep, lax.rem(shard + step, shards))
        pl.semaphore_signal(barrier, inc=1, device_id=peer, device_id_type=MESH)
    pl.semaphore_wait(barrier, shards - 1)

    def copy(step):
        return pltpu.make_async_remote_copy(
            src_ref=own,
            dst_ref=slots.at[shard],
            send_sem=send.at[step - 1],
            recv_sem=recv.at[step - 1],
            device_id=(rep, lax.rem(shard + step, shards)),
            device_id_type=MESH,
        )

    for step in range(1, shards):
        copy(step).start()
    slots[shard] = own[...]
    for step in range(1, shards):
        copy(step).wait()
    total[...] = functools.reduce(jnp.add, [slots[o] for o in range(shards)])


def sum_in_group(tree, shards):
    leaves, kind = jax.tree.flatten(tree)
    flat = jnp.concatenate([leaf.reshape(-1) for leaf in leaves])
    rows = -(-flat.shape[0] // 1024) * 8
    block = jnp.pad(flat, (0, rows * 128 - flat.shape[0])).reshape(rows, 128)
    total = pl.pallas_call(
        functools.partial(exchange_kernel, shards),
        out_shape=jax.ShapeDtypeStruct(block.shape, jnp.float32),
        in_specs=[pl.BlockSpec(memory_space=pltpu.VMEM)],
        out_specs=pl.BlockSpec(memory_space=pltpu.VMEM),
        scratch_shapes=[
            pltpu.VMEM((shards,) + block.shape, jnp.float32),
            pltpu.SemaphoreType.DMA((shards - 1,)),
            pltpu.SemaphoreType.DMA((shards - 1,)),
        ],
        compiler_params=pltpu.CompilerParams(collective_id=3, has_side_effects=True),
    )(block).reshape(-1)
    parts, first = [], 0
    for leaf in leaves:
        parts.append(total[first : first + leaf.size].reshape(leaf.shape))
        first += leaf.size
    return jax.tree.unflatten(kind, parts)


def on_device(
    latents,
    noises,
    velocity,
    times,
    labels,
    dropped,
    blocks_in,
    blocks_out,
    head_side,
    embed_side,
    state_in_row,
    state_in_col,
    state_out_row,
    state_out_col,
    state_head_row,
    state_head_col,
    state_embed_row,
    state_embed_col,
):
    images = latents.shape[0]
    width = head_side.shape[0]
    shard_count = lax.axis_size("shard")
    place = lax.axis_index("shard")
    in_cols = blocks_in.shape[2]
    out_cols = blocks_out.shape[2]
    head_cols = head_side.shape[1]
    embed_cols = embed_side.shape[1]
    group = images * shard_count
    in_low = blocks_in[0].astype(jnp.bfloat16)
    out_low = blocks_out[0].astype(jnp.bfloat16)
    head_low = head_side.astype(jnp.bfloat16)
    embed_low = embed_side.astype(jnp.bfloat16)
    t_value = (times.astype(jnp.float32) + 1.0) / step_count
    classes = jnp.where(dropped == 1, CLASSES - 1, labels).astype(jnp.float32)
    lines = LINE
    traits = jnp.zeros((group, FREQ + 128), jnp.float32)
    traits = lax.dynamic_update_slice(
        traits,
        jnp.concatenate([time_freq(t_value, FREQ), jnp.broadcast_to(classes[:, None], (images, 128))], 1),
        (place * images, 0),
    )
    in_t, head_win_t, gathered = gather_call(in_low, out_low, head_low, embed_low, traits, shard_count, lines)
    fc2_t, fc1_t, o_t, qkv_t, cond_full, time_act, time_one, modul, final_mod, patch_w, head_t, all_traits = gathered
    freq_low = all_traits[:, :FREQ].astype(jnp.bfloat16)
    onehot = all_traits[:, FREQ : FREQ + 1] == jnp.arange(CLASSES, dtype=jnp.float32)[None, :]
    cond = silu(cond_full).astype(jnp.bfloat16)
    tcol = t_value[:, None, None]
    state = (
        (1.0 - tcol) * latents.reshape(images, TOK, PATCH)
        + tcol * noises.reshape(images, TOK, PATCH)
    ).astype(jnp.bfloat16)
    *heavy, few, d_mod, d_fm = pass_call(
        images,
        state.reshape(images * TOK, PATCH),
        velocity.reshape(images * TOK, PATCH),
        jnp.repeat(t_value, TOK)[:, None],
        positions(GRID, width),
        patch_w,
        head_t,
        modul,
        final_mod,
        [fc2_t, fc1_t, o_t, qkv_t],
    )
    tables = (
        windows(in_cols, shard_count),
        windows(head_cols, shard_count),
        windows(embed_cols, shard_count),
        shard_count,
    )
    sums = reduce_call(
        lines,
        tables,
        heavy,
        [d_mod, d_fm, few, in_t, head_win_t, cond_full, time_one],
    )
    heavy_in, heavy_out = own_heavy(sums[:4], in_cols, out_cols)
    d_in, d_fin, d_two, d_full, d_one, few_sum = sums[4:]

    def own_columns(item, cols):
        return lax.dynamic_slice_in_dim(item, lax.rem(place * cols, 128), cols, 1)

    loss_sum = few_sum[2 * PATCH, 0]
    d_full_own = lax.dynamic_slice_in_dim(d_full, place * embed_cols, embed_cols, 1)
    g_table = lax.dot_general(
        onehot.astype(jnp.float32),
        d_full_own,
        (((0,), (0,)), ((), ())),
        precision=lax.Precision.HIGHEST,
    )
    own_patch = lax.dynamic_slice_in_dim(few_sum[:PATCH], place * embed_cols, embed_cols, 1)
    own_head = jnp.pad(few_sum[PATCH : 2 * PATCH].T, ((0, 0), (3 * width, 0)))
    own_head = lax.dynamic_slice_in_dim(own_head, place * head_cols, head_cols, 1)
    totals = (
        (own_columns(weight_grad(cond, d_in), in_cols) + heavy_in)[None],
        heavy_out[None],
        own_columns(weight_grad(time_act, d_two) + weight_grad(cond, d_fin), head_cols) + own_head,
        jnp.concatenate([own_patch, own_columns(weight_grad(freq_low, d_one), embed_cols), g_table], 0),
    )
    blocks = lax.axis_size("rep") // (2 * lines)
    if blocks > 1:
        apart = [[k * 2 * lines + j for k in range(blocks)] for j in range(2 * lines)]
        totals, loss_sum = lax.psum((totals, loss_sum), "rep", axis_index_groups=apart)
    weights = (blocks_in, blocks_out, head_side, embed_side)
    rows_old = (state_in_row, state_out_row, state_head_row, state_embed_row)
    cols_old = (state_in_col, state_out_col, state_head_col, state_embed_col)
    cols_new = [
        decay * col_state + (1.0 - decay) * (jnp.mean(gradient * gradient, -2) + eps_one)
        for gradient, col_state in zip(totals, cols_old)
    ]
    row_parts = [jnp.sum(gradient * gradient, -1) for gradient in totals]
    row_scaled = [
        jnp.sum(gradient * gradient / col_next[..., None, :], -1)
        for gradient, col_next in zip(totals, cols_new)
    ]
    weight_sq = [jnp.sum(weight * weight, axis=(-2, -1)) for weight in weights]
    row_sums, row_scaled, weight_sq = sum_in_group((row_parts, row_scaled, weight_sq), shard_count)
    rows_new = [
        decay * row_state
        + (1.0 - decay) * (row_sum / (gradient.shape[-1] * shard_count) + eps_one)
        for row_sum, gradient, row_state in zip(row_sums, totals, rows_old)
    ]
    row_means = [jnp.mean(row_next, -1) for row_next in rows_new]
    total_sq = sum(
        jnp.sum(row_mean * jnp.sum(scaled / row_next, -1))
        for scaled, row_next, row_mean in zip(row_scaled, rows_new, row_means)
    )
    count = sum((weight.size for weight in weights)) * shard_count
    update_rms = jnp.sqrt(total_sq / count)
    factor = jnp.maximum(1.0, update_rms / clip_level)
    news = []
    for index in range(4):
        numel = weights[index].shape[-2] * weights[index].shape[-1] * shard_count
        weight_rms = jnp.sqrt(weight_sq[index] / numel)
        step_size = rate * jnp.maximum(eps_two, weight_rms) / factor
        row_scale = jnp.asarray(step_size)[..., None] * lax.rsqrt(
            rows_new[index] / row_means[index][..., None]
        )
        news.append(
            weights[index]
            - totals[index] * row_scale[..., :, None] * lax.rsqrt(cols_new[index])[..., None, :]
        )
    return (
        loss_sum,
        update_rms,
        totals[0],
        totals[1],
        totals[2],
        totals[3],
        rows_new[0],
        cols_new[0],
        rows_new[1],
        cols_new[1],
        rows_new[2],
        cols_new[2],
        rows_new[3],
        cols_new[3],
        news[0],
        news[1],
        news[2],
        news[3],
    )


def solution(mesh):
    placed = (
        P(("rep", "shard"), None),
        P(("rep", "shard"), None),
        P(("rep", "shard"), None),
        P(("rep", "shard")),
        P(("rep", "shard")),
        P(("rep", "shard")),
        P(None, None, "shard"),
        P(None, None, "shard"),
        P(None, "shard"),
        P(None, "shard"),
        P(),
        P(None, "shard"),
        P(),
        P(None, "shard"),
        P(),
        P("shard"),
        P(),
        P("shard"),
    )
    return jax.shard_map(
        on_device,
        mesh=mesh,
        in_specs=placed,
        out_specs=(
            P(),
            P(),
            P(None, None, "shard"),
            P(None, None, "shard"),
            P(None, "shard"),
            P(None, "shard"),
            P(),
            P(None, "shard"),
            P(),
            P(None, "shard"),
            P(),
            P("shard"),
            P(),
            P("shard"),
            P(None, None, "shard"),
            P(None, None, "shard"),
            P(None, "shard"),
            P(None, "shard"),
        ),
        check_vma=False,
    )
```

time: 743 us -> 479 us (0.64)
  Pallas kernels: 119 us -> 351 us
  blocking collectives: 221 us -> 0 us
  waiting for transfers between devices: 148 us -> 0 us
  matrix products: 93.9 us -> 10.1 us
  local copies, waits for them, and re-layouts: 59.7 us -> 32.7 us
  other arithmetic: 68.9 us -> 58.5 us
  between operations: 25.9 us -> 17.5 us
    pallas_call x1 -> x4, Pallas kernels: 119 us -> 351 us  [the longest x1 154 us: reduce_call(): pl.pallas_call(functools.partial(reduce_kernel, lines, chunks, tables), o...]
    all_gather x6 -> x0, blocking collectives: 125 us -> none  [the longest x1 45.6 us: on_device(): d_low = lax.all_gather(d_low, both, axis=0, tiled=True)]
    psum x2 -> x0, blocking collectives: 95.8 us -> none  [the longest x1 84 us: on_device(): lax.psum((loss_local, jnp.concatenate([g_patch, g_head_t], 0)), both)]
    psum x2 -> x0, waiting for transfers between devices: 92.7 us -> none  [the longest x1 59 us: on_device(): lax.psum((loss_local, jnp.concatenate([g_patch, g_head_t], 0)), both)]
    dot_general x24 -> x0, matrix products: 64.2 us -> none  [the longest x5 20.3 us: input_grad_t(): return jnp.matmul(back, weight_t, preferred_element_type=jnp.float32)]
    all_gather x3 -> x0, waiting for transfers between devices: 37.7 us -> none  [the longest x1 33 us: gather_heavy(): all_in = lax.all_gather(in_low, 'shard', axis=1, tiled=True)]
    all_gather x3 -> x0, local copies, waits for them, and re-layouts: 20.2 us -> none  [the longest x1 20.1 us: gather_heavy(): all_in = lax.all_gather(in_low, 'shard', axis=1, tiled=True)]
    dot_general x10 -> x4, matrix products: 26.8 us -> 8.66 us  [weight_grad(): lax.dot_general(flat_left, flat_back, (((0,), (0,)), ((), ())), preferred...]
  transfers between devices with their start and end apart: 6 -> 0, of which waited for: 5 -> 0; matrix products, arithmetic and copies ran while one was open for 12% -> 0% of each run, Pallas kernels for 0% -> 0%
where the time goes in v3:
time: 479 us; the launch traced here: 470 us
  Pallas kernels  351 us (73%)
  other arithmetic  58.5 us (12%)
  local copies, waits for them, and re-layouts  32.7 us (7%)
  between operations  17.5 us (4%)
  matrix products  10.1 us (2%)
    pallas_call x1, Pallas kernels, reduce_call(): pl.pallas_call(functools.partial(reduce_kernel, lines, chunks, tables), o...  154 us
    pallas_call x1, Pallas kernels, gather_call(): pl.pallas_call(functools.partial(gather_kernel, plan), out_shape=[jax.Sha...  105 us
    pallas_call x1, Pallas kernels, pass_call(): pl.pallas_call(functools.partial(pass_kernel, images), out_shape=[jax.Sha...  70.2 us
    pallas_call x1, Pallas kernels, sum_in_group(): pl.pallas_call(functools.partial(exchange_kernel, shards), out_shape=jax....  21.6 us
    sub x4, other arithmetic, on_device(): weights[index]  14.6 us
    dynamic_update_slice x2, local copies, waits for them, and re-layouts, window(): return lax.dynamic_update_slice_in_dim(target, item_t, offsets[place], 0)  11.4 us
    reduce_sum x4, other arithmetic, on_device(): jnp.mean(gradient * gradient, -2) + eps_one  10.3 us
    reduce_sum x4, other arithmetic, on_device(): weight_sq = [jnp.sum(weight * weight, axis=(-2, -1)) for weight in weights]  9.81 us

profile of v3, /device:TPU:0, one launch (start us, length us, event | category | flops | bytes accessed | tf_op | source)
XLA Modules:
  0.0 470.1 jit_solution(8897788827714838247)
XLA Ops:
  3.8 2.1 broadcast_in_dim.20
  6.0 5.5 %bitcast_dynamic-update-slice_fusion.in_t.refs_7_ = bf16[2560,768]{1,0:T(8,128)(2,1)} fusion(bf16[2560,768]{1,0:T(8,128)(2,1)} %broadcast_in_dim.20, s32[]{:T(128)S(6)} %select_n.69, f32[1,768,2496]{1,2,0:T(8,128)} %param.27), kind=kLoop, calls=%fused_computation.11 | loop fusion | flops 1916928 | bytes 11501572 | tf_op jit(solution)/shard_map/dynamic_update_slice | solution.py:956
  14.7 6.0 %dynamic_update_slice.14 = bf16[256,1273]{0,1:T(8,128)(2,1)} dynamic-update-slice(bf16[256,1273]{0,1:T(8,128)(2,1)} %broadcast_in_dim.22, bf16[192,1273]{0,1:T(8,128)(2,1)S(1)} %bitcast.107, s32[]{:T(128)S(6)} %select_n.71, s32[]{:T(128)} %constant.64.clone.1) | dynamic-update-slice | bytes 977668 | tf_op jit(solution)/shard_map/dynamic_update_slice | solution.py:956
  23.6 3.9 multiply_reduce_fusion.4
  28.6 5.4 %dynamic_update_slice.13.head_t.refs_8_ = bf16[768,768]{1,0:T(8,128)(2,1)} dynamic-update-slice(bf16[768,768]{1,0:T(8,128)(2,1)} %broadcast_in_dim.21, bf16[580,768]{1,0:T(8,128)(2,1)} %get-tuple-element.112, s32[]{:T(128)S(6)} %select_n.70, s32[]{:T(128)} %constant.64.clone.1) | dynamic-update-slice | bytes 1781764 | tf_op jit(solution)/shard_map/dynamic_update_slice | solution.py:956
  34.3 2.4 multiply_reduce_fusion.3
  36.7 105.5 %shard_map.340 = (bf16[768,3072]{1,0:T(8,128)(2,1)}, bf16[3072,768]{1,0:T(8,128)(2,1)}, bf16[768,768]{1,0:T(8,128)(2,1)}, bf16[2304,768]{1,0:T(8,128)(2,1)}, f32...) custom-call(bf16[2560,768]{1,0:T(8,128)(2,1)} %bitcast_dynamic-updat, ...), custom_call_target="tpu_custom_call" | custom-call | tf_op jit(solution)/shard_map/pallas_call | solution.py:997
  142.2 1.9 multiply_sine_fusion.1
  148.3 70.2 %shard_map.341 = (bf16[768,3072]{1,0:T(8,128)(2,1)}, bf16[3072,768]{1,0:T(8,128)(2,1)}, bf16[768,768]{1,0:T(8,128)(2,1)}, bf16[2304,768]{1,0:T(8,128)(2,1)}, f32...) custom-call(bf16[512,16]{1,0:T(8,128)(2,1)} %add_convert_fusion.state, f32[512,16]{1,0:T(8,128)} %reshape.292.target, ...), custom_call_target="tpu_custom_call" | custom-call | tf_op jit(solution)/shard_map/pallas_call | solution.py:1254
  218.5 153.9 %shard_map.342 = (bf16[768,3072]{1,0:T(8,128)(2,1)}, bf16[3072,768]{1,0:T(8,128)(2,1)}, bf16[768,768]{1,0:T(8,128)(2,1)}, bf16[2304,768]{1,0:T(8,128)(2,1)}, bf1...) custom-call(bf16[768,3072]{1,0:T(8,128)(2,1)} %get-tuple-element.55., ...), custom_call_target="tpu_custom_call" | custom-call | tf_op jit(solution)/shard_map/pallas_call | solution.py:570
  372.6 1.5 fusion.12
  380.4 1.9 fusion.32
  382.3 2.2 multiply_reduce_fusion.5
  390.9 4.3 fusion.33
  395.3 7.6 %multiply_reduce_fusion.1 = (f32[2496]{0:T(1024)S(1)}, f32[768,2496]{0,1:T(8,128)S(1)}) fusion(s32[]{:T(128)S(6)} %select_n.75, bf16[3072,768]{1,0:T(8,128)(2,1)} %get-tuple-element.67, bf16[2304,768]{1,0:T(8,128)(2,1)S(1)} %copy-done.10, bf16[2496]{0:T(1024)(128)(2,1)S(1)} %pad_dynamic-slice_fusion.3, f32[768,2560]{0,1:T(8,128)} %fusion.33, s32[]{:T(128)S(6)} %select_n.74), kind=kLoop, calls=%fused_computation.7 | loop fusion | flops 17249856 | bytes 23607944 | tf_op jit(solution)/shard_map/reduce_sum | solution.py:1421
  406.1 2.6 multiply_reduce_fusion
  408.8 2.7 concatenate.23
  412.1 21.6 %shard_map.343 = f32[104,128]{1,0:T(8,128)} custom-call(f32[104,128]{1,0:T(8,128)} %pad_bitcast_fusion.own), custom_call_target="tpu_custom_call" | custom-call | tf_op jit(solution)/shard_map/pallas_call | solution.py:1295
  445.4 1.5 fusion.43
  447.6 2.8 multiply_subtract_fusion.1
  451.2 3.6 multiply_subtract_fusion
  456.5 4.2 fusion.9
  461.5 4.0 bitcast_subtract_fusion
  465.4 1.8 convert_bitcast_fusion
  (165 shorter events, 33.5 us)
Async XLA Ops:
  6.0 6.8 %copy-start.9 = (f32[1273,192]{0,1:T(8,128)S(1)}, f32[1273,192]{0,1:T(8,128)}, u32[]{:S(2)}) copy-start(f32[1273,192]{0,1:T(8,128)} %param.30) | copy-start | bytes 2932996
  11.4 9.3 %copy-start.45 = (s32[4]{0:T(128)S(1)}, s32[4]{0:T(128)}, u32[]{:S(2)}) copy-start(s32[4]{0:T(128)} %constant.181.clone) | copy-start | bytes 52
  20.7 13.3 %copy-start.42 = (s32[2]{0:T(128)S(1)}, s32[2]{0:T(128)}, u32[]{:S(2)}) copy-start(s32[2]{0:T(128)} %param.24) | copy-start | bytes 28
  20.7 13.4 %copy-start.43 = (s32[2]{0:T(128)S(1)}, s32[2]{0:T(128)}, u32[]{:S(2)}) copy-start(s32[2]{0:T(128)} %param.25) | copy-start | bytes 28
  20.7 13.4 %copy-start.44 = (s32[2]{0:T(128)S(1)}, s32[2]{0:T(128)}, u32[]{:S(2)}) copy-start(s32[2]{0:T(128)} %param.26) | copy-start | bytes 28
  20.8 13.5 %copy-start.6 = (f32[1,3840,192]{1,2,0:T(8,128)S(1)}, f32[1,3840,192]{1,2,0:T(8,128)}, u32[]{:S(2)}) copy-start(f32[1,3840,192]{1,2,0:T(8,128)} %param.28) | copy-start | bytes 8847364
  218.5 154.0 %copy-start.14 = (f32[64,384]{1,0:T(8,128)S(1)}, f32[64,384]{1,0:T(8,128)}, u32[]{:S(2)}) copy-start(f32[64,384]{1,0:T(8,128)} %get-tuple-element.73) | copy-start | bytes 294916
  395.2 10.8 %slice-start = ((s8[7667712]{0:T(1024)(128)(4,1)}), s8[4194304]{0:T(1024)(128)(4,1)S(1)}, s32[]{:S(2)}) async-start(s8[7667712]{0:T(1024)(128)(4,1)} %bitcast.102), calls=%async_computation | async-start | bytes 8388608
  395.3 7.6 %copy-start.32 = (f32[1,2496]{1,0:T(1,128)S(1)}, f32[1,2496]{1,0:T(1,128)}, u32[]{:S(2)}) copy-start(f32[1,2496]{1,0:T(1,128)} %param.32) | copy-start | bytes 29956
  395.3 10.7 %slice-start.1 = ((s8[7667712]{0:T(1024)(128)(4,1)}), s8[3473408]{0:T(1024)(128)(4,1)S(1)}, s32[]{:S(2)}) async-start(s8[7667712]{0:T(1024)(128)(4,1)} %bitcast.102), calls=%async_computation.1 | async-start | bytes 6946816
  406.1 27.7 %copy-start.33 = (f32[1273]{0:T(1024)S(1)}, f32[1273]{0:T(1024)}, u32[]{:S(2)}) copy-start(f32[1273]{0:T(1024)} %param.37) | copy-start | bytes 15280
  406.1 30.4 %copy-start.36 = (f32[768]{0:T(1024)S(1)}, f32[768]{0:T(1024)}, u32[]{:S(2)}) copy-start(f32[768]{0:T(1024)} %param.35) | copy-start | bytes 9220
  406.1 34.7 %copy-start.30 = (f32[1,3840]{1,0:T(1,128)S(1)}, f32[1,3840]{1,0:T(1,128)}, u32[]{:S(2)}) copy-start(f32[1,3840]{1,0:T(1,128)} %param.33) | copy-start | bytes 46084
  406.1 37.3 %copy-start.39 = (f32[1,768]{1,0:T(1,128)S(1)}, f32[1,768]{1,0:T(1,128)}, u32[]{:S(2)}) copy-start(f32[1,768]{1,0:T(1,128)} %param.31) | copy-start | bytes 9220
  408.8 42.4 %copy-start.29 = (f32[580]{0:T(1024)S(1)}, f32[580]{0:T(1024)}, u32[]{:S(2)}) copy-start(f32[580]{0:T(1024)} %get-tuple-element.96) | copy-start | bytes 6964
  435.2 19.7 %copy-start.24 = (f32[1273]{0:T(1024)}, f32[1273]{0:T(1024)S(1)}, u32[]{:S(2)}) copy-start(f32[1273]{0:T(1024)S(1)} %get-tuple-element.100) | copy-start | bytes 15280
  437.9 16.9 %copy-start.28 = (f32[768]{0:T(1024)}, f32[768]{0:T(1024)S(1)}, u32[]{:S(2)}) copy-start(f32[768]{0:T(1024)S(1)} %get-tuple-element.101) | copy-start | bytes 9220
  441.4 15.0 %copy-start.17 = (f32[1,3840]{1,0:T(1,128)}, f32[1,3840]{1,0:T(1,128)S(1)}, u32[]{:S(2)}) copy-start(f32[1,3840]{1,0:T(1,128)S(1)} %get-tuple-element.102) | copy-start | bytes 46084
  444.0 17.4 %copy-start.31 = (f32[1,768]{1,0:T(1,128)}, f32[1,768]{1,0:T(1,128)S(1)}, u32[]{:S(2)}) copy-start(f32[1,768]{1,0:T(1,128)S(1)} %get-tuple-element.103) | copy-start | bytes 9220
  447.6 13.8 %slice-start.2 = ((s8[7667712]{0:T(1024)(128)(4,1)}), s8[3473408]{0:T(1024)(128)(4,1)S(1)}, s32[]{:S(2)}) async-start(s8[7667712]{0:T(1024)(128)(4,1)} %bitcast.104), calls=%async_computation.2 | async-start | bytes 6946816
  450.4 6.1 %copy-start.38 = (f32[1,192]{1,0:T(1,128)S(1)}, f32[1,192]{1,0:T(1,128)}, u32[]{:S(2)}) copy-start(f32[1,192]{1,0:T(1,128)} %get-tuple-element.98) | copy-start | bytes 2308
  451.1 5.3 %copy-start.8 = (bf16[192,768]{1,0:T(8,128)(2,1)S(1)}, bf16[192,768]{1,0:T(8,128)(2,1)}, u32[]{:S(2)}) copy-start(bf16[192,768]{1,0:T(8,128)(2,1)} %copy-done.7) | copy-start | bytes 884740
  451.2 10.2 %slice-start.3 = ((s8[7667712]{0:T(1024)(128)(4,1)}), s8[4194304]{0:T(1024)(128)(4,1)S(1)}, s32[]{:S(2)}) async-start(s8[7667712]{0:T(1024)(128)(4,1)} %bitcast.104), calls=%async_computation.3 | async-start | bytes 8388608
  451.2 10.2 %copy-start.1 = (f32[768,2496]{0,1:T(8,128)S(1)}, f32[768,2496]{0,1:T(8,128)}, u32[]{:S(2)}) copy-start(f32[768,2496]{0,1:T(8,128)} %copy-done) | copy-start | bytes 23003140
  (26 other events, 83.8 us)

commit v4 on v3

--- a/solution.py
+++ b/solution.py
@@ -90,14 +90,15 @@
     by_core, by_y, by_x, by_z = (scratch[k * count : (k + 1) * count] for k in range(4))
     send, recv, zsend, zrecv, wsend, wrecv = scratch[4 * count : 4 * count + 6]
     (
-        few_got, few_held, few_line, group_slot, pair_own, pair_got, line_slot, part_own, part_slot, act_own, act_slot,
+        few_got, few_y, few_x, few_held, few_line, mod_got, fm_got, mod_sum, fm_sum, group_slot, part_own, part_slot,
+        act_own, act_slot, pair_own, pair_got, line_in, line_rest, line_full,
         few_send, few_recv, group_send, group_recv, line_send, line_recv,
     ) = scratch[4 * count + 6 :]
     (in_starts, in_tiles), (head_starts, head_tiles), (embed_starts, embed_tiles), shards = tables
     rep, shard = lax.axis_index("rep"), lax.axis_index("shard")
-    place = lax.rem(rep, 2 * lines)
-    base = rep - place
-    x, z = lax.rem(place, 2), lax.div(place, 2)
+    place_here = lax.rem(rep, 2 * lines)
+    base = rep - place_here
+    x, z = lax.rem(place_here, 2), lax.div(place_here, 2)
     core, y = lax.rem(shard, 2), lax.div(shard, 2)
     to_core = (rep, shard + 1 - 2 * core)
     to_y = (rep, shard + 2 - 4 * y)
@@ -306,21 +307,33 @@
 
     width = in_t.shape[1]
     mod_tiles, wide = 6 * width // 128, width // 128
-    images = pair_own.shape[0]
-    in_lanes = in_tiles * 128
+    images = d_mod.shape[0]
+    in_lanes, head_lanes, embed_lanes = in_tiles * 128, head_tiles * 128, embed_tiles * 128
+    rest_lanes = 2 * head_lanes + embed_lanes
     head_places = [o for o in range(shards) if head_starts[o] < wide]
-
-    def few_copy(k, peer):
-        return remote(few if k == 0 else few_held.at[k - 1], few_got.at[k], few_send.at[k], few_recv.at[k], peer)
+    mod_places = [o for o in range(shards) if in_starts[o] < mod_tiles]
+    few_rows = few.shape[0] // 2
+    half = pl.ds(pl.multiple_of(core * few_rows, 8), few_rows)
+    other_half = pl.ds(pl.multiple_of((1 - core) * few_rows, 8), few_rows)
+
+    def is_in(where, places):
+        return functools.reduce(jnp.logical_or, [where == o for o in places])
+
+    few_core = remote(few.at[other_half], few_got, few_send.at[0], few_recv.at[0], to_core)
+    few_over_y = remote(few_held.at[0], few_y, few_send.at[1], few_recv.at[1], to_y)
+    few_over_x = remote(few_held.at[1], few_x, few_send.at[2], few_recv.at[2], to_x)
+    few_back = remote(few_sum.at[half], few_sum.at[half], few_send.at[3], few_recv.at[3], to_core)
+    few_back_arrival = remote(few_sum.at[other_half], few_sum.at[other_half], few_send.at[3], few_recv.at[3], to_core)
+    mod_core = remote(d_mod, mod_got, few_send.at[4], few_recv.at[4], to_core)
+    fm_core = remote(d_fm, fm_got, few_send.at[5], few_recv.at[5], to_core)
+    pair_copy_x = remote(pair_own, pair_got, few_send.at[6], few_recv.at[6], to_x)
 
     def few_line_copy(step):
-        return remote(
-            few_line.at[z], few_line.at[z], few_send.at[2 + step], few_recv.at[2 + step], line_peer(step)
-        )
+        return remote(few_line.at[z], few_line.at[z], few_send.at[6 + step], few_recv.at[6 + step], line_peer(step))
 
     def few_line_arrival(step):
         origin = lax.rem(z + lines - step, lines)
-        return remote(few_line.at[origin], few_line.at[origin], few_send.at[2 + step], few_recv.at[2 + step], to_core)
+        return remote(few_line.at[origin], few_line.at[origin], few_send.at[6 + step], few_recv.at[6 + step], to_core)
 
     def group_parts(place):
         parts = []
@@ -333,15 +346,14 @@
             parts.append((1, (first - wide) * 128, in_lanes + lead, (final - first) * 128))
         return parts
 
-    def group_copy(place, k, origin):
+    def group_copy(place, k):
         which, lane, own, lanes = group_parts(place)[k]
-        step = lax.rem(place - origin + shards, shards) - 1
         return remote(
-            (d_mod, d_fm)[which].at[:, pl.ds(lane, lanes)],
-            group_slot.at[origin, :, pl.ds(own, lanes)],
-            group_send.at[k, step],
-            group_recv.at[k, step],
-            (rep, jnp.int32(place)),
+            (mod_sum, fm_sum)[which].at[:, pl.ds(lane, lanes)],
+            group_slot.at[:, pl.ds(own, lanes)],
+            group_send.at[k, 0],
+            group_recv.at[k, 0],
+            to_y,
         )
 
     def to_others(kind, source, slots, step):
@@ -357,112 +369,115 @@
         origin = lax.rem(shard + shards - step, shards)
         return remote(slots.at[origin], slots.at[origin], group_send.at[kind, 0], group_recv.at[kind, step - 1], to_core)
 
-    def pair_x_copy():
-        return remote(pair_own, pair_got, few_send.at[lines + 2], few_recv.at[lines + 2], to_x)
-
-    def line_d_copy(step):
-        return remote(
-            line_slot.at[z], line_slot.at[z], line_send.at[step - 1], line_recv.at[step - 1], line_peer(step)
-        )
-
-    def line_d_arrival(step):
+    slots_of = (line_rest, line_full, line_in)
+
+    def line_copy_d(kind, step):
+        slots = slots_of[kind]
+        return remote(slots.at[z], slots.at[z], line_send.at[kind, step - 1], line_recv.at[kind, step - 1], line_peer(step))
+
+    def line_arrival_d(kind, step):
+        slots = slots_of[kind]
         origin = lax.rem(z + lines - step, lines)
-        return remote(line_slot.at[origin], line_slot.at[origin], line_send.at[0], line_recv.at[step - 1], to_core)
-
-    def is_in(where, places):
-        return functools.reduce(jnp.logical_or, [where == o for o in places])
+        return remote(slots.at[origin], slots.at[origin], line_send.at[kind, 0], line_recv.at[kind, step - 1], to_core)
+
+    def on_line(action):
+        for step in range(1, lines):
+            action(0, step)
+            action(1, step)
+
+            @pl.when(is_in(shard, mod_places))
+            def _():
+                action(2, step)
 
     def side0():
-        few_copy(0, to_core).start()
+        mod_core.start()
+        fm_core.start()
+        few_core.start()
+
+    def side1():
+        mod_core.wait_recv()
+        mod_sum[...] = d_mod[...] + mod_got[...]
+        fm_core.wait_recv()
+        fm_sum[...] = d_fm[...] + fm_got[...]
         for place in range(shards):
-            for k, (which, lane, own, lanes) in enumerate(group_parts(place)):
-
-                @pl.when(shard != place)
-                def _():
-                    group_copy(place, k, shard).start()
-
-    def side1():
-        few_copy(0, to_core).wait_recv()
-        few_held[0] = few[...] + few_got[0]
-        few_copy(1, to_y).start()
+
+            @pl.when(to_y[1] == place)
+            def _():
+                for k in range(len(group_parts(place))):
+                    group_copy(place, k).start()
+
+        few_core.wait_recv()
+        few_held[0] = few[half] + few_got[...]
+        few_over_y.start()
+
+    def side2():
         pair_own[...] = jnp.zeros_like(pair_own)
         for place in range(shards):
 
             @pl.when(shard == place)
             def _():
                 for k, (which, lane, own, lanes) in enumerate(group_parts(place)):
-                    total = (d_mod, d_fm)[which][:, lane : lane + lanes]
-                    for origin in range(shards):
-                        if origin != place:
-                            group_copy(place, k, jnp.int32(origin)).wait_recv()
-                            total += group_slot[origin, :, own : own + lanes]
-                    pair_own[:, own : own + lanes] = total
-
-        pair_x_copy().start()
-
-    def side2():
-        few_copy(1, to_y).wait_recv()
-        few_held[1] = few_held[0] + few_got[1]
-        few_copy(2, to_x).start()
-        pair_x_copy().wait_recv()
-        own, got = pair_own[...], pair_got[...]
-        both = jnp.concatenate([jnp.where(x == 0, own, got), jnp.where(x == 0, got, own)], 0)
-        line_slot[z] = both.astype(jnp.bfloat16)
-        for step in range(1, lines):
-            line_d_copy(step).start()
-
-    def side3():
-        few_copy(2, to_x).wait_recv()
-        few_line[z] = few_held[1] + few_got[2]
-        for step in range(1, lines):
-            few_line_copy(step).start()
-        for step in range(1, lines):
-            line_d_arrival(step).wait_recv()
-        for at in range(lines):
-            span = slice(at * 2 * images, (at + 1) * 2 * images)
-            d_in[span, :] = line_slot[at, :, :in_lanes]
-            d_head[span, :] = line_slot[at, :, in_lanes:]
-        part_own[...] = jnp.dot(d_in[...], in_t[...], preferred_element_type=jnp.float32) + jnp.dot(
-            d_head[...], head_t[...], preferred_element_type=jnp.float32
+                    group_copy(place, k).wait_recv()
+                    pair_own[:, own : own + lanes] = (
+                        (mod_sum, fm_sum)[which][:, lane : lane + lanes] + group_slot[:, own : own + lanes]
+                    )
+
+        part_own[...] = jnp.dot(
+            pair_own[:, in_lanes : in_lanes + head_lanes].astype(jnp.bfloat16),
+            head_t[...],
+            preferred_element_type=jnp.float32,
         )
+
+        @pl.when(is_in(shard, mod_places))
+        def _():
+            part_own[...] += jnp.dot(
+                pair_own[:, :in_lanes].astype(jnp.bfloat16), in_t[...], preferred_element_type=jnp.float32
+            )
+
         part_slot[shard] = part_own[...]
         for step in range(1, shards):
             to_others(2, part_own, part_slot, step).start()
-
-    def side4():
-        for step in range(1, lines):
-            few_line_arrival(step).wait_recv()
-        few_sum[...] = functools.reduce(jnp.add, [few_line[at] for at in range(lines)])
+        few_over_y.wait_recv()
+        few_held[1] = few_held[0] + few_y[...]
+        few_over_x.start()
+
+    def side3():
         for step in range(1, shards):
             from_others(2, part_slot, step).wait_recv()
         d_cond = functools.reduce(jnp.add, [part_slot[o] for o in range(shards)])
-        value = cond_full[...]
+        value = cond_full[pl.ds(pl.multiple_of(place_here * images, 8), images), :]
         gate = jax.nn.sigmoid(value)
-        d_full[...] = d_cond * (gate + value * gate * (1.0 - gate))
-        d_two[...] = jnp.zeros_like(d_two)
-        for place in head_places:
+        d_value = d_cond * (gate + value * gate * (1.0 - gate))
+        for place in range(shards):
 
             @pl.when(shard == place)
             def _():
-                lanes = min(head_tiles, wide - head_starts[place]) * 128
-                first = head_starts[place] * 128
-                d_two[:, :lanes] = d_full[:, first : first + lanes].astype(jnp.bfloat16)
-
-        @pl.when(is_in(shard, head_places))
-        def _():
-            act_own[...] = jnp.dot(d_two[...], head_t[...], preferred_element_type=jnp.float32)
-            act_slot[shard] = act_own[...]
-            for step in range(1, shards):
-                to_others(3, act_own, act_slot, step).start()
-
-    def side5():
+                first = embed_starts[place] * 128
+                pair_own[:, in_lanes + rest_lanes :] = d_value[:, first : first + embed_lanes]
+                if place in head_places:
+                    lanes = min(head_tiles, wide - head_starts[place]) * 128
+                    first = head_starts[place] * 128
+                    start = in_lanes + head_lanes
+                    d_two_own = d_value[:, first : first + lanes].astype(jnp.bfloat16)
+                    pair_own[:, start : start + lanes] = d_two_own.astype(jnp.float32)
+                    act_own[...] = jnp.dot(d_two_own, head_t[:lanes, :], preferred_element_type=jnp.float32)
+                    act_slot[shard] = act_own[...]
+                    for step in range(1, shards):
+                        to_others(3, act_own, act_slot, step).start()
+
+        few_over_x.wait_recv()
+        few_line[z] = few_held[1] + few_x[...]
+        for step in range(1, lines):
+            few_line_copy(step).start()
+
+    def side4():
         for step in range(1, shards):
 
             @pl.when(is_in(lax.rem(shard + shards - step, shards), head_places))
             def _():
                 from_others(3, act_slot, step).wait_recv()
 
-        value = time_one[...]
+        value = time_one[pl.ds(pl.multiple_of(place_here * images, 8), images), :]
         gate = jax.nn.sigmoid(value)
         slope = gate + value * gate * (1.0 - gate)
         for place in range(shards):
@@ -470,24 +485,54 @@
             @pl.when(shard == place)
             def _():
                 first = embed_starts[place] * 128
-                d_act = functools.reduce(
-                    jnp.add, [act_slot[o, :, first : first + embed_tiles * 128] for o in head_places]
-                )
-                d_one[...] = (slope * d_act).astype(jnp.bfloat16)
+                d_act = functools.reduce(jnp.add, [act_slot[o, :, first : first + embed_lanes] for o in head_places])
+                start = in_lanes + 2 * head_lanes
+                pair_own[:, start : start + embed_lanes] = (slope * d_act).astype(jnp.bfloat16).astype(jnp.float32)
+
+        pair_copy_x.start()
+        for step in range(1, lines):
+            few_line_arrival(step).wait_recv()
+        few_sum[half] = functools.reduce(jnp.add, [few_line[at] for at in range(lines)])
+        few_back.start()
+
+    def side5():
+        pair_copy_x.wait_recv()
+        own, got = pair_own[...], pair_got[...]
+        both = jnp.concatenate([jnp.where(x == 0, own, got), jnp.where(x == 0, got, own)], 0)
+        line_in[z] = both[:, :in_lanes].astype(jnp.bfloat16)
+        line_rest[z] = both[:, in_lanes : in_lanes + rest_lanes].astype(jnp.bfloat16)
+        line_full[z] = both[:, in_lanes + rest_lanes :]
+        on_line(lambda kind, step: line_copy_d(kind, step).start())
+
+    def side6():
+        on_line(lambda kind, step: line_arrival_d(kind, step).wait_recv())
+        for at in range(lines):
+            span = slice(at * 2 * images, (at + 1) * 2 * images)
+            d_head[span, :] = line_rest[at, :, :head_lanes]
+            d_two[span, :] = line_rest[at, :, head_lanes : 2 * head_lanes]
+            d_one[span, :] = line_rest[at, :, 2 * head_lanes :]
+            d_full[span, :] = line_full[at]
+        d_in[...] = jnp.zeros_like(d_in)
+
+        @pl.when(is_in(shard, mod_places))
+        def _():
+            for at in range(lines):
+                d_in[at * 2 * images : (at + 1) * 2 * images, :] = line_in[at]
+
+        few_back_arrival.wait_recv()
 
     def side_end():
-        for k, peer in enumerate((to_core, to_y, to_x)):
-            few_copy(k, peer).wait_send()
-        pair_x_copy().wait_send()
+        for copy in (few_core, few_over_y, few_over_x, few_back, mod_core, fm_core, pair_copy_x):
+            copy.wait_send()
         for step in range(1, lines):
             few_line_copy(step).wait_send()
-            line_d_copy(step).wait_send()
+        on_line(lambda kind, step: line_copy_d(kind, step).wait_send())
         for place in range(shards):
-            for k in range(len(group_parts(place))):
-
-                @pl.when(shard != place)
-                def _():
-                    group_copy(place, k, shard).wait_send()
+
+            @pl.when(to_y[1] == place)
+            def _():
+                for k in range(len(group_parts(place))):
+                    group_copy(place, k).wait_send()
 
         for step in range(1, shards):
             to_others(2, part_own, part_slot, step).wait_send()
@@ -497,11 +542,12 @@
             for step in range(1, shards):
                 to_others(3, act_own, act_slot, step).wait_send()
 
-    beside = (side0, side1, side2, side3, side4, side5)
+    beside = (side0, side1, side2, side3, side4, side5, side6)
+    beside_at = (12, 14, 16, 18, 20, 22, 24)
     stages = (stage0, stage1, stage2, stage3, stage4, stage5, stage6, stage7, stage8)
     for tick in range(count + len(stages) - 1):
-        if tick < len(beside):
-            beside[tick]()
+        if tick in beside_at:
+            beside[beside_at.index(tick)]()
         for k, stage in enumerate(stages):
             if 0 <= tick - k < count:
                 stage(tick - k)
@@ -543,29 +589,40 @@
     (_, in_tiles), (_, head_tiles), (_, embed_tiles), shards = tables
     few, cond_full = light[2], light[5]
     group, rows = light[0].shape[0], cond_full.shape[0]
-    lanes = (in_tiles + head_tiles) * 128
+    in_lanes, head_lanes, embed_lanes = in_tiles * 128, head_tiles * 128, embed_tiles * 128
+    rest_lanes = 2 * head_lanes + embed_lanes
+    few_half = (few.shape[0] // 2, width)
+    pair = (group, in_lanes + rest_lanes + embed_lanes)
     sizes = [(part_rows, part_lanes) for _, _, part_rows, _, part_lanes, _ in chunks]
     dma = pltpu.SemaphoreType.DMA
     shapes = [(item.shape, low) for item in heavy] + [
         ((rows, in_tiles * 128), low),
         ((rows, head_tiles * 128), low),
         ((rows, head_tiles * 128), low),
-        ((rows, width), full),
-        ((rows, embed_tiles * 128), low),
+        ((rows, embed_lanes), full),
+        ((rows, embed_lanes), low),
         (few.shape, full),
     ]
     scratch = [
-        ((3,) + few.shape, full),
-        ((2,) + few.shape, full),
-        ((lines,) + few.shape, full),
-        ((shards, group, lanes), full),
-        ((group, lanes), full),
-        ((group, lanes), full),
-        ((lines, 2 * group, lanes), low),
-        ((rows, width), full),
-        ((shards, rows, width), full),
-        ((rows, width), full),
-        ((shards, rows, width), full),
+        (few_half, full),
+        (few_half, full),
+        (few_half, full),
+        ((2,) + few_half, full),
+        ((lines,) + few_half, full),
+        (light[0].shape, full),
+        (light[1].shape, full),
+        (light[0].shape, full),
+        (light[1].shape, full),
+        ((group, in_lanes + head_lanes), full),
+        ((group, width), full),
+        ((shards, group, width), full),
+        ((group, width), full),
+        ((shards, group, width), full),
+        (pair, full),
+        (pair, full),
+        ((lines, 2 * group, in_lanes), low),
+        ((lines, 2 * group, rest_lanes), low),
+        ((lines, 2 * group, embed_lanes), full),
     ]
     return pl.pallas_call(
         functools.partial(reduce_kernel, lines, chunks, tables),
@@ -586,12 +643,12 @@
         ]
         + [pltpu.VMEM(*item) for item in scratch]
         + [
-            dma((lines + 3,)),
-            dma((lines + 3,)),
+            dma((lines + 6,)),
+            dma((lines + 6,)),
             dma((4, shards - 1)),
             dma((4, shards - 1)),
-            dma((lines - 1,)),
-            dma((lines - 1,)),
+            dma((3, lines - 1)),
+            dma((3, lines - 1)),
         ],
         compiler_params=pltpu.CompilerParams(
             collective_id=1, has_side_effects=True, vmem_limit_bytes=63 * 1024 * 1024
@@ -599,20 +656,14 @@
     )(*heavy, *light)
 
 
-def own_heavy(sums, in_cols, out_cols):
-    fc2, fc1, attn_out, qkv = sums
-    width = attn_out.shape[1]
-    place = lax.axis_index("shard")
-    padded = jnp.concatenate([jnp.zeros((6 * width, width), jnp.bfloat16), qkv, fc1], 0)
-    own_in = lax.dynamic_slice_in_dim(padded, place * in_cols, in_cols, 0)
-    own_out = jnp.concatenate(
-        [
-            lax.dynamic_slice_in_dim(item, place * out_cols, out_cols, 0)
-            for item in (attn_out, fc2)
-        ],
-        1,
-    )
-    return own_in.T.astype(jnp.float32), own_out.T.astype(jnp.float32)
+def placed_traits(traits, lanes):
+    lead = -(-(PATCH + FREQ) // 128) * 128
+    lane = lax.broadcasted_iota(jnp.int32, (traits.shape[0], lead), 1)
+    here = jnp.logical_and(lane >= PATCH, lane < PATCH + FREQ)
+    freq = jnp.where(here, traits[:, :lead], 0.0).astype(jnp.bfloat16)
+    named = lax.broadcasted_iota(jnp.int32, (traits.shape[0], lanes), 1).astype(jnp.float32)
+    onehot = jnp.where(named == traits[:, lead : lead + 1], 1.0, 0.0).astype(jnp.bfloat16)
+    return freq, onehot
 
 
 def windows(cols, shards):
@@ -625,7 +676,7 @@
     every = []
     for place in range(shards):
         parts = []
-        for array, low, high, most in ((3, 6 * width, 9 * width, 960), (1, 9 * width, 13 * width, 832)):
+        for array, low, high, most in ((3, 6 * width, 9 * width, 640), (1, 9 * width, 13 * width, 640)):
             first, last = max(low, place * in_cols), min(high, (place + 1) * in_cols)
             while first < last:
                 rows = min(most, last - first)
@@ -768,62 +819,17 @@
 
     xs, zs, cs = (xsend, xrecv), (zsend, zrecv), (csend, crecv)
 
-    for place in range(shards):
-
-        @pl.when(shard == place)
-        def _():
-            for k in range(len(segments[place])):
-                y_copy(place, k).start()
-                owner_copy(place, k).start()
-                own_copy(place, k).start()
-
-    def trait_line(step):
-        return remote(
-            line_slot.at[z], line_slot.at[z], trait_send.at[step], trait_recv.at[step], line_peer(step)
-        )
-
-    def trait_line_arrival(step):
-        origin = lax.rem(z + lines - step, lines)
-        return remote(line_slot.at[origin], line_slot.at[origin], trait_send.at[step], trait_recv.at[step], to_core)
-
-    trait_pair = remote(trait_own, trait_got, trait_send.at[0], trait_recv.at[0], to_x)
-    trait_slot[shard] = traits[...]
-    exchange(7, traits, trait_slot)
-    arrive(7, trait_slot)
-    trait_own[...] = functools.reduce(jnp.add, [trait_slot[o] for o in range(shards)])
-    trait_pair.start()
-    trait_pair.wait_recv()
-    own, got = trait_own[...], trait_got[...]
-    line_slot[z] = jnp.concatenate([jnp.where(x == 0, own, got), jnp.where(x == 0, got, own)], 0)
-    for step in range(1, lines):
-        trait_line(step).start()
-    for step in range(1, lines):
-        trait_line_arrival(step).wait_recv()
-    count_in_line = 2 * traits.shape[0]
-    for at in range(lines):
-        all_traits[at * count_in_line : (at + 1) * count_in_line, :] = line_slot[at]
-    freq = all_traits[:, :FREQ].astype(jnp.bfloat16)
-    classes = embed.shape[0] - PATCH - FREQ
-    named = lax.broadcasted_iota(jnp.int32, (all_traits.shape[0], classes), 1).astype(jnp.float32)
-    onehot = jnp.where(named == all_traits[:, FREQ : FREQ + 1], 1.0, 0.0).astype(jnp.bfloat16)
-
-    own_one = jnp.dot(freq, embed[PATCH : PATCH + FREQ, :], preferred_element_type=jnp.float32)
-    time_one[...] = own_one
-    s1_slot[shard] = (own_one * jax.nn.sigmoid(own_one)).astype(jnp.bfloat16)
-    tab_slot[shard] = jnp.dot(onehot, embed[PATCH + FREQ :, :], preferred_element_type=jnp.float32)
-    patch_slot[shard] = embed[0:PATCH, :]
-    exchange(0, s1_slot.at[shard], s1_slot)
-    exchange(1, tab_slot.at[shard], tab_slot)
-    exchange(2, patch_slot.at[shard], patch_slot)
-    last_place = [o for o in range(shards) if 0 <= 3 * width // 128 - head_starts[o] < head_tiles][-1]
-    last_row = (3 * width // 128 - head_starts[last_place]) * 128
-    last_own[...] = head_t[last_row : last_row + 16, :]
-
-    @pl.when(shard == last_place)
-    def _():
-        last[...] = last_own[...]
-        for step in range(1, shards):
-            remote(last_own, last, small_send.at[6, step - 1], small_recv.at[6, 0], others[step - 1]).start()
+    def begin(k, across):
+        for place in range(shards):
+            if k < len(segments[place]):
+
+                @pl.when(shard == place)
+                def _():
+                    if across:
+                        y_copy(place, k).start()
+                    else:
+                        owner_copy(place, k).start()
+                        own_copy(place, k).start()
 
     def relay(place, stage, k):
         if stage == 0:
@@ -852,11 +858,63 @@
                     if 0 <= tick - stage < len(segments[place]):
                         relay(place, stage, tick - stage)
 
-    ticks = max(len(parts) for parts in segments) + 2
+    def trait_line(step):
+        return remote(
+            line_slot.at[z], line_slot.at[z], trait_send.at[step], trait_recv.at[step], line_peer(step)
+        )
+
+    def trait_line_arrival(step):
+        origin = lax.rem(z + lines - step, lines)
+        return remote(line_slot.at[origin], line_slot.at[origin], trait_send.at[step], trait_recv.at[step], to_core)
+
+    trait_pair = remote(trait_own, trait_got, trait_send.at[0], trait_recv.at[0], to_x)
+    trait_slot[shard] = traits[...]
+    exchange(7, traits, trait_slot)
+    begin(0, True)
+    arrive(7, trait_slot)
+    trait_own[...] = functools.reduce(jnp.add, [trait_slot[o] for o in range(shards)])
+    trait_pair.start()
+    begin(1, True)
+    trait_pair.wait_recv()
+    own, got = trait_own[...], trait_got[...]
+    line_slot[z] = jnp.concatenate([jnp.where(x == 0, own, got), jnp.where(x == 0, got, own)], 0)
+    for step in range(1, lines):
+        trait_line(step).start()
+    relay_tick(0)
+    begin(2, True)
+    for step in range(1, lines):
+        trait_line_arrival(step).wait_recv()
+    count_in_line = 2 * traits.shape[0]
+    for at in range(lines):
+        all_traits[at * count_in_line : (at + 1) * count_in_line, :] = line_slot[at]
+    freq, onehot = placed_traits(all_traits[...], embed.shape[1])
+
+    nt = (((1,), (1,)), ((), ()))
+    own_one = lax.dot_general(freq, embed[:, : freq.shape[1]], nt, preferred_element_type=jnp.float32)
+    time_one[...] = own_one
+    s1_slot[shard] = (own_one * jax.nn.sigmoid(own_one)).astype(jnp.bfloat16)
+    tab_slot[shard] = lax.dot_general(onehot, embed[...], nt, preferred_element_type=jnp.float32)
+    eye = lax.broadcasted_iota(jnp.int32, (PATCH, 128), 0) == lax.broadcasted_iota(jnp.int32, (PATCH, 128), 1)
+    eye = jnp.where(eye, 1.0, 0.0).astype(jnp.bfloat16)
+    patch_slot[shard] = lax.dot_general(eye, embed[:, :128], nt, preferred_element_type=jnp.float32).astype(jnp.bfloat16)
+    exchange(0, s1_slot.at[shard], s1_slot)
+    exchange(1, tab_slot.at[shard], tab_slot)
+    exchange(2, patch_slot.at[shard], patch_slot)
+    relay_tick(1)
+    begin(3, True)
+    last_place = [o for o in range(shards) if 0 <= 3 * width // 128 - head_starts[o] < head_tiles][-1]
+    last_row = (3 * width // 128 - head_starts[last_place]) * 128
+    last_own[...] = head_t[last_row : last_row + 16, :]
+
+    @pl.when(shard == last_place)
+    def _():
+        last[...] = last_own[...]
+        for step in range(1, shards):
+            remote(last_own, last, small_send.at[6, step - 1], small_recv.at[6, 0], others[step - 1]).start()
+
     head_places = [o for o in range(shards) if head_starts[o] * 128 < width]
     fm_places = [o for o in range(shards) if (head_starts[o] + head_tiles) * 128 > width]
     mod_places = [o for o in range(shards) if in_starts[o] * 128 < 6 * width]
-    nt = (((1,), (1,)), ((), ()))
     group = modul.shape[0]
 
     arrive(0, s1_slot)
@@ -864,7 +922,8 @@
     two_own[...] = lax.dot_general(time_act[...], head_t[...], nt, preferred_element_type=jnp.float32)
     two_slot[shard] = two_own[...]
     exchange(3, two_own, two_slot, head_places)
-    relay_tick(0)
+    relay_tick(2)
+    begin(4, True)
     arrive(1, tab_slot)
     arrive(3, two_slot, head_places)
     place_tiles(cond_full, tab_slot, embed_starts, embed_tiles, range(shards), jnp.float32)
@@ -881,15 +940,24 @@
     fm_own[...] = lax.dot_general(cond, head_t[...], nt, preferred_element_type=jnp.float32)
     fm_slot[shard] = fm_own[...]
     exchange(5, fm_own, fm_slot, fm_places)
-    relay_tick(1)
+    relay_tick(3)
+    begin(5, True)
+    begin(0, False)
+    begin(1, False)
+    begin(2, False)
+    begin(3, False)
+    begin(4, False)
+    begin(5, False)
     arrive(2, patch_slot)
     place_tiles(patch, patch_slot, embed_starts, embed_tiles, range(shards), jnp.bfloat16)
     arrive(4, mod_slot, mod_places)
     arrive(5, fm_slot, fm_places)
     place_tiles(modul, mod_slot, in_starts, in_tiles, mod_places, jnp.float32)
     place_tiles(fmod, fm_slot, head_starts, head_tiles, fm_places, jnp.float32, width // 128)
-    for tick in range(2, ticks):
-        relay_tick(tick)
+    relay_tick(4)
+    relay_tick(5)
+    relay_tick(6)
+    relay_tick(7)
 
     for place in range(shards):
         count = len(segments[place])
@@ -945,24 +1013,27 @@
         remote(last_own, last, small_send.at[6, 0], small_recv.at[6, 0], to_core).wait_recv()
 
 
-def gather_call(in_low, out_low, head_low, embed_low, traits, shards, lines):
+def gather_call(in_t, out_t, head_t, embed_t, traits, shards, lines):
     place = lax.axis_index("shard")
-    width = head_low.shape[0]
+    width = head_t.shape[1]
     low, full = jnp.bfloat16, jnp.float32
 
-    def window(item_t, starts, tiles, cols):
-        offsets = jnp.asarray([o * cols - start * 128 for o, start in enumerate(starts)], jnp.int32)
-        target = jnp.zeros((tiles * 128, item_t.shape[1]), item_t.dtype)
-        return lax.dynamic_update_slice_in_dim(target, item_t, offsets[place], 0)
-
-    in_cols, head_cols, embed_cols = in_low.shape[1], head_low.shape[1], embed_low.shape[1]
+    def window(item_t, starts, tiles, lanes):
+        rows = item_t.shape[0]
+        offsets = [o * rows - start * 128 for o, start in enumerate(starts)]
+        most = max(offsets)
+        padded = jnp.pad(item_t, ((most, tiles * 128 - rows), (0, lanes - item_t.shape[1])))
+        begin = most - jnp.asarray(offsets, jnp.int32)[place]
+        return lax.dynamic_slice_in_dim(padded, begin, tiles * 128, 0).astype(low)
+
+    in_cols, head_cols, embed_cols = in_t.shape[0], head_t.shape[0], embed_t.shape[0]
     in_starts, in_tiles = windows(in_cols, shards)
     head_starts, head_tiles = windows(head_cols, shards)
     embed_starts, embed_tiles = windows(embed_cols, shards)
-    in_t = window(in_low.T, in_starts, in_tiles, in_cols)
-    head_t = window(head_low.T, head_starts, head_tiles, head_cols)
-    embed = window(embed_low.T, embed_starts, embed_tiles, embed_cols).T
-    segments = heavy_segments(width, in_cols, in_starts, out_low.shape[1], shards)
+    in_t = window(in_t, in_starts, in_tiles, width)
+    head_t = window(head_t, head_starts, head_tiles, width)
+    embed = window(embed_t, embed_starts, embed_tiles, -(-embed_t.shape[1] // 128) * 128)
+    segments = heavy_segments(width, in_cols, in_starts, out_t.shape[0], shards)
     plan = (segments, (in_starts, in_tiles), (head_starts, head_tiles), (embed_starts, embed_tiles), lines)
     group = traits.shape[0]
     rows = 2 * lines * group
@@ -1015,7 +1086,7 @@
         compiler_params=pltpu.CompilerParams(
             collective_id=2, has_side_effects=True, vmem_limit_bytes=60 * 1024 * 1024
         ),
-    )(in_t, out_low.T, head_t, embed, traits)
+    )(in_t, out_t.astype(low), head_t, embed, traits)
     return in_t, head_t, outs
 
 
@@ -1145,8 +1216,9 @@
         back[span[image], :] = d_value
         put_row(d_mod, image, 5, d_value * mlp[span[image], :])
         d_qkv[span[image], pl.ds(0, width)] = (piece(modul, image, 5) * d_value).astype(low)
-    few[pl.ds(PATCH, PATCH), :] = g_last
-    few[pl.ds(2 * PATCH, 8), :] = jnp.full((8, width), loss, jnp.float32)
+    few[pl.ds(PATCH, 8), :] = jnp.full((8, width), loss, jnp.float32)
+    few[pl.ds(PATCH + 8, PATCH), :] = g_last
+    few[pl.ds(2 * PATCH + 8, 8), :] = jnp.zeros((8, width), jnp.float32)
 
     d_mlp = d_qkv.at[:, pl.ds(0, width)]
 
@@ -1247,7 +1319,7 @@
     width = patch.shape[1]
     low, full = jnp.bfloat16, jnp.float32
     shapes = [(item.shape, low) for item in heavy] + [
-        ((2 * PATCH + 8, width), full),
+        ((2 * PATCH + 16, width), full),
         (modul.shape, full),
         (fmod.shape, full),
     ]
@@ -1261,7 +1333,246 @@
     )(state, target, weight_t, pos, patch, last, modul, fmod, *heavy)
 
 
-def exchange_kernel(shards, own, total, slots, send, recv):
+def own_segments(width, in_cols, in_starts, out_rows, shards):
+    every = []
+    for place in range(shards):
+        parts = []
+        for array, low, high in ((3, 6 * width, 9 * width), (1, 9 * width, 13 * width)):
+            first, last = max(low, place * in_cols), min(high, (place + 1) * in_cols)
+            if first < last:
+                parts.append((array, first - low, last - first, first - in_starts[place] * 128))
+        every.append(parts)
+    return every
+
+
+def total_kernel(
+    tables, segments, fc2, fc1, attn_out, qkv, w_in, w_out, w_head, w_embed,
+    d_in, d_fin, d_two, d_one, d_full, few, cond_full, time_act, traits, c_in, c_out, c_head, c_embed,
+    g_in, g_out, g_head, g_embed, n_in, n_out, n_head, n_embed, stats,
+    own_t, own_out, grad_t, head_t, t_out, t_head, t_embed, v_in, v_out, v_head, v_embed,
+    load, write, fetch,
+):
+    (in_starts, in_tiles), (head_starts, head_tiles), (embed_starts, embed_tiles), shards = tables
+    arrays = (fc2, fc1, attn_out, qkv)
+    shard = lax.axis_index("shard")
+    width = cond_full.shape[1]
+    in_cols, head_cols, embed_cols, out_cols = (item.shape[0] for item in (w_in, w_head, w_embed, w_out))
+    full, low = jnp.float32, jnp.bfloat16
+    span = lane_span(width, w_embed.shape[1])
+
+    weights = ((w_in, v_in), (w_out, v_out), (w_head, v_head), (w_embed, v_embed))
+    reads = [pltpu.make_async_copy(source, target, load.at[k]) for k, (source, target) in enumerate(weights)]
+    for copy in reads:
+        copy.start()
+
+    def heavy_copies(place):
+        copies = []
+        for k, (array, row, rows, at) in enumerate(segments[place]):
+            copies.append(
+                pltpu.make_async_copy(
+                    arrays[array].at[pl.ds(row, rows), :], own_t.at[pl.ds(at, rows), :], fetch.at[k]
+                )
+            )
+        for k, array in ((2, 2), (3, 0)):
+            lane = 0 if array == 2 else width
+            copies.append(
+                pltpu.make_async_copy(
+                    arrays[array].at[pl.ds(place * out_cols, out_cols), :],
+                    own_out.at[:, pl.ds(lane, arrays[array].shape[1])],
+                    fetch.at[k],
+                )
+            )
+        return copies
+
+    for place in range(shards):
+
+        @pl.when(shard == place)
+        def _():
+            for copy in heavy_copies(place):
+                copy.start()
+            edges = [0]
+            for _, _, rows, at in segments[place]:
+                edges += [at, at + rows]
+            edges.append(in_tiles * 128)
+            for start, stop in zip(edges[0::2], edges[1::2]):
+                if start < stop:
+                    own_t[start:stop, :] = jnp.zeros((stop - start, width), low)
+
+    def decayed(state, total, count):
+        return decay * state + (1.0 - decay) * (total / count + eps_one)
+
+    def to_lanes(column):
+        return jnp.broadcast_to(column, (column.shape[0], 128)).T[:1, :]
+
+    def to_column(lanes):
+        return jnp.broadcast_to(lanes, (128, lanes.shape[1])).T[:, :1]
+
+    def squares_of(value, state, fresh_out, start, size):
+        square = value * value
+        sums = to_lanes(jnp.sum(square, -1, keepdims=True))[:, :size]
+        fresh = decayed(state[:, start : start + size], sums, value.shape[1])
+        fresh_out[:, start : start + size] = fresh
+        inverse = 1.0 / fresh
+        if size < value.shape[0]:
+            inverse = jnp.concatenate([inverse, jnp.zeros((1, value.shape[0] - size), full)], 1)
+        return jnp.sum(square, 0, keepdims=True), jnp.sum(square * to_column(inverse), 0, keepdims=True)
+
+    def put(start, plain, scaled):
+        stats[:, start : start + plain.shape[1]] = plain
+        stats[:, span + start : span + start + plain.shape[1]] = scaled
+
+    def column_blocks(total):
+        return [(start, min(128, total - start)) for start in range(0, total, 128)]
+
+    def by_blocks(take, total, state, fresh_out, place):
+        plain, scaled = jnp.zeros((1, width), full), jnp.zeros((1, width), full)
+        for start, size in column_blocks(total):
+            value = take(start, size)
+            if size < 128:
+                value = jnp.concatenate([value, jnp.zeros((128 - size, width), full)], 0)
+            more, more_scaled = squares_of(value, state, fresh_out, start, size)
+            plain, scaled = plain + more, scaled + more_scaled
+        put(place, plain, scaled)
+
+    cond = cond_full[...]
+    cond = (cond * jax.nn.sigmoid(cond)).astype(low)
+
+    lanes_all = -(-w_embed.shape[1] // 128) * 128
+    freq, onehot = placed_traits(traits[...], lanes_all)
+    square_one = lax.broadcasted_iota(jnp.int32, (PATCH, lanes_all), 0)
+    eye = jnp.where(square_one == lax.broadcasted_iota(jnp.int32, (PATCH, lanes_all), 1), 1.0, 0.0).astype(low)
+
+    def exact(value, picks):
+        total = None
+        for _ in range(3):
+            part = value.astype(low)
+            value = value - part.astype(full)
+            term = mxu(part, picks, TN)
+            total = term if total is None else total + term
+        return total
+
+    for place in range(shards):
+
+        @pl.when(shard == place)
+        def _():
+            lead = place * embed_cols - embed_starts[place] * 128
+            lanes = slice(embed_starts[place] * 128, (embed_starts[place] + embed_tiles) * 128)
+            value = exact(d_full[...], onehot) + exact(few[0:PATCH, lanes], eye)
+            value = value[lead : lead + embed_cols, :]
+            time = mxu(d_one[...], freq, TN)[lead : lead + embed_cols, :]
+            t_embed[:, : freq.shape[1]] = value[:, : freq.shape[1]] + time
+            t_embed[:, freq.shape[1] :] = value[:, freq.shape[1] : w_embed.shape[1]]
+
+    pltpu.make_async_copy(t_embed, g_embed, write.at[3]).start()
+    value = jnp.concatenate([t_embed[...], jnp.zeros((embed_cols, lanes_all - w_embed.shape[1]), full)], 1)
+    square = value * value
+    fresh = decayed(c_embed[...], to_lanes(jnp.sum(square, -1, keepdims=True)), w_embed.shape[1])
+    n_embed[...] = fresh
+    put(7 * width, jnp.sum(square, 0, keepdims=True), jnp.sum(square * to_column(1.0 / fresh), 0, keepdims=True))
+
+    head_t[...] = mxu(d_two[...], time_act[...], TN) + mxu(d_fin[...], cond, TN)
+    last_place = [o for o in range(shards) if 0 <= 3 * width // 128 - head_starts[o] < head_tiles][-1]
+    last_row = (3 * width // 128 - head_starts[last_place]) * 128
+
+    @pl.when(shard == last_place)
+    def _():
+        head_t[last_row : last_row + PATCH, :] = few[PATCH + 8 : 2 * PATCH + 8, :]
+
+    for place in range(shards):
+
+        @pl.when(shard == place)
+        def _():
+            lead = place * head_cols - head_starts[place] * 128
+            t_head[...] = head_t[lead : lead + head_cols, :]
+
+    pltpu.make_async_copy(t_head, g_head, write.at[2]).start()
+    by_blocks(lambda start, size: t_head[start : start + size, :], head_cols, c_head, n_head, 6 * width)
+
+    for place in range(shards):
+
+        @pl.when(shard == place)
+        def _():
+            for copy in heavy_copies(place):
+                copy.wait()
+
+    def light(index, carry):
+        part = pl.ds(pl.multiple_of(index * 128, 128), 128)
+        grad_t[part, :] = mxu(d_in[:, part], cond, TN) + own_t[part, :].astype(full)
+        return carry
+
+    lax.fori_loop(0, in_tiles, light, 0)
+    lead = lax.rem(shard * in_cols, 128)
+    write_in = pltpu.make_async_copy(grad_t.at[pl.ds(pl.multiple_of(lead, 64), in_cols), :], g_in, write.at[0])
+    write_in.start()
+    by_blocks(
+        lambda start, size: grad_t[pl.ds(pl.multiple_of(lead + start, 64), size), :], in_cols, c_in, n_in, 0
+    )
+
+    sums = jnp.zeros((out_cols, 1), full)
+    for index in range(5):
+        value = own_out[:, index * width : (index + 1) * width].astype(full)
+        t_out[:, index * width : (index + 1) * width] = value
+        sums += jnp.sum(value * value, -1, keepdims=True)
+    pltpu.make_async_copy(t_out, g_out, write.at[1]).start()
+    fresh = decayed(c_out[...], to_lanes(sums), 5 * width)
+    n_out[...] = fresh
+    column = to_column(1.0 / fresh)
+    for index in range(5):
+        value = t_out[:, index * width : (index + 1) * width]
+        square = value * value
+        put(width + index * width, jnp.sum(square, 0, keepdims=True), jnp.sum(square * column, 0, keepdims=True))
+
+    for copy in reads:
+        copy.wait()
+    for k, (_, value) in enumerate(weights):
+        rows, cols = value.shape
+
+        def squares(index, carry):
+            block = value[pl.ds(pl.multiple_of(index * 64, 64), 64), :]
+            return carry + jnp.sum(block * block, 0, keepdims=True)
+
+        total = lax.fori_loop(0, rows // 64, squares, jnp.zeros((1, cols), full))
+        if rows % 64:
+            block = value[rows // 64 * 64 :, :]
+            total += jnp.sum(block * block, 0, keepdims=True)
+        start = 2 * span + k * 128
+        stats[:, start : start + 128] = jnp.broadcast_to(jnp.sum(total, -1, keepdims=True) / 128.0, (1, 128))
+    write_in.wait()
+    for k, (source, target) in enumerate(((t_out, g_out), (t_head, g_head), (t_embed, g_embed))):
+        pltpu.make_async_copy(source, target, write.at[k + 1]).wait()
+
+
+def lane_span(width, embed_rows):
+    return 7 * width + -(-embed_rows // 128) * 128
+
+
+def total_call(tables, heavy, weights, light, cols):
+    (in_starts, in_tiles), (_, head_tiles), _, shards = tables
+    low, full = jnp.bfloat16, jnp.float32
+    width = heavy[2].shape[0]
+    w_in, w_out, w_head, w_embed = weights
+    lanes = 2 * lane_span(width, w_embed.shape[1]) + 4 * 128
+    segments = own_segments(width, w_in.shape[0], in_starts, w_out.shape[0], shards)
+    shapes = [(item.shape, full) for item in weights] + [(item.shape, full) for item in cols] + [((1, lanes), full)]
+    anywhere, vmem = pl.BlockSpec(memory_space=pl.ANY), pl.BlockSpec(memory_space=pltpu.VMEM)
+    scratch = [
+        ((in_tiles * 128, width), low),
+        (w_out.shape, low),
+        ((in_tiles * 128, width), full),
+        ((head_tiles * 128, width), full),
+    ]
+    scratch += [(item.shape, full) for item in weights[1:]] + [(item.shape, full) for item in weights]
+    return pl.pallas_call(
+        functools.partial(total_kernel, tables, segments),
+        out_shape=[jax.ShapeDtypeStruct(*item) for item in shapes],
+        in_specs=[anywhere] * 8 + [vmem] * (len(light) + 4),
+        out_specs=[anywhere] * 4 + [vmem] * 5,
+        scratch_shapes=[pltpu.VMEM(*item) for item in scratch] + [pltpu.SemaphoreType.DMA((4,))] * 3,
+        compiler_params=pltpu.CompilerParams(vmem_limit_bytes=60 * 1024 * 1024),
+    )(*heavy, *weights, *light, *cols)
+
+
+def finish_kernel(shards, sizes, own, r_in, r_out, r_head, r_embed, n_in, n_out, n_head, n_embed, s_in, s_out, s_head, s_embed, rms, slots, send, recv):
     rep, shard = lax.axis_index("rep"), lax.axis_index("shard")
     barrier = pltpu.get_barrier_semaphore()
     for step in range(1, shards):
@@ -1284,31 +1595,43 @@
     slots[shard] = own[...]
     for step in range(1, shards):
         copy(step).wait()
-    total[...] = functools.reduce(jnp.add, [slots[o] for o in range(shards)])
-
-
-def sum_in_group(tree, shards):
-    leaves, kind = jax.tree.flatten(tree)
-    flat = jnp.concatenate([leaf.reshape(-1) for leaf in leaves])
-    rows = -(-flat.shape[0] // 1024) * 8
-    block = jnp.pad(flat, (0, rows * 128 - flat.shape[0])).reshape(rows, 128)
-    total = pl.pallas_call(
-        functools.partial(exchange_kernel, shards),
-        out_shape=jax.ShapeDtypeStruct(block.shape, jnp.float32),
-        in_specs=[pl.BlockSpec(memory_space=pltpu.VMEM)],
-        out_specs=pl.BlockSpec(memory_space=pltpu.VMEM),
+    total = functools.reduce(jnp.add, [slots[o] for o in range(shards)])
+    states, fresh, scales = (r_in, r_out, r_head, r_embed), (n_in, n_out, n_head, n_embed), (s_in, s_out, s_head, s_embed)
+    starts, start = [], 0
+    for rows, _ in sizes:
+        starts.append(start)
+        start += -(-rows // 128) * 128
+    update, means = jnp.zeros((1, 1), jnp.float32), []
+    for k, (rows, cols) in enumerate(sizes):
+        row = decay * states[k][...] + (1.0 - decay) * (total[:, starts[k] : starts[k] + rows] / cols + eps_one)
+        fresh[k][...] = row
+        mean = jnp.mean(row, -1, keepdims=True)
+        means.append(mean)
+        update += mean * jnp.sum(total[:, start + starts[k] : start + starts[k] + rows] / row, -1, keepdims=True)
+    update = jnp.sqrt(update / sum(rows * cols for rows, cols in sizes))
+    rms[...] = jnp.broadcast_to(update, rms.shape)
+    factor = jnp.maximum(1.0, update / clip_level)
+    for k, (rows, cols) in enumerate(sizes):
+        first = 2 * start + k * 128
+        weight = jnp.sqrt(jnp.sum(total[:, first : first + 128], -1, keepdims=True) / (rows * cols))
+        scales[k][...] = rate * jnp.maximum(eps_two, weight) / factor * lax.rsqrt(fresh[k][...] / means[k])
+
+
+def finish_call(shards, sizes, stats, rows_old):
+    full = jnp.float32
+    shapes = [((1, rows), full) for rows, _ in sizes] * 2 + [((1, 128), full)]
+    return pl.pallas_call(
+        functools.partial(finish_kernel, shards, sizes),
+        out_shape=[jax.ShapeDtypeStruct(*item) for item in shapes],
+        in_specs=[pl.BlockSpec(memory_space=pltpu.VMEM)] * 5,
+        out_specs=[pl.BlockSpec(memory_space=pltpu.VMEM)] * len(shapes),
         scratch_shapes=[
-            pltpu.VMEM((shards,) + block.shape, jnp.float32),
+            pltpu.VMEM((shards,) + stats.shape, full),
             pltpu.SemaphoreType.DMA((shards - 1,)),
             pltpu.SemaphoreType.DMA((shards - 1,)),
         ],
         compiler_params=pltpu.CompilerParams(collective_id=3, has_side_effects=True),
-    )(block).reshape(-1)
-    parts, first = [], 0
-    for leaf in leaves:
-        parts.append(total[first : first + leaf.size].reshape(leaf.shape))
-        first += leaf.size
-    return jax.tree.unflatten(kind, parts)
+    )(stats, *rows_old)
 
 
 def on_device(
@@ -1336,28 +1659,28 @@
     shard_count = lax.axis_size("shard")
     place = lax.axis_index("shard")
     in_cols = blocks_in.shape[2]
-    out_cols = blocks_out.shape[2]
     head_cols = head_side.shape[1]
     embed_cols = embed_side.shape[1]
     group = images * shard_count
-    in_low = blocks_in[0].astype(jnp.bfloat16)
-    out_low = blocks_out[0].astype(jnp.bfloat16)
-    head_low = head_side.astype(jnp.bfloat16)
-    embed_low = embed_side.astype(jnp.bfloat16)
+    weights = (blocks_in[0].T, blocks_out[0].T, head_side.T, embed_side.T)
     t_value = (times.astype(jnp.float32) + 1.0) / step_count
-    classes = jnp.where(dropped == 1, CLASSES - 1, labels).astype(jnp.float32)
+    classes = (PATCH + FREQ + jnp.where(dropped == 1, CLASSES - 1, labels)).astype(jnp.float32)
     lines = LINE
-    traits = jnp.zeros((group, FREQ + 128), jnp.float32)
+    lead = -(-(PATCH + FREQ) // 128) * 128
+    own_traits = jnp.concatenate(
+        [
+            jnp.zeros((images, PATCH), jnp.float32),
+            time_freq(t_value, FREQ),
+            jnp.zeros((images, lead - PATCH - FREQ), jnp.float32),
+            jnp.broadcast_to(classes[:, None], (images, 128)),
+        ],
+        1,
+    )
     traits = lax.dynamic_update_slice(
-        traits,
-        jnp.concatenate([time_freq(t_value, FREQ), jnp.broadcast_to(classes[:, None], (images, 128))], 1),
-        (place * images, 0),
+        jnp.zeros((group, lead + 128), jnp.float32), own_traits, (place * images, 0)
     )
-    in_t, head_win_t, gathered = gather_call(in_low, out_low, head_low, embed_low, traits, shard_count, lines)
+    in_t, head_win_t, gathered = gather_call(*weights, traits, shard_count, lines)
     fc2_t, fc1_t, o_t, qkv_t, cond_full, time_act, time_one, modul, final_mod, patch_w, head_t, all_traits = gathered
-    freq_low = all_traits[:, :FREQ].astype(jnp.bfloat16)
-    onehot = all_traits[:, FREQ : FREQ + 1] == jnp.arange(CLASSES, dtype=jnp.float32)[None, :]
-    cond = silu(cond_full).astype(jnp.bfloat16)
     tcol = t_value[:, None, None]
     state = (
         (1.0 - tcol) * latents.reshape(images, TOK, PATCH)
@@ -1387,89 +1710,57 @@
         heavy,
         [d_mod, d_fm, few, in_t, head_win_t, cond_full, time_one],
     )
-    heavy_in, heavy_out = own_heavy(sums[:4], in_cols, out_cols)
     d_in, d_fin, d_two, d_full, d_one, few_sum = sums[4:]
-
-    def own_columns(item, cols):
-        return lax.dynamic_slice_in_dim(item, lax.rem(place * cols, 128), cols, 1)
-
-    loss_sum = few_sum[2 * PATCH, 0]
-    d_full_own = lax.dynamic_slice_in_dim(d_full, place * embed_cols, embed_cols, 1)
-    g_table = lax.dot_general(
-        onehot.astype(jnp.float32),
-        d_full_own,
-        (((0,), (0,)), ((), ())),
-        precision=lax.Precision.HIGHEST,
+    loss_sum = few_sum[PATCH, 0]
+    rows_old = (state_in_row, state_out_row, state_head_row[None], state_embed_row[None])
+    cols_old = (state_in_col, state_out_col, state_head_col[None], state_embed_col[None])
+    *outs, stats = total_call(
+        tables,
+        sums[:4],
+        weights,
+        [d_in, d_fin, d_two, d_one, d_full, few_sum, cond_full, time_act, all_traits],
+        cols_old,
     )
-    own_patch = lax.dynamic_slice_in_dim(few_sum[:PATCH], place * embed_cols, embed_cols, 1)
-    own_head = jnp.pad(few_sum[PATCH : 2 * PATCH].T, ((0, 0), (3 * width, 0)))
-    own_head = lax.dynamic_slice_in_dim(own_head, place * head_cols, head_cols, 1)
-    totals = (
-        (own_columns(weight_grad(cond, d_in), in_cols) + heavy_in)[None],
-        heavy_out[None],
-        own_columns(weight_grad(time_act, d_two) + weight_grad(cond, d_fin), head_cols) + own_head,
-        jnp.concatenate([own_patch, own_columns(weight_grad(freq_low, d_one), embed_cols), g_table], 0),
-    )
+    totals, cols_new = outs[:4], outs[4:]
     blocks = lax.axis_size("rep") // (2 * lines)
     if blocks > 1:
         apart = [[k * 2 * lines + j for k in range(blocks)] for j in range(2 * lines)]
         totals, loss_sum = lax.psum((totals, loss_sum), "rep", axis_index_groups=apart)
-    weights = (blocks_in, blocks_out, head_side, embed_side)
-    rows_old = (state_in_row, state_out_row, state_head_row, state_embed_row)
-    cols_old = (state_in_col, state_out_col, state_head_col, state_embed_col)
-    cols_new = [
-        decay * col_state + (1.0 - decay) * (jnp.mean(gradient * gradient, -2) + eps_one)
-        for gradient, col_state in zip(totals, cols_old)
+        cols_new, plain, scaled = [], [], []
+        for gradient, col_state in zip(totals, cols_old):
+            square = gradient * gradient
+            fresh = decay * col_state + (1.0 - decay) * (jnp.mean(square, 1)[None] + eps_one)
+            pad = (0, -gradient.shape[1] % 128)
+            cols_new.append(fresh)
+            plain.append(jnp.pad(jnp.sum(square, 0), pad))
+            scaled.append(jnp.pad(jnp.sum(square / fresh[0][:, None], 0), pad))
+        spans = sum(item.shape[0] for item in plain) * 2
+        stats = jnp.concatenate(plain + scaled + [stats[0, spans:]])[None]
+    sizes = [(weight.shape[1], weight.shape[0] * shard_count) for weight in weights]
+    *outs, rms = finish_call(shard_count, sizes, stats, rows_old)
+    rows_new, scales = outs[:4], outs[4:]
+    update_rms = rms[0, 0]
+    news = [
+        (weight - gradient * scale * lax.rsqrt(col_next[0])[:, None]).T
+        for weight, gradient, scale, col_next in zip(weights, totals, scales, cols_new)
     ]
-    row_parts = [jnp.sum(gradient * gradient, -1) for gradient in totals]
-    row_scaled = [
-        jnp.sum(gradient * gradient / col_next[..., None, :], -1)
-        for gradient, col_next in zip(totals, cols_new)
-    ]
-    weight_sq = [jnp.sum(weight * weight, axis=(-2, -1)) for weight in weights]
-    row_sums, row_scaled, weight_sq = sum_in_group((row_parts, row_scaled, weight_sq), shard_count)
-    rows_new = [
-        decay * row_state
-        + (1.0 - decay) * (row_sum / (gradient.shape[-1] * shard_count) + eps_one)
-        for row_sum, gradient, row_state in zip(row_sums, totals, rows_old)
-    ]
-    row_means = [jnp.mean(row_next, -1) for row_next in rows_new]
-    total_sq = sum(
-        jnp.sum(row_mean * jnp.sum(scaled / row_next, -1))
-        for scaled, row_next, row_mean in zip(row_scaled, rows_new, row_means)
-    )
-    count = sum((weight.size for weight in weights)) * shard_count
-    update_rms = jnp.sqrt(total_sq / count)
-    factor = jnp.maximum(1.0, update_rms / clip_level)
-    news = []
-    for index in range(4):
-        numel = weights[index].shape[-2] * weights[index].shape[-1] * shard_count
-        weight_rms = jnp.sqrt(weight_sq[index] / numel)
-        step_size = rate * jnp.maximum(eps_two, weight_rms) / factor
-        row_scale = jnp.asarray(step_size)[..., None] * lax.rsqrt(
-            rows_new[index] / row_means[index][..., None]
-        )
-        news.append(
-            weights[index]
-            - totals[index] * row_scale[..., :, None] * lax.rsqrt(cols_new[index])[..., None, :]
-        )
     return (
         loss_sum,
         update_rms,
-        totals[0],
-        totals[1],
-        totals[2],
-        totals[3],
+        totals[0].T[None],
+        totals[1].T[None],
+        totals[2].T,
+        totals[3].T,
         rows_new[0],
         cols_new[0],
         rows_new[1],
         cols_new[1],
-        rows_new[2],
-        cols_new[2],
-        rows_new[3],
-        cols_new[3],
-        news[0],
-        news[1],
+        rows_new[2][0],
+        cols_new[2][0],
+        rows_new[3][0],
+        cols_new[3][0],
+        news[0][None],
+        news[1][None],
         news[2],
         news[3],
     )

time: 479 us -> 372 us (0.78)
  Pallas kernels: 351 us -> 312 us
  other arithmetic: 58.5 us -> 26.3 us
  local copies, waits for them, and re-layouts: 32.7 us -> 19.8 us
  between operations: 17.5 us -> 6.03 us
  matrix products: 10.1 us -> 0 us
    pallas_call x1, Pallas kernels: 105 us -> 71.3 us  [gather_call(): pl.pallas_call(functools.partial(gather_kernel, plan), out_shape=[jax.Sha...]
    reduce_sum x16 -> x0, other arithmetic: 28.5 us -> none  [the longest x4 10.3 us: on_device(): jnp.mean(gradient * gradient, -2) + eps_one]
    sub x4 -> x0, other arithmetic: 14.6 us -> none  [on_device(): weights[index]]
    pallas_call x1, Pallas kernels: 154 us -> 142 us  [reduce_call(): pl.pallas_call(functools.partial(reduce_kernel, lines, chunks, tables), o...]
    dynamic_update_slice x2 -> x1, local copies, waits for them, and re-layouts: 11.4 us -> 0.01 us  [on_device(): lax.dynamic_update_slice(jnp.zeros((group, lead + 128), jnp.float32), own...]
    broadcast_in_dim x1 -> x2, other arithmetic: 1.79 us -> 13 us  [the longest x1 9.23 us: on_device(): news[0][None]]
    convert_element_type x1 -> x3, local copies, waits for them, and re-layouts: 0.24 us -> 10.7 us  [window(): return lax.dynamic_slice_in_dim(padded, begin, tiles * 128, 0).astype(low)]
    dot_general x5 -> x0, matrix products: 10.1 us -> none  [the longest x4 8.66 us: weight_grad(): lax.dot_general(flat_left, flat_back, (((0,), (0,)), ((), ())), preferred...]
where the time goes in v4:
time: 372 us; the launch traced here: 365 us
  Pallas kernels  312 us (84%)
  other arithmetic  26.3 us (7%)
  local copies, waits for them, and re-layouts  19.8 us (5%)
  between operations  6.03 us (2%)
    pallas_call x1, Pallas kernels, reduce_call(): pl.pallas_call(functools.partial(reduce_kernel, lines, chunks, tables), o...  142 us
    pallas_call x1, Pallas kernels, gather_call(): pl.pallas_call(functools.partial(gather_kernel, plan), out_shape=[jax.Sha...  71.3 us
    pallas_call x1, Pallas kernels, pass_call(): pl.pallas_call(functools.partial(pass_kernel, images), out_shape=[jax.Sha...  70.2 us
    pallas_call x1, Pallas kernels, total_call(): pl.pallas_call(functools.partial(total_kernel, tables, segments), out_sha...  18.5 us
    convert_element_type x3, local copies, waits for them, and re-layouts, window(): return lax.dynamic_slice_in_dim(padded, begin, tiles * 128, 0).astype(low)  10.7 us
    pallas_call x1, Pallas kernels, finish_call(): pl.pallas_call(functools.partial(finish_kernel, shards, sizes), out_shape...  10.4 us
    broadcast_in_dim x1, other arithmetic, on_device(): news[0][None]  9.23 us

profile of v4, /device:TPU:0, one launch (start us, length us, event | category | flops | bytes accessed | tf_op | source)
XLA Modules:
  0.0 364.6 jit_solution(530146017266991470)
XLA Ops:
  0.7 1.2 dynamic_slice.18
  3.2 5.6 %fusion.in_t.refs_7_ = bf16[2560,768]{1,0:T(8,128)(2,1)} fusion(s32[]{:T(128)S(6)} %select_n.48, f32[2496,768]{1,0:T(8,128)} %bitcast.55), kind=kLoop, calls=%fused_computation.1 | loop fusion | bytes 11599876 | tf_op jit(solution)/shard_map/convert_element_type | solution.py:1027
  9.6 2.2 fusion.2.embed
  13.7 2.9 fusion.1.head_t.refs_8_
  17.0 1.3 bitcast_convert_fusion.out_t
  18.3 71.3 %shard_map.340 = (bf16[768,3072]{1,0:T(8,128)(2,1)}, bf16[3072,768]{1,0:T(8,128)(2,1)}, bf16[768,768]{1,0:T(8,128)(2,1)}, bf16[2304,768]{1,0:T(8,128)(2,1)}, f32...) custom-call(bf16[2560,768]{1,0:T(8,128)(2,1)} %fusion.in_t.refs_7_, ...), custom_call_target="tpu_custom_call" | custom-call | tf_op jit(solution)/shard_map/pallas_call | solution.py:1068
  89.7 1.9 multiply_sine_fusion.1
  91.6 1.1 pad_maximum_fusion.pos
  93.1 0.9 add_convert_fusion.state
  94.0 0.9 copy.43
  94.9 0.8 reshape.126.target
  95.7 70.2 %shard_map.341 = (bf16[768,3072]{1,0:T(8,128)(2,1)}, bf16[3072,768]{1,0:T(8,128)(2,1)}, bf16[768,768]{1,0:T(8,128)(2,1)}, bf16[2304,768]{1,0:T(8,128)(2,1)}, f32...) custom-call(bf16[512,16]{1,0:T(8,128)(2,1)} %add_convert_fusion.state, f32[512,16]{1,0:T(8,128)} %reshape.126.target, ...), custom_call_target="tpu_custom_call" | custom-call | tf_op jit(solution)/shard_map/pallas_call | solution.py:1326
  166.0 142.0 %shard_map.342 = (bf16[768,3072]{1,0:T(8,128)(2,1)}, bf16[3072,768]{1,0:T(8,128)(2,1)}, bf16[768,768]{1,0:T(8,128)(2,1)}, bf16[2304,768]{1,0:T(8,128)(2,1)}, bf1...) custom-call(bf16[768,3072]{1,0:T(8,128)(2,1)} %get-tuple-element.73., ...), custom_call_target="tpu_custom_call" | custom-call | tf_op jit(solution)/shard_map/pallas_call | solution.py:627
  308.6 18.5 %shard_map.343 = (f32[2496,768]{1,0:T(8,128)}, f32[192,3840]{1,0:T(8,128)}, f32[580,768]{1,0:T(8,128)}, f32[192,1273]{1,0:T(8,128)}, f32[1,2496]{1,0:T(1,128)}, ...) custom-call(bf16[768,3072]{1,0:T(8,128)(2,1)} %get-tuple-element.83.fc2, ...), custom_call_target="tpu_custom_call" | custom-call | tf_op jit(solution)/shard_map/pallas_call | solution.py:1565
  328.2 10.4 %shard_map.344 = (f32[1,768]{1,0:T(1,128)}, f32[1,3840]{1,0:T(1,128)}, f32[1,768]{1,0:T(1,128)}, f32[1,1273]{1,0:T(1,128)}, f32[1,768]{1,0:T(1,128)}, /*index=5*...) custom-call(f32[1,13824]{1,0:T(1,128)} %get-tuple-element.94.own, f32[1,768]{1,0:T(1,128)} %r_in.1, ...), custom_call_target="tpu_custom_call" | custom-call | tf_op jit(solution)/shard_map/pallas_call | solution.py:1623
  338.7 0.7 reduce.7
  339.4 0.7 rsqrt.39
  340.1 2.3 subtract_bitcast_fusion.3
  342.5 3.6 subtract_bitcast_fusion.2
  346.2 3.8 %subtract_bitcast_fusion.1 = f32[1,3840,192]{1,2,0:T(8,128)} fusion(f32[192,3840]{1,0:T(8,128)} %get-tuple-element.97, f32[192]{0:T(256)S(1)} %bitcast.70, f32[3840]{0:T(1024)S(1)} %reduce.5, f32[1,3840,192]{1,2,0:T(8,128)S(1)} %copy-done.1), kind=kLoop, calls=%fused_computation.3 | loop fusion | flops 2211840 | bytes 8863488 | tf_op jit(solution)/shard_map/broadcast_in_dim | solution.py:1763
  350.2 9.2 %subtract_bitcast_fusion = f32[1,768,2496]{1,2,0:T(8,128)} fusion(f32[2496,768]{1,0:T(8,128)} %get-tuple-element.96, f32[2496]{0:T(1024)S(1)} %rsqrt_reduce_fusion, f32[768]{0:T(1024)S(1)} %reduce.3, f32[1,768,2496]{1,2,0:T(8,128)} %param.27), kind=kLoop, calls=%fused_computation.2 | loop fusion | flops 5750784 | bytes 23016192 | tf_op jit(solution)/shard_map/broadcast_in_dim | solution.py:1762
  359.4 0.6 reduce.2
  360.0 0.6 reduce
  360.6 1.2 slice.6
  (84 shorter events, 4.5 us)
Async XLA Ops:
  3.2 8.6 %copy-start.25 = (s32[4]{0:T(128)S(1)}, s32[4]{0:T(128)}, u32[]{:S(2)}) copy-start(s32[4]{0:T(128)} %constant.93.clone) | copy-start | bytes 52
  8.8 7.9 %copy-start.21 = (s32[2]{0:T(128)S(1)}, s32[2]{0:T(128)}, u32[]{:S(2)}) copy-start(s32[2]{0:T(128)} %param.24) | copy-start | bytes 28
  8.8 8.0 %copy-start.22 = (s32[2]{0:T(128)S(1)}, s32[2]{0:T(128)}, u32[]{:S(2)}) copy-start(s32[2]{0:T(128)} %param.25) | copy-start | bytes 28
  8.8 8.0 %copy-start.23 = (s32[2]{0:T(128)S(1)}, s32[2]{0:T(128)}, u32[]{:S(2)}) copy-start(s32[2]{0:T(128)} %param.26) | copy-start | bytes 28
  8.8 8.2 %copy-start = (f32[1,3840,192]{1,2,0:T(8,128)S(1)}, f32[1,3840,192]{1,2,0:T(8,128)}, u32[]{:S(2)}) copy-start(f32[1,3840,192]{1,2,0:T(8,128)} %param.28) | copy-start | bytes 8847364
  89.6 3.4 copy-start.5
  89.6 5.2 %copy-start.6 = (f32[2,4096]{1,0:T(2,128)S(1)}, f32[2,4096]{1,0:T(2,128)}, u32[]{:S(2)}) copy-start(f32[2,4096]{1,0:T(2,128)} %param.23) | copy-start | bytes 98308
  166.0 142.0 %copy-start.14 = (f32[580]{0:T(1024)S(1)}, f32[580]{0:T(1024)}, u32[]{:S(2)}) copy-start(f32[580]{0:T(1024)} %param.36) | copy-start | bytes 6964
  308.5 18.5 %copy-start.11 = (f32[1273]{0:T(1024)S(1)}, f32[1273]{0:T(1024)}, u32[]{:S(2)}) copy-start(f32[1273]{0:T(1024)} %param.37) | copy-start | bytes 15280
  308.5 19.1 %copy-start.13 = (f32[768]{0:T(1024)S(1)}, f32[768]{0:T(1024)}, u32[]{:S(2)}) copy-start(f32[768]{0:T(1024)} %param.35) | copy-start | bytes 9220
  308.6 31.5 %copy-start.2 = (f32[1273,192]{0,1:T(8,128)S(1)}, f32[1273,192]{0,1:T(8,128)}, u32[]{:S(2)}) copy-start(f32[1273,192]{0,1:T(8,128)} %param.30) | copy-start | bytes 2932996
  327.0 15.4 %copy-start.19 = (f32[1,580]{1,0:T(1,128)S(1)}, f32[1,580]{1,0:T(1,128)}, u32[]{:S(2)}) copy-start(f32[1,580]{1,0:T(1,128)} %get-tuple-element.105) | copy-start | bytes 6964
  338.7 3.7 %copy-start.18 = (f32[1,768]{1,0:T(1,128)S(1)}, f32[1,768]{1,0:T(1,128)}, u32[]{:S(2)}) copy-start(f32[1,768]{1,0:T(1,128)} %get-tuple-element.110) | copy-start | bytes 9220
  342.4 3.7 %copy-start.9 = (f32[1,3840]{1,0:T(1,128)S(1)}, f32[1,3840]{1,0:T(1,128)}, u32[]{:S(2)}) copy-start(f32[1,3840]{1,0:T(1,128)} %get-tuple-element.109) | copy-start | bytes 46084
  342.4 3.8 %copy-start.20 = (f32[1,192]{1,0:T(1,128)S(1)}, f32[1,192]{1,0:T(1,128)}, u32[]{:S(2)}) copy-start(f32[1,192]{1,0:T(1,128)} %get-tuple-element.154) | copy-start | bytes 2308
  342.4 3.8 %copy-start.1 = (f32[1,3840,192]{1,2,0:T(8,128)S(1)}, f32[1,3840,192]{1,2,0:T(8,128)}, u32[]{:S(2)}) copy-start(f32[1,3840,192]{1,2,0:T(8,128)} %param.28) | copy-start | bytes 8847364
  342.5 7.6 %copy-start.7 = (f32[580]{0:T(1024)}, f32[580]{0:T(1024)S(1)}, u32[]{:S(2)}) copy-start(f32[580]{0:T(1024)S(1)} %reduce.1) | copy-start | bytes 6964
  346.2 3.9 %copy-start.17 = (f32[1,768]{1,0:T(1,128)S(1)}, f32[1,768]{1,0:T(1,128)}, u32[]{:S(2)}) copy-start(f32[1,768]{1,0:T(1,128)} %get-tuple-element.108) | copy-start | bytes 9220
  346.2 3.9 %copy-start.10 = (f32[1,2496]{1,0:T(1,128)S(1)}, f32[1,2496]{1,0:T(1,128)}, u32[]{:S(2)}) copy-start(f32[1,2496]{1,0:T(1,128)} %get-tuple-element.152) | copy-start | bytes 29956
  350.1 9.3 %copy-start.12 = (f32[1,1273]{1,0:T(1,128)S(1)}, f32[1,1273]{1,0:T(1,128)}, u32[]{:S(2)}) copy-start(f32[1,1273]{1,0:T(1,128)} %get-tuple-element.106) | copy-start | bytes 15280
  350.1 9.9 %copy-start.16 = (f32[1,768]{1,0:T(1,128)S(1)}, f32[1,768]{1,0:T(1,128)}, u32[]{:S(2)}) copy-start(f32[1,768]{1,0:T(1,128)} %get-tuple-element.104) | copy-start | bytes 9220
  350.2 11.7 %copy-start.24 = (f32[1,128]{1,0:T(1,128)S(1)}, f32[1,128]{1,0:T(1,128)}, u32[]{:S(2)}) copy-start(f32[1,128]{1,0:T(1,128)} %get-tuple-element.95) | copy-start | bytes 1540
  350.2 11.7 %copy-start.15 = (f32[1,768]{1,0:T(1,128)S(1)}, f32[1,768]{1,0:T(1,128)}, u32[]{:S(2)}) copy-start(f32[1,768]{1,0:T(1,128)} %get-tuple-element.151) | copy-start | bytes 9220
  350.2 12.3 %copy-start.8 = (f32[1,3840]{1,0:T(1,128)S(1)}, f32[1,3840]{1,0:T(1,128)}, u32[]{:S(2)}) copy-start(f32[1,3840]{1,0:T(1,128)} %get-tuple-element.153) | copy-start | bytes 46084
  (2 other events, 4.5 us)

commit v5 on v4

--- a/solution.py
+++ b/solution.py
@@ -59,14 +59,45 @@
 MESH = pl.DeviceIdType.MESH
 LINE = 4
 PIECES = 4
+PARTS = (4, 4, 2)
+ORDER = (
+    (0, 0), (0, 1), (0, 2), (1, 0), (9, 0), (1, 1), (0, 3), (9, 1), (1, 2), (0, 4), (0, 5), (1, 3), (9, 2),
+    (2, 0), (0, 6), (1, 4), (1, 5), (0, 7), (9, 4), (2, 1), (1, 6), (3, 0), (0, 8), (1, 7), (9, 5), (2, 2),
+    (0, 9), (3, 1), (0, 10), (1, 8), (4, 0), (9, 6), (2, 4), (0, 11), (3, 2), (0, 12), (0, 13), (0, 14), (4, 1),
+    (9, 7), (2, 5), (3, 4), (6, 0), (0, 15), (9, 3), (2, 6), (2, 7), (3, 5), (4, 2), (4, 4), (9, 8), (6, 1),
+    (1, 9), (7, 0), (0, 16), (0, 17), (3, 6), (2, 3), (9, 9), (3, 7), (4, 5), (1, 10), (1, 11), (6, 2), (7, 1),
+    (8, 0), (2, 8), (9, 10), (3, 3), (5, 4), (8, 1), (4, 6), (7, 2), (2, 9), (4, 7), (3, 8), (8, 2), (9, 11),
+    (5, 5), (2, 10), (4, 3), (3, 9), (6, 4), (5, 6), (5, 7), (3, 10), (2, 11), (4, 8), (6, 5), (6, 3), (7, 4),
+    (6, 6), (4, 9), (3, 11), (8, 4), (6, 7), (4, 10), (6, 8), (7, 5), (6, 9), (7, 3), (8, 5), (4, 11), (8, 3),
+    (5, 10), (7, 6), (8, 6), (5, 11), (7, 7), (6, 10), (7, 8), (8, 7), (7, 9), (6, 11), (8, 8), (8, 9), (7, 10),
+    (8, 10), (7, 11), (8, 11),
+)
+BESIDE_AT = (44, 54, 65, 76, 87, 97, 108)
+SLOTS = 3
+NN = (((1,), (0,)), ((), ()))
+NT = (((1,), (1,)), ((), ()))
+TN = (((0,), (0,)), ((), ()))
+
+
+def mxu(left, right, kind):
+    return lax.dot_general(left, right, kind, preferred_element_type=jnp.float32)
+
+
+def blocks_of(total, size, body):
+    def step(index, carry):
+        body(pl.ds(pl.multiple_of(index * size, size), size))
+        return carry
+
+    lax.fori_loop(0, total // size, step, 0)
 
 
 def heavy_chunks(width):
-    half, third = width // 2, width // 3
-    parts = [(0, 0, width, 2 * third * k, third, False) for k in range(6)]
-    parts += [(1, 2 * third * k, 2 * third, 0, half, True) for k in range(6)]
+    half = width // 2
+    fc2, fc1, kv = PARTS
+    parts = [(0, 0, width, 4 * width // fc2 * k, 2 * width // fc2, False) for k in range(fc2)]
+    parts += [(1, 4 * width // fc1 * k, 4 * width // fc1, 0, half, True) for k in range(fc1)]
     parts += [(2, 0, width, 0, half, False), (3, 0, width, 0, half, False)]
-    parts += [(3, width + 2 * third * k, 2 * third, 0, half, True) for k in range(3)]
+    parts += [(3, width + 2 * width // kv * k, 2 * width // kv, 0, half, True) for k in range(kv)]
     return tuple(parts)
 
 
@@ -81,19 +112,24 @@
     lax.fori_loop(0, rows // block, body, 0)
 
 
-def reduce_kernel(lines, chunks, tables, *refs):
+def step_kernel(lines, chunks, tables, *refs):
     count = len(chunks)
-    grads, refs = refs[:4], refs[4:]
-    (d_mod, d_fm, few, in_t, head_t, cond_full, time_one), refs = refs[:7], refs[7:]
+    heavy, refs = refs[:4], refs[4:]
+    (in_far, state, target, weight_t, pos, patch, last, modul, fmod, head_t, cond_full, time_one), refs = refs[:12], refs[12:]
     finals, refs = refs[:4], refs[4:]
     (d_in, d_head, d_two, d_full, d_one, few_sum), scratch = refs[:6], refs[6:]
-    by_core, by_y, by_x, by_z = (scratch[k * count : (k + 1) * count] for k in range(4))
+    held, by_y, by_x, by_z = (scratch[k * count : (k + 1) * count] for k in range(4))
     send, recv, zsend, zrecv, wsend, wrecv = scratch[4 * count : 4 * count + 6]
+    scratch = scratch[4 * count + 6 :]
+    (stage_wide, stage_tall, land_wide, land_tall, free_wide, free_tall, fetch, d_mod, d_fm, few), scratch = scratch[:10], scratch[10:]
+    (
+        stream, hat_one, hat_two, root_one, root_two, a_low, qkv_low, mixed, proj, b_low, active, mlp, d_mlp,
+    ), scratch = scratch[:13], scratch[13:]
     (
         few_got, few_y, few_x, few_held, few_line, mod_got, fm_got, mod_sum, fm_sum, group_slot, part_own, part_slot,
         act_own, act_slot, pair_own, pair_got, line_in, line_rest, line_full,
         few_send, few_recv, group_send, group_recv, line_send, line_recv,
-    ) = scratch[4 * count + 6 :]
+    ) = scratch
     (in_starts, in_tiles), (head_starts, head_tiles), (embed_starts, embed_tiles), shards = tables
     rep, shard = lax.axis_index("rep"), lax.axis_index("shard")
     place_here = lax.rem(rep, 2 * lines)
@@ -117,11 +153,15 @@
         )
     pl.semaphore_wait(barrier, 4 + lines - 1)
 
+    width, tokens = head_t.shape[1], state.shape[0]
+    in_blocks = [active.at[:, pl.ds(k * width, width)] for k in range(4)] + [d_mlp]
+
+    def far_copy(k):
+        return pltpu.make_async_copy(in_far.at[pl.ds(k * tokens, tokens), :], in_blocks[k], fetch.at[4 + k])
+
     stride = lines // PIECES
     owns = lax.rem(z, stride) == 0
     mine = lax.div(z, stride)
-    sends = []
-
     def remote(source, target, send_sem, recv_sem, peer):
         return pltpu.make_async_remote_copy(
             src_ref=source,
@@ -141,16 +181,31 @@
             pl.ds(pl.multiple_of(row, 16), rows), pl.ds(pl.multiple_of(lane + which * lanes, 128), lanes)
         ]
 
+    turn = {i: sum(chunks[j][0] == 0 for j in range(i)) if chunks[i][0] == 0 else sum(chunks[j][0] != 0 for j in range(i)) for i in range(count)}
+
+    def slot_of(i, wide, tall):
+        if chunks[i][0] == 0:
+            return wide.at[turn[i] % SLOTS]
+        return tall.at[turn[i] % SLOTS, pl.ds(0, chunks[i][2])]
+
+    def turn_away(i, steps):
+        for j in range(count):
+            if (chunks[j][0] == 0) == (chunks[i][0] == 0) and turn[j] == turn[i] + steps:
+                return j
+        return None
+
     def core_copy(i):
-        array, row, rows = chunks[i][:3]
         return remote(
-            lanes_at(i, grads[array], row, rows, 1 - core), by_core[i], send.at[i, 0], recv.at[i, 0], to_core
+            slot_of(i, stage_wide, stage_tall), slot_of(i, land_wide, land_tall), send.at[i, 0], recv.at[i, 0], to_core
         )
+
+    def free_of(i):
+        return free_wide if chunks[i][0] == 0 else free_tall
 
     def y_copy(i):
         half = chunks[i][2] // 2
         return remote(
-            rows_of(by_core[i], (1 - y) * half, half), by_y[i], send.at[i, 1], recv.at[i, 1], to_y
+            rows_of(held[i], (1 - y) * half, half), by_y[i], send.at[i, 1], recv.at[i, 1], to_y
         )
 
     def x_copy(i):
@@ -176,8 +231,8 @@
         return lanes_at(i, finals[array], row + side * (rows // 2) + start, size, which)
 
     def cross_copy(i):
-        size = chunks[i][2] // 4 // PIECES
-        part = final_rows(i, 0, (x * PIECES + mine) * size, size, core)
+        quarter = chunks[i][2] // 4
+        part = final_rows(i, 0, x * quarter, quarter, core)
         return remote(part, part, send.at[i, 3], recv.at[i, 3], to_y)
 
     def line_copy(i, which, side, step):
@@ -213,19 +268,34 @@
         else:
             action(0, y)
 
-    def stage0(i):
+    def produce(i, left, right):
+        rows, lanes = chunks[i][2], chunks[i][4]
+        before, after = turn_away(i, -SLOTS), turn_away(i, SLOTS)
+        if before is not None:
+            core_copy(before).wait_send()
+        staged = slot_of(i, stage_wide, stage_tall)
+
+        def block(part):
+            value = mxu(left[:, part], right[...], TN)
+            first, second = value[:, :lanes], value[:, lanes:]
+            held[i][part, :] = jnp.where(core == 0, first, second).astype(jnp.bfloat16)
+            staged[part, :] = jnp.where(core == 0, second, first).astype(jnp.bfloat16)
+
+        blocks_of(rows, 256, block)
+        if before is not None:
+            pl.semaphore_wait(free_of(i), 1)
         core_copy(i).start()
 
     def stage1(i):
-        array, row, rows = chunks[i][:3]
         core_copy(i).wait_recv()
-        add_rows(by_core[i], by_core[i], lanes_at(i, grads[array], row, rows, core), rows)
-        y_copy(i).start()
+        add_rows(held[i], held[i], slot_of(i, land_wide, land_tall), chunks[i][2])
+        if turn_away(i, SLOTS) is not None:
+            pl.semaphore_signal(free_of(i), inc=1, device_id=to_core, device_id_type=MESH)
 
     def stage2(i):
         half = chunks[i][2] // 2
         y_copy(i).wait_recv()
-        add_rows(by_y[i], by_y[i], rows_of(by_core[i], y * half, half), half)
+        add_rows(by_y[i], by_y[i], rows_of(held[i], y * half, half), half)
         x_copy(i).start()
 
     def stage3(i):
@@ -259,40 +329,35 @@
                 return carry
 
             lax.fori_loop(0, size // 16, body, 0)
-            if chunks[i][5]:
-
-                @pl.when(y == 0)
-                def _():
-                    cross_copy(i).start()
-
-                @pl.when(y == 1)
-                def _():
-                    for step in range(1, lines):
-                        line_copy(i, 0, 1, step).start()
-            else:
-                for step in range(1, lines):
-                    line_copy(i, 0, y, step).start()
+            for step in range(1, lines):
+                line_copy(i, 0, y, step).start()
+
+    def line_wait(i):
+        for piece in range(PIECES):
+
+            @pl.when(z != piece * stride)
+            def _():
+                line_arrival(i, 0, y, piece).wait_recv()
 
     def stage5(i):
+        @pl.when(y == 0)
+        def _():
+            line_wait(i)
+            cross_copy(i).start()
+
+    def stage6(i):
         if chunks[i][5]:
 
-            @pl.when(jnp.logical_and(owns, y == 1))
+            @pl.when(y == 1)
             def _():
+                line_wait(i)
+                pair_copy(i, 0, 1, x).start()
                 cross_copy(i).wait_recv()
-                for step in range(1, lines):
-                    line_copy(i, 1, 0, step).start()
-
-    def stage6(i):
-        def action(which, side):
-            for piece in range(PIECES):
-
-                @pl.when(z != piece * stride)
-                def _():
-                    line_arrival(i, which, side, piece).wait_recv()
-
-            pair_copy(i, which, side, x).start()
-
-        sides(i, action)
+                pair_copy(i, 1, 0, x).start()
+
+        else:
+            line_wait(i)
+            pair_copy(i, 0, y, x).start()
 
     def stage7(i):
         def action(which, side):
@@ -305,7 +370,6 @@
         sides(i, lambda which, side: last_copy(i, which, side, 1 - core).wait_recv())
 
 
-    width = in_t.shape[1]
     mod_tiles, wide = 6 * width // 128, width // 128
     images = d_mod.shape[0]
     in_lanes, head_lanes, embed_lanes = in_tiles * 128, head_tiles * 128, embed_tiles * 128
@@ -430,9 +494,10 @@
 
         @pl.when(is_in(shard, mod_places))
         def _():
-            part_own[...] += jnp.dot(
-                pair_own[:, :in_lanes].astype(jnp.bfloat16), in_t[...], preferred_element_type=jnp.float32
-            )
+            for k in range(len(in_blocks)):
+                far_copy(k).wait()
+                lanes = pair_own[:, k * tokens : (k + 1) * tokens].astype(jnp.bfloat16)
+                part_own[...] += jnp.dot(lanes, in_blocks[k][...], preferred_element_type=jnp.float32)
 
         part_slot[shard] = part_own[...]
         for step in range(1, shards):
@@ -543,18 +608,223 @@
                 to_others(3, act_own, act_slot, step).wait_send()
 
     beside = (side0, side1, side2, side3, side4, side5, side6)
-    beside_at = (12, 14, 16, 18, 20, 22, 24)
-    stages = (stage0, stage1, stage2, stage3, stage4, stage5, stage6, stage7, stage8)
-    for tick in range(count + len(stages) - 1):
-        if tick in beside_at:
-            beside[beside_at.index(tick)]()
-        for k, stage in enumerate(stages):
-            if 0 <= tick - k < count:
-                stage(tick - k)
+    low = jnp.bfloat16
+    per = tokens // TOK
+    row = [shard * per + image for image in range(per)]
+    span = [pl.ds(image * TOK, TOK) for image in range(per)]
+    cut = 256
+
+    def piece(ref, image, index):
+        return ref[pl.ds(row[image], 1), pl.ds(index * width, width)]
+
+    def normed(value):
+        center = value - jnp.mean(value, -1, keepdims=True)
+        root = lax.rsqrt(jnp.mean(center * center, -1, keepdims=True) + eps_norm)
+        return center * root, root
+
+    def norm_back(d_hat, hat, root):
+        return root * (d_hat - jnp.mean(d_hat, -1, keepdims=True) - hat * jnp.mean(d_hat * hat, -1, keepdims=True))
+
+    def put_row(ref, image, index, value):
+        ref[pl.ds(row[image], 1), pl.ds(index * width, width)] = (
+            jnp.sum(value, 0, keepdims=True).astype(low).astype(jnp.float32)
+        )
+
+    fc2, fc1, attn_out, qkv = finals
+
+    def load(k):
+        return pltpu.make_async_copy(heavy[k], finals[k], fetch.at[k])
+
+    for k in (3, 2, 1, 0):
+        load(k).start()
+    d_mod[...] = jnp.zeros_like(d_mod)
+    d_fm[...] = jnp.zeros_like(d_fm)
+
+    for image in range(per):
+        value = mxu(state[span[image], :], patch[...], NN) + pos[...]
+        stream[span[image], :] = value
+        hat, root = normed(value)
+        hat_one[span[image], :] = hat
+        root_one[span[image], :] = root
+        a_low[span[image], :] = (hat * (1.0 + piece(modul, image, 1)) + piece(modul, image, 0)).astype(low)
+
+    def qkv_block(part):
+        qkv_low[:, part] = mxu(a_low[...], qkv[part, :], NT).astype(low)
+
+    load(3).wait()
+    blocks_of(3 * width, cut, qkv_block)
+    load(2).wait()
+    lane = lax.broadcasted_iota(jnp.int32, (TOK, 128), 1)
+    first = lane < 64
+    scale = 0.125
+
+    def softmax(query, key):
+        score = mxu(query, key, NT) * scale
+        expo = jnp.exp(score - jnp.max(score, -1, keepdims=True))
+        return expo / jnp.sum(expo, -1, keepdims=True)
+
+    def take(ref, image, start):
+        return ref[span[image], pl.ds(pl.multiple_of(start, 128), 128)]
+
+    def attend(pair, carry):
+        for image in range(per):
+            query, key, value = (take(qkv_low, image, index * width + pair * 128) for index in range(3))
+            outs = []
+            for side in (first, jnp.logical_not(first)):
+                probs = softmax(jnp.where(side, query, jnp.zeros_like(query)), key)
+                outs.append(mxu(probs.astype(low), value, NN))
+            mixed[span[image], pl.ds(pl.multiple_of(pair * 128, 128), 128)] = jnp.where(first, outs[0], outs[1]).astype(low)
+        return carry
+
+    lax.fori_loop(0, width // 128, attend, 0)
+    for image in range(per):
+        got = mxu(mixed[span[image], :], attn_out[...], NT)
+        proj[span[image], :] = got
+        value = stream[span[image], :] + piece(modul, image, 2) * got
+        stream[span[image], :] = value
+        hat, root = normed(value)
+        hat_two[span[image], :] = hat
+        root_two[span[image], :] = root
+        b_low[span[image], :] = (hat * (1.0 + piece(modul, image, 4)) + piece(modul, image, 3)).astype(low)
+
+    def upper_block(part):
+        value = mxu(b_low[...], fc1[part, :], NT)
+        active[:, part] = (
+            0.5 * value * (1.0 + jnp.tanh(0.7978845608 * (value + 0.044715 * value * value * value)))
+        ).astype(low)
+
+    load(1).wait()
+    blocks_of(4 * width, cut, upper_block)
+    load(0).wait()
+
+    def mlp_block(part):
+        mlp[:, part] = mxu(active[...], fc2[part, :], NT)
+
+    blocks_of(width, cut, mlp_block)
+    loss = jnp.zeros((), jnp.float32)
+    g_last = jnp.zeros((PATCH, width), jnp.float32)
+    for image in range(per):
+        value = stream[span[image], :] + piece(modul, image, 5) * mlp[span[image], :]
+        hat, root = normed(value)
+        gain = 1.0 + piece(fmod, image, 1)
+        final = (hat * gain + piece(fmod, image, 0)).astype(low)
+        diff = mxu(final, last[...], NT) - target[span[image], :]
+        share = weight_t[span[image], :] * diff
+        loss += 0.5 * jnp.sum(share * diff)
+        d_out = share.astype(low)
+        g_last += mxu(d_out, final, TN)
+        d_final = mxu(d_out, last[...], NN)
+        put_row(d_fm, image, 0, d_final)
+        put_row(d_fm, image, 1, d_final * hat)
+        d_value = norm_back(d_final * gain, hat, root)
+        stream[span[image], :] = d_value
+        put_row(d_mod, image, 5, d_value * mlp[span[image], :])
+        d_mlp[span[image], :] = (piece(modul, image, 5) * d_value).astype(low)
+    few[pl.ds(PATCH, 8), :] = jnp.full((8, width), loss, jnp.float32)
+    few[pl.ds(PATCH + 8, PATCH), :] = g_last
+    few[pl.ds(2 * PATCH + 8, 8), :] = jnp.zeros((8, width), jnp.float32)
+
+    of_fc2 = [i for i in range(count) if chunks[i][0] == 0]
+    of_fc1 = [i for i in range(count) if chunks[i][0] == 1]
+    of_o = [i for i in range(count) if chunks[i][0] == 2]
+    of_qkv = [i for i in range(count) if chunks[i][0] == 3]
+
+    def fc2_step(i):
+        first, lanes = chunks[i][3], 2 * chunks[i][4]
+        part = pl.ds(first, lanes)
+        value = mxu(b_low[...], fc1[part, :], NT)
+        inner = jnp.tanh(0.7978845608 * (value + 0.044715 * value * value * value))
+        slope = 0.5 * (1.0 + inner) + 0.5 * value * (1.0 - inner * inner) * 0.7978845608 * (
+            1.0 + 3.0 * 0.044715 * value * value
+        )
+        d_upper = (slope * mxu(d_mlp[...], fc2[:, part], NN)).astype(low)
+        produce(i, d_mlp, active.at[:, part])
+        active[:, part] = d_upper
+
+    def fc1_step(i):
+        part = pl.ds(chunks[i][1], chunks[i][2])
+        more = mxu(active[:, part], fc1[part, :], NN)
+        if i == of_fc1[0]:
+            mlp[...] = more
+        else:
+            mlp[...] += more
+        produce(i, active.at[:, part], b_low)
+
+    def o_step(i):
+        for image in range(per):
+            d_normed = mlp[span[image], :]
+            hat = hat_two[span[image], :]
+            put_row(d_mod, image, 3, d_normed)
+            put_row(d_mod, image, 4, d_normed * hat)
+            d_value = stream[span[image], :] + norm_back(
+                d_normed * (1.0 + piece(modul, image, 4)), hat, root_two[span[image], :]
+            )
+            stream[span[image], :] = d_value
+            put_row(d_mod, image, 2, d_value * proj[span[image], :])
+            b_low[span[image], :] = (piece(modul, image, 2) * d_value).astype(low)
+        active[:, pl.ds(0, width)] = mxu(b_low[...], attn_out[...], NN).astype(low)
+        produce(i, b_low, mixed)
+
+    def attend_back(pair):
+        for image in range(per):
+            query, key, value = (take(qkv_low, image, index * width + pair * 128) for index in range(3))
+            d_out = take(active, image, pair * 128)
+            d_query, d_key, d_value = [], [], []
+            for side in (first, jnp.logical_not(first)):
+                none = jnp.zeros_like(query)
+                probs = softmax(jnp.where(side, query, none), key)
+                d_prob = mxu(jnp.where(side, d_out, none), value, NT)
+                d_score = (probs * (d_prob - jnp.sum(probs * d_prob, -1, keepdims=True))).astype(low)
+                d_value.append(mxu(probs.astype(low), d_out, TN))
+                d_query.append(mxu(d_score, key, NN) * scale)
+                d_key.append(mxu(d_score, query, TN) * scale)
+            for index, both in enumerate((d_query, d_key, d_value)):
+                qkv_low[span[image], pl.ds(pl.multiple_of(index * width + pair * 128, 128), 128)] = jnp.where(
+                    first, both[0], both[1]
+                ).astype(low)
+
+    def norm_one_step():
+        @pl.when(is_in(shard, mod_places))
+        def _():
+            for k in range(len(in_blocks)):
+                far_copy(k).start()
+
+        g_patch = jnp.zeros((PATCH, width), jnp.float32)
+        for image in range(per):
+            d_normed = mxu(qkv_low[span[image], :], qkv[...], NN)
+            hat = hat_one[span[image], :]
+            put_row(d_mod, image, 0, d_normed)
+            put_row(d_mod, image, 1, d_normed * hat)
+            d_value = stream[span[image], :] + norm_back(
+                d_normed * (1.0 + piece(modul, image, 1)), hat, root_one[span[image], :]
+            )
+            g_patch += mxu(state[span[image], :], d_value.astype(low), TN)
+        few[pl.ds(0, PATCH), :] = g_patch
+
+    def qkv_step(i):
+        if i == of_qkv[0]:
+            norm_one_step()
+        produce(i, qkv_low.at[:, pl.ds(chunks[i][1], chunks[i][2])], a_low)
+
+    def over_y(i):
+        y_copy(i).start()
+
+    stages = (None, stage1, stage2, stage3, stage4, stage5, stage6, stage7, stage8, over_y)
+    steps = [(fc2_step, i) for i in of_fc2] + [(fc1_step, i) for i in of_fc1] + [(o_step, i) for i in of_o]
+    steps += [(attend_back, pair) for pair in range(width // 128)] + [(qkv_step, i) for i in of_qkv]
+    for j, (k, i) in enumerate(ORDER):
+        if j in BESIDE_AT:
+            beside[BESIDE_AT.index(j)]()
+        if k == 0:
+            step, arg = steps[i]
+            step(arg)
+        else:
+            stages[k](i)
 
     side_end()
     for i in range(count):
-        core_copy(i).wait_send()
+        if turn_away(i, SLOTS) is None:
+            core_copy(i).wait_send()
         y_copy(i).wait_send()
         x_copy(i).wait_send()
         for piece in range(PIECES):
@@ -565,43 +835,61 @@
 
         if chunks[i][5]:
 
-            @pl.when(jnp.logical_and(owns, y == 0))
+            @pl.when(y == 0)
             def _():
                 cross_copy(i).wait_send()
 
+        @pl.when(owns)
+        def _():
+            for step in range(1, lines):
+                line_copy(i, 0, y, step).wait_send()
+
         def action(which, side):
-            @pl.when(owns)
-            def _():
-                for step in range(1, lines):
-                    line_copy(i, which, side, step).wait_send()
-
             pair_copy(i, which, side, x).wait_send()
             last_copy(i, which, side, core).wait_send()
 
         sides(i, action)
 
 
-def reduce_call(lines, tables, heavy, light):
+def step_call(lines, tables, images, heavy, in_t, light):
     width = heavy[2].shape[0]
     chunks = heavy_chunks(width)
     count = len(chunks)
     low, full = jnp.bfloat16, jnp.float32
     (_, in_tiles), (_, head_tiles), (_, embed_tiles), shards = tables
-    few, cond_full = light[2], light[5]
-    group, rows = light[0].shape[0], cond_full.shape[0]
+    state, modul, fmod, cond_full = light[0], light[6], light[7], light[9]
+    tokens, group, rows = state.shape[0], modul.shape[0], cond_full.shape[0]
     in_lanes, head_lanes, embed_lanes = in_tiles * 128, head_tiles * 128, embed_tiles * 128
     rest_lanes = 2 * head_lanes + embed_lanes
-    few_half = (few.shape[0] // 2, width)
+    few = (2 * PATCH + 16, width)
+    few_half = (few[0] // 2, width)
     pair = (group, in_lanes + rest_lanes + embed_lanes)
     sizes = [(part_rows, part_lanes) for _, _, part_rows, _, part_lanes, _ in chunks]
+    wide = [item for item, chunk in zip(sizes, chunks) if chunk[0] == 0][0]
+    tall = max(item for item, chunk in zip(sizes, chunks) if chunk[0] != 0)
     dma = pltpu.SemaphoreType.DMA
     shapes = [(item.shape, low) for item in heavy] + [
-        ((rows, in_tiles * 128), low),
-        ((rows, head_tiles * 128), low),
-        ((rows, head_tiles * 128), low),
+        ((rows, in_lanes), low),
+        ((rows, head_lanes), low),
+        ((rows, head_lanes), low),
         ((rows, embed_lanes), full),
         ((rows, embed_lanes), low),
-        (few.shape, full),
+        (few, full),
+    ]
+    pass_scratch = [
+        ((tokens, width), full),
+        ((tokens, width), full),
+        ((tokens, width), full),
+        ((tokens, 1), full),
+        ((tokens, 1), full),
+        ((tokens, width), low),
+        ((tokens, 3 * width), low),
+        ((tokens, width), low),
+        ((tokens, width), full),
+        ((tokens, width), low),
+        ((tokens, 4 * width), low),
+        ((tokens, width), full),
+        ((tokens, width), low),
     ]
     scratch = [
         (few_half, full),
@@ -609,10 +897,10 @@
         (few_half, full),
         ((2,) + few_half, full),
         ((lines,) + few_half, full),
-        (light[0].shape, full),
-        (light[1].shape, full),
-        (light[0].shape, full),
-        (light[1].shape, full),
+        (modul.shape, full),
+        (fmod.shape, full),
+        (modul.shape, full),
+        (fmod.shape, full),
         ((group, in_lanes + head_lanes), full),
         ((group, width), full),
         ((shards, group, width), full),
@@ -624,11 +912,12 @@
         ((lines, 2 * group, rest_lanes), low),
         ((lines, 2 * group, embed_lanes), full),
     ]
+    vmem, anywhere = pl.BlockSpec(memory_space=pltpu.VMEM), pl.BlockSpec(memory_space=pl.ANY)
     return pl.pallas_call(
-        functools.partial(reduce_kernel, lines, chunks, tables),
+        functools.partial(step_kernel, lines, chunks, tables),
         out_shape=[jax.ShapeDtypeStruct(*item) for item in shapes],
-        in_specs=[pl.BlockSpec(memory_space=pltpu.VMEM)] * (4 + len(light)),
-        out_specs=[pl.BlockSpec(memory_space=pltpu.VMEM)] * len(shapes),
+        in_specs=[anywhere] * 5 + [vmem] * len(light),
+        out_specs=[vmem] * len(shapes),
         scratch_shapes=[pltpu.VMEM((r, c), low) for r, c in sizes]
         + [pltpu.VMEM((r // 2, c), low) for r, c in sizes]
         + [pltpu.VMEM((r // 4, c), low) for r, c in sizes]
@@ -641,6 +930,10 @@
             dma((count, 2, lines - 1)),
             dma((count, 2, PIECES)),
         ]
+        + [pltpu.VMEM((SLOTS,) + item, low) for item in (wide, tall)] * 2
+        + [pltpu.SemaphoreType.REGULAR, pltpu.SemaphoreType.REGULAR, dma((9,))]
+        + [pltpu.VMEM(*item) for item in ((modul.shape, full), (fmod.shape, full), (few, full))]
+        + [pltpu.VMEM(*item) for item in pass_scratch]
         + [pltpu.VMEM(*item) for item in scratch]
         + [
             dma((lines + 6,)),
@@ -651,9 +944,9 @@
             dma((3, lines - 1)),
         ],
         compiler_params=pltpu.CompilerParams(
-            collective_id=1, has_side_effects=True, vmem_limit_bytes=63 * 1024 * 1024
+            collective_id=1, has_side_effects=True, vmem_limit_bytes=64 * 1024 * 1024 - 65536
         ),
-    )(*heavy, *light)
+    )(*heavy, in_t, *light)
 
 
 def placed_traits(traits, lanes):
@@ -1090,249 +1383,6 @@
     return in_t, head_t, outs
 
 
-NN = (((1,), (0,)), ((), ()))
-NT = (((1,), (1,)), ((), ()))
-TN = (((0,), (0,)), ((), ()))
-
-
-def mxu(left, right, kind):
-    return lax.dot_general(left, right, kind, preferred_element_type=jnp.float32)
-
-
-def blocks_of(total, size, body):
-    def step(index, carry):
-        body(pl.ds(pl.multiple_of(index * size, size), size))
-        return carry
-
-    lax.fori_loop(0, total // size, step, 0)
-
-
-def pass_kernel(
-    images, state, target, weight_t, pos, patch, last, modul, fmod, fc2, fc1, attn_out, qkv,
-    g_fc2, g_fc1, g_o, g_qkv, few, d_mod, d_fm,
-    stream, hat_one, hat_two, root_one, root_two, a_low, qkv_low, mixed, proj, b_low, upper, active, mlp, back, d_qkv,
-):
-    width = patch.shape[1]
-    tokens = images * TOK
-    low = jnp.bfloat16
-    shard = lax.axis_index("shard")
-    row = [shard * images + image for image in range(images)]
-    span = [pl.ds(image * TOK, TOK) for image in range(images)]
-    cut = 256
-
-    def piece(ref, image, index):
-        return ref[pl.ds(row[image], 1), pl.ds(index * width, width)]
-
-    def normed(value):
-        center = value - jnp.mean(value, -1, keepdims=True)
-        root = lax.rsqrt(jnp.mean(center * center, -1, keepdims=True) + eps_norm)
-        return center * root, root
-
-    def norm_back(d_hat, hat, root):
-        return root * (d_hat - jnp.mean(d_hat, -1, keepdims=True) - hat * jnp.mean(d_hat * hat, -1, keepdims=True))
-
-    def put_row(ref, image, index, value):
-        ref[pl.ds(row[image], 1), pl.ds(index * width, width)] = (
-            jnp.sum(value, 0, keepdims=True).astype(low).astype(jnp.float32)
-        )
-
-    d_mod[...] = jnp.zeros_like(d_mod)
-    d_fm[...] = jnp.zeros_like(d_fm)
-
-    for image in range(images):
-        value = mxu(state[span[image], :], patch[...], NN) + pos[...]
-        stream[span[image], :] = value
-        hat, root = normed(value)
-        hat_one[span[image], :] = hat
-        root_one[span[image], :] = root
-        a_low[span[image], :] = (hat * (1.0 + piece(modul, image, 1)) + piece(modul, image, 0)).astype(low)
-
-    def qkv_block(part):
-        qkv_low[:, part] = mxu(a_low[...], qkv[part, :], NT).astype(low)
-
-    blocks_of(3 * width, cut, qkv_block)
-    lane = lax.broadcasted_iota(jnp.int32, (TOK, 128), 1)
-    first = lane < 64
-    scale = 0.125
-
-    def softmax(query, key):
-        score = mxu(query, key, NT) * scale
-        expo = jnp.exp(score - jnp.max(score, -1, keepdims=True))
-        return expo / jnp.sum(expo, -1, keepdims=True)
-
-    def take(ref, image, start):
-        return ref[span[image], pl.ds(pl.multiple_of(start, 128), 128)]
-
-    def attend(pair, carry):
-        for image in range(images):
-            query, key, value = (take(qkv_low, image, index * width + pair * 128) for index in range(3))
-            outs = []
-            for side in (first, jnp.logical_not(first)):
-                probs = softmax(jnp.where(side, query, jnp.zeros_like(query)), key)
-                outs.append(mxu(probs.astype(low), value, NN))
-            mixed[span[image], pl.ds(pl.multiple_of(pair * 128, 128), 128)] = jnp.where(first, outs[0], outs[1]).astype(low)
-        return carry
-
-    lax.fori_loop(0, width // 128, attend, 0)
-    for image in range(images):
-        got = mxu(mixed[span[image], :], attn_out[...], NT)
-        proj[span[image], :] = got
-        value = stream[span[image], :] + piece(modul, image, 2) * got
-        stream[span[image], :] = value
-        hat, root = normed(value)
-        hat_two[span[image], :] = hat
-        root_two[span[image], :] = root
-        b_low[span[image], :] = (hat * (1.0 + piece(modul, image, 4)) + piece(modul, image, 3)).astype(low)
-
-    def upper_block(part):
-        value = mxu(b_low[...], fc1[part, :], NT)
-        upper[:, part] = value
-        active[:, part] = (
-            0.5 * value * (1.0 + jnp.tanh(0.7978845608 * (value + 0.044715 * value * value * value)))
-        ).astype(low)
-
-    blocks_of(4 * width, cut, upper_block)
-
-    def mlp_block(part):
-        mlp[:, part] = mxu(active[...], fc2[part, :], NT)
-
-    blocks_of(width, cut, mlp_block)
-    loss = jnp.zeros((), jnp.float32)
-    g_last = jnp.zeros((PATCH, width), jnp.float32)
-    for image in range(images):
-        value = stream[span[image], :] + piece(modul, image, 5) * mlp[span[image], :]
-        hat, root = normed(value)
-        gain = 1.0 + piece(fmod, image, 1)
-        final = (hat * gain + piece(fmod, image, 0)).astype(low)
-        diff = mxu(final, last[...], NT) - target[span[image], :]
-        share = weight_t[span[image], :] * diff
-        loss += 0.5 * jnp.sum(share * diff)
-        d_out = share.astype(low)
-        g_last += mxu(d_out, final, TN)
-        d_final = mxu(d_out, last[...], NN)
-        put_row(d_fm, image, 0, d_final)
-        put_row(d_fm, image, 1, d_final * hat)
-        d_value = norm_back(d_final * gain, hat, root)
-        back[span[image], :] = d_value
-        put_row(d_mod, image, 5, d_value * mlp[span[image], :])
-        d_qkv[span[image], pl.ds(0, width)] = (piece(modul, image, 5) * d_value).astype(low)
-    few[pl.ds(PATCH, 8), :] = jnp.full((8, width), loss, jnp.float32)
-    few[pl.ds(PATCH + 8, PATCH), :] = g_last
-    few[pl.ds(2 * PATCH + 8, 8), :] = jnp.zeros((8, width), jnp.float32)
-
-    d_mlp = d_qkv.at[:, pl.ds(0, width)]
-
-    def fc2_block(part):
-        g_fc2[:, part] = mxu(d_mlp[...], active[:, part], TN).astype(low)
-        value = upper[:, part]
-        inner = jnp.tanh(0.7978845608 * (value + 0.044715 * value * value * value))
-        slope = 0.5 * (1.0 + inner) + 0.5 * value * (1.0 - inner * inner) * 0.7978845608 * (
-            1.0 + 3.0 * 0.044715 * value * value
-        )
-        active[:, part] = (slope * mxu(d_mlp[...], fc2[:, part], NN)).astype(low)
-
-    blocks_of(4 * width, cut, fc2_block)
-
-    def fc1_block(part):
-        g_fc1[part, :] = mxu(active[:, part], b_low[...], TN).astype(low)
-
-    blocks_of(4 * width, cut, fc1_block)
-    for image in range(images):
-        d_normed = mxu(active[span[image], :], fc1[...], NN)
-        hat = hat_two[span[image], :]
-        put_row(d_mod, image, 3, d_normed)
-        put_row(d_mod, image, 4, d_normed * hat)
-        d_value = back[span[image], :] + norm_back(
-            d_normed * (1.0 + piece(modul, image, 4)), hat, root_two[span[image], :]
-        )
-        back[span[image], :] = d_value
-        put_row(d_mod, image, 2, d_value * proj[span[image], :])
-        b_low[span[image], :] = (piece(modul, image, 2) * d_value).astype(low)
-
-    def o_block(part):
-        g_o[part, :] = mxu(b_low[:, part], mixed[...], TN).astype(low)
-
-    blocks_of(width, cut, o_block)
-    d_mixed = active.at[:, pl.ds(0, width)]
-    d_mixed[...] = mxu(b_low[...], attn_out[...], NN).astype(low)
-
-    def attend_back(pair, carry):
-        for image in range(images):
-            query, key, value = (take(qkv_low, image, index * width + pair * 128) for index in range(3))
-            d_out = take(active, image, pair * 128)
-            d_query, d_key, d_value = [], [], []
-            for side in (first, jnp.logical_not(first)):
-                none = jnp.zeros_like(query)
-                probs = softmax(jnp.where(side, query, none), key)
-                d_prob = mxu(jnp.where(side, d_out, none), value, NT)
-                d_score = (probs * (d_prob - jnp.sum(probs * d_prob, -1, keepdims=True))).astype(low)
-                d_value.append(mxu(probs.astype(low), d_out, TN))
-                d_query.append(mxu(d_score, key, NN) * scale)
-                d_key.append(mxu(d_score, query, TN) * scale)
-            for index, both in enumerate((d_query, d_key, d_value)):
-                d_qkv[span[image], pl.ds(pl.multiple_of(index * width + pair * 128, 128), 128)] = jnp.where(
-                    first, both[0], both[1]
-                ).astype(low)
-        return carry
-
-    lax.fori_loop(0, width // 128, attend_back, 0)
-
-    def g_qkv_block(part):
-        g_qkv[part, :] = mxu(d_qkv[:, part], a_low[...], TN).astype(low)
-
-    blocks_of(3 * width, cut, g_qkv_block)
-    g_patch = jnp.zeros((PATCH, width), jnp.float32)
-    for image in range(images):
-        d_normed = mxu(d_qkv[span[image], :], qkv[...], NN)
-        hat = hat_one[span[image], :]
-        put_row(d_mod, image, 0, d_normed)
-        put_row(d_mod, image, 1, d_normed * hat)
-        d_value = back[span[image], :] + norm_back(
-            d_normed * (1.0 + piece(modul, image, 1)), hat, root_one[span[image], :]
-        )
-        g_patch += mxu(state[span[image], :], d_value.astype(low), TN)
-    few[pl.ds(0, PATCH), :] = g_patch
-
-
-def pass_scratch(tokens, width):
-    low, full = jnp.bfloat16, jnp.float32
-    return [
-        ((tokens, width), full),
-        ((tokens, width), full),
-        ((tokens, width), full),
-        ((tokens, 1), full),
-        ((tokens, 1), full),
-        ((tokens, width), low),
-        ((tokens, 3 * width), low),
-        ((tokens, width), low),
-        ((tokens, width), full),
-        ((tokens, width), low),
-        ((tokens, 4 * width), full),
-        ((tokens, 4 * width), low),
-        ((tokens, width), full),
-        ((tokens, width), full),
-        ((tokens, 3 * width), low),
-    ]
-
-
-def pass_call(images, state, target, weight_t, pos, patch, last, modul, fmod, heavy):
-    width = patch.shape[1]
-    low, full = jnp.bfloat16, jnp.float32
-    shapes = [(item.shape, low) for item in heavy] + [
-        ((2 * PATCH + 16, width), full),
-        (modul.shape, full),
-        (fmod.shape, full),
-    ]
-    return pl.pallas_call(
-        functools.partial(pass_kernel, images),
-        out_shape=[jax.ShapeDtypeStruct(*item) for item in shapes],
-        in_specs=[pl.BlockSpec(memory_space=pltpu.VMEM)] * 12,
-        out_specs=[pl.BlockSpec(memory_space=pltpu.VMEM)] * len(shapes),
-        scratch_shapes=[pltpu.VMEM(*item) for item in pass_scratch(state.shape[0], width)],
-        compiler_params=pltpu.CompilerParams(vmem_limit_bytes=63 * 1024 * 1024),
-    )(state, target, weight_t, pos, patch, last, modul, fmod, *heavy)
-
-
 def own_segments(width, in_cols, in_starts, out_rows, shards):
     every = []
     for place in range(shards):
@@ -1686,29 +1736,31 @@
         (1.0 - tcol) * latents.reshape(images, TOK, PATCH)
         + tcol * noises.reshape(images, TOK, PATCH)
     ).astype(jnp.bfloat16)
-    *heavy, few, d_mod, d_fm = pass_call(
-        images,
-        state.reshape(images * TOK, PATCH),
-        velocity.reshape(images * TOK, PATCH),
-        jnp.repeat(t_value, TOK)[:, None],
-        positions(GRID, width),
-        patch_w,
-        head_t,
-        modul,
-        final_mod,
-        [fc2_t, fc1_t, o_t, qkv_t],
-    )
     tables = (
         windows(in_cols, shard_count),
         windows(head_cols, shard_count),
         windows(embed_cols, shard_count),
         shard_count,
     )
-    sums = reduce_call(
+    sums = step_call(
         lines,
         tables,
-        heavy,
-        [d_mod, d_fm, few, in_t, head_win_t, cond_full, time_one],
+        images,
+        [fc2_t, fc1_t, o_t, qkv_t],
+        in_t,
+        [
+            state.reshape(images * TOK, PATCH),
+            velocity.reshape(images * TOK, PATCH),
+            jnp.repeat(t_value, TOK)[:, None],
+            positions(GRID, width),
+            patch_w,
+            head_t,
+            modul,
+            final_mod,
+            head_win_t,
+            cond_full,
+            time_one,
+        ],
     )
     d_in, d_fin, d_two, d_full, d_one, few_sum = sums[4:]
     loss_sum = few_sum[PATCH, 0]

time: 372 us -> 339 us (0.911)
  Pallas kernels: 312 us -> 279 us
    pallas_call x2 -> x1, Pallas kernels: 212 us -> 173 us  [step_call(): pl.pallas_call(functools.partial(step_kernel, lines, chunks, tables), out...]
    pallas_call x1, Pallas kernels: 10.4 us -> 16.3 us  [finish_call(): pl.pallas_call(functools.partial(finish_kernel, shards, sizes), out_shape...]
where the time goes in v5:
time: 339 us; the launch traced here: 332 us
  Pallas kernels  279 us (82%)
  other arithmetic  26.3 us (8%)
  local copies, waits for them, and re-layouts  20.5 us (6%)
  between operations  6.08 us (2%)
    pallas_call x1, Pallas kernels, step_call(): pl.pallas_call(functools.partial(step_kernel, lines, chunks, tables), out...  173 us
    pallas_call x1, Pallas kernels, gather_call(): pl.pallas_call(functools.partial(gather_kernel, plan), out_shape=[jax.Sha...  71.3 us
    pallas_call x1, Pallas kernels, total_call(): pl.pallas_call(functools.partial(total_kernel, tables, segments), out_sha...  18.5 us
    pallas_call x1, Pallas kernels, finish_call(): pl.pallas_call(functools.partial(finish_kernel, shards, sizes), out_shape...  16.3 us
    convert_element_type x3, local copies, waits for them, and re-layouts, window(): return lax.dynamic_slice_in_dim(padded, begin, tiles * 128, 0).astype(low)  10.7 us
    broadcast_in_dim x1, other arithmetic, on_device(): news[0][None]  9.25 us

profile of v5, /device:TPU:0, one launch (start us, length us, event | category | flops | bytes accessed | tf_op | source)
XLA Modules:
  0.0 332.2 jit_solution(6998181309016896744)
XLA Ops:
  0.7 1.2 dynamic_slice.18
  3.2 5.5 %fusion.in_t.refs_4_ = bf16[2560,768]{1,0:T(8,128)(2,1)} fusion(s32[]{:T(128)S(6)} %select_n.46, f32[2496,768]{1,0:T(8,128)} %bitcast.55), kind=kLoop, calls=%fused_computation.1 | loop fusion | bytes 11599876 | tf_op jit(solution)/shard_map/convert_element_type | solution.py:1320
  9.5 2.2 fusion.2.embed
  13.7 2.9 fusion.1.head_t.refs_13_
  16.9 1.3 bitcast_convert_fusion.out_t
  18.2 71.3 %shard_map.340 = (bf16[768,3072]{1,0:T(8,128)(2,1)}, bf16[3072,768]{1,0:T(8,128)(2,1)}, bf16[768,768]{1,0:T(8,128)(2,1)}, bf16[2304,768]{1,0:T(8,128)(2,1)}, f32...) custom-call(bf16[2560,768]{1,0:T(8,128)(2,1)} %fusion.in_t.refs_4_, ...), custom_call_target="tpu_custom_call" | custom-call | tf_op jit(solution)/shard_map/pallas_call | solution.py:1361
  89.6 1.9 multiply_sine_fusion.1
  91.5 1.1 pad_maximum_fusion.refs_8_
  93.1 0.9 add_convert_fusion.refs_5_
  93.9 0.9 copy.43
  94.8 0.8 reshape.126.refs_6_
  95.6 173.3 %shard_map.341 = (bf16[768,3072]{1,0:T(8,128)(2,1)}, bf16[3072,768]{1,0:T(8,128)(2,1)}, bf16[768,768]{1,0:T(8,128)(2,1)}, bf16[2304,768]{1,0:T(8,128)(2,1)}, bf1...) custom-call(bf16[768,3072]{1,0:T(8,128)(2,1)} %get-tuple-element.58., ...), custom_call_target="tpu_custom_call" | custom-call | tf_op jit(solution)/shard_map/pallas_call | solution.py:916
  268.9 1.3 broadcast_in_dim.60.c_head
  270.2 18.5 %shard_map.342 = (f32[2496,768]{1,0:T(8,128)}, f32[192,3840]{1,0:T(8,128)}, f32[580,768]{1,0:T(8,128)}, f32[192,1273]{1,0:T(8,128)}, f32[1,2496]{1,0:T(1,128)}, ...) custom-call(bf16[768,3072]{1,0:T(8,128)(2,1)} %get-tuple-element.69.fc2, ...), custom_call_target="tpu_custom_call" | custom-call | tf_op jit(solution)/shard_map/pallas_call | solution.py:1615
  289.9 16.3 %shard_map.343 = (f32[1,768]{1,0:T(1,128)}, f32[1,3840]{1,0:T(1,128)}, f32[1,768]{1,0:T(1,128)}, f32[1,1273]{1,0:T(1,128)}, f32[1,768]{1,0:T(1,128)}, /*index=5*...) custom-call(f32[1,13824]{1,0:T(1,128)} %get-tuple-element.80.own, f32[1,768]{1,0:T(1,128)} %r_in.1, ...), custom_call_target="tpu_custom_call" | custom-call | tf_op jit(solution)/shard_map/pallas_call | solution.py:1673
  306.2 0.7 reduce.7
  306.9 0.7 rsqrt.39
  307.6 2.3 subtract_bitcast_fusion.3
  310.0 3.6 %subtract_bitcast_fusion.2 = f32[768,580]{0,1:T(8,128)} fusion(f32[580,768]{1,0:T(8,128)} %get-tuple-element.84, f32[580]{0:T(1024)S(1)} %rsqrt.38, f32[768]{0:T(1024)S(1)} %reduce.6, f32[768,580]{0,1:T(8,128)} %param.29), kind=kLoop, calls=%fused_computation.6 | loop fusion | flops 1336320 | bytes 5350672 | tf_op jit(solution)/shard_map/transpose | solution.py:1796
  313.7 3.8 %subtract_bitcast_fusion.1 = f32[1,3840,192]{1,2,0:T(8,128)} fusion(f32[192,3840]{1,0:T(8,128)} %get-tuple-element.83, f32[192]{0:T(256)S(1)} %bitcast.70, f32[3840]{0:T(1024)S(1)} %reduce.5, f32[1,3840,192]{1,2,0:T(8,128)S(1)} %copy-done.1), kind=kLoop, calls=%fused_computation.3 | loop fusion | flops 2211840 | bytes 8863488 | tf_op jit(solution)/shard_map/broadcast_in_dim | solution.py:1815
  317.7 9.2 %subtract_bitcast_fusion = f32[1,768,2496]{1,2,0:T(8,128)} fusion(f32[2496,768]{1,0:T(8,128)} %get-tuple-element.82, f32[2496]{0:T(1024)S(1)} %rsqrt_reduce_fusion, f32[768]{0:T(1024)S(1)} %reduce.3, f32[1,768,2496]{1,2,0:T(8,128)} %param.27), kind=kLoop, calls=%fused_computation.2 | loop fusion | flops 5750784 | bytes 23016192 | tf_op jit(solution)/shard_map/broadcast_in_dim | solution.py:1814
  326.9 0.6 reduce.2
  327.5 0.6 reduce
  328.2 1.2 slice.6
  (81 shorter events, 3.9 us)
Async XLA Ops:
  3.2 8.6 %copy-start.24 = (s32[4]{0:T(128)S(1)}, s32[4]{0:T(128)}, u32[]{:S(2)}) copy-start(s32[4]{0:T(128)} %constant.93.clone) | copy-start | bytes 52
  8.7 7.9 %copy-start.20 = (s32[2]{0:T(128)S(1)}, s32[2]{0:T(128)}, u32[]{:S(2)}) copy-start(s32[2]{0:T(128)} %param.24) | copy-start | bytes 28
  8.7 8.0 %copy-start.21 = (s32[2]{0:T(128)S(1)}, s32[2]{0:T(128)}, u32[]{:S(2)}) copy-start(s32[2]{0:T(128)} %param.25) | copy-start | bytes 28
  8.7 8.0 %copy-start.22 = (s32[2]{0:T(128)S(1)}, s32[2]{0:T(128)}, u32[]{:S(2)}) copy-start(s32[2]{0:T(128)} %param.26) | copy-start | bytes 28
  8.7 8.2 %copy-start = (f32[1,3840,192]{1,2,0:T(8,128)S(1)}, f32[1,3840,192]{1,2,0:T(8,128)}, u32[]{:S(2)}) copy-start(f32[1,3840,192]{1,2,0:T(8,128)} %param.28) | copy-start | bytes 8847364
  89.5 3.2 copy-start.4
  89.5 3.4 %copy-start.5 = (f32[2,4096]{1,0:T(2,128)S(1)}, f32[2,4096]{1,0:T(2,128)}, u32[]{:S(2)}) copy-start(f32[2,4096]{1,0:T(2,128)} %param.22) | copy-start | bytes 98308
  89.6 5.2 %copy-start.6 = (f32[2,4096]{1,0:T(2,128)S(1)}, f32[2,4096]{1,0:T(2,128)}, u32[]{:S(2)}) copy-start(f32[2,4096]{1,0:T(2,128)} %param.23) | copy-start | bytes 98308
  270.2 18.5 %copy-start.11 = (f32[1273]{0:T(1024)S(1)}, f32[1273]{0:T(1024)}, u32[]{:S(2)}) copy-start(f32[1273]{0:T(1024)} %param.37) | copy-start | bytes 15280
  270.2 19.1 %copy-start.13 = (f32[768]{0:T(1024)S(1)}, f32[768]{0:T(1024)}, u32[]{:S(2)}) copy-start(f32[768]{0:T(1024)} %param.35) | copy-start | bytes 9220
  270.2 37.4 %copy-start.2 = (f32[1273,192]{0,1:T(8,128)S(1)}, f32[1273,192]{0,1:T(8,128)}, u32[]{:S(2)}) copy-start(f32[1273,192]{0,1:T(8,128)} %param.30) | copy-start | bytes 2932996
  288.7 21.2 %copy-start.18 = (f32[1,580]{1,0:T(1,128)S(1)}, f32[1,580]{1,0:T(1,128)}, u32[]{:S(2)}) copy-start(f32[1,580]{1,0:T(1,128)} %get-tuple-element.91) | copy-start | bytes 6964
  306.2 3.7 %copy-start.17 = (f32[1,768]{1,0:T(1,128)S(1)}, f32[1,768]{1,0:T(1,128)}, u32[]{:S(2)}) copy-start(f32[1,768]{1,0:T(1,128)} %get-tuple-element.96) | copy-start | bytes 9220
  309.9 3.7 %copy-start.9 = (f32[1,3840]{1,0:T(1,128)S(1)}, f32[1,3840]{1,0:T(1,128)}, u32[]{:S(2)}) copy-start(f32[1,3840]{1,0:T(1,128)} %get-tuple-element.95) | copy-start | bytes 46084
  309.9 3.8 %copy-start.19 = (f32[1,192]{1,0:T(1,128)S(1)}, f32[1,192]{1,0:T(1,128)}, u32[]{:S(2)}) copy-start(f32[1,192]{1,0:T(1,128)} %get-tuple-element.140) | copy-start | bytes 2308
  309.9 3.8 %copy-start.1 = (f32[1,3840,192]{1,2,0:T(8,128)S(1)}, f32[1,3840,192]{1,2,0:T(8,128)}, u32[]{:S(2)}) copy-start(f32[1,3840,192]{1,2,0:T(8,128)} %param.28) | copy-start | bytes 8847364
  310.0 7.6 %copy-start.7 = (f32[580]{0:T(1024)}, f32[580]{0:T(1024)S(1)}, u32[]{:S(2)}) copy-start(f32[580]{0:T(1024)S(1)} %reduce.1) | copy-start | bytes 6964
  313.7 3.9 %copy-start.16 = (f32[1,768]{1,0:T(1,128)S(1)}, f32[1,768]{1,0:T(1,128)}, u32[]{:S(2)}) copy-start(f32[1,768]{1,0:T(1,128)} %get-tuple-element.94) | copy-start | bytes 9220
  313.7 3.9 %copy-start.10 = (f32[1,2496]{1,0:T(1,128)S(1)}, f32[1,2496]{1,0:T(1,128)}, u32[]{:S(2)}) copy-start(f32[1,2496]{1,0:T(1,128)} %get-tuple-element.138) | copy-start | bytes 29956
  317.6 9.3 %copy-start.12 = (f32[1,1273]{1,0:T(1,128)S(1)}, f32[1,1273]{1,0:T(1,128)}, u32[]{:S(2)}) copy-start(f32[1,1273]{1,0:T(1,128)} %get-tuple-element.92) | copy-start | bytes 15280
  317.6 9.9 %copy-start.15 = (f32[1,768]{1,0:T(1,128)S(1)}, f32[1,768]{1,0:T(1,128)}, u32[]{:S(2)}) copy-start(f32[1,768]{1,0:T(1,128)} %get-tuple-element.90) | copy-start | bytes 9220
  317.6 11.7 %copy-start.23 = (f32[1,128]{1,0:T(1,128)S(1)}, f32[1,128]{1,0:T(1,128)}, u32[]{:S(2)}) copy-start(f32[1,128]{1,0:T(1,128)} %get-tuple-element.81) | copy-start | bytes 1540
  317.7 11.7 %copy-start.14 = (f32[1,768]{1,0:T(1,128)S(1)}, f32[1,768]{1,0:T(1,128)}, u32[]{:S(2)}) copy-start(f32[1,768]{1,0:T(1,128)} %get-tuple-element.137) | copy-start | bytes 9220
  317.7 12.3 %copy-start.8 = (f32[1,3840]{1,0:T(1,128)S(1)}, f32[1,3840]{1,0:T(1,128)}, u32[]{:S(2)}) copy-start(f32[1,3840]{1,0:T(1,128)} %get-tuple-element.139) | copy-start | bytes 46084
  (1 other events, 1.3 us)

commit v6 on v5

--- a/solution.py
+++ b/solution.py
@@ -3,6 +3,7 @@
 
 import jax
 import jax.numpy as jnp
+import numpy as np
 from jax import lax
 from jax.experimental import pallas as pl
 from jax.experimental.pallas import tpu as pltpu
@@ -32,13 +33,11 @@
 
 def positions(grid, width):
     quarter = width // 4
-    omega = 1.0 / 10000.0 ** (jnp.arange(quarter, dtype=jnp.float32) / quarter)
-    index = jnp.arange(grid * grid, dtype=jnp.int32)
-    row_pos = (index // grid).astype(jnp.float32)[:, None] * omega[None, :]
-    col_pos = (index % grid).astype(jnp.float32)[:, None] * omega[None, :]
-    return jnp.concatenate(
-        [jnp.sin(row_pos), jnp.cos(row_pos), jnp.sin(col_pos), jnp.cos(col_pos)], 1
-    )
+    omega = (1.0 / 10000.0 ** (np.arange(quarter, dtype=np.float32) / quarter)).astype(np.float32)
+    index = np.arange(grid * grid)
+    row_pos = (index // grid).astype(np.float32)[:, None] * omega[None, :]
+    col_pos = (index % grid).astype(np.float32)[:, None] * omega[None, :]
+    return np.concatenate([np.sin(row_pos), np.cos(row_pos), np.sin(col_pos), np.cos(col_pos)], 1)
 
 
 def time_freq(t_value, width):
@@ -112,12 +111,11 @@
     lax.fori_loop(0, rows // block, body, 0)
 
 
-def step_kernel(lines, chunks, tables, *refs):
+def step_kernel(lines, chunks, tables, in_cols, *refs):
     count = len(chunks)
-    heavy, refs = refs[:4], refs[4:]
-    (in_far, state, target, weight_t, pos, patch, last, modul, fmod, head_t, cond_full, time_one), refs = refs[:12], refs[12:]
+    (in_far, out_far, state, target, weight_t, pos, head_t, embed, traits), refs = refs[:9], refs[9:]
     finals, refs = refs[:4], refs[4:]
-    (d_in, d_head, d_two, d_full, d_one, few_sum), scratch = refs[:6], refs[6:]
+    (d_in, d_head, d_two, d_full, d_one, few_sum, cond_full, time_act, all_traits), scratch = refs[:9], refs[9:]
     held, by_y, by_x, by_z = (scratch[k * count : (k + 1) * count] for k in range(4))
     send, recv, zsend, zrecv, wsend, wrecv = scratch[4 * count : 4 * count + 6]
     scratch = scratch[4 * count + 6 :]
@@ -129,8 +127,10 @@
         few_got, few_y, few_x, few_held, few_line, mod_got, fm_got, mod_sum, fm_sum, group_slot, part_own, part_slot,
         act_own, act_slot, pair_own, pair_got, line_in, line_rest, line_full,
         few_send, few_recv, group_send, group_recv, line_send, line_recv,
-    ) = scratch
+    ) = scratch[:25]
+    gather_refs = scratch[25:]
     (in_starts, in_tiles), (head_starts, head_tiles), (embed_starts, embed_tiles), shards = tables
+    time_one, modul, fmod, patch, last = gather_refs[:5]
     rep, shard = lax.axis_index("rep"), lax.axis_index("shard")
     place_here = lax.rem(rep, 2 * lines)
     base = rep - place_here
@@ -631,12 +631,12 @@
         )
 
     fc2, fc1, attn_out, qkv = finals
-
-    def load(k):
-        return pltpu.make_async_copy(heavy[k], finals[k], fetch.at[k])
-
-    for k in (3, 2, 1, 0):
-        load(k).start()
+    segments = heavy_segments(width, in_cols, in_starts, out_far.shape[0], shards)
+    plan = (segments,) + tables[:3] + (lines,)
+    relay_tick, arrived, finish = gather_steps(
+        plan, remote, line_peer, in_blocks, far_copy, out_far, in_far, head_t, embed, traits,
+        *finals, cond_full, time_act, time_one, modul, fmod, patch, last, all_traits, *gather_refs[5:],
+    )
     d_mod[...] = jnp.zeros_like(d_mod)
     d_fm[...] = jnp.zeros_like(d_fm)
 
@@ -651,9 +651,11 @@
     def qkv_block(part):
         qkv_low[:, part] = mxu(a_low[...], qkv[part, :], NT).astype(low)
 
-    load(3).wait()
+    relay_tick(4)
+    arrived(3)
+    relay_tick(5)
     blocks_of(3 * width, cut, qkv_block)
-    load(2).wait()
+    relay_tick(6)
     lane = lax.broadcasted_iota(jnp.int32, (TOK, 128), 1)
     first = lane < 64
     scale = 0.125
@@ -677,6 +679,8 @@
         return carry
 
     lax.fori_loop(0, width // 128, attend, 0)
+    relay_tick(7)
+    arrived(2)
     for image in range(per):
         got = mxu(mixed[span[image], :], attn_out[...], NT)
         proj[span[image], :] = got
@@ -693,9 +697,10 @@
             0.5 * value * (1.0 + jnp.tanh(0.7978845608 * (value + 0.044715 * value * value * value)))
         ).astype(low)
 
-    load(1).wait()
+    arrived(1)
     blocks_of(4 * width, cut, upper_block)
-    load(0).wait()
+    arrived(0)
+    finish()
 
     def mlp_block(part):
         mlp[:, part] = mxu(active[...], fc2[part, :], NT)
@@ -851,14 +856,18 @@
         sides(i, action)
 
 
-def step_call(lines, tables, images, heavy, in_t, light):
-    width = heavy[2].shape[0]
+def step_call(lines, tables, in_cols, far, light):
+    width = far[0].shape[1]
     chunks = heavy_chunks(width)
     count = len(chunks)
     low, full = jnp.bfloat16, jnp.float32
     (_, in_tiles), (_, head_tiles), (_, embed_tiles), shards = tables
-    state, modul, fmod, cond_full = light[0], light[6], light[7], light[9]
-    tokens, group, rows = state.shape[0], modul.shape[0], cond_full.shape[0]
+    state, traits = light[0], light[6]
+    tokens, group = state.shape[0], traits.shape[0]
+    rows = 2 * lines * group
+    modul_shape, fmod_shape = (group, 6 * width), (group, 2 * width)
+    segments = heavy_segments(width, in_cols, tables[0][0], far[1].shape[0], shards)
+    most = max(len(parts) for parts in segments)
     in_lanes, head_lanes, embed_lanes = in_tiles * 128, head_tiles * 128, embed_tiles * 128
     rest_lanes = 2 * head_lanes + embed_lanes
     few = (2 * PATCH + 16, width)
@@ -868,13 +877,17 @@
     wide = [item for item, chunk in zip(sizes, chunks) if chunk[0] == 0][0]
     tall = max(item for item, chunk in zip(sizes, chunks) if chunk[0] != 0)
     dma = pltpu.SemaphoreType.DMA
-    shapes = [(item.shape, low) for item in heavy] + [
+    heavy = [(width, 4 * width), (4 * width, width), (width, width), (3 * width, width)]
+    shapes = [(item, low) for item in heavy] + [
         ((rows, in_lanes), low),
         ((rows, head_lanes), low),
         ((rows, head_lanes), low),
         ((rows, embed_lanes), full),
         ((rows, embed_lanes), low),
         (few, full),
+        ((rows, width), full),
+        ((rows, width), low),
+        ((rows, traits.shape[1]), full),
     ]
     pass_scratch = [
         ((tokens, width), full),
@@ -897,10 +910,10 @@
         (few_half, full),
         ((2,) + few_half, full),
         ((lines,) + few_half, full),
-        (modul.shape, full),
-        (fmod.shape, full),
-        (modul.shape, full),
-        (fmod.shape, full),
+        (modul_shape, full),
+        (fmod_shape, full),
+        (modul_shape, full),
+        (fmod_shape, full),
         ((group, in_lanes + head_lanes), full),
         ((group, width), full),
         ((shards, group, width), full),
@@ -912,11 +925,32 @@
         ((lines, 2 * group, rest_lanes), low),
         ((lines, 2 * group, embed_lanes), full),
     ]
+    gather_scratch = [
+        ((rows, embed_lanes), full),
+        (modul_shape, full),
+        (fmod_shape, full),
+        ((PATCH, width), low),
+        ((PATCH, width), low),
+        ((shards, rows, embed_lanes), low),
+        ((shards, rows, embed_lanes), full),
+        ((shards, PATCH, embed_lanes), low),
+        ((shards, rows, head_lanes), full),
+        ((rows, head_lanes), full),
+        ((shards, group, in_lanes), full),
+        ((group, in_lanes), full),
+        ((shards, group, head_lanes), full),
+        ((group, head_lanes), full),
+        ((PATCH, width), low),
+        ((shards,) + traits.shape, full),
+        (traits.shape, full),
+        (traits.shape, full),
+        ((lines, 2 * group, traits.shape[1]), full),
+    ]
     vmem, anywhere = pl.BlockSpec(memory_space=pltpu.VMEM), pl.BlockSpec(memory_space=pl.ANY)
     return pl.pallas_call(
-        functools.partial(step_kernel, lines, chunks, tables),
+        functools.partial(step_kernel, lines, chunks, tables, in_cols),
         out_shape=[jax.ShapeDtypeStruct(*item) for item in shapes],
-        in_specs=[anywhere] * 5 + [vmem] * len(light),
+        in_specs=[anywhere] * len(far) + [vmem] * len(light),
         out_specs=[vmem] * len(shapes),
         scratch_shapes=[pltpu.VMEM((r, c), low) for r, c in sizes]
         + [pltpu.VMEM((r // 2, c), low) for r, c in sizes]
@@ -932,7 +966,7 @@
         ]
         + [pltpu.VMEM((SLOTS,) + item, low) for item in (wide, tall)] * 2
         + [pltpu.SemaphoreType.REGULAR, pltpu.SemaphoreType.REGULAR, dma((9,))]
-        + [pltpu.VMEM(*item) for item in ((modul.shape, full), (fmod.shape, full), (few, full))]
+        + [pltpu.VMEM(*item) for item in ((modul_shape, full), (fmod_shape, full), (few, full))]
         + [pltpu.VMEM(*item) for item in pass_scratch]
         + [pltpu.VMEM(*item) for item in scratch]
         + [
@@ -942,11 +976,16 @@
             dma((4, shards - 1)),
             dma((3, lines - 1)),
             dma((3, lines - 1)),
-        ],
+        ]
+        + [pltpu.VMEM(*item) for item in gather_scratch]
+        + [dma((most,)), dma((most,))]
+        + [dma((most, 2))] * 4
+        + [dma((most, 4))] * 2
+        + [dma((most,)), dma((most,)), dma((8, shards - 1)), dma((8, shards - 1)), dma((most,)), dma((lines,)), dma((lines,))],
         compiler_params=pltpu.CompilerParams(
             collective_id=1, has_side_effects=True, vmem_limit_bytes=64 * 1024 * 1024 - 65536
         ),
-    )(*heavy, in_t, *light)
+    )(*far, *light)
 
 
 def placed_traits(traits, lanes):
@@ -982,12 +1021,14 @@
     return every
 
 
-def gather_kernel(
-    plan, in_t, out_t, head_t, embed, traits,
+def gather_steps(
+    plan, remote, line_peer, in_blocks, far_copy,
+    out_t, in_t, head_t, embed, traits,
     fc2, fc1, attn_out, qkv, cond_full, time_act, time_one, modul, fmod, patch, last, all_traits,
     s1_slot, tab_slot, patch_slot, two_slot, two_own, mod_slot, mod_own, fm_slot, fm_own, last_own,
+    trait_slot, trait_own, trait_got, line_slot,
     ysend, yrecv, xsend, xrecv, zsend, zrecv, csend, crecv, osend, orecv, small_send, small_recv, local_sem,
-    trait_slot, trait_own, trait_got, line_slot, trait_send, trait_recv,
+    trait_send, trait_recv,
 ):
     segments, (in_starts, in_tiles), (head_starts, head_tiles), (embed_starts, embed_tiles), lines = plan
     shards = len(segments)
@@ -1003,21 +1044,14 @@
     to_x = (rep + 1 - 2 * x, shard)
     to_z = (rep + 2 - 4 * zb, shard)
     width = head_t.shape[1]
-
-    barrier = pltpu.get_barrier_semaphore()
     others = [(rep, lax.rem(shard + step, shards)) for step in range(1, shards)]
-
-    def line_peer(step):
-        return (rep - place_here + lax.rem(z + step, lines) * 2 + x, shard)
-
-    for peer in others + [to_x] + [line_peer(step) for step in range(1, lines)]:
-        pl.semaphore_signal(barrier, inc=1, device_id=peer, device_id_type=MESH)
-    pl.semaphore_wait(barrier, shards + lines - 1)
-
-    def remote(source, target, send_sem, recv_sem, peer):
-        return pltpu.make_async_remote_copy(
-            src_ref=source, dst_ref=target, send_sem=send_sem, recv_sem=recv_sem, device_id=peer, device_id_type=MESH
-        )
+    mod_places = [o for o in range(shards) if in_starts[o] * 128 < 6 * width]
+    computes_mod = functools.reduce(jnp.logical_or, [shard == o for o in mod_places])
+
+    @pl.when(computes_mod)
+    def _():
+        for k in range(len(in_blocks)):
+            far_copy(k).start()
 
     def small(kind, source, slots, step):
         return remote(
@@ -1207,7 +1241,6 @@
 
     head_places = [o for o in range(shards) if head_starts[o] * 128 < width]
     fm_places = [o for o in range(shards) if (head_starts[o] + head_tiles) * 128 > width]
-    mod_places = [o for o in range(shards) if in_starts[o] * 128 < 6 * width]
     group = modul.shape[0]
 
     arrive(0, s1_slot)
@@ -1227,8 +1260,15 @@
                 cond_full[:, span] += two_slot[o, :, (tile - head_starts[o]) * 128 : (tile - head_starts[o] + 1) * 128]
     mine = cond_full[pl.ds(pl.multiple_of(place_here * group, 8), group), :]
     cond = (mine * jax.nn.sigmoid(mine)).astype(jnp.bfloat16)
-    mod_own[...] = lax.dot_general(cond, in_t[...], nt, preferred_element_type=jnp.float32)
-    mod_slot[shard] = mod_own[...]
+
+    @pl.when(computes_mod)
+    def _():
+        for k, block in enumerate(in_blocks):
+            far_copy(k).wait()
+            span = slice(k * block.shape[0], (k + 1) * block.shape[0])
+            mod_own[:, span] = lax.dot_general(cond, block[...], nt, preferred_element_type=jnp.float32)
+        mod_slot[shard] = mod_own[...]
+
     exchange(4, mod_own, mod_slot, mod_places)
     fm_own[...] = lax.dot_general(cond, head_t[...], nt, preferred_element_type=jnp.float32)
     fm_slot[shard] = fm_own[...]
@@ -1247,69 +1287,75 @@
     arrive(5, fm_slot, fm_places)
     place_tiles(modul, mod_slot, in_starts, in_tiles, mod_places, jnp.float32)
     place_tiles(fmod, fm_slot, head_starts, head_tiles, fm_places, jnp.float32, width // 128)
-    relay_tick(4)
-    relay_tick(5)
-    relay_tick(6)
-    relay_tick(7)
-
-    for place in range(shards):
-        count = len(segments[place])
-
-        @pl.when(shard == place)
-        def _():
-            for k in range(count):
-                y_copy(place, k).wait_send()
-                owner_copy(place, k).wait_send()
-                own_copy(place, k).wait()
-
-        @pl.when(to_core[1] == place)
-        def _():
-            for k in range(count):
-                remote(target_part(place, k), target_part(place, k), osend.at[k], orecv.at[k], to_core).wait_recv()
-
-        @pl.when(to_y[1] == place)
-        def _():
-            for k in range(count):
-                hop(quarter(place, k, me), xs, k, 0, to_x).wait_send()
-                hop(quarter(place, k, me), zs, k, 0, to_z).wait_send()
-                hop(half_of(place, k, across_x, False), zs, k, 1, to_z).wait_send()
-                hop(half_of(place, k, along_z, True), xs, k, 1, to_x).wait_send()
-                for slot, index in enumerate((me, across_x, along_z, corner)):
-                    hop(quarter(place, k, index), cs, k, slot, to_core).wait_send()
-
-        @pl.when(shards - 1 - shard == place)
-        def _():
-            for k in range(count):
-                for slot, index in enumerate((me, across_x, along_z, corner)):
-                    remote(
-                        quarter(place, k, index), quarter(place, k, index), csend.at[k, slot], crecv.at[k, slot], to_core
-                    ).wait_recv()
-
-    trait_pair.wait_send()
-    for step in range(1, lines):
-        trait_line(step).wait_send()
-    sent(7, traits, trait_slot)
-    sent(0, s1_slot.at[shard], s1_slot)
-    sent(1, tab_slot.at[shard], tab_slot)
-    sent(2, patch_slot.at[shard], patch_slot)
-    sent(3, two_own, two_slot, head_places)
-    sent(4, mod_own, mod_slot, mod_places)
-    sent(5, fm_own, fm_slot, fm_places)
-
-    @pl.when(shard == last_place)
-    def _():
-        for step in range(1, shards):
-            remote(last_own, last, small_send.at[6, step - 1], small_recv.at[6, 0], others[step - 1]).wait_send()
 
     @pl.when(shard != last_place)
     def _():
         remote(last_own, last, small_send.at[6, 0], small_recv.at[6, 0], to_core).wait_recv()
 
-
-def gather_call(in_t, out_t, head_t, embed_t, traits, shards, lines):
+    def arrived(array):
+        for place in range(shards):
+            of_array = [k for k, part in enumerate(segments[place]) if part[2] == array]
+
+            @pl.when(shard == place)
+            def _():
+                for k in of_array:
+                    own_copy(place, k).wait()
+
+            @pl.when(to_core[1] == place)
+            def _():
+                for k in of_array:
+                    remote(target_part(place, k), target_part(place, k), osend.at[k], orecv.at[k], to_core).wait_recv()
+
+            @pl.when(shards - 1 - shard == place)
+            def _():
+                for k in of_array:
+                    for slot, index in enumerate((me, across_x, along_z, corner)):
+                        part = quarter(place, k, index)
+                        remote(part, part, csend.at[k, slot], crecv.at[k, slot], to_core).wait_recv()
+
+    def finish():
+        for place in range(shards):
+            count = len(segments[place])
+
+            @pl.when(shard == place)
+            def _():
+                for k in range(count):
+                    y_copy(place, k).wait_send()
+                    owner_copy(place, k).wait_send()
+
+            @pl.when(to_y[1] == place)
+            def _():
+                for k in range(count):
+                    hop(quarter(place, k, me), xs, k, 0, to_x).wait_send()
+                    hop(quarter(place, k, me), zs, k, 0, to_z).wait_send()
+                    hop(half_of(place, k, across_x, False), zs, k, 1, to_z).wait_send()
+                    hop(half_of(place, k, along_z, True), xs, k, 1, to_x).wait_send()
+                    for slot, index in enumerate((me, across_x, along_z, corner)):
+                        hop(quarter(place, k, index), cs, k, slot, to_core).wait_send()
+
+        trait_pair.wait_send()
+        for step in range(1, lines):
+            trait_line(step).wait_send()
+        sent(7, traits, trait_slot)
+        sent(0, s1_slot.at[shard], s1_slot)
+        sent(1, tab_slot.at[shard], tab_slot)
+        sent(2, patch_slot.at[shard], patch_slot)
+        sent(3, two_own, two_slot, head_places)
+        sent(4, mod_own, mod_slot, mod_places)
+        sent(5, fm_own, fm_slot, fm_places)
+
+        @pl.when(shard == last_place)
+        def _():
+            for step in range(1, shards):
+                remote(last_own, last, small_send.at[6, step - 1], small_recv.at[6, 0], others[step - 1]).wait_send()
+
+    return relay_tick, arrived, finish
+
+
+def windowed(in_t, out_t, head_t, embed_t, shards):
     place = lax.axis_index("shard")
     width = head_t.shape[1]
-    low, full = jnp.bfloat16, jnp.float32
+    low = jnp.bfloat16
 
     def window(item_t, starts, tiles, lanes):
         rows = item_t.shape[0]
@@ -1326,61 +1372,7 @@
     in_t = window(in_t, in_starts, in_tiles, width)
     head_t = window(head_t, head_starts, head_tiles, width)
     embed = window(embed_t, embed_starts, embed_tiles, -(-embed_t.shape[1] // 128) * 128)
-    segments = heavy_segments(width, in_cols, in_starts, out_t.shape[0], shards)
-    plan = (segments, (in_starts, in_tiles), (head_starts, head_tiles), (embed_starts, embed_tiles), lines)
-    group = traits.shape[0]
-    rows = 2 * lines * group
-    most = max(len(parts) for parts in segments)
-    shapes = [
-        ((width, 4 * width), low),
-        ((4 * width, width), low),
-        ((width, width), low),
-        ((3 * width, width), low),
-        ((rows, width), full),
-        ((rows, width), low),
-        ((rows, embed_tiles * 128), full),
-        ((group, 6 * width), full),
-        ((group, 2 * width), full),
-        ((PATCH, width), low),
-        ((PATCH, width), low),
-        ((rows, traits.shape[1]), full),
-    ]
-    scratch = [
-        ((shards, rows, embed_tiles * 128), low),
-        ((shards, rows, embed_tiles * 128), full),
-        ((shards, PATCH, embed_tiles * 128), low),
-        ((shards, rows, head_tiles * 128), full),
-        ((rows, head_tiles * 128), full),
-        ((shards, group, in_tiles * 128), full),
-        ((group, in_tiles * 128), full),
-        ((shards, group, head_tiles * 128), full),
-        ((group, head_tiles * 128), full),
-        ((PATCH, width), low),
-    ]
-    dma = pltpu.SemaphoreType.DMA
-    outs = pl.pallas_call(
-        functools.partial(gather_kernel, plan),
-        out_shape=[jax.ShapeDtypeStruct(*item) for item in shapes],
-        in_specs=[pl.BlockSpec(memory_space=pltpu.VMEM)] * 5,
-        out_specs=[pl.BlockSpec(memory_space=pltpu.VMEM)] * len(shapes),
-        scratch_shapes=[pltpu.VMEM(*item) for item in scratch]
-        + [dma((most,)), dma((most,))]
-        + [dma((most, 2))] * 4
-        + [dma((most, 4))] * 2
-        + [dma((most,)), dma((most,)), dma((8, shards - 1)), dma((8, shards - 1)), dma((most,))]
-        + [
-            pltpu.VMEM((shards,) + traits.shape, full),
-            pltpu.VMEM(traits.shape, full),
-            pltpu.VMEM(traits.shape, full),
-            pltpu.VMEM((lines, 2 * group, traits.shape[1]), full),
-            dma((lines,)),
-            dma((lines,)),
-        ],
-        compiler_params=pltpu.CompilerParams(
-            collective_id=2, has_side_effects=True, vmem_limit_bytes=60 * 1024 * 1024
-        ),
-    )(in_t, out_t.astype(low), head_t, embed, traits)
-    return in_t, head_t, outs
+    return in_t, out_t.astype(low), head_t, embed
 
 
 def own_segments(width, in_cols, in_starts, out_rows, shards):
@@ -1729,8 +1721,7 @@
     traits = lax.dynamic_update_slice(
         jnp.zeros((group, lead + 128), jnp.float32), own_traits, (place * images, 0)
     )
-    in_t, head_win_t, gathered = gather_call(*weights, traits, shard_count, lines)
-    fc2_t, fc1_t, o_t, qkv_t, cond_full, time_act, time_one, modul, final_mod, patch_w, head_t, all_traits = gathered
+    in_t, out_t, head_t, embed = windowed(*weights, shard_count)
     tcol = t_value[:, None, None]
     state = (
         (1.0 - tcol) * latents.reshape(images, TOK, PATCH)
@@ -1745,24 +1736,19 @@
     sums = step_call(
         lines,
         tables,
-        images,
-        [fc2_t, fc1_t, o_t, qkv_t],
-        in_t,
+        in_cols,
+        [in_t, out_t],
         [
             state.reshape(images * TOK, PATCH),
             velocity.reshape(images * TOK, PATCH),
             jnp.repeat(t_value, TOK)[:, None],
-            positions(GRID, width),
-            patch_w,
+            jnp.asarray(positions(GRID, width)),
             head_t,
-            modul,
-            final_mod,
-            head_win_t,
-            cond_full,
-            time_one,
+            embed,
+            traits,
         ],
     )
-    d_in, d_fin, d_two, d_full, d_one, few_sum = sums[4:]
+    d_in, d_fin, d_two, d_full, d_one, few_sum, cond_full, time_act, all_traits = sums[4:]
     loss_sum = few_sum[PATCH, 0]
     rows_old = (state_in_row, state_out_row, state_head_row[None], state_embed_row[None])
     cols_old = (state_in_col, state_out_col, state_head_col[None], state_embed_col[None])

time: 339 us -> 313 us (0.923)
  Pallas kernels: 279 us -> 258 us
    pallas_call x2 -> x1, Pallas kernels: 245 us -> 223 us  [step_call(): pl.pallas_call(functools.partial(step_kernel, lines, chunks, tables, in_c...]
where the time goes in v6:
time: 313 us; the launch traced here: 308 us
  Pallas kernels  258 us (82%)
  other arithmetic  23.3 us (7%)
  local copies, waits for them, and re-layouts  20.9 us (7%)
  between operations  5.59 us (2%)
    pallas_call x1, Pallas kernels, step_call(): pl.pallas_call(functools.partial(step_kernel, lines, chunks, tables, in_c...  223 us
    pallas_call x1, Pallas kernels, total_call(): pl.pallas_call(functools.partial(total_kernel, tables, segments), out_sha...  18.5 us
    pallas_call x1, Pallas kernels, finish_call(): pl.pallas_call(functools.partial(finish_kernel, shards, sizes), out_shape...  17.2 us
    convert_element_type x3, local copies, waits for them, and re-layouts, window(): return lax.dynamic_slice_in_dim(padded, begin, tiles * 128, 0).astype(low)  10.7 us
    broadcast_in_dim x1, other arithmetic, on_device(): news[0][None]  9.25 us

profile of v6, /device:TPU:0, one launch (start us, length us, event | category | flops | bytes accessed | tf_op | source)
XLA Modules:
  0.0 308.2 jit_solution(5912799140085164880)
XLA Ops:
  0.7 1.2 dynamic_slice.18
  3.2 5.5 %fusion.refs_0_ = bf16[2560,768]{1,0:T(8,128)(2,1)} fusion(s32[]{:T(128)S(6)} %select_n.22, f32[2496,768]{1,0:T(8,128)} %bitcast.55), kind=kLoop, calls=%fused_computation.1 | loop fusion | bytes 11599876 | tf_op jit(solution)/shard_map/convert_element_type | solution.py:1366
  9.5 2.3 fusion.2.refs_7_
  11.7 0.6 dynamic_slice.20
  13.6 2.9 fusion.1.refs_6_
  17.8 0.9 add_convert_fusion.refs_2_
  18.7 0.9 copy.44
  19.5 1.3 bitcast_convert_fusion.refs_1_
  20.8 0.8 reshape.96.refs_3_
  21.6 222.7 %shard_map.349 = (bf16[768,3072]{1,0:T(8,128)(2,1)}, bf16[3072,768]{1,0:T(8,128)(2,1)}, bf16[768,768]{1,0:T(8,128)(2,1)}, bf16[2304,768]{1,0:T(8,128)(2,1)}, bf1...) custom-call(bf16[2560,768]{1,0:T(8,128)(2,1)} %fusion.refs_0_, ...), custom_call_target="tpu_custom_call" | custom-call | tf_op jit(solution)/shard_map/pallas_call | solution.py:950
  244.3 1.3 broadcast_in_dim.56.c_head
  245.6 18.5 %shard_map.350 = (f32[2496,768]{1,0:T(8,128)}, f32[192,3840]{1,0:T(8,128)}, f32[580,768]{1,0:T(8,128)}, f32[192,1273]{1,0:T(8,128)}, f32[1,2496]{1,0:T(1,128)}, ...) custom-call(bf16[768,3072]{1,0:T(8,128)(2,1)} %get-tuple-element.50.fc2, ...), custom_call_target="tpu_custom_call" | custom-call | tf_op jit(solution)/shard_map/pallas_call | solution.py:1607
  264.1 0.6 broadcast_in_dim.59.r_embed
  265.3 17.2 %shard_map.351 = (f32[1,768]{1,0:T(1,128)}, f32[1,3840]{1,0:T(1,128)}, f32[1,768]{1,0:T(1,128)}, f32[1,1273]{1,0:T(1,128)}, f32[1,768]{1,0:T(1,128)}, /*index=5*...) custom-call(f32[1,13824]{1,0:T(1,128)} %get-tuple-element.62.own, f32[1,768]{1,0:T(1,128)} %r_in.1, ...), custom_call_target="tpu_custom_call" | custom-call | tf_op jit(solution)/shard_map/pallas_call | solution.py:1665
  282.5 0.7 reduce.7
  283.2 0.7 rsqrt.39
  283.9 2.3 subtract_bitcast_fusion.3
  286.3 3.6 %subtract_bitcast_fusion.2 = f32[768,580]{0,1:T(8,128)} fusion(f32[580,768]{1,0:T(8,128)} %get-tuple-element.66, f32[580]{0:T(1024)S(1)} %rsqrt.38, f32[768]{0:T(1024)S(1)} %reduce.6, f32[768,580]{0,1:T(8,128)} %param.30), kind=kLoop, calls=%fused_computation.6 | loop fusion | flops 1336320 | bytes 5350672 | tf_op jit(solution)/shard_map/transpose | solution.py:1782
  290.0 3.8 %subtract_bitcast_fusion.1 = f32[1,3840,192]{1,2,0:T(8,128)} fusion(f32[192,3840]{1,0:T(8,128)} %get-tuple-element.65, f32[192]{0:T(256)S(1)} %bitcast.70, f32[3840]{0:T(1024)S(1)} %reduce.5, f32[1,3840,192]{1,2,0:T(8,128)S(1)} %copy-done.1), kind=kLoop, calls=%fused_computation.3 | loop fusion | flops 2211840 | bytes 8863488 | tf_op jit(solution)/shard_map/broadcast_in_dim | solution.py:1801
  294.0 9.2 %subtract_bitcast_fusion = f32[1,768,2496]{1,2,0:T(8,128)} fusion(f32[2496,768]{1,0:T(8,128)} %get-tuple-element.64, f32[2496]{0:T(1024)S(1)} %rsqrt_reduce_fusion, f32[768]{0:T(1024)S(1)} %reduce.3, f32[1,768,2496]{1,2,0:T(8,128)} %param.28), kind=kLoop, calls=%fused_computation.2 | loop fusion | flops 5750784 | bytes 23016192 | tf_op jit(solution)/shard_map/broadcast_in_dim | solution.py:1800
  303.2 0.6 reduce.2
  303.9 0.6 reduce
  304.5 1.2 slice.6
  306.3 0.6 copy.51
  (76 shorter events, 2.6 us)
Async XLA Ops:
  3.2 8.5 %copy-start.24 = (s32[4]{0:T(128)S(1)}, s32[4]{0:T(128)}, u32[]{:S(2)}) copy-start(s32[4]{0:T(128)} %constant.61.clone) | copy-start | bytes 52
  8.7 7.8 %copy-start.20 = (s32[2]{0:T(128)S(1)}, s32[2]{0:T(128)}, u32[]{:S(2)}) copy-start(s32[2]{0:T(128)} %param.25) | copy-start | bytes 28
  8.7 8.0 %copy-start.21 = (s32[2]{0:T(128)S(1)}, s32[2]{0:T(128)}, u32[]{:S(2)}) copy-start(s32[2]{0:T(128)} %param.26) | copy-start | bytes 28
  8.7 8.0 %copy-start.22 = (s32[2]{0:T(128)S(1)}, s32[2]{0:T(128)}, u32[]{:S(2)}) copy-start(s32[2]{0:T(128)} %param.27) | copy-start | bytes 28
  8.7 8.8 %copy-start.4 = (f32[2,4096]{1,0:T(2,128)S(1)}, f32[2,4096]{1,0:T(2,128)}, u32[]{:S(2)}) copy-start(f32[2,4096]{1,0:T(2,128)} %param.22) | copy-start | bytes 98308
  8.7 8.9 %copy-start.5 = (f32[2,4096]{1,0:T(2,128)S(1)}, f32[2,4096]{1,0:T(2,128)}, u32[]{:S(2)}) copy-start(f32[2,4096]{1,0:T(2,128)} %param.23) | copy-start | bytes 98308
  9.4 10.1 %copy-start = (f32[1,3840,192]{1,2,0:T(8,128)S(1)}, f32[1,3840,192]{1,2,0:T(8,128)}, u32[]{:S(2)}) copy-start(f32[1,3840,192]{1,2,0:T(8,128)} %param.29) | copy-start | bytes 8847364
  17.5 3.3 %copy-start.6 = (f32[2,4096]{1,0:T(2,128)S(1)}, f32[2,4096]{1,0:T(2,128)}, u32[]{:S(2)}) copy-start(f32[2,4096]{1,0:T(2,128)} %param.24) | copy-start | bytes 98308
  245.6 18.5 %copy-start.11 = (f32[1273]{0:T(1024)S(1)}, f32[1273]{0:T(1024)}, u32[]{:S(2)}) copy-start(f32[1273]{0:T(1024)} %param.38) | copy-start | bytes 15280
  245.6 19.1 %copy-start.13 = (f32[768]{0:T(1024)S(1)}, f32[768]{0:T(1024)}, u32[]{:S(2)}) copy-start(f32[768]{0:T(1024)} %param.36) | copy-start | bytes 9220
  245.6 38.3 %copy-start.2 = (f32[1273,192]{0,1:T(8,128)S(1)}, f32[1273,192]{0,1:T(8,128)}, u32[]{:S(2)}) copy-start(f32[1273,192]{0,1:T(8,128)} %param.31) | copy-start | bytes 2932996
  264.1 22.1 %copy-start.18 = (f32[1,580]{1,0:T(1,128)S(1)}, f32[1,580]{1,0:T(1,128)}, u32[]{:S(2)}) copy-start(f32[1,580]{1,0:T(1,128)} %get-tuple-element.73) | copy-start | bytes 6964
  282.5 3.7 %copy-start.17 = (f32[1,768]{1,0:T(1,128)S(1)}, f32[1,768]{1,0:T(1,128)}, u32[]{:S(2)}) copy-start(f32[1,768]{1,0:T(1,128)} %get-tuple-element.78) | copy-start | bytes 9220
  286.2 3.7 %copy-start.9 = (f32[1,3840]{1,0:T(1,128)S(1)}, f32[1,3840]{1,0:T(1,128)}, u32[]{:S(2)}) copy-start(f32[1,3840]{1,0:T(1,128)} %get-tuple-element.77) | copy-start | bytes 46084
  286.2 3.8 %copy-start.19 = (f32[1,192]{1,0:T(1,128)S(1)}, f32[1,192]{1,0:T(1,128)}, u32[]{:S(2)}) copy-start(f32[1,192]{1,0:T(1,128)} %get-tuple-element.114) | copy-start | bytes 2308
  286.2 3.8 %copy-start.1 = (f32[1,3840,192]{1,2,0:T(8,128)S(1)}, f32[1,3840,192]{1,2,0:T(8,128)}, u32[]{:S(2)}) copy-start(f32[1,3840,192]{1,2,0:T(8,128)} %param.29) | copy-start | bytes 8847364
  286.3 7.6 %copy-start.7 = (f32[580]{0:T(1024)}, f32[580]{0:T(1024)S(1)}, u32[]{:S(2)}) copy-start(f32[580]{0:T(1024)S(1)} %reduce.1) | copy-start | bytes 6964
  290.0 3.9 %copy-start.16 = (f32[1,768]{1,0:T(1,128)S(1)}, f32[1,768]{1,0:T(1,128)}, u32[]{:S(2)}) copy-start(f32[1,768]{1,0:T(1,128)} %get-tuple-element.76) | copy-start | bytes 9220
  290.0 3.9 %copy-start.10 = (f32[1,2496]{1,0:T(1,128)S(1)}, f32[1,2496]{1,0:T(1,128)}, u32[]{:S(2)}) copy-start(f32[1,2496]{1,0:T(1,128)} %get-tuple-element.112) | copy-start | bytes 29956
  293.9 9.3 %copy-start.12 = (f32[1,1273]{1,0:T(1,128)S(1)}, f32[1,1273]{1,0:T(1,128)}, u32[]{:S(2)}) copy-start(f32[1,1273]{1,0:T(1,128)} %get-tuple-element.74) | copy-start | bytes 15280
  293.9 9.9 %copy-start.15 = (f32[1,768]{1,0:T(1,128)S(1)}, f32[1,768]{1,0:T(1,128)}, u32[]{:S(2)}) copy-start(f32[1,768]{1,0:T(1,128)} %get-tuple-element.72) | copy-start | bytes 9220
  293.9 11.7 %copy-start.23 = (f32[1,128]{1,0:T(1,128)S(1)}, f32[1,128]{1,0:T(1,128)}, u32[]{:S(2)}) copy-start(f32[1,128]{1,0:T(1,128)} %get-tuple-element.63) | copy-start | bytes 1540
  294.0 11.7 %copy-start.14 = (f32[1,768]{1,0:T(1,128)S(1)}, f32[1,768]{1,0:T(1,128)}, u32[]{:S(2)}) copy-start(f32[1,768]{1,0:T(1,128)} %get-tuple-element.111) | copy-start | bytes 9220
  294.0 12.3 %copy-start.8 = (f32[1,3840]{1,0:T(1,128)S(1)}, f32[1,3840]{1,0:T(1,128)}, u32[]{:S(2)}) copy-start(f32[1,3840]{1,0:T(1,128)} %get-tuple-element.113) | copy-start | bytes 46084
  (1 other events, 0.6 us)

commit v7 on v6

--- a/solution.py
+++ b/solution.py
@@ -58,20 +58,25 @@
 MESH = pl.DeviceIdType.MESH
 LINE = 4
 PIECES = 4
-PARTS = (4, 4, 2)
+PARTS = (6, 6, 3)
 ORDER = (
-    (0, 0), (0, 1), (0, 2), (1, 0), (9, 0), (1, 1), (0, 3), (9, 1), (1, 2), (0, 4), (0, 5), (1, 3), (9, 2),
-    (2, 0), (0, 6), (1, 4), (1, 5), (0, 7), (9, 4), (2, 1), (1, 6), (3, 0), (0, 8), (1, 7), (9, 5), (2, 2),
-    (0, 9), (3, 1), (0, 10), (1, 8), (4, 0), (9, 6), (2, 4), (0, 11), (3, 2), (0, 12), (0, 13), (0, 14), (4, 1),
-    (9, 7), (2, 5), (3, 4), (6, 0), (0, 15), (9, 3), (2, 6), (2, 7), (3, 5), (4, 2), (4, 4), (9, 8), (6, 1),
-    (1, 9), (7, 0), (0, 16), (0, 17), (3, 6), (2, 3), (9, 9), (3, 7), (4, 5), (1, 10), (1, 11), (6, 2), (7, 1),
-    (8, 0), (2, 8), (9, 10), (3, 3), (5, 4), (8, 1), (4, 6), (7, 2), (2, 9), (4, 7), (3, 8), (8, 2), (9, 11),
-    (5, 5), (2, 10), (4, 3), (3, 9), (6, 4), (5, 6), (5, 7), (3, 10), (2, 11), (4, 8), (6, 5), (6, 3), (7, 4),
-    (6, 6), (4, 9), (3, 11), (8, 4), (6, 7), (4, 10), (6, 8), (7, 5), (6, 9), (7, 3), (8, 5), (4, 11), (8, 3),
-    (5, 10), (7, 6), (8, 6), (5, 11), (7, 7), (6, 10), (7, 8), (8, 7), (7, 9), (6, 11), (8, 8), (8, 9), (7, 10),
-    (8, 10), (7, 11), (8, 11),
+    (0, 0), (0, 1), (0, 2), (1, 0), (9, 0), (0, 3), (1, 1), (9, 1), (0, 4), (1, 2), (9, 2), (0, 5), (1, 3),
+    (2, 0), (9, 3), (0, 6), (1, 4), (0, 7), (2, 1), (9, 4), (1, 5), (0, 8), (3, 0), (1, 6), (9, 5), (2, 2),
+    (0, 9), (1, 7), (3, 1), (1, 8), (9, 6), (2, 3), (0, 10), (0, 11), (1, 9), (2, 4), (9, 7), (3, 2), (4, 0),
+    (0, 12), (9, 8), (1, 10), (1, 11), (2, 5), (3, 3), (2, 6), (9, 9), (3, 4), (4, 1), (0, 13), (1, 12), (2, 7),
+    (9, 10), (4, 2), (6, 0), (3, 5), (0, 14), (2, 8), (3, 6), (9, 11), (4, 3), (0, 15), (4, 4), (2, 9), (3, 7),
+    (9, 12), (6, 1), (7, 0), (0, 16), (3, 8), (2, 10), (6, 2), (4, 5), (0, 17), (4, 6), (3, 9), (2, 11), (6, 3),
+    (7, 1), (8, 0), (0, 18), (3, 10), (6, 4), (0, 19), (2, 12), (3, 11), (4, 7), (4, 8), (4, 9), (4, 10), (5, 6),
+    (6, 5), (1, 13), (9, 13), (7, 2), (7, 3), (7, 4), (8, 1), (0, 20), (3, 12), (0, 21), (0, 22), (4, 11),
+    (6, 6), (5, 7), (7, 5), (8, 2), (8, 3), (8, 4), (1, 14), (9, 14), (5, 8), (1, 15), (1, 16), (5, 9), (2, 13),
+    (5, 10), (8, 5), (6, 7), (7, 6), (4, 12), (9, 15), (5, 11), (2, 14), (6, 8), (3, 13), (8, 6), (6, 9),
+    (9, 16), (6, 10), (7, 7), (6, 12), (3, 14), (2, 15), (6, 11), (7, 8), (8, 7), (4, 13), (2, 16), (7, 9),
+    (8, 8), (4, 14), (7, 10), (8, 9), (7, 12), (6, 13), (3, 15), (8, 10), (5, 14), (8, 12), (7, 11), (3, 16),
+    (7, 13), (4, 15), (6, 14), (8, 11), (8, 13), (4, 16), (5, 15), (7, 14), (5, 16), (8, 14), (6, 15), (6, 16),
+    (7, 15), (8, 15), (7, 16), (8, 16),
 )
-BESIDE_AT = (44, 54, 65, 76, 87, 97, 108)
+BESIDE_AT = (84, 95, 107, 119, 131, 143, 155)
+SQUARES_AT = (106, 119, 133)
 SLOTS = 3
 NN = (((1,), (0,)), ((), ()))
 NT = (((1,), (1,)), ((), ()))
@@ -113,13 +118,13 @@
 
 def step_kernel(lines, chunks, tables, in_cols, *refs):
     count = len(chunks)
-    (in_far, out_far, state, target, weight_t, pos, head_t, embed, traits), refs = refs[:9], refs[9:]
+    (in_far, out_far, w_in, w_out, state, target, weight_t, pos, head_t, embed, traits), refs = refs[:11], refs[11:]
     finals, refs = refs[:4], refs[4:]
-    (d_in, d_head, d_two, d_full, d_one, few_sum, cond_full, time_act, all_traits), scratch = refs[:9], refs[9:]
+    (d_in, d_head, d_two, d_full, d_one, few_sum, cond_full, time_act, all_traits, weight_sq), scratch = refs[:10], refs[10:]
     held, by_y, by_x, by_z = (scratch[k * count : (k + 1) * count] for k in range(4))
     send, recv, zsend, zrecv, wsend, wrecv = scratch[4 * count : 4 * count + 6]
     scratch = scratch[4 * count + 6 :]
-    (stage_wide, stage_tall, land_wide, land_tall, free_wide, free_tall, fetch, d_mod, d_fm, few), scratch = scratch[:10], scratch[10:]
+    (stage_wide, stage_tall, land_wide, land_tall, free_wide, free_tall, fetch, weight_load, d_mod, d_fm, few), scratch = scratch[:11], scratch[11:]
     (
         stream, hat_one, hat_two, root_one, root_two, a_low, qkv_low, mixed, proj, b_low, active, mlp, d_mlp,
     ), scratch = scratch[:13], scratch[13:]
@@ -607,6 +612,40 @@
             for step in range(1, shards):
                 to_others(3, act_own, act_slot, step).wait_send()
 
+    room = (stream, hat_one, hat_two, proj, mlp)
+    rounds = []
+    for source in (w_in,):
+        blocks = [(start, min(tokens, source.shape[0] - start)) for start in range(0, source.shape[0], tokens)]
+        rounds.append([(source.at[pl.ds(start, size), :], size) for start, size in blocks])
+    rounds.append([(w_out.at[:, pl.ds(k * width, width)], w_out.shape[0]) for k in range(w_out.shape[1] // width)])
+
+    def weight_copies(index):
+        return [
+            pltpu.make_async_copy(source, room[k].at[pl.ds(0, size), :], weight_load.at[k])
+            for k, (source, size) in enumerate(rounds[index])
+        ]
+
+    def squares_step(index):
+        if index > 0:
+            total = jnp.zeros((1, width), jnp.float32)
+            for k, copy in enumerate(weight_copies(index - 1)):
+                copy.wait()
+                size = rounds[index - 1][k][1]
+                whole = size // 64 * 64
+
+                def add(block, carry):
+                    value = room[k][pl.ds(pl.multiple_of(block * 64, 64), 64), :]
+                    return carry + jnp.sum(value * value, 0, keepdims=True)
+
+                total = lax.fori_loop(0, size // 64, add, total)
+                if whole < size:
+                    value = room[k][whole:size, :]
+                    total += jnp.sum(value * value, 0, keepdims=True)
+            weight_sq[:, (index - 1) * width : index * width] = total
+        if index < len(rounds):
+            for copy in weight_copies(index):
+                copy.start()
+
     beside = (side0, side1, side2, side3, side4, side5, side6)
     low = jnp.bfloat16
     per = tokens // TOK
@@ -653,9 +692,8 @@
 
     relay_tick(4)
     arrived(3)
+    blocks_of(3 * width, cut, qkv_block)
     relay_tick(5)
-    blocks_of(3 * width, cut, qkv_block)
-    relay_tick(6)
     lane = lax.broadcasted_iota(jnp.int32, (TOK, 128), 1)
     first = lane < 64
     scale = 0.125
@@ -679,6 +717,7 @@
         return carry
 
     lax.fori_loop(0, width // 128, attend, 0)
+    relay_tick(6)
     relay_tick(7)
     arrived(2)
     for image in range(per):
@@ -820,6 +859,8 @@
     for j, (k, i) in enumerate(ORDER):
         if j in BESIDE_AT:
             beside[BESIDE_AT.index(j)]()
+        if j in SQUARES_AT:
+            squares_step(SQUARES_AT.index(j))
         if k == 0:
             step, arg = steps[i]
             step(arg)
@@ -888,6 +929,7 @@
         ((rows, width), full),
         ((rows, width), low),
         ((rows, traits.shape[1]), full),
+        ((1, 2 * width), full),
     ]
     pass_scratch = [
         ((tokens, width), full),
@@ -965,7 +1007,7 @@
             dma((count, 2, PIECES)),
         ]
         + [pltpu.VMEM((SLOTS,) + item, low) for item in (wide, tall)] * 2
-        + [pltpu.SemaphoreType.REGULAR, pltpu.SemaphoreType.REGULAR, dma((9,))]
+        + [pltpu.SemaphoreType.REGULAR, pltpu.SemaphoreType.REGULAR, dma((9,)), dma((5,))]
         + [pltpu.VMEM(*item) for item in ((modul_shape, full), (fmod_shape, full), (few, full))]
         + [pltpu.VMEM(*item) for item in pass_scratch]
         + [pltpu.VMEM(*item) for item in scratch]
@@ -1359,10 +1401,9 @@
 
     def window(item_t, starts, tiles, lanes):
         rows = item_t.shape[0]
-        offsets = [o * rows - start * 128 for o, start in enumerate(starts)]
-        most = max(offsets)
+        most = max(o * rows - start * 128 for o, start in enumerate(starts))
         padded = jnp.pad(item_t, ((most, tiles * 128 - rows), (0, lanes - item_t.shape[1])))
-        begin = most - jnp.asarray(offsets, jnp.int32)[place]
+        begin = most - lax.rem(place * rows, 128)
         return lax.dynamic_slice_in_dim(padded, begin, tiles * 128, 0).astype(low)
 
     in_cols, head_cols, embed_cols = in_t.shape[0], head_t.shape[0], embed_t.shape[0]
@@ -1389,9 +1430,9 @@
 
 def total_kernel(
     tables, segments, fc2, fc1, attn_out, qkv, w_in, w_out, w_head, w_embed,
-    d_in, d_fin, d_two, d_one, d_full, few, cond_full, time_act, traits, c_in, c_out, c_head, c_embed,
+    d_in, d_fin, d_two, d_one, d_full, few, cond_full, time_act, traits, weight_sq, c_in, c_out, c_head, c_embed,
     g_in, g_out, g_head, g_embed, n_in, n_out, n_head, n_embed, stats,
-    own_t, own_out, grad_t, head_t, t_out, t_head, t_embed, v_in, v_out, v_head, v_embed,
+    own_t, own_out, grad_t, head_t, t_out, t_head, t_embed, v_head, v_embed,
     load, write, fetch,
 ):
     (in_starts, in_tiles), (head_starts, head_tiles), (embed_starts, embed_tiles), shards = tables
@@ -1402,8 +1443,7 @@
     full, low = jnp.float32, jnp.bfloat16
     span = lane_span(width, w_embed.shape[1])
 
-    weights = ((w_in, v_in), (w_out, v_out), (w_head, v_head), (w_embed, v_embed))
-    reads = [pltpu.make_async_copy(source, target, load.at[k]) for k, (source, target) in enumerate(weights)]
+    reads = [pltpu.make_async_copy(w_head, v_head, load.at[0]), pltpu.make_async_copy(w_embed, v_embed, load.at[1])]
     for copy in reads:
         copy.start()
 
@@ -1566,17 +1606,9 @@
 
     for copy in reads:
         copy.wait()
-    for k, (_, value) in enumerate(weights):
-        rows, cols = value.shape
-
-        def squares(index, carry):
-            block = value[pl.ds(pl.multiple_of(index * 64, 64), 64), :]
-            return carry + jnp.sum(block * block, 0, keepdims=True)
-
-        total = lax.fori_loop(0, rows // 64, squares, jnp.zeros((1, cols), full))
-        if rows % 64:
-            block = value[rows // 64 * 64 :, :]
-            total += jnp.sum(block * block, 0, keepdims=True)
+    squares = [weight_sq[:, k * width : (k + 1) * width] for k in (0, 1)]
+    squares += [jnp.sum(value[...] * value[...], 0, keepdims=True) for value in (v_head, v_embed)]
+    for k, total in enumerate(squares):
         start = 2 * span + k * 128
         stats[:, start : start + 128] = jnp.broadcast_to(jnp.sum(total, -1, keepdims=True) / 128.0, (1, 128))
     write_in.wait()
@@ -1603,7 +1635,7 @@
         ((in_tiles * 128, width), full),
         ((head_tiles * 128, width), full),
     ]
-    scratch += [(item.shape, full) for item in weights[1:]] + [(item.shape, full) for item in weights]
+    scratch += [(item.shape, full) for item in weights[1:]] + [(item.shape, full) for item in weights[2:]]
     return pl.pallas_call(
         functools.partial(total_kernel, tables, segments),
         out_shape=[jax.ShapeDtypeStruct(*item) for item in shapes],
@@ -1737,7 +1769,7 @@
         lines,
         tables,
         in_cols,
-        [in_t, out_t],
+        [in_t, out_t] + list(weights[:2]),
         [
             state.reshape(images * TOK, PATCH),
             velocity.reshape(images * TOK, PATCH),
@@ -1748,7 +1780,7 @@
             traits,
         ],
     )
-    d_in, d_fin, d_two, d_full, d_one, few_sum, cond_full, time_act, all_traits = sums[4:]
+    d_in, d_fin, d_two, d_full, d_one, few_sum, cond_full, time_act, all_traits, weight_sq = sums[4:]
     loss_sum = few_sum[PATCH, 0]
     rows_old = (state_in_row, state_out_row, state_head_row[None], state_embed_row[None])
     cols_old = (state_in_col, state_out_col, state_head_col[None], state_embed_col[None])
@@ -1756,7 +1788,7 @@
         tables,
         sums[:4],
         weights,
-        [d_in, d_fin, d_two, d_one, d_full, few_sum, cond_full, time_act, all_traits],
+        [d_in, d_fin, d_two, d_one, d_full, few_sum, cond_full, time_act, all_traits, weight_sq],
         cols_old,
     )
     totals, cols_new = outs[:4], outs[4:]

time: 313 us -> 298 us (0.952)
  Pallas kernels: 258 us -> 247 us
  between operations: 5.59 us -> 2.33 us
    pallas_call x1, Pallas kernels: 17.2 us -> 12.1 us  [finish_call(): pl.pallas_call(functools.partial(finish_kernel, shards, sizes), out_shape...]
    pallas_call x1, Pallas kernels: 18.5 us -> 15.1 us  [total_call(): pl.pallas_call(functools.partial(total_kernel, tables, segments), out_sha...]
where the time goes in v7:
time: 298 us; the launch traced here: 292 us
  Pallas kernels  247 us (83%)
  other arithmetic  23.3 us (8%)
  local copies, waits for them, and re-layouts  19.1 us (6%)
    pallas_call x1, Pallas kernels, step_call(): pl.pallas_call(functools.partial(step_kernel, lines, chunks, tables, in_c...  220 us
    pallas_call x1, Pallas kernels, total_call(): pl.pallas_call(functools.partial(total_kernel, tables, segments), out_sha...  15.1 us
    pallas_call x1, Pallas kernels, finish_call(): pl.pallas_call(functools.partial(finish_kernel, shards, sizes), out_shape...  12.1 us
    convert_element_type x3, local copies, waits for them, and re-layouts, window(): return lax.dynamic_slice_in_dim(padded, begin, tiles * 128, 0).astype(low)  10.7 us
    broadcast_in_dim x1, other arithmetic, on_device(): news[0][None]  9.25 us

profile of v7, /device:TPU:0, one launch (start us, length us, event | category | flops | bytes accessed | tf_op | source)
XLA Modules:
  0.0 292.1 jit_solution(11010679403397169411)
XLA Ops:
  0.7 5.5 %fusion.refs_0_ = bf16[2560,768]{1,0:T(8,128)(2,1)} fusion(s32[]{:T(128)S(6)} %select_n.16, f32[2496,768]{1,0:T(8,128)} %bitcast.50), kind=kLoop, calls=%fused_computation.1 | loop fusion | bytes 11599876 | tf_op jit(solution)/shard_map/convert_element_type | solution.py:1407
  6.2 3.1 %fusion.1.refs_8_ = bf16[768,768]{1,0:T(8,128)(2,1)} fusion(s32[]{:T(128)S(6)} %select_n.17, f32[580,768]{1,0:T(8,128)} %bitcast.55), kind=kLoop, calls=%fused_computation.5 | loop fusion | bytes 2961412 | tf_op jit(solution)/shard_map/convert_element_type | solution.py:1407
  9.3 2.1 fusion.2.refs_9_
  12.6 0.9 add_convert_fusion.refs_4_
  13.5 0.9 copy.41
  14.4 1.3 bitcast_convert_fusion.refs_1_
  15.6 0.8 reshape.84.refs_5_
  16.5 220.3 %shard_map.322 = (bf16[768,3072]{1,0:T(8,128)(2,1)}, bf16[3072,768]{1,0:T(8,128)(2,1)}, bf16[768,768]{1,0:T(8,128)(2,1)}, bf16[2304,768]{1,0:T(8,128)(2,1)}, bf1...) custom-call(bf16[2560,768]{1,0:T(8,128)(2,1)} %fusion.refs_0_, ...), custom_call_target="tpu_custom_call" | custom-call | tf_op jit(solution)/shard_map/pallas_call | solution.py:992
  236.8 1.3 broadcast_in_dim.56.c_head
  238.0 15.1 %shard_map.323 = (f32[2496,768]{1,0:T(8,128)}, f32[192,3840]{1,0:T(8,128)}, f32[580,768]{1,0:T(8,128)}, f32[192,1273]{1,0:T(8,128)}, f32[1,2496]{1,0:T(1,128)}, ...) custom-call(bf16[768,3072]{1,0:T(8,128)(2,1)} %get-tuple-element.51.fc2, ...), custom_call_target="tpu_custom_call" | custom-call | tf_op jit(solution)/shard_map/pallas_call | solution.py:1639
  253.1 0.6 broadcast_in_dim.59.r_embed
  253.7 0.6 broadcast_in_dim.58.r_head
  254.3 12.1 %shard_map.324 = (f32[1,768]{1,0:T(1,128)}, f32[1,3840]{1,0:T(1,128)}, f32[1,768]{1,0:T(1,128)}, f32[1,1273]{1,0:T(1,128)}, f32[1,768]{1,0:T(1,128)}, /*index=5*...) custom-call(f32[1,13824]{1,0:T(1,128)} %get-tuple-element.64.own, f32[1,768]{1,0:T(1,128)} %r_in.1, ...), custom_call_target="tpu_custom_call" | custom-call | tf_op jit(solution)/shard_map/pallas_call | solution.py:1697
  266.4 0.7 reduce.7
  267.1 0.7 rsqrt.39
  267.8 2.3 subtract_bitcast_fusion.3
  270.2 3.6 %subtract_bitcast_fusion.2 = f32[768,580]{0,1:T(8,128)} fusion(f32[580,768]{1,0:T(8,128)} %get-tuple-element.68, f32[580]{0:T(1024)S(1)} %rsqrt.38, f32[768]{0:T(1024)S(1)} %reduce.6, f32[768,580]{0,1:T(8,128)} %param.27), kind=kLoop, calls=%fused_computation.6 | loop fusion | flops 1336320 | bytes 5350672 | tf_op jit(solution)/shard_map/transpose | solution.py:1814
  273.9 3.8 %subtract_bitcast_fusion.1 = f32[1,3840,192]{1,2,0:T(8,128)} fusion(f32[192,3840]{1,0:T(8,128)} %get-tuple-element.67, f32[192]{0:T(256)S(1)} %bitcast.67, f32[3840]{0:T(1024)S(1)} %reduce.5, f32[1,3840,192]{1,2,0:T(8,128)S(1)} %copy-done.1), kind=kLoop, calls=%fused_computation.3 | loop fusion | flops 2211840 | bytes 8863488 | tf_op jit(solution)/shard_map/broadcast_in_dim | solution.py:1833
  277.9 9.2 %subtract_bitcast_fusion = f32[1,768,2496]{1,2,0:T(8,128)} fusion(f32[2496,768]{1,0:T(8,128)} %get-tuple-element.66, f32[2496]{0:T(1024)S(1)} %rsqrt_reduce_fusion, f32[768]{0:T(1024)S(1)} %reduce.3, f32[1,768,2496]{1,2,0:T(8,128)} %param.25), kind=kLoop, calls=%fused_computation.2 | loop fusion | flops 5750784 | bytes 23016192 | tf_op jit(solution)/shard_map/broadcast_in_dim | solution.py:1832
  287.1 0.6 reduce.2
  287.8 0.6 reduce
  288.4 1.2 slice.6
  289.6 0.6 copy.47
  290.2 0.6 copy.48
  (72 shorter events, 1.4 us)
Async XLA Ops:
  6.2 5.2 %copy-start.20 = (s32[2]{0:T(128)S(1)}, s32[2]{0:T(128)}, u32[]{:S(2)}) copy-start(s32[2]{0:T(128)} %param.22) | copy-start | bytes 28
  6.2 5.4 %copy-start.21 = (s32[2]{0:T(128)S(1)}, s32[2]{0:T(128)}, u32[]{:S(2)}) copy-start(s32[2]{0:T(128)} %param.23) | copy-start | bytes 28
  6.2 5.4 %copy-start.22 = (s32[2]{0:T(128)S(1)}, s32[2]{0:T(128)}, u32[]{:S(2)}) copy-start(s32[2]{0:T(128)} %param.24) | copy-start | bytes 28
  6.2 6.2 %copy-start.4 = (f32[2,4096]{1,0:T(2,128)S(1)}, f32[2,4096]{1,0:T(2,128)}, u32[]{:S(2)}) copy-start(f32[2,4096]{1,0:T(2,128)} %param.19) | copy-start | bytes 98308
  6.2 6.3 %copy-start.5 = (f32[2,4096]{1,0:T(2,128)S(1)}, f32[2,4096]{1,0:T(2,128)}, u32[]{:S(2)}) copy-start(f32[2,4096]{1,0:T(2,128)} %param.20) | copy-start | bytes 98308
  6.2 8.2 %copy-start = (f32[1,3840,192]{1,2,0:T(8,128)S(1)}, f32[1,3840,192]{1,2,0:T(8,128)}, u32[]{:S(2)}) copy-start(f32[1,3840,192]{1,2,0:T(8,128)} %param.26) | copy-start | bytes 8847364
  11.7 0.6 copy-start.3
  12.3 3.3 %copy-start.6 = (f32[2,4096]{1,0:T(2,128)S(1)}, f32[2,4096]{1,0:T(2,128)}, u32[]{:S(2)}) copy-start(f32[2,4096]{1,0:T(2,128)} %param.21) | copy-start | bytes 98308
  238.0 15.1 %copy-start.11 = (f32[1273]{0:T(1024)S(1)}, f32[1273]{0:T(1024)}, u32[]{:S(2)}) copy-start(f32[1273]{0:T(1024)} %param.35) | copy-start | bytes 15280
  238.0 15.7 %copy-start.13 = (f32[768]{0:T(1024)S(1)}, f32[768]{0:T(1024)}, u32[]{:S(2)}) copy-start(f32[768]{0:T(1024)} %param.33) | copy-start | bytes 9220
  238.0 29.8 %copy-start.2 = (f32[1273,192]{0,1:T(8,128)S(1)}, f32[1273,192]{0,1:T(8,128)}, u32[]{:S(2)}) copy-start(f32[1273,192]{0,1:T(8,128)} %param.28) | copy-start | bytes 2932996
  253.1 17.1 %copy-start.18 = (f32[1,580]{1,0:T(1,128)S(1)}, f32[1,580]{1,0:T(1,128)}, u32[]{:S(2)}) copy-start(f32[1,580]{1,0:T(1,128)} %get-tuple-element.75) | copy-start | bytes 6964
  266.4 3.7 %copy-start.17 = (f32[1,768]{1,0:T(1,128)S(1)}, f32[1,768]{1,0:T(1,128)}, u32[]{:S(2)}) copy-start(f32[1,768]{1,0:T(1,128)} %get-tuple-element.80) | copy-start | bytes 9220
  270.1 3.7 %copy-start.9 = (f32[1,3840]{1,0:T(1,128)S(1)}, f32[1,3840]{1,0:T(1,128)}, u32[]{:S(2)}) copy-start(f32[1,3840]{1,0:T(1,128)} %get-tuple-element.79) | copy-start | bytes 46084
  270.1 3.8 %copy-start.19 = (f32[1,192]{1,0:T(1,128)S(1)}, f32[1,192]{1,0:T(1,128)}, u32[]{:S(2)}) copy-start(f32[1,192]{1,0:T(1,128)} %get-tuple-element.116) | copy-start | bytes 2308
  270.1 3.8 %copy-start.1 = (f32[1,3840,192]{1,2,0:T(8,128)S(1)}, f32[1,3840,192]{1,2,0:T(8,128)}, u32[]{:S(2)}) copy-start(f32[1,3840,192]{1,2,0:T(8,128)} %param.26) | copy-start | bytes 8847364
  270.2 7.6 %copy-start.7 = (f32[580]{0:T(1024)}, f32[580]{0:T(1024)S(1)}, u32[]{:S(2)}) copy-start(f32[580]{0:T(1024)S(1)} %reduce.1) | copy-start | bytes 6964
  273.9 3.9 %copy-start.16 = (f32[1,768]{1,0:T(1,128)S(1)}, f32[1,768]{1,0:T(1,128)}, u32[]{:S(2)}) copy-start(f32[1,768]{1,0:T(1,128)} %get-tuple-element.78) | copy-start | bytes 9220
  273.9 3.9 %copy-start.10 = (f32[1,2496]{1,0:T(1,128)S(1)}, f32[1,2496]{1,0:T(1,128)}, u32[]{:S(2)}) copy-start(f32[1,2496]{1,0:T(1,128)} %get-tuple-element.114) | copy-start | bytes 29956
  277.8 9.3 %copy-start.12 = (f32[1,1273]{1,0:T(1,128)S(1)}, f32[1,1273]{1,0:T(1,128)}, u32[]{:S(2)}) copy-start(f32[1,1273]{1,0:T(1,128)} %get-tuple-element.76) | copy-start | bytes 15280
  277.9 9.9 %copy-start.15 = (f32[1,768]{1,0:T(1,128)S(1)}, f32[1,768]{1,0:T(1,128)}, u32[]{:S(2)}) copy-start(f32[1,768]{1,0:T(1,128)} %get-tuple-element.74) | copy-start | bytes 9220
  277.9 11.7 %copy-start.23 = (f32[1,128]{1,0:T(1,128)S(1)}, f32[1,128]{1,0:T(1,128)}, u32[]{:S(2)}) copy-start(f32[1,128]{1,0:T(1,128)} %get-tuple-element.65) | copy-start | bytes 1540
  277.9 11.7 %copy-start.14 = (f32[1,768]{1,0:T(1,128)S(1)}, f32[1,768]{1,0:T(1,128)}, u32[]{:S(2)}) copy-start(f32[1,768]{1,0:T(1,128)} %get-tuple-element.113) | copy-start | bytes 9220
  277.9 12.3 %copy-start.8 = (f32[1,3840]{1,0:T(1,128)S(1)}, f32[1,3840]{1,0:T(1,128)}, u32[]{:S(2)}) copy-start(f32[1,3840]{1,0:T(1,128)} %get-tuple-element.115) | copy-start | bytes 46084

commit v8 on v7

--- a/solution.py
+++ b/solution.py
@@ -119,8 +119,9 @@
 def step_kernel(lines, chunks, tables, in_cols, *refs):
     count = len(chunks)
     (in_far, out_far, w_in, w_out, state, target, weight_t, pos, head_t, embed, traits), refs = refs[:11], refs[11:]
-    finals, refs = refs[:4], refs[4:]
+    (own_t, own_out), refs = refs[:2], refs[2:]
     (d_in, d_head, d_two, d_full, d_one, few_sum, cond_full, time_act, all_traits, weight_sq), scratch = refs[:10], refs[10:]
+    finals, scratch = scratch[:4], scratch[4:]
     held, by_y, by_x, by_z = (scratch[k * count : (k + 1) * count] for k in range(4))
     send, recv, zsend, zrecv, wsend, wrecv = scratch[4 * count : 4 * count + 6]
     scratch = scratch[4 * count + 6 :]
@@ -867,6 +868,32 @@
         else:
             stages[k](i)
 
+    out_rows = out_far.shape[0]
+
+    def own_copies(place):
+        copies = [
+            pltpu.make_async_copy(
+                finals[array].at[pl.ds(row, rows), :], own_t.at[pl.ds(at, rows), :], fetch.at[n]
+            )
+            for n, (array, row, rows, at) in enumerate(own_segments(width, in_cols, in_starts, out_rows, shards)[place])
+        ]
+        for n, array, lane in ((2, 2, 0), (3, 0, width)):
+            copies.append(
+                pltpu.make_async_copy(
+                    finals[array].at[pl.ds(place * out_rows, out_rows), :],
+                    own_out.at[:, pl.ds(lane, finals[array].shape[1])],
+                    fetch.at[n],
+                )
+            )
+        return copies
+
+    for place in range(shards):
+
+        @pl.when(shard == place)
+        def _():
+            for copy in own_copies(place):
+                copy.start()
+
     side_end()
     for i in range(count):
         if turn_away(i, SLOTS) is None:
@@ -895,6 +922,13 @@
             last_copy(i, which, side, core).wait_send()
 
         sides(i, action)
+
+    for place in range(shards):
+
+        @pl.when(shard == place)
+        def _():
+            for copy in own_copies(place):
+                copy.wait()
 
 
 def step_call(lines, tables, in_cols, far, light):
@@ -919,7 +953,7 @@
     tall = max(item for item, chunk in zip(sizes, chunks) if chunk[0] != 0)
     dma = pltpu.SemaphoreType.DMA
     heavy = [(width, 4 * width), (4 * width, width), (width, width), (3 * width, width)]
-    shapes = [(item, low) for item in heavy] + [
+    shapes = [((in_lanes, width), low), ((far[1].shape[0], 5 * width), low)] + [
         ((rows, in_lanes), low),
         ((rows, head_lanes), low),
         ((rows, head_lanes), low),
@@ -993,8 +1027,9 @@
         functools.partial(step_kernel, lines, chunks, tables, in_cols),
         out_shape=[jax.ShapeDtypeStruct(*item) for item in shapes],
         in_specs=[anywhere] * len(far) + [vmem] * len(light),
-        out_specs=[vmem] * len(shapes),
-        scratch_shapes=[pltpu.VMEM((r, c), low) for r, c in sizes]
+        out_specs=[anywhere] * 2 + [vmem] * (len(shapes) - 2),
+        scratch_shapes=[pltpu.VMEM(item, low) for item in heavy]
+        + [pltpu.VMEM((r, c), low) for r, c in sizes]
         + [pltpu.VMEM((r // 2, c), low) for r, c in sizes]
         + [pltpu.VMEM((r // 4, c), low) for r, c in sizes]
         + [pltpu.VMEM((lines - 1, r // 4 // PIECES, c), low) for r, c in sizes]
@@ -1429,14 +1464,13 @@
 
 
 def total_kernel(
-    tables, segments, fc2, fc1, attn_out, qkv, w_in, w_out, w_head, w_embed,
+    tables, segments, far_t, far_out, w_in, w_out, w_head, w_embed,
     d_in, d_fin, d_two, d_one, d_full, few, cond_full, time_act, traits, weight_sq, c_in, c_out, c_head, c_embed,
-    g_in, g_out, g_head, g_embed, n_in, n_out, n_head, n_embed, stats,
-    own_t, own_out, grad_t, head_t, t_out, t_head, t_embed, v_head, v_embed,
+    g_in, g_out, g_head, g_embed, n_in, n_out, n_head, n_embed, stats, loss,
+    own_t, own_out, grad_t, head_t, head_fresh, t_out, t_head, t_embed, v_head, v_embed,
     load, write, fetch,
 ):
     (in_starts, in_tiles), (head_starts, head_tiles), (embed_starts, embed_tiles), shards = tables
-    arrays = (fc2, fc1, attn_out, qkv)
     shard = lax.axis_index("shard")
     width = cond_full.shape[1]
     in_cols, head_cols, embed_cols, out_cols = (item.shape[0] for item in (w_in, w_head, w_embed, w_out))
@@ -1448,23 +1482,11 @@
         copy.start()
 
     def heavy_copies(place):
-        copies = []
-        for k, (array, row, rows, at) in enumerate(segments[place]):
-            copies.append(
-                pltpu.make_async_copy(
-                    arrays[array].at[pl.ds(row, rows), :], own_t.at[pl.ds(at, rows), :], fetch.at[k]
-                )
-            )
-        for k, array in ((2, 2), (3, 0)):
-            lane = 0 if array == 2 else width
-            copies.append(
-                pltpu.make_async_copy(
-                    arrays[array].at[pl.ds(place * out_cols, out_cols), :],
-                    own_out.at[:, pl.ds(lane, arrays[array].shape[1])],
-                    fetch.at[k],
-                )
-            )
-        return copies
+        copies = [
+            pltpu.make_async_copy(far_t.at[pl.ds(at, rows), :], own_t.at[pl.ds(at, rows), :], fetch.at[k])
+            for k, (_, _, rows, at) in enumerate(segments[place])
+        ]
+        return copies + [pltpu.make_async_copy(far_out, own_out, fetch.at[2])]
 
     for place in range(shards):
 
@@ -1548,9 +1570,11 @@
     pltpu.make_async_copy(t_embed, g_embed, write.at[3]).start()
     value = jnp.concatenate([t_embed[...], jnp.zeros((embed_cols, lanes_all - w_embed.shape[1]), full)], 1)
     square = value * value
-    fresh = decayed(c_embed[...], to_lanes(jnp.sum(square, -1, keepdims=True)), w_embed.shape[1])
-    n_embed[...] = fresh
+    fresh = decayed(c_embed[...].reshape(1, embed_cols), to_lanes(jnp.sum(square, -1, keepdims=True)), w_embed.shape[1])
+    n_embed[...] = fresh.reshape(n_embed.shape)
     put(7 * width, jnp.sum(square, 0, keepdims=True), jnp.sum(square * to_column(1.0 / fresh), 0, keepdims=True))
+
+    loss[0, 0] = few[PATCH : PATCH + 1, 0:1][0, 0]
 
     head_t[...] = mxu(d_two[...], time_act[...], TN) + mxu(d_fin[...], cond, TN)
     last_place = [o for o in range(shards) if 0 <= 3 * width // 128 - head_starts[o] < head_tiles][-1]
@@ -1568,7 +1592,9 @@
             t_head[...] = head_t[lead : lead + head_cols, :]
 
     pltpu.make_async_copy(t_head, g_head, write.at[2]).start()
-    by_blocks(lambda start, size: t_head[start : start + size, :], head_cols, c_head, n_head, 6 * width)
+    head_state = c_head[...].reshape(1, head_cols)
+    by_blocks(lambda start, size: t_head[start : start + size, :], head_cols, head_state, head_fresh, 6 * width)
+    n_head[...] = head_fresh[...].reshape(n_head.shape)
 
     for place in range(shards):
 
@@ -1623,24 +1649,25 @@
 def total_call(tables, heavy, weights, light, cols):
     (in_starts, in_tiles), (_, head_tiles), _, shards = tables
     low, full = jnp.bfloat16, jnp.float32
-    width = heavy[2].shape[0]
+    width = heavy[0].shape[1]
     w_in, w_out, w_head, w_embed = weights
     lanes = 2 * lane_span(width, w_embed.shape[1]) + 4 * 128
     segments = own_segments(width, w_in.shape[0], in_starts, w_out.shape[0], shards)
-    shapes = [(item.shape, full) for item in weights] + [(item.shape, full) for item in cols] + [((1, lanes), full)]
+    shapes = [(item.shape, full) for item in weights] + [(item.shape, full) for item in cols] + [((1, lanes), full), ((1, 1), full)]
     anywhere, vmem = pl.BlockSpec(memory_space=pl.ANY), pl.BlockSpec(memory_space=pltpu.VMEM)
     scratch = [
         ((in_tiles * 128, width), low),
         (w_out.shape, low),
         ((in_tiles * 128, width), full),
         ((head_tiles * 128, width), full),
+        ((1, w_head.shape[0]), full),
     ]
     scratch += [(item.shape, full) for item in weights[1:]] + [(item.shape, full) for item in weights[2:]]
     return pl.pallas_call(
         functools.partial(total_kernel, tables, segments),
         out_shape=[jax.ShapeDtypeStruct(*item) for item in shapes],
-        in_specs=[anywhere] * 8 + [vmem] * (len(light) + 4),
-        out_specs=[anywhere] * 4 + [vmem] * 5,
+        in_specs=[anywhere] * 6 + [vmem] * (len(light) + 4),
+        out_specs=[anywhere] * 4 + [vmem] * 5 + [pl.BlockSpec(memory_space=pltpu.SMEM)],
         scratch_shapes=[pltpu.VMEM(*item) for item in scratch] + [pltpu.SemaphoreType.DMA((4,))] * 3,
         compiler_params=pltpu.CompilerParams(vmem_limit_bytes=60 * 1024 * 1024),
     )(*heavy, *weights, *light, *cols)
@@ -1675,30 +1702,33 @@
     for rows, _ in sizes:
         starts.append(start)
         start += -(-rows // 128) * 128
-    update, means = jnp.zeros((1, 1), jnp.float32), []
+    update, means, news = jnp.zeros((1, 1), jnp.float32), [], []
     for k, (rows, cols) in enumerate(sizes):
-        row = decay * states[k][...] + (1.0 - decay) * (total[:, starts[k] : starts[k] + rows] / cols + eps_one)
-        fresh[k][...] = row
+        row = decay * states[k][...].reshape(1, rows) + (1.0 - decay) * (
+            total[:, starts[k] : starts[k] + rows] / cols + eps_one
+        )
+        fresh[k][...] = row.reshape(fresh[k].shape)
+        news.append(row)
         mean = jnp.mean(row, -1, keepdims=True)
         means.append(mean)
         update += mean * jnp.sum(total[:, start + starts[k] : start + starts[k] + rows] / row, -1, keepdims=True)
     update = jnp.sqrt(update / sum(rows * cols for rows, cols in sizes))
-    rms[...] = jnp.broadcast_to(update, rms.shape)
+    rms[0, 0] = update[0, 0]
     factor = jnp.maximum(1.0, update / clip_level)
     for k, (rows, cols) in enumerate(sizes):
         first = 2 * start + k * 128
         weight = jnp.sqrt(jnp.sum(total[:, first : first + 128], -1, keepdims=True) / (rows * cols))
-        scales[k][...] = rate * jnp.maximum(eps_two, weight) / factor * lax.rsqrt(fresh[k][...] / means[k])
+        scales[k][...] = rate * jnp.maximum(eps_two, weight) / factor * lax.rsqrt(news[k] / means[k])
 
 
 def finish_call(shards, sizes, stats, rows_old):
     full = jnp.float32
-    shapes = [((1, rows), full) for rows, _ in sizes] * 2 + [((1, 128), full)]
+    shapes = [(item.shape, full) for item in rows_old] + [((1, rows), full) for rows, _ in sizes] + [((1, 1), full)]
     return pl.pallas_call(
         functools.partial(finish_kernel, shards, sizes),
         out_shape=[jax.ShapeDtypeStruct(*item) for item in shapes],
         in_specs=[pl.BlockSpec(memory_space=pltpu.VMEM)] * 5,
-        out_specs=[pl.BlockSpec(memory_space=pltpu.VMEM)] * len(shapes),
+        out_specs=[pl.BlockSpec(memory_space=pltpu.VMEM)] * (len(shapes) - 1) + [pl.BlockSpec(memory_space=pltpu.SMEM)],
         scratch_shapes=[
             pltpu.VMEM((shards,) + stats.shape, full),
             pltpu.SemaphoreType.DMA((shards - 1,)),
@@ -1780,18 +1810,18 @@
             traits,
         ],
     )
-    d_in, d_fin, d_two, d_full, d_one, few_sum, cond_full, time_act, all_traits, weight_sq = sums[4:]
-    loss_sum = few_sum[PATCH, 0]
-    rows_old = (state_in_row, state_out_row, state_head_row[None], state_embed_row[None])
-    cols_old = (state_in_col, state_out_col, state_head_col[None], state_embed_col[None])
-    *outs, stats = total_call(
+    d_in, d_fin, d_two, d_full, d_one, few_sum, cond_full, time_act, all_traits, weight_sq = sums[2:]
+    rows_old = (state_in_row, state_out_row, state_head_row, state_embed_row)
+    cols_old = (state_in_col, state_out_col, state_head_col, state_embed_col)
+    *outs, stats, loss = total_call(
         tables,
-        sums[:4],
+        sums[:2],
         weights,
         [d_in, d_fin, d_two, d_one, d_full, few_sum, cond_full, time_act, all_traits, weight_sq],
         cols_old,
     )
     totals, cols_new = outs[:4], outs[4:]
+    loss_sum = loss.reshape(())
     blocks = lax.axis_size("rep") // (2 * lines)
     if blocks > 1:
         apart = [[k * 2 * lines + j for k in range(blocks)] for j in range(2 * lines)]
@@ -1799,19 +1829,19 @@
         cols_new, plain, scaled = [], [], []
         for gradient, col_state in zip(totals, cols_old):
             square = gradient * gradient
-            fresh = decay * col_state + (1.0 - decay) * (jnp.mean(square, 1)[None] + eps_one)
+            fresh = decay * col_state + (1.0 - decay) * (jnp.mean(square, 1).reshape(col_state.shape) + eps_one)
             pad = (0, -gradient.shape[1] % 128)
             cols_new.append(fresh)
             plain.append(jnp.pad(jnp.sum(square, 0), pad))
-            scaled.append(jnp.pad(jnp.sum(square / fresh[0][:, None], 0), pad))
+            scaled.append(jnp.pad(jnp.sum(square / fresh.reshape(-1)[:, None], 0), pad))
         spans = sum(item.shape[0] for item in plain) * 2
         stats = jnp.concatenate(plain + scaled + [stats[0, spans:]])[None]
     sizes = [(weight.shape[1], weight.shape[0] * shard_count) for weight in weights]
     *outs, rms = finish_call(shard_count, sizes, stats, rows_old)
     rows_new, scales = outs[:4], outs[4:]
-    update_rms = rms[0, 0]
+    update_rms = rms.reshape(())
     news = [
-        (weight - gradient * scale * lax.rsqrt(col_next[0])[:, None]).T
+        (weight - gradient * scale * lax.rsqrt(col_next.reshape(-1))[:, None]).T
         for weight, gradient, scale, col_next in zip(weights, totals, scales, cols_new)
     ]
     return (
@@ -1825,10 +1855,10 @@
         cols_new[0],
         rows_new[1],
         cols_new[1],
-        rows_new[2][0],
-        cols_new[2][0],
-        rows_new[3][0],
-        cols_new[3][0],
+        rows_new[2],
+        cols_new[2],
+        rows_new[3],
+        cols_new[3],
         news[0][None],
         news[1][None],
         news[2],

time: 298 us -> 290 us (0.973)
  the two profiles are of different devices: /device:TPU:0 before, /device:TPU:7 now
where the time goes in v8:
time: 290 us; the launch traced here: 285 us
  Pallas kernels  247 us (85%)
  other arithmetic  21 us (7%)
  local copies, waits for them, and re-layouts  14.8 us (5%)
  between operations  2.92 us (1%)
    pallas_call x1, Pallas kernels, step_call(): pl.pallas_call(functools.partial(step_kernel, lines, chunks, tables, in_c...  224 us
    pallas_call x1, Pallas kernels, total_call(): pl.pallas_call(functools.partial(total_kernel, tables, segments), out_sha...  16.3 us
    broadcast_in_dim x1, other arithmetic, on_device(): news[0][None]  9.44 us
    convert_element_type x3, local copies, waits for them, and re-layouts, window(): return lax.dynamic_slice_in_dim(padded, begin, tiles * 128, 0).astype(low)  8.09 us
    pallas_call x1, Pallas kernels, finish_call(): pl.pallas_call(functools.partial(finish_kernel, shards, sizes), out_shape...  6.55 us

profile of v8, /device:TPU:7, one launch (start us, length us, event | category | flops | bytes accessed | tf_op | source)
XLA Modules:
  0.0 285.4 jit_solution(17841639530701944305)
XLA Ops:
  0.7 5.6 %fusion.refs_0_ = bf16[2560,768]{1,0:T(8,128)(2,1)} fusion(s32[]{:T(128)S(6)} %select_n.16, f32[2496,768]{1,0:T(8,128)} %bitcast.47), kind=kLoop, calls=%fused_computation.1 | loop fusion | bytes 11599876 | tf_op jit(solution)/shard_map/convert_element_type | solution.py:1442
  6.4 1.3 bitcast_convert_fusion.refs_1_
  7.6 0.1 reshape.83
  7.8 0.1 reshape.82
  8.1 0.9 add_convert_fusion.refs_4_
  9.0 0.8 reshape.84.refs_5_
  9.8 0.9 copy.41
  10.7 1.5 fusion.1.refs_8_
  12.2 0.9 fusion.2.refs_9_
  13.4 0.6 broadcast_in_dim.20
  14.1 0.6 constant_dynamic-update-slice_fusion.refs_10_
  14.6 223.8 %shard_map.322 = (bf16[2560,768]{1,0:T(8,128)(2,1)}, bf16[192,3840]{1,0:T(8,128)(2,1)}, bf16[64,2560]{1,0:T(8,128)(2,1)}, bf16[64,768]{1,0:T(8,128)(2,1)}, bf16[...) custom-call(bf16[2560,768]{1,0:T(8,128)(2,1)} %fusion.refs_0_, ...), custom_call_target="tpu_custom_call" | custom-call | tf_op jit(solution)/shard_map/pallas_call | solution.py:1026
  238.5 16.3 %shard_map.323 = (f32[2496,768]{1,0:T(8,128)}, f32[192,3840]{1,0:T(8,128)}, f32[580,768]{1,0:T(8,128)}, f32[192,1273]{1,0:T(8,128)}, f32[1,2496]{1,0:T(1,128)}, ...) custom-call(bf16[2560,768]{1,0:T(8,128)(2,1)} %get-tuple-element.49.far_t, ...), custom_call_target="tpu_custom_call" | custom-call | tf_op jit(solution)/shard_map/pallas_call | solution.py:1666
  254.8 6.5 %shard_map.324 = (f32[1,768]{1,0:T(1,128)}, f32[1,3840]{1,0:T(1,128)}, f32[768]{0:T(1024)}, f32[1273]{0:T(1024)}, f32[1,768]{1,0:T(1,128)}, /*index=5*/f32[1,384...) custom-call(f32[1,13824]{1,0:T(1,128)} %get-tuple-element.62.own, f32[1,768]{1,0:T(1,128)} %r_in.1, ...), custom_call_target="tpu_custom_call" | custom-call | tf_op jit(solution)/shard_map/pallas_call | solution.py:1727
  261.3 0.7 rsqrt_reduce_fusion
  262.1 0.7 reduce
  262.8 9.4 %subtract_bitcast_fusion = f32[1,768,2496]{1,2,0:T(8,128)} fusion(f32[2496,768]{1,0:T(8,128)} %get-tuple-element.64, f32[2496]{0:T(1024)S(1)} %rsqrt_reduce_fusion, f32[768]{0:T(1024)S(1)} %reduce, f32[1,768,2496]{1,2,0:T(8,128)} %param.25), kind=kLoop, calls=%fused_computation.2 | loop fusion | flops 5750784 | bytes 23016192 | tf_op jit(solution)/shard_map/broadcast_in_dim | solution.py:1862
  272.4 3.8 %subtract_bitcast_fusion.1 = f32[1,3840,192]{1,2,0:T(8,128)} fusion(f32[192,3840]{1,0:T(8,128)} %get-tuple-element.65, f32[192]{0:T(256)S(1)} %bitcast.64, f32[3840]{0:T(1024)S(1)} %reduce.2, f32[1,3840,192]{1,2,0:T(8,128)S(1)} %copy-done.1), kind=kLoop, calls=%fused_computation.3 | loop fusion | flops 2211840 | bytes 8863488 | tf_op jit(solution)/shard_map/broadcast_in_dim | solution.py:1863
  276.3 3.6 %subtract_bitcast_fusion.2 = f32[768,580]{0,1:T(8,128)} fusion(f32[580,768]{1,0:T(8,128)} %get-tuple-element.66, f32[580]{0:T(1024)S(1)} %rsqrt.30, f32[768]{0:T(1024)S(1)} %reduce.3, f32[768,580]{0,1:T(8,128)} %param.27), kind=kLoop, calls=%fused_computation.6 | loop fusion | flops 1336320 | bytes 5350672 | tf_op jit(solution)/shard_map/transpose | solution.py:1844
  280.0 1.1 subtract_bitcast_fusion.3
  281.7 0.6 copy.49
  282.3 0.6 copy.50
  282.9 0.6 copy.51
  283.5 0.6 copy.52
  (63 shorter events, 0.6 us)
Async XLA Ops:
  0.7 5.7 %copy-start = (f32[1,3840,192]{1,2,0:T(8,128)S(1)}, f32[1,3840,192]{1,2,0:T(8,128)}, u32[]{:S(2)}) copy-start(f32[1,3840,192]{1,2,0:T(8,128)} %param.26) | copy-start | bytes 8847364
  6.3 1.3 copy-start.6
  6.3 1.4 copy-start.7
  6.3 1.6 copy-start.19
  6.3 2.6 copy-start.8
  6.3 4.3 %copy-start.2 = (f32[768,580]{0,1:T(8,128)S(1)}, f32[768,580]{0,1:T(8,128)}, u32[]{:S(2)}) copy-start(f32[768,580]{0,1:T(8,128)} %param.27) | copy-start | bytes 5345284
  7.6 4.6 %copy-start.3 = (f32[1273,192]{0,1:T(8,128)S(1)}, f32[1273,192]{0,1:T(8,128)}, u32[]{:S(2)}) copy-start(f32[1273,192]{0,1:T(8,128)} %param.28) | copy-start | bytes 2932996
  8.1 5.2 %copy-start.20 = (s32[2]{0:T(128)S(1)}, s32[2]{0:T(128)}, u32[]{:S(2)}) copy-start(s32[2]{0:T(128)} %param.23) | copy-start | bytes 28
  8.1 5.2 %copy-start.21 = (s32[2]{0:T(128)S(1)}, s32[2]{0:T(128)}, u32[]{:S(2)}) copy-start(s32[2]{0:T(128)} %param.24) | copy-start | bytes 28
  262.8 9.5 %copy-start.17 = (f32[1,192]{1,0:T(1,128)S(1)}, f32[1,192]{1,0:T(1,128)}, u32[]{:S(2)}) copy-start(f32[1,192]{1,0:T(1,128)} %get-tuple-element.114) | copy-start | bytes 2308
  262.8 9.5 %copy-start.10 = (f32[1,3840]{1,0:T(1,128)S(1)}, f32[1,3840]{1,0:T(1,128)}, u32[]{:S(2)}) copy-start(f32[1,3840]{1,0:T(1,128)} %get-tuple-element.77) | copy-start | bytes 46084
  262.8 9.5 %copy-start.1 = (f32[1,3840,192]{1,2,0:T(8,128)S(1)}, f32[1,3840,192]{1,2,0:T(8,128)}, u32[]{:S(2)}) copy-start(f32[1,3840,192]{1,2,0:T(8,128)} %param.26) | copy-start | bytes 8847364
  272.3 3.8 %copy-start.13 = (f32[580]{0:T(1024)S(1)}, f32[580]{0:T(1024)}, u32[]{:S(2)}) copy-start(f32[580]{0:T(1024)} %get-tuple-element.116) | copy-start | bytes 6964
  272.3 3.9 %copy-start.16 = (f32[1,768]{1,0:T(1,128)S(1)}, f32[1,768]{1,0:T(1,128)}, u32[]{:S(2)}) copy-start(f32[1,768]{1,0:T(1,128)} %get-tuple-element.78) | copy-start | bytes 9220
  276.2 3.7 %copy-start.18 = (f32[192]{0:T(256)S(1)}, f32[192]{0:T(256)}, u32[]{:S(2)}) copy-start(f32[192]{0:T(256)} %get-tuple-element.118) | copy-start | bytes 2308
  276.2 3.7 %copy-start.12 = (f32[1,1273]{1,0:T(1,128)S(1)}, f32[1,1273]{1,0:T(1,128)}, u32[]{:S(2)}) copy-start(f32[1,1273]{1,0:T(1,128)} %get-tuple-element.79) | copy-start | bytes 15280
  276.2 3.8 %copy-start.4 = (f32[1273,192]{0,1:T(8,128)S(1)}, f32[1273,192]{0,1:T(8,128)}, u32[]{:S(2)}) copy-start(f32[1273,192]{0,1:T(8,128)} %param.28) | copy-start | bytes 2932996
  276.2 3.8 %copy-start.5 = (f32[192,1273]{1,0:T(8,128)S(1)}, f32[192,1273]{1,0:T(8,128)}, u32[]{:S(2)}) copy-start(f32[192,1273]{1,0:T(8,128)} %get-tuple-element.67) | copy-start | bytes 2932996
  276.2 5.5 %copy-start.15 = (f32[1,768]{1,0:T(1,128)S(1)}, f32[1,768]{1,0:T(1,128)}, u32[]{:S(2)}) copy-start(f32[1,768]{1,0:T(1,128)} %get-tuple-element.111) | copy-start | bytes 9220
  276.3 6.0 %copy-start.9 = (f32[1,3840]{1,0:T(1,128)S(1)}, f32[1,3840]{1,0:T(1,128)}, u32[]{:S(2)}) copy-start(f32[1,3840]{1,0:T(1,128)} %get-tuple-element.113) | copy-start | bytes 46084
  276.3 6.6 %copy-start.14 = (f32[768]{0:T(1024)S(1)}, f32[768]{0:T(1024)}, u32[]{:S(2)}) copy-start(f32[768]{0:T(1024)} %get-tuple-element.115) | copy-start | bytes 9220
  276.3 7.2 %copy-start.11 = (f32[1273]{0:T(1024)S(1)}, f32[1273]{0:T(1024)}, u32[]{:S(2)}) copy-start(f32[1273]{0:T(1024)} %get-tuple-element.117) | copy-start | bytes 15280

commit v9 on v8

--- a/solution.py
+++ b/solution.py
@@ -693,7 +693,7 @@
 
     relay_tick(4)
     arrived(3)
-    blocks_of(3 * width, cut, qkv_block)
+    blocks_of(3 * width, width, qkv_block)
     relay_tick(5)
     lane = lax.broadcasted_iota(jnp.int32, (TOK, 128), 1)
     first = lane < 64
@@ -738,14 +738,14 @@
         ).astype(low)
 
     arrived(1)
-    blocks_of(4 * width, cut, upper_block)
+    blocks_of(4 * width, 2 * cut, upper_block)
     arrived(0)
     finish()
 
     def mlp_block(part):
         mlp[:, part] = mxu(active[...], fc2[part, :], NT)
 
-    blocks_of(width, cut, mlp_block)
+    blocks_of(width, width, mlp_block)
     loss = jnp.zeros((), jnp.float32)
     g_last = jnp.zeros((PATCH, width), jnp.float32)
     for image in range(per):
@@ -1612,9 +1612,6 @@
     lead = lax.rem(shard * in_cols, 128)
     write_in = pltpu.make_async_copy(grad_t.at[pl.ds(pl.multiple_of(lead, 64), in_cols), :], g_in, write.at[0])
     write_in.start()
-    by_blocks(
-        lambda start, size: grad_t[pl.ds(pl.multiple_of(lead + start, 64), size), :], in_cols, c_in, n_in, 0
-    )
 
     sums = jnp.zeros((out_cols, 1), full)
     for index in range(5):
@@ -1629,6 +1626,10 @@
         value = t_out[:, index * width : (index + 1) * width]
         square = value * value
         put(width + index * width, jnp.sum(square, 0, keepdims=True), jnp.sum(square * column, 0, keepdims=True))
+
+    by_blocks(
+        lambda start, size: grad_t[pl.ds(pl.multiple_of(lead + start, 64), size), :], in_cols, c_in, n_in, 0
+    )
 
     for copy in reads:
         copy.wait()

time: 290 us -> 290 us (level)
  the two profiles are of different devices: /device:TPU:7 before, /device:TPU:0 now
where the time goes in v9:
time: 290 us; the launch traced here: 285 us
  Pallas kernels  246 us (85%)
  other arithmetic  21 us (7%)
  local copies, waits for them, and re-layouts  14.8 us (5%)
  between operations  2.92 us (1%)
    pallas_call x1, Pallas kernels, step_call(): pl.pallas_call(functools.partial(step_kernel, lines, chunks, tables, in_c...  216 us
    pallas_call x1, Pallas kernels, total_call(): pl.pallas_call(functools.partial(total_kernel, tables, segments), out_sha...  15.4 us
    pallas_call x1, Pallas kernels, finish_call(): pl.pallas_call(functools.partial(finish_kernel, shards, sizes), out_shape...  14.6 us
    broadcast_in_dim x1, other arithmetic, on_device(): news[0][None]  9.44 us
    convert_element_type x3, local copies, waits for them, and re-layouts, window(): return lax.dynamic_slice_in_dim(padded, begin, tiles * 128, 0).astype(low)  8.09 us

profile of v9, /device:TPU:0, one launch (start us, length us, event | category | flops | bytes accessed | tf_op | source)
XLA Modules:
  0.0 284.9 jit_solution(14917860042693151499)
XLA Ops:
  0.7 5.6 %fusion.refs_0_ = bf16[2560,768]{1,0:T(8,128)(2,1)} fusion(s32[]{:T(128)S(6)} %select_n.16, f32[2496,768]{1,0:T(8,128)} %bitcast.47), kind=kLoop, calls=%fused_computation.1 | loop fusion | bytes 11599876 | tf_op jit(solution)/shard_map/convert_element_type | solution.py:1442
  6.4 1.3 bitcast_convert_fusion.refs_1_
  7.6 0.1 reshape.83
  7.8 0.1 reshape.82
  8.1 0.9 add_convert_fusion.refs_4_
  9.0 0.8 reshape.84.refs_5_
  9.8 0.9 copy.41
  10.7 1.5 fusion.1.refs_8_
  12.2 0.9 fusion.2.refs_9_
  13.4 0.6 broadcast_in_dim.20
  14.1 0.6 constant_dynamic-update-slice_fusion.refs_10_
  14.6 216.2 %shard_map.322 = (bf16[2560,768]{1,0:T(8,128)(2,1)}, bf16[192,3840]{1,0:T(8,128)(2,1)}, bf16[64,2560]{1,0:T(8,128)(2,1)}, bf16[64,768]{1,0:T(8,128)(2,1)}, bf16[...) custom-call(bf16[2560,768]{1,0:T(8,128)(2,1)} %fusion.refs_0_, ...), custom_call_target="tpu_custom_call" | custom-call | tf_op jit(solution)/shard_map/pallas_call | solution.py:1026
  230.8 15.4 %shard_map.323 = (f32[2496,768]{1,0:T(8,128)}, f32[192,3840]{1,0:T(8,128)}, f32[580,768]{1,0:T(8,128)}, f32[192,1273]{1,0:T(8,128)}, f32[1,2496]{1,0:T(1,128)}, ...) custom-call(bf16[2560,768]{1,0:T(8,128)(2,1)} %get-tuple-element.49.far_t, ...), custom_call_target="tpu_custom_call" | custom-call | tf_op jit(solution)/shard_map/pallas_call | solution.py:1667
  246.2 14.6 %shard_map.324 = (f32[1,768]{1,0:T(1,128)}, f32[1,3840]{1,0:T(1,128)}, f32[768]{0:T(1024)}, f32[1273]{0:T(1024)}, f32[1,768]{1,0:T(1,128)}, /*index=5*/f32[1,384...) custom-call(f32[1,13824]{1,0:T(1,128)} %get-tuple-element.62.own, f32[1,768]{1,0:T(1,128)} %r_in.1, ...), custom_call_target="tpu_custom_call" | custom-call | tf_op jit(solution)/shard_map/pallas_call | solution.py:1728
  260.8 0.7 rsqrt_reduce_fusion
  261.6 0.7 reduce
  262.3 9.4 %subtract_bitcast_fusion = f32[1,768,2496]{1,2,0:T(8,128)} fusion(f32[2496,768]{1,0:T(8,128)} %get-tuple-element.64, f32[2496]{0:T(1024)S(1)} %rsqrt_reduce_fusion, f32[768]{0:T(1024)S(1)} %reduce, f32[1,768,2496]{1,2,0:T(8,128)} %param.25), kind=kLoop, calls=%fused_computation.2 | loop fusion | flops 5750784 | bytes 23016192 | tf_op jit(solution)/shard_map/broadcast_in_dim | solution.py:1863
  271.8 3.8 %subtract_bitcast_fusion.1 = f32[1,3840,192]{1,2,0:T(8,128)} fusion(f32[192,3840]{1,0:T(8,128)} %get-tuple-element.65, f32[192]{0:T(256)S(1)} %bitcast.64, f32[3840]{0:T(1024)S(1)} %reduce.2, f32[1,3840,192]{1,2,0:T(8,128)S(1)} %copy-done.1), kind=kLoop, calls=%fused_computation.3 | loop fusion | flops 2211840 | bytes 8863488 | tf_op jit(solution)/shard_map/broadcast_in_dim | solution.py:1864
  275.8 3.6 %subtract_bitcast_fusion.2 = f32[768,580]{0,1:T(8,128)} fusion(f32[580,768]{1,0:T(8,128)} %get-tuple-element.66, f32[580]{0:T(1024)S(1)} %rsqrt.30, f32[768]{0:T(1024)S(1)} %reduce.3, f32[768,580]{0,1:T(8,128)} %param.27), kind=kLoop, calls=%fused_computation.6 | loop fusion | flops 1336320 | bytes 5350672 | tf_op jit(solution)/shard_map/transpose | solution.py:1845
  279.5 1.1 subtract_bitcast_fusion.3
  281.2 0.6 copy.49
  281.8 0.6 copy.50
  282.4 0.6 copy.51
  283.0 0.6 copy.52
  (63 shorter events, 0.6 us)
Async XLA Ops:
  0.7 5.7 %copy-start = (f32[1,3840,192]{1,2,0:T(8,128)S(1)}, f32[1,3840,192]{1,2,0:T(8,128)}, u32[]{:S(2)}) copy-start(f32[1,3840,192]{1,2,0:T(8,128)} %param.26) | copy-start | bytes 8847364
  6.3 1.3 copy-start.6
  6.3 1.4 copy-start.7
  6.3 1.6 copy-start.19
  6.3 2.6 copy-start.8
  6.3 4.3 %copy-start.2 = (f32[768,580]{0,1:T(8,128)S(1)}, f32[768,580]{0,1:T(8,128)}, u32[]{:S(2)}) copy-start(f32[768,580]{0,1:T(8,128)} %param.27) | copy-start | bytes 5345284
  7.6 4.6 %copy-start.3 = (f32[1273,192]{0,1:T(8,128)S(1)}, f32[1273,192]{0,1:T(8,128)}, u32[]{:S(2)}) copy-start(f32[1273,192]{0,1:T(8,128)} %param.28) | copy-start | bytes 2932996
  8.1 5.2 %copy-start.20 = (s32[2]{0:T(128)S(1)}, s32[2]{0:T(128)}, u32[]{:S(2)}) copy-start(s32[2]{0:T(128)} %param.23) | copy-start | bytes 28
  8.1 5.2 %copy-start.21 = (s32[2]{0:T(128)S(1)}, s32[2]{0:T(128)}, u32[]{:S(2)}) copy-start(s32[2]{0:T(128)} %param.24) | copy-start | bytes 28
  262.3 9.5 %copy-start.17 = (f32[1,192]{1,0:T(1,128)S(1)}, f32[1,192]{1,0:T(1,128)}, u32[]{:S(2)}) copy-start(f32[1,192]{1,0:T(1,128)} %get-tuple-element.114) | copy-start | bytes 2308
  262.3 9.5 %copy-start.10 = (f32[1,3840]{1,0:T(1,128)S(1)}, f32[1,3840]{1,0:T(1,128)}, u32[]{:S(2)}) copy-start(f32[1,3840]{1,0:T(1,128)} %get-tuple-element.77) | copy-start | bytes 46084
  262.3 9.5 %copy-start.1 = (f32[1,3840,192]{1,2,0:T(8,128)S(1)}, f32[1,3840,192]{1,2,0:T(8,128)}, u32[]{:S(2)}) copy-start(f32[1,3840,192]{1,2,0:T(8,128)} %param.26) | copy-start | bytes 8847364
  271.8 3.8 %copy-start.13 = (f32[580]{0:T(1024)S(1)}, f32[580]{0:T(1024)}, u32[]{:S(2)}) copy-start(f32[580]{0:T(1024)} %get-tuple-element.116) | copy-start | bytes 6964
  271.8 3.9 %copy-start.16 = (f32[1,768]{1,0:T(1,128)S(1)}, f32[1,768]{1,0:T(1,128)}, u32[]{:S(2)}) copy-start(f32[1,768]{1,0:T(1,128)} %get-tuple-element.78) | copy-start | bytes 9220
  275.7 3.7 %copy-start.18 = (f32[192]{0:T(256)S(1)}, f32[192]{0:T(256)}, u32[]{:S(2)}) copy-start(f32[192]{0:T(256)} %get-tuple-element.118) | copy-start | bytes 2308
  275.7 3.7 %copy-start.12 = (f32[1,1273]{1,0:T(1,128)S(1)}, f32[1,1273]{1,0:T(1,128)}, u32[]{:S(2)}) copy-start(f32[1,1273]{1,0:T(1,128)} %get-tuple-element.79) | copy-start | bytes 15280
  275.7 3.8 %copy-start.4 = (f32[1273,192]{0,1:T(8,128)S(1)}, f32[1273,192]{0,1:T(8,128)}, u32[]{:S(2)}) copy-start(f32[1273,192]{0,1:T(8,128)} %param.28) | copy-start | bytes 2932996
  275.7 3.8 %copy-start.5 = (f32[192,1273]{1,0:T(8,128)S(1)}, f32[192,1273]{1,0:T(8,128)}, u32[]{:S(2)}) copy-start(f32[192,1273]{1,0:T(8,128)} %get-tuple-element.67) | copy-start | bytes 2932996
  275.7 5.5 %copy-start.15 = (f32[1,768]{1,0:T(1,128)S(1)}, f32[1,768]{1,0:T(1,128)}, u32[]{:S(2)}) copy-start(f32[1,768]{1,0:T(1,128)} %get-tuple-element.111) | copy-start | bytes 9220
  275.7 6.0 %copy-start.9 = (f32[1,3840]{1,0:T(1,128)S(1)}, f32[1,3840]{1,0:T(1,128)}, u32[]{:S(2)}) copy-start(f32[1,3840]{1,0:T(1,128)} %get-tuple-element.113) | copy-start | bytes 46084
  275.8 6.6 %copy-start.14 = (f32[768]{0:T(1024)S(1)}, f32[768]{0:T(1024)}, u32[]{:S(2)}) copy-start(f32[768]{0:T(1024)} %get-tuple-element.115) | copy-start | bytes 9220
  275.8 7.2 %copy-start.11 = (f32[1273]{0:T(1024)S(1)}, f32[1273]{0:T(1024)}, u32[]{:S(2)}) copy-start(f32[1273]{0:T(1024)} %get-tuple-element.117) | copy-start | bytes 15280
